TPU v7x, 32 devices: a whole 2x2x4 slice. The times are simulated.
32 devices in a mesh: req: 8 (over z, x), row: 2 (over core), col: 2 (over y).
Axes of the slice: x: 2, y: 2, z: 4, core: 2. Of those that a mesh axis runs over, the one named last changes fastest.
Arguments:
- image_qkv: bfloat16 [192, 24, 3, 1280], P(('req', 'row'), 'col'), parts along dimension 0, may hold values from -6 to 6
- text_kv: bfloat16 [768, 2, 1280], P(('req', 'row'), None, 'col'), parts along dimension 0, may hold values from -6 to 6
- gain_query: float32 [64], replicated, may hold values from 1 to 3
- gain_key: float32 [64], replicated, may hold values from 1 to 3
- gain_text: float32 [64], replicated, may hold values from 1 to 3
- out_weight: bfloat16 [1280, 2432], P('col', 'row'), may hold values from -0.15625 to 0.15625
- final_weight: bfloat16 [64, 2432], P(None, 'row'), may hold values from -0.125 to 0.125
- hidden: bfloat16 [192, 24, 2432], P(('req', 'row'), 'col'), parts along dimension 0, may hold values from -6 to 6
- modulation: float32 [24, 2432], P('req'), parts along dimension 0, may hold values from -3 to 3
- latent: float32 [384, 768], P(('req', 'row'), 'col'), parts along dimension 0, may hold values from -6 to 6
- step_index: int32 [8], P('req'), parts along dimension 0, may hold values from 0 to 20
- step_count: int32 [8], P('req'), parts along dimension 0, may hold values from 1 to 5
Outputs:
- velocity: float32 [384, 768], P(('req', 'row'), 'col'), parts along dimension 0
- latent_next: float32 [384, 768], P(('req', 'row'), 'col'), parts along dimension 0
There are 8 independent parts, one for each index of `req`. A program takes and returns all parts, laid end to end along the dimension named above; an argument that names none is the same for every part. Nothing has to cross between parts.
All inputs are finite; a program needn't handle non-finite values.
Results may differ from a plain program's by a relative error of at most 0.009.
Values may be sent and summed in bfloat16 or wider, within the bound.
No kernel may reach another device: no remote copies, remote signals or barrier semaphores. Data moves between devices by JAX's collectives and lax.ppermute only.
A program may use at most 128 MiB of HBM per device.

v0:
```python
import functools
import math

import jax
import jax.numpy as jnp
from jax import lax
from jax.experimental import pallas as pl
from jax.experimental.pallas import tpu as pltpu
from jax.sharding import PartitionSpec as P

HEAD = 64
CH = 16
PATCH = 2
STEPS = 28
SHIFT_FACTOR = 3.0
LANES = 128
EPS = 1e-06
VMEM_LIMIT = 16 * 1024 * 1024
VMEM_MOST = 60 * 1024 * 1024
LOADS = 9
FIRST = 768
SWAP = [(0, 1), (1, 0)]


def noise_level(step_number):
    fraction = 1.0 - step_number.astype(jnp.float32) / STEPS
    return SHIFT_FACTOR * fraction / (1.0 + (SHIFT_FACTOR - 1.0) * fraction)


def same_head(width):
    row = lax.broadcasted_iota(jnp.int32, (width, width), 0) // HEAD
    col = lax.broadcasted_iota(jnp.int32, (width, width), 1) // HEAD
    return (row == col).astype(jnp.bfloat16)


def head_norms(pairs):
    ones = same_head(LANES)
    squares = []
    for x, _ in pairs:
        for at in range(0, x.shape[1], LANES):
            square = x[:, at : at + LANES] * x[:, at : at + LANES]
            high = square.astype(jnp.bfloat16)
            low = (square - high.astype(jnp.float32)).astype(jnp.bfloat16)
            squares.append(jnp.concatenate([high, low], axis=1))
    totals = jnp.dot(
        jnp.concatenate(squares, axis=0),
        jnp.concatenate([ones, ones], axis=0),
        preferred_element_type=jnp.float32,
    )
    inverse = lax.rsqrt(totals * (1.0 / HEAD) + EPS)
    results, start = [], 0
    for x, gain in pairs:
        gain = jnp.concatenate([gain, gain], axis=1)
        pieces = []
        for at in range(0, x.shape[1], LANES):
            factor = inverse[start : start + x.shape[0]]
            pieces.append((x[:, at : at + LANES] * factor * gain).astype(jnp.bfloat16))
            start += x.shape[0]
        results.append(jnp.concatenate(pieces, axis=1))
    return results


def load_half(x_ref, held, sems, column):
    tokens, _, width = held.shape
    at = pl.multiple_of(column * width, LANES)
    step = tokens // sems.shape[0]
    copies = [
        pltpu.make_async_copy(
            x_ref.at[start : start + step, :, pl.ds(at, width)],
            held.at[start : start + step],
            sems.at[start // step],
        )
        for start in range(0, tokens, step)
    ]
    for copy in copies:
        copy.start()
    return [(slice(at * step, at * step + step), copy) for at, copy in enumerate(copies)]


def halves(ref):
    rows = ref.shape[0] // 2
    return ref.at[:rows], ref.at[rows:]


def split_kernel(
    x_ref,
    gain_q_ref,
    gain_k_ref,
    gain_t_ref,
    q_first_ref,
    q_second_ref,
    kv_ref,
    gains,
    held,
    sems,
    gain_sems,
):
    blocks = load_half(x_ref, held, sems, 1 - lax.axis_index("col"))
    gain_copies = [
        pltpu.make_async_copy(ref, gains.at[at : at + 1], gain_sems.at[at])
        for at, ref in enumerate((gain_q_ref, gain_k_ref, gain_t_ref))
    ]
    for copy in gain_copies:
        copy.start()
    cut = q_first_ref.shape[0]
    k_ref, v_ref = halves(kv_ref)
    for rows, copy in blocks:
        copy.wait()
        q, k, v = held[rows].astype(jnp.float32).transpose(1, 0, 2).astype(jnp.bfloat16)
        k_ref[rows] = k
        v_ref[rows] = v
        if rows.stop <= cut:
            q_first_ref[rows] = q
        else:
            q_second_ref[rows.start - cut : rows.stop - cut] = q
    for copy in gain_copies:
        copy.wait()


def q_norm_kernel(x_ref, gains, out_ref):
    (out_ref[...],) = head_norms([(x_ref[...].astype(jnp.float32), gains[0:1])])


def kv_norm_kernel(x_ref, gains, out_ref):
    (k_ref, v_ref), (k_out, v_out) = halves(x_ref), halves(out_ref)
    v_out[...] = v_ref[...]
    (k_out[...],) = head_norms([(k_ref[...].astype(jnp.float32), gains[1:2])])


def keys_and_values(refs):
    pairs = [halves(ref) for ref in refs]
    return [keys for keys, _ in pairs], [values for _, values in pairs]


def prep_own_kernel(
    x_ref,
    text_ref,
    gains,
    mine_ref,
    theirs_ref,
    kv_ref,
    q_ref,
    gains_out,
    weight_ref,
    held,
    sems,
    stack_sems,
):
    tokens = q_ref.shape[0]
    k_ref, v_ref = halves(kv_ref)
    gains_out[...] = gains[...]
    blocks = load_half(x_ref, held, sems, lax.axis_index("col"))
    rows = mine_ref.shape[0]
    row = lax.axis_index("row")
    stacks = [
        pltpu.make_async_copy(
            ref, weight_ref.at[pl.ds(pl.multiple_of(place * rows, 16), rows)], stack_sems.at[at]
        )
        for at, (ref, place) in enumerate(((mine_ref, row), (theirs_ref, 1 - row)))
    ]
    for stack in stacks:
        stack.start()
    text = text_ref[...].astype(jnp.float32).transpose(1, 0, 2)
    v_ref[tokens:] = text[1].astype(jnp.bfloat16)
    for _, copy in blocks:
        copy.wait()
    q, k, v = held[...].transpose(1, 0, 2)
    v_ref[:tokens] = v
    k_ref[:tokens], k_ref[tokens:], q_ref[...] = head_norms(
        [
            (k.astype(jnp.float32), gains[1:2]),
            (text[0], gains[2:3]),
            (q.astype(jnp.float32), gains[0:1]),
        ]
    )
    for stack in stacks:
        stack.wait()


def attend(q, keys_refs, values_refs, attended_ref):
    tokens, width = q.shape
    first = lax.broadcasted_iota(jnp.int32, (tokens, LANES), 1) < HEAD
    scale = math.log2(math.e) / math.sqrt(HEAD)
    zero = jnp.zeros((tokens, LANES), jnp.bfloat16)
    ones = jnp.ones((sum(ref.shape[0] for ref in keys_refs), LANES), jnp.bfloat16)

    def scores_of(at):
        lanes = slice(at, at + LANES)
        keys = jnp.concatenate([ref[:, lanes] for ref in keys_refs], axis=0)
        block = q[:, lanes]
        both = jnp.concatenate(
            [jnp.where(first, block, zero), jnp.where(first, zero, block)], axis=0
        )
        return lax.dot_general(
            both, keys, (((1,), (1,)), ((), ())), preferred_element_type=jnp.float32
        )

    def finish(at, scores):
        lanes = slice(at, at + LANES)
        values = jnp.concatenate([ref[:, lanes] for ref in values_refs], axis=0)
        weights = jnp.exp2(scores * scale).astype(jnp.bfloat16)
        out = jnp.dot(
            weights,
            jnp.concatenate([values, ones], axis=1),
            preferred_element_type=jnp.float32,
        )
        weighted = jnp.where(first, out[:tokens, :LANES], out[tokens:, :LANES])
        total = jnp.where(first, out[:tokens, LANES:], out[tokens:, LANES:])
        attended_ref[:, lanes] = (weighted / total).astype(jnp.bfloat16)

    ahead = scores_of(0)
    for at in range(0, width, LANES):
        scores = ahead
        if at + LANES < width:
            ahead = scores_of(at + LANES)
        finish(at, scores)


def project(attended, weight_ref, start, upto, store, step):
    for at in range(start, upto, step):
        to = min(at + step, upto)
        product = lax.dot_general(
            attended,
            weight_ref[at:to],
            (((1,), (1,)), ((), ())),
            preferred_element_type=jnp.float32,
        )
        store(at, to, product.astype(jnp.bfloat16))


def attend_kernel(*refs):
    q_ref, (w_ref, out_ref, attended) = refs[0], refs[5:]
    attend(q_ref[...], *keys_and_values(refs[1:5]), attended)

    def keep(at, to, product):
        out_ref[:, at:to] = product

    project(attended[...], w_ref, 0, out_ref.shape[1], keep, FIRST)


def rest_kernel(attended_ref, w_ref, out_ref):
    features, start = w_ref.shape[0], w_ref.shape[0] - out_ref.shape[1]

    def keep(at, to, product):
        out_ref[:, at - start : to - start] = product

    project(attended_ref[...], w_ref, start, features, keep, 640)


def own_kernel(*refs):
    q_ref = refs[0]
    w_ref, hidden_ref, mod_ref, got_ref, mine_ref, theirs_ref = refs[5:11]
    out_ref, finals_ref, attended = refs[11:]
    attend(q_ref[...], *keys_and_values(refs[1:5]), attended)
    tile_rows = hidden_ref.shape[0]

    def keep(at, to, product):
        part = mod_ref[2:3, at:to] * product.astype(jnp.float32)
        held = jnp.concatenate(
            [hidden_ref[row, :, at:to].astype(jnp.float32) for row in range(tile_rows)], axis=0
        )
        out_ref[:, at:to] = held + part

    project(attended[...], w_ref, 0, w_ref.shape[0], keep, 640)
    upto, to = got_ref.shape
    out_ref[:upto, :to] += mod_ref[2:3, :to] * got_ref[...].astype(jnp.float32)
    is_first = lax.axis_index("row") == 0
    mine = mine_ref[...].astype(jnp.float32)
    theirs = theirs_ref[...].astype(jnp.float32)
    finals_ref[...] = jnp.concatenate(
        [jnp.where(is_first, mine, theirs), jnp.where(is_first, theirs, mine)], axis=1
    ).astype(jnp.bfloat16)


def one_hot(dims, condition):
    row = lax.broadcasted_iota(jnp.int32, dims, 0)
    col = lax.broadcasted_iota(jnp.int32, dims, 1)
    return jnp.where(condition(row, col), 1.0, 0.0).astype(jnp.bfloat16)


def to_pixels(velocity, tile_cols):
    tokens, values = velocity.shape
    side = values // PATCH
    out_rows, out_lanes = tokens // tile_cols * PATCH, tile_cols * side
    terms, rest = [], velocity
    for _ in range(3):
        term = rest.astype(jnp.bfloat16)
        rest = rest - term.astype(jnp.float32)
        terms.append(term)
    terms = jnp.concatenate(terms, axis=0)
    row = lax.broadcasted_iota(jnp.int32, (3 * tokens, out_lanes), 0)
    col = lax.broadcasted_iota(jnp.int32, (3 * tokens, out_lanes), 1)
    here = col // side == row % tile_cols
    total = jnp.zeros((out_rows, out_lanes), jnp.float32)
    for at in range(PATCH):
        spread = one_hot((values, out_lanes), lambda r, c: r == c % side + at * side)
        wide = jnp.dot(terms, spread, preferred_element_type=jnp.float32)
        wide = jnp.where(here, wide, 0.0).astype(jnp.bfloat16)
        pick = one_hot(
            (out_rows, 3 * tokens), lambda r, c: r == c % tokens // tile_cols * PATCH + at
        )
        total += jnp.dot(pick, wide, preferred_element_type=jnp.float32)
    return total


def final_kernel(
    start,
    index_ref,
    count_ref,
    mixed_ref,
    rest_ref,
    mod_ref,
    final_ref,
    latent_ref,
    *refs,
):
    velocity_ref, next_ref = refs[-2:]
    tokens = rest_ref.shape[0]
    step = 48
    parts = []
    for at in range(0, tokens, step):
        rows = slice(start + at, start + at + step)
        had = mixed_ref.shape[1] - rest_ref.shape[1]
        mixed = mixed_ref[rows]
        got = rest_ref[at : at + step].astype(jnp.float32)
        added = mixed[:, had:] + mod_ref[2:3, had:] * got
        mixed = jnp.concatenate([mixed[:, :had], added], axis=1) if had else added
        mean = jnp.mean(mixed, axis=-1, keepdims=True)
        centered = mixed - mean
        var = jnp.mean(centered * centered, axis=-1, keepdims=True)
        normed = (
            centered * lax.rsqrt(var + EPS) * (1.0 + mod_ref[1:2]) + mod_ref[0:1]
        ).astype(jnp.bfloat16)
        parts.append(
            lax.dot_general(
                normed,
                final_ref[...],
                (((1,), (1,)), ((), ())),
                preferred_element_type=jnp.float32,
            )
        )
    tile_cols = latent_ref.shape[1] // (final_ref.shape[0] // PATCH)
    velocity = to_pixels(jnp.concatenate(parts, axis=0), tile_cols)
    first = start // tile_cols * PATCH
    pixels = slice(first, first + velocity.shape[0])
    index = jnp.full(velocity.shape, index_ref[0], jnp.int32)
    count = jnp.full(velocity.shape, count_ref[0], jnp.int32)
    euler_step = noise_level(index + count) - noise_level(index)
    for before_ref, after_ref in zip(refs[:-2], refs[-2:]):
        after_ref[:first] = before_ref[:first]
    velocity_ref[pixels] = velocity
    next_ref[pixels] = latent_ref[pixels] + euler_step * velocity


def params(limit=VMEM_LIMIT):
    return pltpu.CompilerParams(vmem_limit_bytes=limit)


def lasting(duration):
    return pl.CostEstimate(
        flops=int(duration * 1e9), bytes_accessed=int(duration * 3e6), transcendentals=0
    )


def shape(dims, dtype=jnp.bfloat16):
    return jax.ShapeDtypeStruct(dims, dtype)


VMEM = pl.BlockSpec(memory_space=pltpu.VMEM)
ANY = pl.BlockSpec(memory_space=pl.ANY)
HBM = pl.BlockSpec(memory_space=pltpu.HBM)
SMEM = pl.BlockSpec(memory_space=pltpu.SMEM)


def on_device(
    image_qkv,
    text_kv,
    gain_query,
    gain_key,
    gain_text,
    out_weight,
    final_weight,
    hidden,
    modulation,
    latent,
    step_index,
    step_count,
):
    tile_rows, tile_cols, _, all_width = image_qkv.shape
    tokens = tile_rows * tile_cols
    words = text_kv.shape[0]
    width = all_width // lax.axis_size("col")
    features = hidden.shape[2]
    gains = [gain.reshape(1, HEAD) for gain in (gain_query, gain_key, gain_text)]
    x = image_qkv.reshape(tokens, 3, all_width)
    weight_half = out_weight.T
    held = pltpu.VMEM((tokens, 3, width), jnp.bfloat16)
    block = shape((tokens, width))

    loads = pltpu.SemaphoreType.DMA((LOADS,))
    cut = tile_rows // 3 * 2 * tile_cols
    chunks = ((0, cut), (cut, tokens))
    *q_raw, kv_raw, gains = pl.pallas_call(
        split_kernel,
        out_shape=tuple(shape((upto - start, width)) for start, upto in chunks)
        + (shape((2 * tokens, width)), shape((len(gains), HEAD), jnp.float32)),
        in_specs=[HBM] * 4,
        out_specs=(VMEM,) * 4,
        scratch_shapes=[held, loads, pltpu.SemaphoreType.DMA((len(gains),))],
        compiler_params=params(VMEM_MOST),
        name="split",
    )(x, *gains)

    weight_got = lax.ppermute(weight_half, "row", SWAP)
    final_got = lax.ppermute(final_weight, "row", SWAP)
    kv_own, q_own, gains_on, weight = pl.pallas_call(
        prep_own_kernel,
        out_shape=(
            shape((2 * (tokens + words), width)),
            block,
            shape(gains.shape, jnp.float32),
            shape((features, width)),
        ),
        in_specs=[HBM, VMEM, VMEM, ANY, ANY],
        out_specs=(VMEM,) * 4,
        scratch_shapes=[
            held,
            loads,
            pltpu.SemaphoreType.DMA((2,)),
        ],
        compiler_params=params(),
        name="prep_own",
    )(x, text_kv, gains, weight_half, weight_got)
    def normed(kernel, got, duration):
        return pl.pallas_call(
            kernel,
            out_shape=shape(got.shape),
            in_specs=[VMEM, VMEM],
            out_specs=VMEM,
            compiler_params=params(),
            cost_estimate=lasting(duration),
            name=kernel.__name__,
        )(got, gains_on)

    kv_got = normed(kv_norm_kernel, lax.ppermute(kv_raw, "col", SWAP), 0)
    q_got = [
        normed(q_norm_kernel, lax.ppermute(raw, "col", SWAP), duration)
        for raw, duration in zip(q_raw, (4, 1))
    ]
    pairs = []
    for kv in (kv_own, kv_got):
        pairs += [kv, lax.ppermute(kv, "row", SWAP)]

    def attended(q, projected, scratch):
        rows = q.shape[0]
        out_shape = (shape((rows, projected)),) + (() if scratch else (shape((rows, width)),))
        return pl.pallas_call(
            attend_kernel,
            out_shape=out_shape,
            in_specs=[VMEM] * 6,
            out_specs=(VMEM,) * len(out_shape),
            scratch_shapes=[pltpu.VMEM((rows, width), jnp.bfloat16)] if scratch else (),
            compiler_params=params(),
            name="attend",
        )(q, *pairs, weight)

    first, heads = attended(q_got[0], FIRST, False)
    first_got = lax.ppermute(first, "col", SWAP)
    rest = pl.pallas_call(
        rest_kernel,
        out_shape=shape((cut, features - FIRST)),
        in_specs=[VMEM] * 2,
        out_specs=VMEM,
        compiler_params=params(),
        name="rest",
    )(heads, weight)
    rest_got = lax.ppermute(rest, "col", SWAP)
    second_q, rest = lax.optimization_barrier((q_got[1], rest))
    (second,) = attended(second_q, features, True)
    second_got = lax.ppermute(second, "col", SWAP)
    mixed, finals = pl.pallas_call(
        own_kernel,
        out_shape=(shape((tokens, features), jnp.float32), shape((final_weight.shape[0], features))),
        in_specs=[VMEM] * 11,
        out_specs=(VMEM, VMEM),
        scratch_shapes=[pltpu.VMEM((tokens, width), jnp.bfloat16)],
        compiler_params=params(),
        cost_estimate=lasting(60),
        name="own",
    )(q_own, *pairs, weight, hidden, modulation, first_got, final_weight, final_got)
    results = ()
    for (start, _), got in ((chunks[0], rest_got), (chunks[1], second_got)):
        results = pl.pallas_call(
            functools.partial(final_kernel, start),
            out_shape=(shape(latent.shape, jnp.float32),) * 2,
            in_specs=[SMEM] * 2 + [VMEM] * (5 + len(results)),
            out_specs=(VMEM, VMEM),
            compiler_params=params(),
            name="final",
        )(step_index, step_count, mixed, got, modulation, finals, latent, *results)
    return results


def solution(mesh):
    placed = (
        P(("req", "row"), "col", None, None),
        P(("req", "row"), None, "col"),
        P(),
        P(),
        P(),
        P("col", "row"),
        P(None, "row"),
        P(("req", "row"), "col", None),
        P("req", None),
        P(("req", "row"), "col"),
        P("req"),
        P("req"),
    )
    return jax.shard_map(
        on_device,
        mesh=mesh,
        in_specs=placed,
        out_specs=(P(("req", "row"), "col"), P(("req", "row"), "col")),
        check_vma=False,
    )
```

profile of v0, /device:TPU:0, one launch (start us, length us, event | category | flops | bytes accessed | tf_op | source)
XLA Modules:
  0.0 39.3 jit_solution(539788870441572774)
XLA Ops:
  0.6 0.0 copy-start
  0.6 0.5 %collective-permute-start = (bf16[1216,640]{1,0:T(8,128)(2,1)}, bf16[1216,640]{1,0:T(8,128)(2,1)S(1)}, u32[]{:S(2)}, u32[]{:S(2)}) collective-permute-start(bf16[1216,640]{1,0:T(8,128)(2,1)} %bitcast.7), channel_id=1, source_target_pairs={{0,2},{2,0},{1,3},{3,1},{4,6},{6,4},{5,7},{7,5},{8,10},{10,8},{9,1... | collective-permute-start | bytes 4669448 | tf_op jit(solution)/shard_map/ppermute | solution.py:414
  1.2 2.2 %split.1 = (bf16[96,640]{1,0:T(8,128)(2,1)}, bf16[48,640]{1,0:T(8,128)(2,1)}, bf16[288,640]{1,0:T(8,128)(2,1)}, f32[3,64]{1,0:T(4,128)}) custom-call(bf16[144,3,1280]{2,1,0:T(4,128)(2,1)} %bitcast.5, f32[1,64]{1,0:T(1,128)} %bitcast.9, f32[1,64]{1,0:T(1,128)} %bitcast.10, f32[1,64]{1,0:T(1,128)} %bitcast.11), custom_call_target="tpu_custom_call" | custom-call | tf_op jit(solution)/shard_map/split/pallas_call | solution.py:403
  3.3 2.7 %collective-permute-start.2 = (bf16[288,640]{1,0:T(8,128)(2,1)}, bf16[288,640]{1,0:T(8,128)(2,1)S(1)}, u32[]{:S(2)}, u32[]{:S(2)}) collective-permute-start(bf16[288,640]{1,0:T(8,128)(2,1)} %get-tuple-element.20), channel_id=1, source_target_pairs={{0,1},{1,0},{2,3},{3,2},{4,5},{5,4},{6,7},{7,6},{8,9},{9,8},{10,11... | collective-permute-start | bytes 1105928 | tf_op jit(solution)/shard_map/ppermute | solution.py:445
  6.0 0.1 collective-permute-start.4
  6.1 0.0 collective-permute-done.theirs_ref
  6.1 0.0 copy-done
  6.1 0.0 copy-start.1
  6.1 1.4 %copy-done.1 = bf16[640,1216]{0,1:T(8,128)(2,1)S(1)} copy-done((bf16[640,1216]{0,1:T(8,128)(2,1)S(1)}, bf16[640,1216]{0,1:T(8,128)(2,1)}, u32[]{:S(2)}) %copy-start.1) | copy-done | bytes 1556504
  7.5 0.0 copy-start.4
  7.5 0.9 %copy-done.4 = bf16[48,2,640]{2,1,0:T(2,128)(2,1)S(1)} copy-done((bf16[48,2,640]{2,1,0:T(2,128)(2,1)S(1)}, bf16[48,2,640]{2,1,0:T(2,128)(2,1)}, u32[]{:S(2)}) %copy-start.4) | copy-done | bytes 122904
  8.4 0.0 copy-start.5
  8.4 0.7 %copy-done.5 = f32[3,64]{1,0:T(4,128)S(1)} copy-done((f32[3,64]{1,0:T(4,128)S(1)}, f32[3,64]{1,0:T(4,128)}, u32[]{:S(2)}) %copy-start.5) | copy-done | bytes 792
  9.1 0.0 copy-start.7
  9.1 1.9 %prep_own.1 = (bf16[384,640]{1,0:T(8,128)(2,1)S(1)}, bf16[144,640]{1,0:T(8,128)(2,1)S(1)}, f32[3,64]{1,0:T(4,128)S(1)}, bf16[2432,640]{1,0:T(8,128)(2,1)S(1)}) custom-call(bf16[144,3,1280]{2,1,0:T(4,128)(2,1)S(1)} %bitcast.6, bf16[48,2,640]{2,1,0:T(2,128)(2,1)S(1)} %copy-done.4, f32[3,64]{1,0:T(4,128)S(1)} %copy-done.5, bf16[1216,640]{1,0:T(8,128)(2,1)S(1)} %bitcast.8, ...), custom_call_target="tpu_custom_call" | custom-call | tf_op jit(solution)/shard_map/prep_own/pallas_call | solution.py:416
  11.0 0.2 collective-permute-start.1
  11.2 0.0 copy-done.7
  11.2 0.4 collective-permute-start.6
  11.6 0.0 copy-done.8
  11.6 1.9 %collective-permute-start.7 = (bf16[48,640]{1,0:T(8,128)(2,1)S(1)}, bf16[48,640]{1,0:T(8,128)(2,1)S(1)}, u32[]{:S(2)}, u32[]{:S(2)}) collective-permute-start(bf16[48,640]{1,0:T(8,128)(2,1)S(1)} %copy-done.8), channel_id=1, source_target_pairs={{0,1},{1,0},{2,3},{3,2},{4,5},{5,4},{6,7},{7,6},{8,9},{9,8},{10,11... | collective-permute-start | bytes 184328 | tf_op jit(solution)/shard_map/ppermute | solution.py:447
  13.6 2.1 %collective-permute-done.2.x_ref = bf16[288,640]{1,0:T(8,128)(2,1)S(1)} collective-permute-done((bf16[288,640]{1,0:T(8,128)(2,1)}, bf16[288,640]{1,0:T(8,128)(2,1)S(1)}, u32[]{:S(2)}, u32[]{:S(2)}) %collective-permute-start.2) | collective-permute-done | bytes 368672 | tf_op jit(solution)/shard_map/ppermute | solution.py:445
  15.7 0.3 kv_norm_kernel.1.refs_3_
  16.0 0.1 collective-permute-start.3
  16.0 2.3 %collective-permute-done.4.x_ref = bf16[96,640]{1,0:T(8,128)(2,1)S(1)} collective-permute-done((bf16[96,640]{1,0:T(8,128)(2,1)}, bf16[96,640]{1,0:T(8,128)(2,1)S(1)}, u32[]{:S(2)}, u32[]{:S(2)}) %collective-permute-start.4) | collective-permute-done | bytes 122912 | tf_op jit(solution)/shard_map/ppermute | solution.py:447
  18.3 0.2 q_norm_kernel.2.refs_0_
  18.6 0.0 collective-permute-done.3.refs_4_
  18.6 0.0 collective-permute-done.1.refs_2_
  18.6 1.3 %attend.2 = (bf16[96,768]{1,0:T(8,128)(2,1)S(1)}, bf16[96,640]{1,0:T(8,128)(2,1)S(1)}) custom-call(bf16[96,640]{1,0:T(8,128)(2,1)S(1)} %q_norm_kernel.2.refs_0_, bf16[384,640]{1,0:T(8,128)(2,1)S(1)} %get-tuple-element.19.refs_1_, bf16[384,640]{1,0:T(8,128)(2,1)S(1)} %collective-permute-done.1.refs_2_, bf16[288,640]{1,0:T(8,128)(2,1)S(1)} %kv_norm_kernel.1.refs_3_, ...), custom_call_target="tpu_custom_call" | custom-call | tf_op jit(solution)/shard_map/attend/pallas_call | solution.py:457
  19.9 2.0 %collective-permute-start.5 = (bf16[96,768]{1,0:T(8,128)(2,1)S(1)}, bf16[96,768]{1,0:T(8,128)(2,1)S(1)}, u32[]{:S(2)}, u32[]{:S(2)}) collective-permute-start(bf16[96,768]{1,0:T(8,128)(2,1)S(1)} %get-tuple-element.24), channel_id=1, source_target_pairs={{0,1},{1,0},{2,3},{3,2},{4,5},{5,4},{6,7},{7,6},{8,9},{9,8},{10,11... | collective-permute-start | bytes 442376 | tf_op jit(solution)/shard_map/ppermute | solution.py:468
  23.2 0.0 collective-permute-done.7.x_ref
  23.2 0.2 q_norm_kernel.3.refs_0_
  23.4 0.8 %rest.1 = bf16[96,1664]{1,0:T(8,128)(2,1)S(1)} custom-call(bf16[96,640]{1,0:T(8,128)(2,1)S(1)} %get-tuple-element.27.attended_ref, bf16[2432,640]{1,0:T(8,128)(2,1)S(1)} %get-tuple-element.22.refs_5_.w_ref), custom_call_target="tpu_custom_call" | custom-call | tf_op jit(solution)/shard_map/rest/pallas_call | solution.py:469
  24.2 0.0 copy-start.2
  24.2 0.0 copy-start.6
  24.2 0.1 collective-permute-start.9
  24.3 1.7 %attend.3 = bf16[48,2432]{1,0:T(8,128)(2,1)S(1)} custom-call(bf16[48,640]{1,0:T(8,128)(2,1)S(1)} %q_norm_kernel.3.refs_0_, bf16[384,640]{1,0:T(8,128)(2,1)S(1)} %get-tuple-element.19.refs_1_, bf16[384,640]{1,0:T(8,128)(2,1)S(1)} %collective-permute-done.1.refs_2_, bf16[288,640]{1,0:T(8,128)(2,1)S(1)} %kv_norm_kernel.1.refs_3_, ...), custom_call_target="tpu_custom_call" | custom-call | tf_op jit(solution)/shard_map/attend/pallas_call | solution.py:457
  26.0 2.0 %collective-permute-start.8 = (bf16[48,2432]{1,0:T(8,128)(2,1)S(1)}, bf16[48,2432]{1,0:T(8,128)(2,1)S(1)}, u32[]{:S(2)}, u32[]{:S(2)}) collective-permute-start(bf16[48,2432]{1,0:T(8,128)(2,1)S(1)} %attend.3), channel_id=1, source_target_pairs={{0,1},{1,0},{2,3},{3,2},{4,5},{5,4},{6,7},{7,6},{8,9},{9,8},{10,11... | collective-permute-start | bytes 700424 | tf_op jit(solution)/shard_map/ppermute | solution.py:480
  28.1 0.0 collective-permute-done.6.refs_10_
  28.1 0.0 collective-permute-done.5.refs_8_
  28.1 0.0 copy-done.2
  28.1 0.0 copy-done.6
  28.1 0.0 copy-start.3
  28.1 2.4 %own.1 = (f32[144,2432]{1,0:T(8,128)S(1)}, bf16[64,2432]{1,0:T(8,128)(2,1)S(1)}) custom-call(bf16[144,640]{1,0:T(8,128)(2,1)S(1)} %get-tuple-element.18.refs_0_, bf16[384,640]{1,0:T(8,128)(2,1)S(1)} %get-tuple-element.19.refs_1_, bf16[384,640]{1,0:T(8,128)(2,1)S(1)} %collective-permute-done.1.refs_2_, bf16[288,640]{1,0:T(8,128)(2,1)S(1)} %kv_norm_kernel.1.refs_3_, ...), custom_call_target="tpu_custom_call" | custom-call | flops 60000002048 | bytes 180000000 | tf_op jit(solution)/shard_map/own/pallas_call | solution.py:481
  30.5 4.2 %collective-permute-done.9.rest_ref = bf16[96,1664]{1,0:T(8,128)(2,1)S(1)} collective-permute-done((bf16[96,1664]{1,0:T(8,128)(2,1)S(1)}, bf16[96,1664]{1,0:T(8,128)(2,1)S(1)}, u32[]{:S(2)}, u32[]{:S(2)}) %collective-permute-start.9) | collective-permute-done | bytes 319520 | tf_op jit(solution)/shard_map/ppermute | solution.py:477
  34.7 0.0 copy-done.3
  34.7 1.0 %final.2 = (f32[24,384]{1,0:T(8,128)S(1)}, f32[24,384]{1,0:T(8,128)S(1)}) custom-call(s32[1]{0:T(128)S(6)} %copy.14.index_ref, s32[1]{0:T(128)S(6)} %copy.15.count_ref, f32[144,2432]{1,0:T(8,128)S(1)} %get-tuple-element.25.mixed_ref, bf16[96,1664]{1,0:T(8,128)(2,1)S(1)} %collective-permute-done.9.rest_ref, f32[3,2432]{1,0:T(4,128)S(1)} %copy-done.2, ...), custom_call_target="tpu_custom_call" | custom-call | tf_op jit(solution)/shard_map/final/pallas_call | solution.py:493
  35.8 1.9 %collective-permute-done.8.rest_ref = bf16[48,2432]{1,0:T(8,128)(2,1)S(1)} collective-permute-done((bf16[48,2432]{1,0:T(8,128)(2,1)S(1)}, bf16[48,2432]{1,0:T(8,128)(2,1)S(1)}, u32[]{:S(2)}, u32[]{:S(2)}) %collective-permute-start.8) | collective-permute-done | bytes 233504 | tf_op jit(solution)/shard_map/ppermute | solution.py:480
  37.7 1.6 %final.3 = (f32[24,384]{1,0:T(8,128)}, f32[24,384]{1,0:T(8,128)}) custom-call(s32[1]{0:T(128)S(6)} %copy.14.index_ref, s32[1]{0:T(128)S(6)} %copy.15.count_ref, f32[144,2432]{1,0:T(8,128)S(1)} %get-tuple-element.25.mixed_ref, bf16[48,2432]{1,0:T(8,128)(2,1)S(1)} %collective-permute-done.8.rest_ref, f32[3,2432]{1,0:T(4,128)S(1)} %copy-done.2, ...), custom_call_target="tpu_custom_call" | custom-call | tf_op jit(solution)/shard_map/final/pallas_call | solution.py:493
  (1 shorter events, 0.0 us)
Async XLA Ops:
  0.6 5.5 %copy-start = (bf16[12,12,3,1280]{3,2,1,0:T(4,128)(2,1)S(1)}, bf16[12,12,3,1280]{3,2,1,0:T(4,128)(2,1)}, u32[]{:S(2)}) copy-start(bf16[12,12,3,1280]{3,2,1,0:T(4,128)(2,1)} %param.12) | copy-start | bytes 3317764
  0.6 5.5 %collective-permute-start = (bf16[1216,640]{1,0:T(8,128)(2,1)}, bf16[1216,640]{1,0:T(8,128)(2,1)S(1)}, u32[]{:S(2)}, u32[]{:S(2)}) collective-permute-start(bf16[1216,640]{1,0:T(8,128)(2,1)} %bitcast.7), channel_id=1, source_target_pairs={{0,2},{2,0},{1,3},{3,1},{4,6},{6,4},{5,7},{7,5},{8,10},{10,8},{9,1... | collective-permute-start | bytes 4669448 | tf_op jit(solution)/shard_map/ppermute | solution.py:414
  3.3 12.3 %collective-permute-start.2 = (bf16[288,640]{1,0:T(8,128)(2,1)}, bf16[288,640]{1,0:T(8,128)(2,1)S(1)}, u32[]{:S(2)}, u32[]{:S(2)}) collective-permute-start(bf16[288,640]{1,0:T(8,128)(2,1)} %get-tuple-element.20), channel_id=1, source_target_pairs={{0,1},{1,0},{2,3},{3,2},{4,5},{5,4},{6,7},{7,6},{8,9},{9,8},{10,11... | collective-permute-start | bytes 1105928 | tf_op jit(solution)/shard_map/ppermute | solution.py:445
  6.0 12.3 %collective-permute-start.4 = (bf16[96,640]{1,0:T(8,128)(2,1)}, bf16[96,640]{1,0:T(8,128)(2,1)S(1)}, u32[]{:S(2)}, u32[]{:S(2)}) collective-permute-start(bf16[96,640]{1,0:T(8,128)(2,1)} %get-tuple-element.23), channel_id=1, source_target_pairs={{0,1},{1,0},{2,3},{3,2},{4,5},{5,4},{6,7},{7,6},{8,9},{9,8},{10,11... | collective-permute-start | bytes 368648 | tf_op jit(solution)/shard_map/ppermute | solution.py:447
  6.1 1.4 %copy-start.1 = (bf16[640,1216]{0,1:T(8,128)(2,1)S(1)}, bf16[640,1216]{0,1:T(8,128)(2,1)}, u32[]{:S(2)}) copy-start(bf16[640,1216]{0,1:T(8,128)(2,1)} %param.17) | copy-start | bytes 4669444
  7.5 0.9 %copy-start.4 = (bf16[48,2,640]{2,1,0:T(2,128)(2,1)S(1)}, bf16[48,2,640]{2,1,0:T(2,128)(2,1)}, u32[]{:S(2)}) copy-start(bf16[48,2,640]{2,1,0:T(2,128)(2,1)} %text_ref.1) | copy-start | bytes 368644
  8.4 0.7 %copy-start.5 = (f32[3,64]{1,0:T(4,128)S(1)}, f32[3,64]{1,0:T(4,128)}, u32[]{:S(2)}) copy-start(f32[3,64]{1,0:T(4,128)} %get-tuple-element.17.gains) | copy-start | bytes 2308
  9.1 2.2 %copy-start.7 = (bf16[64,1216]{1,0:T(8,128)(2,1)S(1)}, bf16[64,1216]{1,0:T(8,128)(2,1)}, u32[]{:S(2)}) copy-start(bf16[64,1216]{1,0:T(8,128)(2,1)} %refs_9_.1) | copy-start | bytes 466948
  9.1 2.5 %copy-start.8 = (bf16[48,640]{1,0:T(8,128)(2,1)S(1)}, bf16[48,640]{1,0:T(8,128)(2,1)}, u32[]{:S(2)}) copy-start(bf16[48,640]{1,0:T(8,128)(2,1)} %get-tuple-element.26) | copy-start | bytes 184324
  11.0 7.5 %collective-permute-start.1 = (bf16[384,640]{1,0:T(8,128)(2,1)S(1)}, bf16[384,640]{1,0:T(8,128)(2,1)S(1)}, u32[]{:S(2)}, u32[]{:S(2)}) collective-permute-start(bf16[384,640]{1,0:T(8,128)(2,1)S(1)} %get-tuple-element.19.refs_1_), channel_id=1, source_target_pairs={{0,2},{2,0},{1,3},{3,1},{4,6},{6,4},{5,7},{7,5},{8,10},{10,8},{9,1... | collective-permute-start | bytes 1474568 | tf_op jit(solution)/shard_map/ppermute | solution.py:452
  11.2 16.8 %collective-permute-start.6 = (bf16[64,1216]{1,0:T(8,128)(2,1)S(1)}, bf16[64,1216]{1,0:T(8,128)(2,1)S(1)}, u32[]{:S(2)}, u32[]{:S(2)}) collective-permute-start(bf16[64,1216]{1,0:T(8,128)(2,1)S(1)} %copy-done.7), channel_id=1, source_target_pairs={{0,2},{2,0},{1,3},{3,1},{4,6},{6,4},{5,7},{7,5},{8,10},{10,8},{9,1... | collective-permute-start | bytes 466952 | tf_op jit(solution)/shard_map/ppermute | solution.py:415
  11.6 11.6 %collective-permute-start.7 = (bf16[48,640]{1,0:T(8,128)(2,1)S(1)}, bf16[48,640]{1,0:T(8,128)(2,1)S(1)}, u32[]{:S(2)}, u32[]{:S(2)}) collective-permute-start(bf16[48,640]{1,0:T(8,128)(2,1)S(1)} %copy-done.8), channel_id=1, source_target_pairs={{0,1},{1,0},{2,3},{3,2},{4,5},{5,4},{6,7},{7,6},{8,9},{9,8},{10,11... | collective-permute-start | bytes 184328 | tf_op jit(solution)/shard_map/ppermute | solution.py:447
  16.0 2.6 %collective-permute-start.3 = (bf16[288,640]{1,0:T(8,128)(2,1)S(1)}, bf16[288,640]{1,0:T(8,128)(2,1)S(1)}, u32[]{:S(2)}, u32[]{:S(2)}) collective-permute-start(bf16[288,640]{1,0:T(8,128)(2,1)S(1)} %kv_norm_kernel.1.refs_3_), channel_id=1, source_target_pairs={{0,2},{2,0},{1,3},{3,1},{4,6},{6,4},{5,7},{7,5},{8,10},{10,8},{9,1... | collective-permute-start | bytes 1105928 | tf_op jit(solution)/shard_map/ppermute | solution.py:452
  19.9 8.2 %collective-permute-start.5 = (bf16[96,768]{1,0:T(8,128)(2,1)S(1)}, bf16[96,768]{1,0:T(8,128)(2,1)S(1)}, u32[]{:S(2)}, u32[]{:S(2)}) collective-permute-start(bf16[96,768]{1,0:T(8,128)(2,1)S(1)} %get-tuple-element.24), channel_id=1, source_target_pairs={{0,1},{1,0},{2,3},{3,2},{4,5},{5,4},{6,7},{7,6},{8,9},{9,8},{10,11... | collective-permute-start | bytes 442376 | tf_op jit(solution)/shard_map/ppermute | solution.py:468
  24.2 3.9 %copy-start.2 = (f32[3,2432]{1,0:T(4,128)S(1)}, f32[3,2432]{1,0:T(4,128)}, u32[]{:S(2)}) copy-start(f32[3,2432]{1,0:T(4,128)} %mod_ref.3) | copy-start | bytes 87556
  24.2 3.9 %copy-start.6 = (bf16[12,12,2432]{2,1,0:T(8,128)(2,1)S(1)}, bf16[12,12,2432]{2,1,0:T(8,128)(2,1)}, u32[]{:S(2)}) copy-start(bf16[12,12,2432]{2,1,0:T(8,128)(2,1)} %refs_6_.1) | copy-start | bytes 2101252
  24.2 10.5 %collective-permute-start.9 = (bf16[96,1664]{1,0:T(8,128)(2,1)S(1)}, bf16[96,1664]{1,0:T(8,128)(2,1)S(1)}, u32[]{:S(2)}, u32[]{:S(2)}) collective-permute-start(bf16[96,1664]{1,0:T(8,128)(2,1)S(1)} %rest.1), channel_id=1, source_target_pairs={{0,1},{1,0},{2,3},{3,2},{4,5},{5,4},{6,7},{7,6},{8,9},{9,8},{10,11... | collective-permute-start | bytes 958472 | tf_op jit(solution)/shard_map/ppermute | solution.py:477
  26.0 11.7 %collective-permute-start.8 = (bf16[48,2432]{1,0:T(8,128)(2,1)S(1)}, bf16[48,2432]{1,0:T(8,128)(2,1)S(1)}, u32[]{:S(2)}, u32[]{:S(2)}) collective-permute-start(bf16[48,2432]{1,0:T(8,128)(2,1)S(1)} %attend.3), channel_id=1, source_target_pairs={{0,1},{1,0},{2,3},{3,2},{4,5},{5,4},{6,7},{7,6},{8,9},{9,8},{10,11... | collective-permute-start | bytes 700424 | tf_op jit(solution)/shard_map/ppermute | solution.py:480
  28.1 6.7 %copy-start.3 = (f32[24,384]{1,0:T(8,128)S(1)}, f32[24,384]{1,0:T(8,128)}, u32[]{:S(2)}) copy-start(f32[24,384]{1,0:T(8,128)} %latent_ref.3) | copy-start | bytes 110596
where the time goes:
time: 39.5 us; the launch traced here: 39.3 us
  Pallas kernels  13.5 us (34%)
  waiting for transfers between devices  10.6 us (27%)
  starting transfers between devices  10.1 us (26%)
  local copies, waits for them, and re-layouts  3.02 us (8%)
  between operations  2.09 us (5%)
    ppermute x1, waiting for transfers between devices, on_device(): rest_got = lax.ppermute(rest, 'col', SWAP)  4.24 us
    unnamed x18, local copies, waits for them, and re-layouts  3.02 us
    pallas_call x2, Pallas kernels, attended(): pl.pallas_call(attend_kernel, out_shape=out_shape, in_specs=[VMEM] * 6, o...  2.98 us
    ppermute x1, starting transfers between devices, on_device(): kv_got = normed(kv_norm_kernel, lax.ppermute(kv_raw, 'col', SWAP), 0)  2.68 us
    pallas_call x2, Pallas kernels, on_device(): pl.pallas_call(functools.partial(final_kernel, start), out_shape=(shape(l...  2.59 us
    pallas_call x1, Pallas kernels, on_device(): pl.pallas_call(own_kernel, out_shape=(shape((tokens, features), jnp.float...  2.4 us
    ppermute x2, waiting for transfers between devices, on_device(): lax.ppermute(raw, 'col', SWAP)  2.27 us
    pallas_call x1, Pallas kernels, on_device(): pl.pallas_call(split_kernel, out_shape=tuple((shape((upto - start, width)...  2.17 us
  transfers between devices with their start and end apart: 10, of which 4 were waited for; matrix products, arithmetic and copies ran while one was open for 0% of the time, Pallas kernels for 30%

commit v1 on v0

--- a/solution.py
+++ b/solution.py
@@ -249,8 +249,14 @@
 
 def own_kernel(*refs):
     q_ref = refs[0]
-    w_ref, hidden_ref, mod_ref, got_ref, mine_ref, theirs_ref = refs[5:11]
-    out_ref, finals_ref, attended = refs[11:]
+    w_ref, hidden_ref, mod_ref, got_ref, mine_ref, theirs_ref, index_ref, count_ref = refs[5:13]
+    out_ref, finals_ref, euler_ref, attended, index, count, sems = refs[13:]
+    copies = [
+        pltpu.make_async_copy(ref, to, sems.at[at])
+        for at, (ref, to) in enumerate(((index_ref, index), (count_ref, count)))
+    ]
+    for copy in copies:
+        copy.start()
     attend(q_ref[...], *keys_and_values(refs[1:5]), attended)
     tile_rows = hidden_ref.shape[0]
 
@@ -270,6 +276,11 @@
     finals_ref[...] = jnp.concatenate(
         [jnp.where(is_first, mine, theirs), jnp.where(is_first, theirs, mine)], axis=1
     ).astype(jnp.bfloat16)
+    for copy in copies:
+        copy.wait()
+    now = jnp.full(euler_ref.shape, index[0], jnp.int32)
+    then = now + jnp.full(euler_ref.shape, count[0], jnp.int32)
+    euler_ref[...] = noise_level(then) - noise_level(now)
 
 
 def one_hot(dims, condition):
@@ -305,8 +316,7 @@
 
 def final_kernel(
     start,
-    index_ref,
-    count_ref,
+    euler_ref,
     mixed_ref,
     rest_ref,
     mod_ref,
@@ -343,13 +353,10 @@
     velocity = to_pixels(jnp.concatenate(parts, axis=0), tile_cols)
     first = start // tile_cols * PATCH
     pixels = slice(first, first + velocity.shape[0])
-    index = jnp.full(velocity.shape, index_ref[0], jnp.int32)
-    count = jnp.full(velocity.shape, count_ref[0], jnp.int32)
-    euler_step = noise_level(index + count) - noise_level(index)
     for before_ref, after_ref in zip(refs[:-2], refs[-2:]):
         after_ref[:first] = before_ref[:first]
     velocity_ref[pixels] = velocity
-    next_ref[pixels] = latent_ref[pixels] + euler_step * velocity
+    next_ref[pixels] = latent_ref[pixels] + euler_ref[...] * velocity
 
 
 def params(limit=VMEM_LIMIT):
@@ -369,7 +376,6 @@
 VMEM = pl.BlockSpec(memory_space=pltpu.VMEM)
 ANY = pl.BlockSpec(memory_space=pl.ANY)
 HBM = pl.BlockSpec(memory_space=pltpu.HBM)
-SMEM = pl.BlockSpec(memory_space=pltpu.SMEM)
 
 
 def on_device(
@@ -398,7 +404,7 @@
     block = shape((tokens, width))
 
     loads = pltpu.SemaphoreType.DMA((LOADS,))
-    cut = tile_rows // 3 * 2 * tile_cols
+    cut = tile_rows // 3 * tile_cols
     chunks = ((0, cut), (cut, tokens))
     *q_raw, kv_raw, gains = pl.pallas_call(
         split_kernel,
@@ -445,7 +451,7 @@
     kv_got = normed(kv_norm_kernel, lax.ppermute(kv_raw, "col", SWAP), 0)
     q_got = [
         normed(q_norm_kernel, lax.ppermute(raw, "col", SWAP), duration)
-        for raw, duration in zip(q_raw, (4, 1))
+        for raw, duration in zip(q_raw, (3.5, 1))
     ]
     pairs = []
     for kv in (kv_own, kv_got):
@@ -478,26 +484,46 @@
     second_q, rest = lax.optimization_barrier((q_got[1], rest))
     (second,) = attended(second_q, features, True)
     second_got = lax.ppermute(second, "col", SWAP)
-    mixed, finals = pl.pallas_call(
+    mixed, finals, euler = pl.pallas_call(
         own_kernel,
-        out_shape=(shape((tokens, features), jnp.float32), shape((final_weight.shape[0], features))),
-        in_specs=[VMEM] * 11,
-        out_specs=(VMEM, VMEM),
-        scratch_shapes=[pltpu.VMEM((tokens, width), jnp.bfloat16)],
+        out_shape=(
+            shape((tokens, features), jnp.float32),
+            shape((final_weight.shape[0], features)),
+            shape((1, latent.shape[1]), jnp.float32),
+        ),
+        in_specs=[VMEM] * 11 + [HBM] * 2,
+        out_specs=(VMEM,) * 3,
+        scratch_shapes=[
+            pltpu.VMEM((tokens, width), jnp.bfloat16),
+            pltpu.SMEM(step_index.shape, jnp.int32),
+            pltpu.SMEM(step_count.shape, jnp.int32),
+            pltpu.SemaphoreType.DMA((2,)),
+        ],
         compiler_params=params(),
         cost_estimate=lasting(60),
         name="own",
-    )(q_own, *pairs, weight, hidden, modulation, first_got, final_weight, final_got)
+    )(
+        q_own,
+        *pairs,
+        weight,
+        hidden,
+        modulation,
+        first_got,
+        final_weight,
+        final_got,
+        step_index,
+        step_count,
+    )
     results = ()
     for (start, _), got in ((chunks[0], rest_got), (chunks[1], second_got)):
         results = pl.pallas_call(
             functools.partial(final_kernel, start),
             out_shape=(shape(latent.shape, jnp.float32),) * 2,
-            in_specs=[SMEM] * 2 + [VMEM] * (5 + len(results)),
+            in_specs=[VMEM] * (6 + len(results)),
             out_specs=(VMEM, VMEM),
             compiler_params=params(),
             name="final",
-        )(step_index, step_count, mixed, got, modulation, finals, latent, *results)
+        )(euler, mixed, got, modulation, finals, latent, *results)
     return results
 
 

time: 39.5 us -> 40.9 us (1.035)
  waiting for transfers between devices: 10.6 us -> 12.2 us
  starting transfers between devices: 10.1 us -> 9.43 us
    ppermute x1, waiting for transfers between devices: 1.95 us -> 8.05 us  [on_device(): second_got = lax.ppermute(second, 'col', SWAP)]
    ppermute x1, waiting for transfers between devices: 4.24 us -> 0.01 us  [on_device(): rest_got = lax.ppermute(rest, 'col', SWAP)]
    ppermute x1, starting transfers between devices: 2.02 us -> 0.14 us  [on_device(): first_got = lax.ppermute(first, 'col', SWAP)]
    ppermute x1, starting transfers between devices: 2.02 us -> 0.35 us  [on_device(): second_got = lax.ppermute(second, 'col', SWAP)]
    ppermute x1, starting transfers between devices: 0.14 us -> 1.8 us  [on_device(): rest_got = lax.ppermute(rest, 'col', SWAP)]
    ppermute x2, waiting for transfers between devices: 2.27 us -> 0.83 us  [on_device(): lax.ppermute(raw, 'col', SWAP)]
    ppermute x1, waiting for transfers between devices: 2.11 us -> 3.28 us  [on_device(): kv_got = normed(kv_norm_kernel, lax.ppermute(kv_raw, 'col', SWAP), 0)]
    ppermute x2, starting transfers between devices: 2.03 us -> 3.17 us  [on_device(): lax.ppermute(raw, 'col', SWAP)]
  transfers between devices with their start and end apart: 10 -> 10, of which waited for: 4 -> 3; matrix products, arithmetic and copies ran while one was open for 0% -> 0% of each run, Pallas kernels for 30% -> 30%
where the time goes in v1:
time: 40.9 us; the launch traced here: 40.7 us
  Pallas kernels  13.9 us (34%)
  waiting for transfers between devices  12.2 us (30%)
  starting transfers between devices  9.43 us (23%)
  local copies, waits for them, and re-layouts  3.02 us (7%)
  between operations  2.13 us (5%)
    ppermute x1, waiting for transfers between devices, on_device(): second_got = lax.ppermute(second, 'col', SWAP)  8.05 us
    ppermute x1, waiting for transfers between devices, on_device(): kv_got = normed(kv_norm_kernel, lax.ppermute(kv_raw, 'col', SWAP), 0)  3.28 us
    ppermute x2, starting transfers between devices, on_device(): lax.ppermute(raw, 'col', SWAP)  3.17 us
    unnamed x20, local copies, waits for them, and re-layouts  3.02 us
    pallas_call x2, Pallas kernels, attended(): pl.pallas_call(attend_kernel, out_shape=out_shape, in_specs=[VMEM] * 6, o...  2.89 us
    pallas_call x1, Pallas kernels, on_device(): pl.pallas_call(own_kernel, out_shape=(shape((tokens, features), jnp.float...  2.86 us
    ppermute x1, starting transfers between devices, on_device(): kv_got = normed(kv_norm_kernel, lax.ppermute(kv_raw, 'col', SWAP), 0)  2.68 us
    pallas_call x2, Pallas kernels, on_device(): pl.pallas_call(functools.partial(final_kernel, start), out_shape=(shape(l...  2.56 us
  transfers between devices with their start and end apart: 10, of which 3 were waited for; matrix products, arithmetic and copies ran while one was open for 0% of the time, Pallas kernels for 30%

profile of v1, /device:TPU:0, one launch (start us, length us, event | category | flops | bytes accessed | tf_op | source)
XLA Modules:
  0.0 40.7 jit_solution(14422914402526979285)
XLA Ops:
  0.6 0.0 copy-start
  0.6 0.5 %collective-permute-start = (bf16[1216,640]{1,0:T(8,128)(2,1)}, bf16[1216,640]{1,0:T(8,128)(2,1)S(1)}, u32[]{:S(2)}, u32[]{:S(2)}) collective-permute-start(bf16[1216,640]{1,0:T(8,128)(2,1)} %bitcast.7), channel_id=1, source_target_pairs={{0,2},{2,0},{1,3},{3,1},{4,6},{6,4},{5,7},{7,5},{8,10},{10,8},{9,1... | collective-permute-start | bytes 4669448 | tf_op jit(solution)/shard_map/ppermute | solution.py:420
  1.2 2.2 %split.1 = (bf16[48,640]{1,0:T(8,128)(2,1)}, bf16[96,640]{1,0:T(8,128)(2,1)}, bf16[288,640]{1,0:T(8,128)(2,1)}, f32[3,64]{1,0:T(4,128)}) custom-call(bf16[144,3,1280]{2,1,0:T(4,128)(2,1)} %bitcast.5, f32[1,64]{1,0:T(1,128)} %bitcast.9, f32[1,64]{1,0:T(1,128)} %bitcast.10, f32[1,64]{1,0:T(1,128)} %bitcast.11), custom_call_target="tpu_custom_call" | custom-call | tf_op jit(solution)/shard_map/split/pallas_call | solution.py:409
  3.4 2.7 %collective-permute-start.2 = (bf16[288,640]{1,0:T(8,128)(2,1)}, bf16[288,640]{1,0:T(8,128)(2,1)S(1)}, u32[]{:S(2)}, u32[]{:S(2)}) collective-permute-start(bf16[288,640]{1,0:T(8,128)(2,1)} %get-tuple-element.21), channel_id=1, source_target_pairs={{0,1},{1,0},{2,3},{3,2},{4,5},{5,4},{6,7},{7,6},{8,9},{9,8},{10,11... | collective-permute-start | bytes 1105928 | tf_op jit(solution)/shard_map/ppermute | solution.py:451
  6.1 0.0 collective-permute-done.theirs_ref
  6.1 0.0 copy-done
  6.1 0.0 copy-start.1
  6.1 1.4 %copy-done.1 = bf16[640,1216]{0,1:T(8,128)(2,1)S(1)} copy-done((bf16[640,1216]{0,1:T(8,128)(2,1)S(1)}, bf16[640,1216]{0,1:T(8,128)(2,1)}, u32[]{:S(2)}) %copy-start.1) | copy-done | bytes 1556504
  7.5 0.0 copy-start.4
  7.5 0.9 %copy-done.4 = bf16[48,2,640]{2,1,0:T(2,128)(2,1)S(1)} copy-done((bf16[48,2,640]{2,1,0:T(2,128)(2,1)S(1)}, bf16[48,2,640]{2,1,0:T(2,128)(2,1)}, u32[]{:S(2)}) %copy-start.4) | copy-done | bytes 122904
  8.4 0.0 copy-start.5
  8.4 0.7 %copy-done.5 = f32[3,64]{1,0:T(4,128)S(1)} copy-done((f32[3,64]{1,0:T(4,128)S(1)}, f32[3,64]{1,0:T(4,128)}, u32[]{:S(2)}) %copy-start.5) | copy-done | bytes 792
  9.1 1.9 %prep_own.1 = (bf16[384,640]{1,0:T(8,128)(2,1)S(1)}, bf16[144,640]{1,0:T(8,128)(2,1)S(1)}, f32[3,64]{1,0:T(4,128)S(1)}, bf16[2432,640]{1,0:T(8,128)(2,1)S(1)}) custom-call(bf16[144,3,1280]{2,1,0:T(4,128)(2,1)S(1)} %bitcast.6, bf16[48,2,640]{2,1,0:T(2,128)(2,1)S(1)} %copy-done.4, f32[3,64]{1,0:T(4,128)S(1)} %copy-done.5, bf16[1216,640]{1,0:T(8,128)(2,1)S(1)} %bitcast.8, ...), custom_call_target="tpu_custom_call" | custom-call | tf_op jit(solution)/shard_map/prep_own/pallas_call | solution.py:422
  11.0 0.2 collective-permute-start.1
  11.2 0.0 copy-done.9
  11.2 1.2 %collective-permute-start.4 = (bf16[48,640]{1,0:T(8,128)(2,1)S(1)}, bf16[48,640]{1,0:T(8,128)(2,1)S(1)}, u32[]{:S(2)}, u32[]{:S(2)}) collective-permute-start(bf16[48,640]{1,0:T(8,128)(2,1)S(1)} %copy-done.9), channel_id=1, source_target_pairs={{0,1},{1,0},{2,3},{3,2},{4,5},{5,4},{6,7},{7,6},{8,9},{9,8},{10,11... | collective-permute-start | bytes 184328 | tf_op jit(solution)/shard_map/ppermute | solution.py:453
  12.4 3.3 %collective-permute-done.2.x_ref = bf16[288,640]{1,0:T(8,128)(2,1)S(1)} collective-permute-done((bf16[288,640]{1,0:T(8,128)(2,1)}, bf16[288,640]{1,0:T(8,128)(2,1)S(1)}, u32[]{:S(2)}, u32[]{:S(2)}) %collective-permute-start.2) | collective-permute-done | bytes 368672 | tf_op jit(solution)/shard_map/ppermute | solution.py:451
  15.7 0.3 kv_norm_kernel.1.refs_3_
  16.0 0.1 collective-permute-start.3
  16.1 0.0 copy-done.7
  16.1 0.5 %collective-permute-start.6 = (bf16[64,1216]{1,0:T(8,128)(2,1)S(1)}, bf16[64,1216]{1,0:T(8,128)(2,1)S(1)}, u32[]{:S(2)}, u32[]{:S(2)}) collective-permute-start(bf16[64,1216]{1,0:T(8,128)(2,1)S(1)} %copy-done.7), channel_id=1, source_target_pairs={{0,2},{2,0},{1,3},{3,1},{4,6},{6,4},{5,7},{7,5},{8,10},{10,8},{9,1... | collective-permute-start | bytes 466952 | tf_op jit(solution)/shard_map/ppermute | solution.py:421
  16.6 0.0 copy-done.8
  16.6 2.0 %collective-permute-start.7 = (bf16[96,640]{1,0:T(8,128)(2,1)S(1)}, bf16[96,640]{1,0:T(8,128)(2,1)S(1)}, u32[]{:S(2)}, u32[]{:S(2)}) collective-permute-start(bf16[96,640]{1,0:T(8,128)(2,1)S(1)} %copy-done.8), channel_id=1, source_target_pairs={{0,1},{1,0},{2,3},{3,2},{4,5},{5,4},{6,7},{7,6},{8,9},{9,8},{10,11... | collective-permute-start | bytes 368648 | tf_op jit(solution)/shard_map/ppermute | solution.py:453
  19.8 0.0 collective-permute-done.4.x_ref
  19.8 0.2 q_norm_kernel.2.refs_0_
  20.0 0.0 collective-permute-done.3.refs_4_
  20.0 0.0 collective-permute-done.1.refs_2_
  20.1 1.0 %attend.2 = (bf16[48,768]{1,0:T(8,128)(2,1)S(1)}, bf16[48,640]{1,0:T(8,128)(2,1)S(1)}) custom-call(bf16[48,640]{1,0:T(8,128)(2,1)S(1)} %q_norm_kernel.2.refs_0_, bf16[384,640]{1,0:T(8,128)(2,1)S(1)} %get-tuple-element.20.refs_1_, bf16[384,640]{1,0:T(8,128)(2,1)S(1)} %collective-permute-done.1.refs_2_, bf16[288,640]{1,0:T(8,128)(2,1)S(1)} %kv_norm_kernel.1.refs_3_, ...), custom_call_target="tpu_custom_call" | custom-call | tf_op jit(solution)/shard_map/attend/pallas_call | solution.py:463
  21.1 0.1 collective-permute-start.5
  21.3 0.8 %collective-permute-done.7.x_ref = bf16[96,640]{1,0:T(8,128)(2,1)S(1)} collective-permute-done((bf16[96,640]{1,0:T(8,128)(2,1)S(1)}, bf16[96,640]{1,0:T(8,128)(2,1)S(1)}, u32[]{:S(2)}, u32[]{:S(2)}) %collective-permute-start.7) | collective-permute-done | bytes 122912 | tf_op jit(solution)/shard_map/ppermute | solution.py:453
  22.1 0.2 q_norm_kernel.3.refs_0_
  22.4 0.7 %rest.1 = bf16[48,1664]{1,0:T(8,128)(2,1)S(1)} custom-call(bf16[48,640]{1,0:T(8,128)(2,1)S(1)} %get-tuple-element.29.attended_ref, bf16[2432,640]{1,0:T(8,128)(2,1)S(1)} %get-tuple-element.23.refs_5_.w_ref), custom_call_target="tpu_custom_call" | custom-call | tf_op jit(solution)/shard_map/rest/pallas_call | solution.py:475
  23.1 0.0 copy-start.2
  23.1 0.0 copy-start.6
  23.1 1.8 %collective-permute-start.9 = (bf16[48,1664]{1,0:T(8,128)(2,1)S(1)}, bf16[48,1664]{1,0:T(8,128)(2,1)S(1)}, u32[]{:S(2)}, u32[]{:S(2)}) collective-permute-start(bf16[48,1664]{1,0:T(8,128)(2,1)S(1)} %rest.1), channel_id=1, source_target_pairs={{0,1},{1,0},{2,3},{3,2},{4,5},{5,4},{6,7},{7,6},{8,9},{9,8},{10,11... | collective-permute-start | bytes 479240 | tf_op jit(solution)/shard_map/ppermute | solution.py:483
  24.9 1.8 %attend.3 = bf16[96,2432]{1,0:T(8,128)(2,1)S(1)} custom-call(bf16[96,640]{1,0:T(8,128)(2,1)S(1)} %q_norm_kernel.3.refs_0_, bf16[384,640]{1,0:T(8,128)(2,1)S(1)} %get-tuple-element.20.refs_1_, bf16[384,640]{1,0:T(8,128)(2,1)S(1)} %collective-permute-done.1.refs_2_, bf16[288,640]{1,0:T(8,128)(2,1)S(1)} %kv_norm_kernel.1.refs_3_, ...), custom_call_target="tpu_custom_call" | custom-call | tf_op jit(solution)/shard_map/attend/pallas_call | solution.py:463
  26.8 0.3 collective-permute-start.8
  27.1 0.0 collective-permute-done.6.refs_10_
  27.1 0.0 collective-permute-done.5.refs_8_
  27.1 0.0 copy-done.2
  27.1 0.0 copy-done.6
  27.1 0.0 copy-start.3
  27.1 2.9 %own.1 = (f32[144,2432]{1,0:T(8,128)S(1)}, bf16[64,2432]{1,0:T(8,128)(2,1)S(1)}, f32[1,384]{1,0:T(1,128)S(1)}) custom-call(bf16[144,640]{1,0:T(8,128)(2,1)S(1)} %get-tuple-element.19.refs_0_, bf16[384,640]{1,0:T(8,128)(2,1)S(1)} %get-tuple-element.20.refs_1_, bf16[384,640]{1,0:T(8,128)(2,1)S(1)} %collective-permute-done.1.refs_2_, ...), custom_call_target="tpu_custom_call" | custom-call | flops 60000002048 | bytes 180000000 | tf_op jit(solution)/shard_map/own/pallas_call | solution.py:487
  30.0 0.0 collective-permute-done.9.rest_ref
  30.0 0.0 copy-done.3
  30.0 0.9 %final.2 = (f32[24,384]{1,0:T(8,128)S(1)}, f32[24,384]{1,0:T(8,128)S(1)}) custom-call(f32[1,384]{1,0:T(1,128)S(1)} %get-tuple-element.26.euler_ref, f32[144,2432]{1,0:T(8,128)S(1)} %get-tuple-element.27.mixed_ref, bf16[48,1664]{1,0:T(8,128)(2,1)S(1)} %collective-permute-done.9.rest_ref, f32[3,2432]{1,0:T(4,128)S(1)} %copy-done.2, ...), custom_call_target="tpu_custom_call" | custom-call | tf_op jit(solution)/shard_map/final/pallas_call | solution.py:519
  30.9 8.1 %collective-permute-done.8.rest_ref = bf16[96,2432]{1,0:T(8,128)(2,1)S(1)} collective-permute-done((bf16[96,2432]{1,0:T(8,128)(2,1)S(1)}, bf16[96,2432]{1,0:T(8,128)(2,1)S(1)}, u32[]{:S(2)}, u32[]{:S(2)}) %collective-permute-start.8) | collective-permute-done | bytes 466976 | tf_op jit(solution)/shard_map/ppermute | solution.py:486
  39.0 1.7 %final.3 = (f32[24,384]{1,0:T(8,128)}, f32[24,384]{1,0:T(8,128)}) custom-call(f32[1,384]{1,0:T(1,128)S(1)} %get-tuple-element.26.euler_ref, f32[144,2432]{1,0:T(8,128)S(1)} %get-tuple-element.27.mixed_ref, bf16[96,2432]{1,0:T(8,128)(2,1)S(1)} %collective-permute-done.8.rest_ref, f32[3,2432]{1,0:T(4,128)S(1)} %copy-done.2, ...), custom_call_target="tpu_custom_call" | custom-call | tf_op jit(solution)/shard_map/final/pallas_call | solution.py:519
  (3 shorter events, 0.0 us)
Async XLA Ops:
  0.6 5.4 %copy-start = (bf16[12,12,3,1280]{3,2,1,0:T(4,128)(2,1)S(1)}, bf16[12,12,3,1280]{3,2,1,0:T(4,128)(2,1)}, u32[]{:S(2)}) copy-start(bf16[12,12,3,1280]{3,2,1,0:T(4,128)(2,1)} %param.12) | copy-start | bytes 3317764
  0.6 5.4 %collective-permute-start = (bf16[1216,640]{1,0:T(8,128)(2,1)}, bf16[1216,640]{1,0:T(8,128)(2,1)S(1)}, u32[]{:S(2)}, u32[]{:S(2)}) collective-permute-start(bf16[1216,640]{1,0:T(8,128)(2,1)} %bitcast.7), channel_id=1, source_target_pairs={{0,2},{2,0},{1,3},{3,1},{4,6},{6,4},{5,7},{7,5},{8,10},{10,8},{9,1... | collective-permute-start | bytes 4669448 | tf_op jit(solution)/shard_map/ppermute | solution.py:420
  3.4 12.3 %collective-permute-start.2 = (bf16[288,640]{1,0:T(8,128)(2,1)}, bf16[288,640]{1,0:T(8,128)(2,1)S(1)}, u32[]{:S(2)}, u32[]{:S(2)}) collective-permute-start(bf16[288,640]{1,0:T(8,128)(2,1)} %get-tuple-element.21), channel_id=1, source_target_pairs={{0,1},{1,0},{2,3},{3,2},{4,5},{5,4},{6,7},{7,6},{8,9},{9,8},{10,11... | collective-permute-start | bytes 1105928 | tf_op jit(solution)/shard_map/ppermute | solution.py:451
  6.1 1.4 %copy-start.1 = (bf16[640,1216]{0,1:T(8,128)(2,1)S(1)}, bf16[640,1216]{0,1:T(8,128)(2,1)}, u32[]{:S(2)}) copy-start(bf16[640,1216]{0,1:T(8,128)(2,1)} %param.17) | copy-start | bytes 4669444
  7.5 0.9 %copy-start.4 = (bf16[48,2,640]{2,1,0:T(2,128)(2,1)S(1)}, bf16[48,2,640]{2,1,0:T(2,128)(2,1)}, u32[]{:S(2)}) copy-start(bf16[48,2,640]{2,1,0:T(2,128)(2,1)} %text_ref.1) | copy-start | bytes 368644
  8.4 0.7 %copy-start.5 = (f32[3,64]{1,0:T(4,128)S(1)}, f32[3,64]{1,0:T(4,128)}, u32[]{:S(2)}) copy-start(f32[3,64]{1,0:T(4,128)} %get-tuple-element.18.gains) | copy-start | bytes 2308
  9.0 2.2 %copy-start.9 = (bf16[48,640]{1,0:T(8,128)(2,1)S(1)}, bf16[48,640]{1,0:T(8,128)(2,1)}, u32[]{:S(2)}) copy-start(bf16[48,640]{1,0:T(8,128)(2,1)} %get-tuple-element.24) | copy-start | bytes 184324
  9.1 7.0 %copy-start.7 = (bf16[64,1216]{1,0:T(8,128)(2,1)S(1)}, bf16[64,1216]{1,0:T(8,128)(2,1)}, u32[]{:S(2)}) copy-start(bf16[64,1216]{1,0:T(8,128)(2,1)} %refs_9_.1) | copy-start | bytes 466948
  9.1 7.5 %copy-start.8 = (bf16[96,640]{1,0:T(8,128)(2,1)S(1)}, bf16[96,640]{1,0:T(8,128)(2,1)}, u32[]{:S(2)}) copy-start(bf16[96,640]{1,0:T(8,128)(2,1)} %get-tuple-element.28) | copy-start | bytes 368644
  11.0 9.1 %collective-permute-start.1 = (bf16[384,640]{1,0:T(8,128)(2,1)S(1)}, bf16[384,640]{1,0:T(8,128)(2,1)S(1)}, u32[]{:S(2)}, u32[]{:S(2)}) collective-permute-start(bf16[384,640]{1,0:T(8,128)(2,1)S(1)} %get-tuple-element.20.refs_1_), channel_id=1, source_target_pairs={{0,2},{2,0},{1,3},{3,1},{4,6},{6,4},{5,7},{7,5},{8,10},{10,8},{9,1... | collective-permute-start | bytes 1474568 | tf_op jit(solution)/shard_map/ppermute | solution.py:458
  11.2 8.6 %collective-permute-start.4 = (bf16[48,640]{1,0:T(8,128)(2,1)S(1)}, bf16[48,640]{1,0:T(8,128)(2,1)S(1)}, u32[]{:S(2)}, u32[]{:S(2)}) collective-permute-start(bf16[48,640]{1,0:T(8,128)(2,1)S(1)} %copy-done.9), channel_id=1, source_target_pairs={{0,1},{1,0},{2,3},{3,2},{4,5},{5,4},{6,7},{7,6},{8,9},{9,8},{10,11... | collective-permute-start | bytes 184328 | tf_op jit(solution)/shard_map/ppermute | solution.py:453
  16.0 4.0 %collective-permute-start.3 = (bf16[288,640]{1,0:T(8,128)(2,1)S(1)}, bf16[288,640]{1,0:T(8,128)(2,1)S(1)}, u32[]{:S(2)}, u32[]{:S(2)}) collective-permute-start(bf16[288,640]{1,0:T(8,128)(2,1)S(1)} %kv_norm_kernel.1.refs_3_), channel_id=1, source_target_pairs={{0,2},{2,0},{1,3},{3,1},{4,6},{6,4},{5,7},{7,5},{8,10},{10,8},{9,1... | collective-permute-start | bytes 1105928 | tf_op jit(solution)/shard_map/ppermute | solution.py:458
  16.1 11.0 %collective-permute-start.6 = (bf16[64,1216]{1,0:T(8,128)(2,1)S(1)}, bf16[64,1216]{1,0:T(8,128)(2,1)S(1)}, u32[]{:S(2)}, u32[]{:S(2)}) collective-permute-start(bf16[64,1216]{1,0:T(8,128)(2,1)S(1)} %copy-done.7), channel_id=1, source_target_pairs={{0,2},{2,0},{1,3},{3,1},{4,6},{6,4},{5,7},{7,5},{8,10},{10,8},{9,1... | collective-permute-start | bytes 466952 | tf_op jit(solution)/shard_map/ppermute | solution.py:421
  16.6 5.5 %collective-permute-start.7 = (bf16[96,640]{1,0:T(8,128)(2,1)S(1)}, bf16[96,640]{1,0:T(8,128)(2,1)S(1)}, u32[]{:S(2)}, u32[]{:S(2)}) collective-permute-start(bf16[96,640]{1,0:T(8,128)(2,1)S(1)} %copy-done.8), channel_id=1, source_target_pairs={{0,1},{1,0},{2,3},{3,2},{4,5},{5,4},{6,7},{7,6},{8,9},{9,8},{10,11... | collective-permute-start | bytes 368648 | tf_op jit(solution)/shard_map/ppermute | solution.py:453
  21.1 6.0 %collective-permute-start.5 = (bf16[48,768]{1,0:T(8,128)(2,1)S(1)}, bf16[48,768]{1,0:T(8,128)(2,1)S(1)}, u32[]{:S(2)}, u32[]{:S(2)}) collective-permute-start(bf16[48,768]{1,0:T(8,128)(2,1)S(1)} %get-tuple-element.25), channel_id=1, source_target_pairs={{0,1},{1,0},{2,3},{3,2},{4,5},{5,4},{6,7},{7,6},{8,9},{9,8},{10,11... | collective-permute-start | bytes 221192 | tf_op jit(solution)/shard_map/ppermute | solution.py:474
  23.1 4.0 %copy-start.2 = (f32[3,2432]{1,0:T(4,128)S(1)}, f32[3,2432]{1,0:T(4,128)}, u32[]{:S(2)}) copy-start(f32[3,2432]{1,0:T(4,128)} %mod_ref.3) | copy-start | bytes 87556
  23.1 4.0 %copy-start.6 = (bf16[12,12,2432]{2,1,0:T(8,128)(2,1)S(1)}, bf16[12,12,2432]{2,1,0:T(8,128)(2,1)}, u32[]{:S(2)}) copy-start(bf16[12,12,2432]{2,1,0:T(8,128)(2,1)} %refs_6_.1) | copy-start | bytes 2101252
  23.1 6.9 %collective-permute-start.9 = (bf16[48,1664]{1,0:T(8,128)(2,1)S(1)}, bf16[48,1664]{1,0:T(8,128)(2,1)S(1)}, u32[]{:S(2)}, u32[]{:S(2)}) collective-permute-start(bf16[48,1664]{1,0:T(8,128)(2,1)S(1)} %rest.1), channel_id=1, source_target_pairs={{0,1},{1,0},{2,3},{3,2},{4,5},{5,4},{6,7},{7,6},{8,9},{9,8},{10,11... | collective-permute-start | bytes 479240 | tf_op jit(solution)/shard_map/ppermute | solution.py:483
  26.8 12.2 %collective-permute-start.8 = (bf16[96,2432]{1,0:T(8,128)(2,1)S(1)}, bf16[96,2432]{1,0:T(8,128)(2,1)S(1)}, u32[]{:S(2)}, u32[]{:S(2)}) collective-permute-start(bf16[96,2432]{1,0:T(8,128)(2,1)S(1)} %attend.3), channel_id=1, source_target_pairs={{0,1},{1,0},{2,3},{3,2},{4,5},{5,4},{6,7},{7,6},{8,9},{9,8},{10,11... | collective-permute-start | bytes 1400840 | tf_op jit(solution)/shard_map/ppermute | solution.py:486
  27.1 2.9 %copy-start.3 = (f32[24,384]{1,0:T(8,128)S(1)}, f32[24,384]{1,0:T(8,128)}, u32[]{:S(2)}) copy-start(f32[24,384]{1,0:T(8,128)} %latent_ref.3) | copy-start | bytes 110596

commit v2 on v1

--- a/solution.py
+++ b/solution.py
@@ -133,6 +133,8 @@
 
 
 def prep_own_kernel(
+    index_ref,
+    count_ref,
     x_ref,
     text_ref,
     gains,
@@ -141,6 +143,7 @@
     kv_ref,
     q_ref,
     gains_out,
+    euler_ref,
     weight_ref,
     held,
     sems,
@@ -149,6 +152,9 @@
     tokens = q_ref.shape[0]
     k_ref, v_ref = halves(kv_ref)
     gains_out[...] = gains[...]
+    now = jnp.full(euler_ref.shape, index_ref[0], jnp.int32)
+    then = now + jnp.full(euler_ref.shape, count_ref[0], jnp.int32)
+    euler_ref[...] = noise_level(then) - noise_level(now)
     blocks = load_half(x_ref, held, sems, lax.axis_index("col"))
     rows = mine_ref.shape[0]
     row = lax.axis_index("row")
@@ -249,14 +255,8 @@
 
 def own_kernel(*refs):
     q_ref = refs[0]
-    w_ref, hidden_ref, mod_ref, got_ref, mine_ref, theirs_ref, index_ref, count_ref = refs[5:13]
-    out_ref, finals_ref, euler_ref, attended, index, count, sems = refs[13:]
-    copies = [
-        pltpu.make_async_copy(ref, to, sems.at[at])
-        for at, (ref, to) in enumerate(((index_ref, index), (count_ref, count)))
-    ]
-    for copy in copies:
-        copy.start()
+    w_ref, hidden_ref, mod_ref, got_ref, mine_ref, theirs_ref = refs[5:11]
+    out_ref, finals_ref, attended = refs[11:]
     attend(q_ref[...], *keys_and_values(refs[1:5]), attended)
     tile_rows = hidden_ref.shape[0]
 
@@ -276,11 +276,6 @@
     finals_ref[...] = jnp.concatenate(
         [jnp.where(is_first, mine, theirs), jnp.where(is_first, theirs, mine)], axis=1
     ).astype(jnp.bfloat16)
-    for copy in copies:
-        copy.wait()
-    now = jnp.full(euler_ref.shape, index[0], jnp.int32)
-    then = now + jnp.full(euler_ref.shape, count[0], jnp.int32)
-    euler_ref[...] = noise_level(then) - noise_level(now)
 
 
 def one_hot(dims, condition):
@@ -376,6 +371,7 @@
 VMEM = pl.BlockSpec(memory_space=pltpu.VMEM)
 ANY = pl.BlockSpec(memory_space=pl.ANY)
 HBM = pl.BlockSpec(memory_space=pltpu.HBM)
+SMEM = pl.BlockSpec(memory_space=pltpu.SMEM)
 
 
 def on_device(
@@ -419,16 +415,17 @@
 
     weight_got = lax.ppermute(weight_half, "row", SWAP)
     final_got = lax.ppermute(final_weight, "row", SWAP)
-    kv_own, q_own, gains_on, weight = pl.pallas_call(
+    kv_own, q_own, gains_on, euler, weight = pl.pallas_call(
         prep_own_kernel,
         out_shape=(
             shape((2 * (tokens + words), width)),
             block,
             shape(gains.shape, jnp.float32),
+            shape((1, latent.shape[1]), jnp.float32),
             shape((features, width)),
         ),
-        in_specs=[HBM, VMEM, VMEM, ANY, ANY],
-        out_specs=(VMEM,) * 4,
+        in_specs=[SMEM, SMEM, HBM, VMEM, VMEM, ANY, ANY],
+        out_specs=(VMEM,) * 5,
         scratch_shapes=[
             held,
             loads,
@@ -436,7 +433,7 @@
         ],
         compiler_params=params(),
         name="prep_own",
-    )(x, text_kv, gains, weight_half, weight_got)
+    )(step_index, step_count, x, text_kv, gains, weight_half, weight_got)
     def normed(kernel, got, duration):
         return pl.pallas_call(
             kernel,
@@ -451,7 +448,7 @@
     kv_got = normed(kv_norm_kernel, lax.ppermute(kv_raw, "col", SWAP), 0)
     q_got = [
         normed(q_norm_kernel, lax.ppermute(raw, "col", SWAP), duration)
-        for raw, duration in zip(q_raw, (3.5, 1))
+        for raw, duration in zip(q_raw, (4.2, 1))
     ]
     pairs = []
     for kv in (kv_own, kv_got):
@@ -484,21 +481,15 @@
     second_q, rest = lax.optimization_barrier((q_got[1], rest))
     (second,) = attended(second_q, features, True)
     second_got = lax.ppermute(second, "col", SWAP)
-    mixed, finals, euler = pl.pallas_call(
+    mixed, finals = pl.pallas_call(
         own_kernel,
         out_shape=(
             shape((tokens, features), jnp.float32),
             shape((final_weight.shape[0], features)),
-            shape((1, latent.shape[1]), jnp.float32),
         ),
-        in_specs=[VMEM] * 11 + [HBM] * 2,
-        out_specs=(VMEM,) * 3,
-        scratch_shapes=[
-            pltpu.VMEM((tokens, width), jnp.bfloat16),
-            pltpu.SMEM(step_index.shape, jnp.int32),
-            pltpu.SMEM(step_count.shape, jnp.int32),
-            pltpu.SemaphoreType.DMA((2,)),
-        ],
+        in_specs=[VMEM] * 11,
+        out_specs=(VMEM,) * 2,
+        scratch_shapes=[pltpu.VMEM((tokens, width), jnp.bfloat16)],
         compiler_params=params(),
         cost_estimate=lasting(60),
         name="own",
@@ -511,8 +502,6 @@
         first_got,
         final_weight,
         final_got,
-        step_index,
-        step_count,
     )
     results = ()
     for (start, _), got in ((chunks[0], rest_got), (chunks[1], second_got)):

time: 40.9 us -> 39.7 us (0.971)
  waiting for transfers between devices: 12.2 us -> 11 us
  starting transfers between devices: 9.43 us -> 9.94 us
    ppermute x1, waiting for transfers between devices: 3.28 us -> 0.78 us  [on_device(): kv_got = normed(kv_norm_kernel, lax.ppermute(kv_raw, 'col', SWAP), 0)]
    ppermute x1, starting transfers between devices: 0.14 us -> 2.19 us  [on_device(): first_got = lax.ppermute(first, 'col', SWAP)]
    ppermute x1, starting transfers between devices: 0.35 us -> 1.81 us  [on_device(): second_got = lax.ppermute(second, 'col', SWAP)]
    ppermute x1, starting transfers between devices: 1.8 us -> 0.35 us  [on_device(): rest_got = lax.ppermute(rest, 'col', SWAP)]
    ppermute x2, starting transfers between devices: 3.17 us -> 1.94 us  [on_device(): lax.ppermute(raw, 'col', SWAP)]
    ppermute x2, waiting for transfers between devices: 0.83 us -> 1.58 us  [on_device(): lax.ppermute(raw, 'col', SWAP)]
    ppermute x1, waiting for transfers between devices: 0.01 us -> 0.61 us  [on_device(): rest_got = lax.ppermute(rest, 'col', SWAP)]
    pallas_call x1, Pallas kernels: 2.86 us -> 2.41 us  [on_device(): pl.pallas_call(own_kernel, out_shape=(shape((tokens, features), jnp.float...]
  transfers between devices with their start and end apart: 10 -> 10, of which waited for: 3 -> 4; matrix products, arithmetic and copies ran while one was open for 0% -> 0% of each run, Pallas kernels for 30% -> 30%
where the time goes in v2:
time: 39.7 us; the launch traced here: 39.5 us
  Pallas kernels  13.5 us (34%)
  waiting for transfers between devices  11 us (28%)
  starting transfers between devices  9.94 us (25%)
  local copies, waits for them, and re-layouts  3.02 us (8%)
  between operations  2.12 us (5%)
    ppermute x1, waiting for transfers between devices, on_device(): second_got = lax.ppermute(second, 'col', SWAP)  7.99 us
    unnamed x20, local copies, waits for them, and re-layouts  3.02 us
    pallas_call x2, Pallas kernels, attended(): pl.pallas_call(attend_kernel, out_shape=out_shape, in_specs=[VMEM] * 6, o...  2.9 us
    ppermute x1, starting transfers between devices, on_device(): kv_got = normed(kv_norm_kernel, lax.ppermute(kv_raw, 'col', SWAP), 0)  2.68 us
    pallas_call x2, Pallas kernels, on_device(): pl.pallas_call(functools.partial(final_kernel, start), out_shape=(shape(l...  2.56 us
    pallas_call x1, Pallas kernels, on_device(): pl.pallas_call(own_kernel, out_shape=(shape((tokens, features), jnp.float...  2.41 us
    pallas_call x1, Pallas kernels, on_device(): pl.pallas_call(split_kernel, out_shape=tuple((shape((upto - start, width)...  2.2 us
    ppermute x1, starting transfers between devices, on_device(): first_got = lax.ppermute(first, 'col', SWAP)  2.19 us
  transfers between devices with their start and end apart: 10, of which 4 were waited for; matrix products, arithmetic and copies ran while one was open for 0% of the time, Pallas kernels for 30%

profile of v2, /device:TPU:0, one launch (start us, length us, event | category | flops | bytes accessed | tf_op | source)
XLA Modules:
  0.0 39.5 jit_solution(479876989704967621)
XLA Ops:
  0.6 0.0 copy-start
  0.6 0.5 %collective-permute-start = (bf16[1216,640]{1,0:T(8,128)(2,1)}, bf16[1216,640]{1,0:T(8,128)(2,1)S(1)}, u32[]{:S(2)}, u32[]{:S(2)}) collective-permute-start(bf16[1216,640]{1,0:T(8,128)(2,1)} %bitcast.7), channel_id=1, source_target_pairs={{0,2},{2,0},{1,3},{3,1},{4,6},{6,4},{5,7},{7,5},{8,10},{10,8},{9,1... | collective-permute-start | bytes 4669448 | tf_op jit(solution)/shard_map/ppermute | solution.py:416
  1.2 2.2 %split.1 = (bf16[48,640]{1,0:T(8,128)(2,1)}, bf16[96,640]{1,0:T(8,128)(2,1)}, bf16[288,640]{1,0:T(8,128)(2,1)}, f32[3,64]{1,0:T(4,128)}) custom-call(bf16[144,3,1280]{2,1,0:T(4,128)(2,1)} %bitcast.5, f32[1,64]{1,0:T(1,128)} %bitcast.9, f32[1,64]{1,0:T(1,128)} %bitcast.10, f32[1,64]{1,0:T(1,128)} %bitcast.11), custom_call_target="tpu_custom_call" | custom-call | tf_op jit(solution)/shard_map/split/pallas_call | solution.py:405
  3.4 2.7 %collective-permute-start.2 = (bf16[288,640]{1,0:T(8,128)(2,1)}, bf16[288,640]{1,0:T(8,128)(2,1)S(1)}, u32[]{:S(2)}, u32[]{:S(2)}) collective-permute-start(bf16[288,640]{1,0:T(8,128)(2,1)} %get-tuple-element.22), channel_id=1, source_target_pairs={{0,1},{1,0},{2,3},{3,2},{4,5},{5,4},{6,7},{7,6},{8,9},{9,8},{10,11... | collective-permute-start | bytes 1105928 | tf_op jit(solution)/shard_map/ppermute | solution.py:448
  7.4 0.0 collective-permute-done.theirs_ref
  7.4 0.0 copy-done
  7.4 0.0 copy-start.1
  7.4 1.4 %copy-done.1 = bf16[640,1216]{0,1:T(8,128)(2,1)S(1)} copy-done((bf16[640,1216]{0,1:T(8,128)(2,1)S(1)}, bf16[640,1216]{0,1:T(8,128)(2,1)}, u32[]{:S(2)}) %copy-start.1) | copy-done | bytes 1556504
  8.8 0.0 copy-start.4
  8.8 0.9 %copy-done.4 = bf16[48,2,640]{2,1,0:T(2,128)(2,1)S(1)} copy-done((bf16[48,2,640]{2,1,0:T(2,128)(2,1)S(1)}, bf16[48,2,640]{2,1,0:T(2,128)(2,1)}, u32[]{:S(2)}) %copy-start.4) | copy-done | bytes 122904
  9.7 0.0 copy-start.5
  9.7 0.7 %copy-done.5 = f32[3,64]{1,0:T(4,128)S(1)} copy-done((f32[3,64]{1,0:T(4,128)S(1)}, f32[3,64]{1,0:T(4,128)}, u32[]{:S(2)}) %copy-start.5) | copy-done | bytes 792
  10.4 1.9 %prep_own.1 = (bf16[384,640]{1,0:T(8,128)(2,1)S(1)}, bf16[144,640]{1,0:T(8,128)(2,1)S(1)}, f32[3,64]{1,0:T(4,128)S(1)}, f32[1,384]{1,0:T(1,128)S(1)}, bf16[2432,640]{1,0:T(8,128)(2,1)S(1)}) custom-call(s32[1]{0:T(128)S(6)} %copy.14.index_ref, s32[1]{0:T(128)S(6)} %copy.15.count_ref, bf16[144,3,1280]{2,1,0:T(4,128)(2,1)S(1)} %bitcast.6, ...), custom_call_target="tpu_custom_call" | custom-call | tf_op jit(solution)/shard_map/prep_own/pallas_call | solution.py:418
  12.3 0.2 collective-permute-start.1
  12.5 0.0 copy-done.9
  12.5 0.3 collective-permute-start.4
  12.8 0.0 copy-done.7
  12.8 0.2 collective-permute-start.6
  13.0 0.0 copy-done.8
  13.0 1.7 %collective-permute-start.7 = (bf16[96,640]{1,0:T(8,128)(2,1)S(1)}, bf16[96,640]{1,0:T(8,128)(2,1)S(1)}, u32[]{:S(2)}, u32[]{:S(2)}) collective-permute-start(bf16[96,640]{1,0:T(8,128)(2,1)S(1)} %copy-done.8), channel_id=1, source_target_pairs={{0,1},{1,0},{2,3},{3,2},{4,5},{5,4},{6,7},{7,6},{8,9},{9,8},{10,11... | collective-permute-start | bytes 368648 | tf_op jit(solution)/shard_map/ppermute | solution.py:450
  14.6 0.8 %collective-permute-done.2.x_ref = bf16[288,640]{1,0:T(8,128)(2,1)S(1)} collective-permute-done((bf16[288,640]{1,0:T(8,128)(2,1)}, bf16[288,640]{1,0:T(8,128)(2,1)S(1)}, u32[]{:S(2)}, u32[]{:S(2)}) %collective-permute-start.2) | collective-permute-done | bytes 368672 | tf_op jit(solution)/shard_map/ppermute | solution.py:448
  15.4 0.3 kv_norm_kernel.1.refs_3_
  15.7 0.1 collective-permute-start.3
  15.8 1.6 %collective-permute-done.4.x_ref = bf16[48,640]{1,0:T(8,128)(2,1)S(1)} collective-permute-done((bf16[48,640]{1,0:T(8,128)(2,1)S(1)}, bf16[48,640]{1,0:T(8,128)(2,1)S(1)}, u32[]{:S(2)}, u32[]{:S(2)}) %collective-permute-start.4) | collective-permute-done | bytes 61472 | tf_op jit(solution)/shard_map/ppermute | solution.py:450
  17.4 0.2 q_norm_kernel.2.refs_0_
  17.6 0.0 collective-permute-done.3.refs_4_
  17.6 0.0 collective-permute-done.1.refs_2_
  17.6 1.1 %attend.2 = (bf16[48,768]{1,0:T(8,128)(2,1)S(1)}, bf16[48,640]{1,0:T(8,128)(2,1)S(1)}) custom-call(bf16[48,640]{1,0:T(8,128)(2,1)S(1)} %q_norm_kernel.2.refs_0_, bf16[384,640]{1,0:T(8,128)(2,1)S(1)} %get-tuple-element.21.refs_1_, bf16[384,640]{1,0:T(8,128)(2,1)S(1)} %collective-permute-done.1.refs_2_, bf16[288,640]{1,0:T(8,128)(2,1)S(1)} %kv_norm_kernel.1.refs_3_, ...), custom_call_target="tpu_custom_call" | custom-call | tf_op jit(solution)/shard_map/attend/pallas_call | solution.py:460
  18.7 2.2 %collective-permute-start.5 = (bf16[48,768]{1,0:T(8,128)(2,1)S(1)}, bf16[48,768]{1,0:T(8,128)(2,1)S(1)}, u32[]{:S(2)}, u32[]{:S(2)}) collective-permute-start(bf16[48,768]{1,0:T(8,128)(2,1)S(1)} %get-tuple-element.26), channel_id=1, source_target_pairs={{0,1},{1,0},{2,3},{3,2},{4,5},{5,4},{6,7},{7,6},{8,9},{9,8},{10,11... | collective-permute-start | bytes 221192 | tf_op jit(solution)/shard_map/ppermute | solution.py:471
  20.9 0.0 collective-permute-done.7.x_ref
  20.9 0.2 q_norm_kernel.3.refs_0_
  21.1 0.7 %rest.1 = bf16[48,1664]{1,0:T(8,128)(2,1)S(1)} custom-call(bf16[48,640]{1,0:T(8,128)(2,1)S(1)} %get-tuple-element.29.attended_ref, bf16[2432,640]{1,0:T(8,128)(2,1)S(1)} %get-tuple-element.24.refs_5_.w_ref), custom_call_target="tpu_custom_call" | custom-call | tf_op jit(solution)/shard_map/rest/pallas_call | solution.py:472
  21.8 0.0 copy-start.2
  21.9 0.0 copy-start.6
  21.9 0.3 collective-permute-start.9
  22.2 1.9 %attend.3 = bf16[96,2432]{1,0:T(8,128)(2,1)S(1)} custom-call(bf16[96,640]{1,0:T(8,128)(2,1)S(1)} %q_norm_kernel.3.refs_0_, bf16[384,640]{1,0:T(8,128)(2,1)S(1)} %get-tuple-element.21.refs_1_, bf16[384,640]{1,0:T(8,128)(2,1)S(1)} %collective-permute-done.1.refs_2_, bf16[288,640]{1,0:T(8,128)(2,1)S(1)} %kv_norm_kernel.1.refs_3_, ...), custom_call_target="tpu_custom_call" | custom-call | tf_op jit(solution)/shard_map/attend/pallas_call | solution.py:460
  24.1 1.8 %collective-permute-start.8 = (bf16[96,2432]{1,0:T(8,128)(2,1)S(1)}, bf16[96,2432]{1,0:T(8,128)(2,1)S(1)}, u32[]{:S(2)}, u32[]{:S(2)}) collective-permute-start(bf16[96,2432]{1,0:T(8,128)(2,1)S(1)} %attend.3), channel_id=1, source_target_pairs={{0,1},{1,0},{2,3},{3,2},{4,5},{5,4},{6,7},{7,6},{8,9},{9,8},{10,11... | collective-permute-start | bytes 1400840 | tf_op jit(solution)/shard_map/ppermute | solution.py:483
  25.9 0.0 collective-permute-done.6.refs_10_
  25.9 0.0 collective-permute-done.5.refs_8_
  25.9 0.0 copy-done.2
  25.9 0.0 copy-done.6
  25.9 0.0 copy-start.3
  25.9 2.4 %own.1 = (f32[144,2432]{1,0:T(8,128)S(1)}, bf16[64,2432]{1,0:T(8,128)(2,1)S(1)}) custom-call(bf16[144,640]{1,0:T(8,128)(2,1)S(1)} %get-tuple-element.20.refs_0_, bf16[384,640]{1,0:T(8,128)(2,1)S(1)} %get-tuple-element.21.refs_1_, bf16[384,640]{1,0:T(8,128)(2,1)S(1)} %collective-permute-done.1.refs_2_, bf16[288,640]{1,0:T(8,128)(2,1)S(1)} %kv_norm_kernel.1.refs_3_, ...), custom_call_target="tpu_custom_call" | custom-call | flops 60000002048 | bytes 180000000 | tf_op jit(solution)/shard_map/own/pallas_call | solution.py:484
  28.3 0.6 %collective-permute-done.9.rest_ref = bf16[48,1664]{1,0:T(8,128)(2,1)S(1)} collective-permute-done((bf16[48,1664]{1,0:T(8,128)(2,1)S(1)}, bf16[48,1664]{1,0:T(8,128)(2,1)S(1)}, u32[]{:S(2)}, u32[]{:S(2)}) %collective-permute-start.9) | collective-permute-done | bytes 159776 | tf_op jit(solution)/shard_map/ppermute | solution.py:480
  28.9 0.0 copy-done.3
  28.9 0.9 %final.2 = (f32[24,384]{1,0:T(8,128)S(1)}, f32[24,384]{1,0:T(8,128)S(1)}) custom-call(f32[1,384]{1,0:T(1,128)S(1)} %get-tuple-element.19.euler_ref, f32[144,2432]{1,0:T(8,128)S(1)} %get-tuple-element.27.mixed_ref, bf16[48,1664]{1,0:T(8,128)(2,1)S(1)} %collective-permute-done.9.rest_ref, f32[3,2432]{1,0:T(4,128)S(1)} %copy-done.2, ...), custom_call_target="tpu_custom_call" | custom-call | tf_op jit(solution)/shard_map/final/pallas_call | solution.py:508
  29.8 8.0 %collective-permute-done.8.rest_ref = bf16[96,2432]{1,0:T(8,128)(2,1)S(1)} collective-permute-done((bf16[96,2432]{1,0:T(8,128)(2,1)S(1)}, bf16[96,2432]{1,0:T(8,128)(2,1)S(1)}, u32[]{:S(2)}, u32[]{:S(2)}) %collective-permute-start.8) | collective-permute-done | bytes 466976 | tf_op jit(solution)/shard_map/ppermute | solution.py:483
  37.8 1.7 %final.3 = (f32[24,384]{1,0:T(8,128)}, f32[24,384]{1,0:T(8,128)}) custom-call(f32[1,384]{1,0:T(1,128)S(1)} %get-tuple-element.19.euler_ref, f32[144,2432]{1,0:T(8,128)S(1)} %get-tuple-element.27.mixed_ref, bf16[96,2432]{1,0:T(8,128)(2,1)S(1)} %collective-permute-done.8.rest_ref, f32[3,2432]{1,0:T(4,128)S(1)} %copy-done.2, ...), custom_call_target="tpu_custom_call" | custom-call | tf_op jit(solution)/shard_map/final/pallas_call | solution.py:508
  (3 shorter events, 0.0 us)
Async XLA Ops:
  0.6 6.7 %copy-start = (bf16[12,12,3,1280]{3,2,1,0:T(4,128)(2,1)S(1)}, bf16[12,12,3,1280]{3,2,1,0:T(4,128)(2,1)}, u32[]{:S(2)}) copy-start(bf16[12,12,3,1280]{3,2,1,0:T(4,128)(2,1)} %param.12) | copy-start | bytes 3317764
  0.6 6.7 %collective-permute-start = (bf16[1216,640]{1,0:T(8,128)(2,1)}, bf16[1216,640]{1,0:T(8,128)(2,1)S(1)}, u32[]{:S(2)}, u32[]{:S(2)}) collective-permute-start(bf16[1216,640]{1,0:T(8,128)(2,1)} %bitcast.7), channel_id=1, source_target_pairs={{0,2},{2,0},{1,3},{3,1},{4,6},{6,4},{5,7},{7,5},{8,10},{10,8},{9,1... | collective-permute-start | bytes 4669448 | tf_op jit(solution)/shard_map/ppermute | solution.py:416
  3.4 12.1 %collective-permute-start.2 = (bf16[288,640]{1,0:T(8,128)(2,1)}, bf16[288,640]{1,0:T(8,128)(2,1)S(1)}, u32[]{:S(2)}, u32[]{:S(2)}) collective-permute-start(bf16[288,640]{1,0:T(8,128)(2,1)} %get-tuple-element.22), channel_id=1, source_target_pairs={{0,1},{1,0},{2,3},{3,2},{4,5},{5,4},{6,7},{7,6},{8,9},{9,8},{10,11... | collective-permute-start | bytes 1105928 | tf_op jit(solution)/shard_map/ppermute | solution.py:448
  7.4 1.4 %copy-start.1 = (bf16[640,1216]{0,1:T(8,128)(2,1)S(1)}, bf16[640,1216]{0,1:T(8,128)(2,1)}, u32[]{:S(2)}) copy-start(bf16[640,1216]{0,1:T(8,128)(2,1)} %param.17) | copy-start | bytes 4669444
  8.8 0.9 %copy-start.4 = (bf16[48,2,640]{2,1,0:T(2,128)(2,1)S(1)}, bf16[48,2,640]{2,1,0:T(2,128)(2,1)}, u32[]{:S(2)}) copy-start(bf16[48,2,640]{2,1,0:T(2,128)(2,1)} %text_ref.1) | copy-start | bytes 368644
  9.7 0.7 %copy-start.5 = (f32[3,64]{1,0:T(4,128)S(1)}, f32[3,64]{1,0:T(4,128)}, u32[]{:S(2)}) copy-start(f32[3,64]{1,0:T(4,128)} %get-tuple-element.18.gains) | copy-start | bytes 2308
  10.4 2.2 %copy-start.9 = (bf16[48,640]{1,0:T(8,128)(2,1)S(1)}, bf16[48,640]{1,0:T(8,128)(2,1)}, u32[]{:S(2)}) copy-start(bf16[48,640]{1,0:T(8,128)(2,1)} %get-tuple-element.25) | copy-start | bytes 184324
  10.4 2.4 %copy-start.7 = (bf16[64,1216]{1,0:T(8,128)(2,1)S(1)}, bf16[64,1216]{1,0:T(8,128)(2,1)}, u32[]{:S(2)}) copy-start(bf16[64,1216]{1,0:T(8,128)(2,1)} %refs_9_.1) | copy-start | bytes 466948
  10.4 2.6 %copy-start.8 = (bf16[96,640]{1,0:T(8,128)(2,1)S(1)}, bf16[96,640]{1,0:T(8,128)(2,1)}, u32[]{:S(2)}) copy-start(bf16[96,640]{1,0:T(8,128)(2,1)} %get-tuple-element.28) | copy-start | bytes 368644
  12.3 5.3 %collective-permute-start.1 = (bf16[384,640]{1,0:T(8,128)(2,1)S(1)}, bf16[384,640]{1,0:T(8,128)(2,1)S(1)}, u32[]{:S(2)}, u32[]{:S(2)}) collective-permute-start(bf16[384,640]{1,0:T(8,128)(2,1)S(1)} %get-tuple-element.21.refs_1_), channel_id=1, source_target_pairs={{0,2},{2,0},{1,3},{3,1},{4,6},{6,4},{5,7},{7,5},{8,10},{10,8},{9,1... | collective-permute-start | bytes 1474568 | tf_op jit(solution)/shard_map/ppermute | solution.py:455
  12.5 4.8 %collective-permute-start.4 = (bf16[48,640]{1,0:T(8,128)(2,1)S(1)}, bf16[48,640]{1,0:T(8,128)(2,1)S(1)}, u32[]{:S(2)}, u32[]{:S(2)}) collective-permute-start(bf16[48,640]{1,0:T(8,128)(2,1)S(1)} %copy-done.9), channel_id=1, source_target_pairs={{0,1},{1,0},{2,3},{3,2},{4,5},{5,4},{6,7},{7,6},{8,9},{9,8},{10,11... | collective-permute-start | bytes 184328 | tf_op jit(solution)/shard_map/ppermute | solution.py:450
  12.8 13.1 %collective-permute-start.6 = (bf16[64,1216]{1,0:T(8,128)(2,1)S(1)}, bf16[64,1216]{1,0:T(8,128)(2,1)S(1)}, u32[]{:S(2)}, u32[]{:S(2)}) collective-permute-start(bf16[64,1216]{1,0:T(8,128)(2,1)S(1)} %copy-done.7), channel_id=1, source_target_pairs={{0,2},{2,0},{1,3},{3,1},{4,6},{6,4},{5,7},{7,5},{8,10},{10,8},{9,1... | collective-permute-start | bytes 466952 | tf_op jit(solution)/shard_map/ppermute | solution.py:417
  13.0 7.9 %collective-permute-start.7 = (bf16[96,640]{1,0:T(8,128)(2,1)S(1)}, bf16[96,640]{1,0:T(8,128)(2,1)S(1)}, u32[]{:S(2)}, u32[]{:S(2)}) collective-permute-start(bf16[96,640]{1,0:T(8,128)(2,1)S(1)} %copy-done.8), channel_id=1, source_target_pairs={{0,1},{1,0},{2,3},{3,2},{4,5},{5,4},{6,7},{7,6},{8,9},{9,8},{10,11... | collective-permute-start | bytes 368648 | tf_op jit(solution)/shard_map/ppermute | solution.py:450
  15.7 1.9 %collective-permute-start.3 = (bf16[288,640]{1,0:T(8,128)(2,1)S(1)}, bf16[288,640]{1,0:T(8,128)(2,1)S(1)}, u32[]{:S(2)}, u32[]{:S(2)}) collective-permute-start(bf16[288,640]{1,0:T(8,128)(2,1)S(1)} %kv_norm_kernel.1.refs_3_), channel_id=1, source_target_pairs={{0,2},{2,0},{1,3},{3,1},{4,6},{6,4},{5,7},{7,5},{8,10},{10,8},{9,1... | collective-permute-start | bytes 1105928 | tf_op jit(solution)/shard_map/ppermute | solution.py:455
  18.7 7.2 %collective-permute-start.5 = (bf16[48,768]{1,0:T(8,128)(2,1)S(1)}, bf16[48,768]{1,0:T(8,128)(2,1)S(1)}, u32[]{:S(2)}, u32[]{:S(2)}) collective-permute-start(bf16[48,768]{1,0:T(8,128)(2,1)S(1)} %get-tuple-element.26), channel_id=1, source_target_pairs={{0,1},{1,0},{2,3},{3,2},{4,5},{5,4},{6,7},{7,6},{8,9},{9,8},{10,11... | collective-permute-start | bytes 221192 | tf_op jit(solution)/shard_map/ppermute | solution.py:471
  21.8 4.0 %copy-start.2 = (f32[3,2432]{1,0:T(4,128)S(1)}, f32[3,2432]{1,0:T(4,128)}, u32[]{:S(2)}) copy-start(f32[3,2432]{1,0:T(4,128)} %mod_ref.3) | copy-start | bytes 87556
  21.9 4.0 %copy-start.6 = (bf16[12,12,2432]{2,1,0:T(8,128)(2,1)S(1)}, bf16[12,12,2432]{2,1,0:T(8,128)(2,1)}, u32[]{:S(2)}) copy-start(bf16[12,12,2432]{2,1,0:T(8,128)(2,1)} %refs_6_.1) | copy-start | bytes 2101252
  21.9 7.1 %collective-permute-start.9 = (bf16[48,1664]{1,0:T(8,128)(2,1)S(1)}, bf16[48,1664]{1,0:T(8,128)(2,1)S(1)}, u32[]{:S(2)}, u32[]{:S(2)}) collective-permute-start(bf16[48,1664]{1,0:T(8,128)(2,1)S(1)} %rest.1), channel_id=1, source_target_pairs={{0,1},{1,0},{2,3},{3,2},{4,5},{5,4},{6,7},{7,6},{8,9},{9,8},{10,11... | collective-permute-start | bytes 479240 | tf_op jit(solution)/shard_map/ppermute | solution.py:480
  24.1 13.7 %collective-permute-start.8 = (bf16[96,2432]{1,0:T(8,128)(2,1)S(1)}, bf16[96,2432]{1,0:T(8,128)(2,1)S(1)}, u32[]{:S(2)}, u32[]{:S(2)}) collective-permute-start(bf16[96,2432]{1,0:T(8,128)(2,1)S(1)} %attend.3), channel_id=1, source_target_pairs={{0,1},{1,0},{2,3},{3,2},{4,5},{5,4},{6,7},{7,6},{8,9},{9,8},{10,11... | collective-permute-start | bytes 1400840 | tf_op jit(solution)/shard_map/ppermute | solution.py:483
  25.9 3.0 %copy-start.3 = (f32[24,384]{1,0:T(8,128)S(1)}, f32[24,384]{1,0:T(8,128)}, u32[]{:S(2)}) copy-start(f32[24,384]{1,0:T(8,128)} %latent_ref.3) | copy-start | bytes 110596

commit v3 on v2

--- a/solution.py
+++ b/solution.py
@@ -18,7 +18,8 @@
 VMEM_LIMIT = 16 * 1024 * 1024
 VMEM_MOST = 60 * 1024 * 1024
 LOADS = 9
-FIRST = 768
+FIRST = 1280
+STEP = 640
 SWAP = [(0, 1), (1, 0)]
 
 
@@ -133,44 +134,18 @@
 
 
 def prep_own_kernel(
-    index_ref,
-    count_ref,
-    x_ref,
-    text_ref,
-    gains,
-    mine_ref,
-    theirs_ref,
-    kv_ref,
-    q_ref,
-    gains_out,
-    euler_ref,
-    weight_ref,
-    held,
-    sems,
-    stack_sems,
+    index_ref, count_ref, x_ref, text_ref, gains, _, kv_ref, q_ref, gains_out, euler_ref, __
 ):
-    tokens = q_ref.shape[0]
+    tokens, width = q_ref.shape
     k_ref, v_ref = halves(kv_ref)
     gains_out[...] = gains[...]
     now = jnp.full(euler_ref.shape, index_ref[0], jnp.int32)
     then = now + jnp.full(euler_ref.shape, count_ref[0], jnp.int32)
     euler_ref[...] = noise_level(then) - noise_level(now)
-    blocks = load_half(x_ref, held, sems, lax.axis_index("col"))
-    rows = mine_ref.shape[0]
-    row = lax.axis_index("row")
-    stacks = [
-        pltpu.make_async_copy(
-            ref, weight_ref.at[pl.ds(pl.multiple_of(place * rows, 16), rows)], stack_sems.at[at]
-        )
-        for at, (ref, place) in enumerate(((mine_ref, row), (theirs_ref, 1 - row)))
-    ]
-    for stack in stacks:
-        stack.start()
     text = text_ref[...].astype(jnp.float32).transpose(1, 0, 2)
     v_ref[tokens:] = text[1].astype(jnp.bfloat16)
-    for _, copy in blocks:
-        copy.wait()
-    q, k, v = held[...].transpose(1, 0, 2)
+    at = pl.multiple_of(lax.axis_index("col") * width, LANES)
+    q, k, v = x_ref[:, :, pl.ds(at, width)].transpose(1, 0, 2)
     v_ref[:tokens] = v
     k_ref[:tokens], k_ref[tokens:], q_ref[...] = head_norms(
         [
@@ -179,8 +154,6 @@
             (q.astype(jnp.float32), gains[0:1]),
         ]
     )
-    for stack in stacks:
-        stack.wait()
 
 
 def attend(q, keys_refs, values_refs, attended_ref):
@@ -222,59 +195,70 @@
         finish(at, scores)
 
 
-def project(attended, weight_ref, start, upto, store, step):
-    for at in range(start, upto, step):
-        to = min(at + step, upto)
-        product = lax.dot_general(
-            attended,
-            weight_ref[at:to],
-            (((1,), (1,)), ((), ())),
-            preferred_element_type=jnp.float32,
-        )
-        store(at, to, product.astype(jnp.bfloat16))
+def project(attended, halves_refs, start, upto, store):
+    half = halves_refs[0].shape[0]
+    for at in range(start, upto, STEP):
+        to = min(at + STEP, upto)
+        parts = []
+        for place, ref in enumerate(halves_refs):
+            low, high = max(at, place * half), min(to, place * half + half)
+            if low < high:
+                product = lax.dot_general(
+                    attended,
+                    ref[low - place * half : high - place * half],
+                    (((1,), (1,)), ((), ())),
+                    preferred_element_type=jnp.float32,
+                )
+                parts.append(product.astype(jnp.bfloat16))
+        store(at, to, parts[0] if len(parts) == 1 else jnp.concatenate(parts, axis=1))
 
 
 def attend_kernel(*refs):
-    q_ref, (w_ref, out_ref, attended) = refs[0], refs[5:]
+    q_ref, weight_refs, (out_ref, attended) = refs[0], refs[5:7], refs[7:]
     attend(q_ref[...], *keys_and_values(refs[1:5]), attended)
 
     def keep(at, to, product):
         out_ref[:, at:to] = product
 
-    project(attended[...], w_ref, 0, out_ref.shape[1], keep, FIRST)
-
-
-def rest_kernel(attended_ref, w_ref, out_ref):
-    features, start = w_ref.shape[0], w_ref.shape[0] - out_ref.shape[1]
+    project(attended[...], weight_refs, 0, out_ref.shape[1], keep)
+
+
+def rest_kernel(attended_ref, mine_ref, theirs_ref, out_ref):
+    features = 2 * mine_ref.shape[0]
+    start = features - out_ref.shape[1]
 
     def keep(at, to, product):
         out_ref[:, at - start : to - start] = product
 
-    project(attended_ref[...], w_ref, start, features, keep, 640)
+    project(attended_ref[...], (mine_ref, theirs_ref), start, features, keep)
+
+
+def in_order(x, is_first):
+    half = x.shape[1] // 2
+    return jnp.where(is_first, x, jnp.concatenate([x[:, half:], x[:, :half]], axis=1))
 
 
 def own_kernel(*refs):
-    q_ref = refs[0]
-    w_ref, hidden_ref, mod_ref, got_ref, mine_ref, theirs_ref = refs[5:11]
-    out_ref, finals_ref, attended = refs[11:]
+    q_ref, weight_refs = refs[0], refs[5:7]
+    hidden_ref, mod_ref, got_ref, mine_ref, theirs_ref = refs[7:12]
+    out_ref, mod_out, finals_ref, attended = refs[12:]
     attend(q_ref[...], *keys_and_values(refs[1:5]), attended)
-    tile_rows = hidden_ref.shape[0]
+    is_first = lax.axis_index("row") == 0
+    tile_rows, tile_cols, features = hidden_ref.shape
+    mod_out[...] = in_order(mod_ref[...], is_first)
+    out_ref[...] = in_order(
+        jnp.concatenate([hidden_ref[row].astype(jnp.float32) for row in range(tile_rows)], axis=0),
+        is_first,
+    )
 
     def keep(at, to, product):
-        part = mod_ref[2:3, at:to] * product.astype(jnp.float32)
-        held = jnp.concatenate(
-            [hidden_ref[row, :, at:to].astype(jnp.float32) for row in range(tile_rows)], axis=0
-        )
-        out_ref[:, at:to] = held + part
-
-    project(attended[...], w_ref, 0, w_ref.shape[0], keep, 640)
+        out_ref[:, at:to] += mod_out[2:3, at:to] * product.astype(jnp.float32)
+
+    project(attended[...], weight_refs, 0, features, keep)
     upto, to = got_ref.shape
-    out_ref[:upto, :to] += mod_ref[2:3, :to] * got_ref[...].astype(jnp.float32)
-    is_first = lax.axis_index("row") == 0
-    mine = mine_ref[...].astype(jnp.float32)
-    theirs = theirs_ref[...].astype(jnp.float32)
+    out_ref[:upto, :to] += mod_out[2:3, :to] * got_ref[...].astype(jnp.float32)
     finals_ref[...] = jnp.concatenate(
-        [jnp.where(is_first, mine, theirs), jnp.where(is_first, theirs, mine)], axis=1
+        [mine_ref[...].astype(jnp.float32), theirs_ref[...].astype(jnp.float32)], axis=1
     ).astype(jnp.bfloat16)
 
 
@@ -415,25 +399,23 @@
 
     weight_got = lax.ppermute(weight_half, "row", SWAP)
     final_got = lax.ppermute(final_weight, "row", SWAP)
-    kv_own, q_own, gains_on, euler, weight = pl.pallas_call(
+    kv_own, q_own, gains_on, euler, weight_theirs = pl.pallas_call(
         prep_own_kernel,
         out_shape=(
             shape((2 * (tokens + words), width)),
             block,
             shape(gains.shape, jnp.float32),
             shape((1, latent.shape[1]), jnp.float32),
-            shape((features, width)),
+            shape(weight_got.shape),
         ),
-        in_specs=[SMEM, SMEM, HBM, VMEM, VMEM, ANY, ANY],
-        out_specs=(VMEM,) * 5,
-        scratch_shapes=[
-            held,
-            loads,
-            pltpu.SemaphoreType.DMA((2,)),
-        ],
+        in_specs=[SMEM, SMEM, VMEM, VMEM, VMEM, ANY],
+        out_specs=(VMEM,) * 4 + (ANY,),
+        input_output_aliases={5: 4},
         compiler_params=params(),
         name="prep_own",
-    )(step_index, step_count, x, text_kv, gains, weight_half, weight_got)
+    )(step_index, step_count, x, text_kv, gains, weight_got)
+    weights = (weight_half, weight_theirs)
+
     def normed(kernel, got, duration):
         return pl.pallas_call(
             kernel,
@@ -460,35 +442,36 @@
         return pl.pallas_call(
             attend_kernel,
             out_shape=out_shape,
-            in_specs=[VMEM] * 6,
+            in_specs=[VMEM] * 7,
             out_specs=(VMEM,) * len(out_shape),
             scratch_shapes=[pltpu.VMEM((rows, width), jnp.bfloat16)] if scratch else (),
             compiler_params=params(),
             name="attend",
-        )(q, *pairs, weight)
+        )(q, *pairs, *weights)
 
     first, heads = attended(q_got[0], FIRST, False)
     first_got = lax.ppermute(first, "col", SWAP)
     rest = pl.pallas_call(
         rest_kernel,
         out_shape=shape((cut, features - FIRST)),
-        in_specs=[VMEM] * 2,
+        in_specs=[VMEM] * 3,
         out_specs=VMEM,
         compiler_params=params(),
         name="rest",
-    )(heads, weight)
+    )(heads, *weights)
     rest_got = lax.ppermute(rest, "col", SWAP)
     second_q, rest = lax.optimization_barrier((q_got[1], rest))
     (second,) = attended(second_q, features, True)
     second_got = lax.ppermute(second, "col", SWAP)
-    mixed, finals = pl.pallas_call(
+    mixed, mods, finals = pl.pallas_call(
         own_kernel,
         out_shape=(
             shape((tokens, features), jnp.float32),
+            shape(modulation.shape, jnp.float32),
             shape((final_weight.shape[0], features)),
         ),
-        in_specs=[VMEM] * 11,
-        out_specs=(VMEM,) * 2,
+        in_specs=[VMEM] * 12,
+        out_specs=(VMEM,) * 3,
         scratch_shapes=[pltpu.VMEM((tokens, width), jnp.bfloat16)],
         compiler_params=params(),
         cost_estimate=lasting(60),
@@ -496,7 +479,7 @@
     )(
         q_own,
         *pairs,
-        weight,
+        *weights,
         hidden,
         modulation,
         first_got,
@@ -512,7 +495,7 @@
             out_specs=(VMEM, VMEM),
             compiler_params=params(),
             name="final",
-        )(euler, mixed, got, modulation, finals, latent, *results)
+        )(euler, mixed, got, mods, finals, latent, *results)
     return results
 
 

time: 39.7 us -> 38.9 us (0.980)
  waiting for transfers between devices: 11 us -> 12.7 us
  local copies, waits for them, and re-layouts: 3.02 us -> 1.62 us
  Pallas kernels: 13.5 us -> 12.6 us
    ppermute x1, waiting for transfers between devices: 0.78 us -> 3.51 us  [on_device(): kv_got = normed(kv_norm_kernel, lax.ppermute(kv_raw, 'col', SWAP), 0)]
    unnamed x20, local copies, waits for them, and re-layouts: 3.02 us -> 1.62 us
    pallas_call x1, Pallas kernels: 1.94 us -> 0.88 us  [on_device(): pl.pallas_call(prep_own_kernel, out_shape=(shape((2 * (tokens + words), w...]
    ppermute x2, waiting for transfers between devices: 1.58 us -> 0.94 us  [on_device(): lax.ppermute(raw, 'col', SWAP)]
    ppermute x1, waiting for transfers between devices: 0.61 us -> 0.01 us  [on_device(): rest_got = lax.ppermute(rest, 'col', SWAP)]
    ppermute x2, waiting for transfers between devices: 0.01 us -> 0.55 us  [on_device(): pairs += [kv, lax.ppermute(kv, 'row', SWAP)]]
  transfers between devices with their start and end apart: 10 -> 10, of which waited for: 4 -> 4; matrix products, arithmetic and copies ran while one was open for 0% -> 0% of each run, Pallas kernels for 30% -> 28%
where the time goes in v3:
time: 38.9 us; the launch traced here: 38.7 us
  waiting for transfers between devices  12.7 us (33%)
  Pallas kernels  12.6 us (32%)
  starting transfers between devices  9.72 us (25%)
  between operations  2.12 us (5%)
  local copies, waits for them, and re-layouts  1.62 us (4%)
    ppermute x1, waiting for transfers between devices, on_device(): second_got = lax.ppermute(second, 'col', SWAP)  7.66 us
    ppermute x1, waiting for transfers between devices, on_device(): kv_got = normed(kv_norm_kernel, lax.ppermute(kv_raw, 'col', SWAP), 0)  3.51 us
    pallas_call x2, Pallas kernels, attended(): pl.pallas_call(attend_kernel, out_shape=out_shape, in_specs=[VMEM] * 7, o...  3.18 us
    ppermute x1, starting transfers between devices, on_device(): kv_got = normed(kv_norm_kernel, lax.ppermute(kv_raw, 'col', SWAP), 0)  2.68 us
    pallas_call x2, Pallas kernels, on_device(): pl.pallas_call(functools.partial(final_kernel, start), out_shape=(shape(l...  2.57 us
    pallas_call x1, Pallas kernels, on_device(): pl.pallas_call(own_kernel, out_shape=(shape((tokens, features), jnp.float...  2.49 us
    pallas_call x1, Pallas kernels, on_device(): pl.pallas_call(split_kernel, out_shape=tuple((shape((upto - start, width)...  2.2 us
    ppermute x1, starting transfers between devices, on_device(): second_got = lax.ppermute(second, 'col', SWAP)  1.97 us
  transfers between devices with their start and end apart: 10, of which 4 were waited for; matrix products, arithmetic and copies ran while one was open for 0% of the time, Pallas kernels for 28%

profile of v3, /device:TPU:0, one launch (start us, length us, event | category | flops | bytes accessed | tf_op | source)
XLA Modules:
  0.0 38.7 jit_solution(12001013392650509110)
XLA Ops:
  0.6 0.0 copy-start.1
  0.6 0.5 %collective-permute-start = (bf16[1216,640]{1,0:T(8,128)(2,1)}, bf16[1216,640]{1,0:T(8,128)(2,1)S(1)}, u32[]{:S(2)}, u32[]{:S(2)}) collective-permute-start(bf16[1216,640]{1,0:T(8,128)(2,1)} %bitcast.5), channel_id=1, source_target_pairs={{0,2},{2,0},{1,3},{3,1},{4,6},{6,4},{5,7},{7,5},{8,10},{10,8},{9,1... | collective-permute-start | bytes 4669448 | tf_op jit(solution)/shard_map/ppermute | solution.py:400
  1.2 2.2 %split.1 = (bf16[48,640]{1,0:T(8,128)(2,1)}, bf16[96,640]{1,0:T(8,128)(2,1)}, bf16[288,640]{1,0:T(8,128)(2,1)}, f32[3,64]{1,0:T(4,128)}) custom-call(bf16[144,3,1280]{2,1,0:T(4,128)(2,1)} %bitcast.10, f32[1,64]{1,0:T(1,128)} %bitcast.12, f32[1,64]{1,0:T(1,128)} %bitcast.13, f32[1,64]{1,0:T(1,128)} %bitcast.14), custom_call_target="tpu_custom_call" | custom-call | tf_op jit(solution)/shard_map/split/pallas_call | solution.py:389
  3.4 2.7 %collective-permute-start.2 = (bf16[288,640]{1,0:T(8,128)(2,1)}, bf16[288,640]{1,0:T(8,128)(2,1)S(1)}, u32[]{:S(2)}, u32[]{:S(2)}) collective-permute-start(bf16[288,640]{1,0:T(8,128)(2,1)} %get-tuple-element.23), channel_id=1, source_target_pairs={{0,1},{1,0},{2,3},{3,2},{4,5},{5,4},{6,7},{7,6},{8,9},{9,8},{10,11... | collective-permute-start | bytes 1105928 | tf_op jit(solution)/shard_map/ppermute | solution.py:430
  7.4 0.0 collective-permute-done._
  7.4 0.0 copy-done.1
  7.4 0.0 copy-start.3
  7.4 0.9 %copy-done.3 = bf16[48,2,640]{2,1,0:T(2,128)(2,1)S(1)} copy-done((bf16[48,2,640]{2,1,0:T(2,128)(2,1)S(1)}, bf16[48,2,640]{2,1,0:T(2,128)(2,1)}, u32[]{:S(2)}) %copy-start.3) | copy-done | bytes 122904
  8.3 0.7 %copy-done.4 = f32[3,64]{1,0:T(4,128)S(1)} copy-done((f32[3,64]{1,0:T(4,128)S(1)}, f32[3,64]{1,0:T(4,128)}, u32[]{:S(2)}) %copy-start.4) | copy-done | bytes 792
  9.0 0.0 copy-start.9
  9.0 0.9 %prep_own.1 = (bf16[384,640]{1,0:T(8,128)(2,1)S(1)}, bf16[144,640]{1,0:T(8,128)(2,1)S(1)}, f32[3,64]{1,0:T(4,128)S(1)}, f32[1,384]{1,0:T(1,128)S(1)}, bf16[1216,640]{1,0:T(8,128)(2,1)S(1)}) custom-call(s32[1]{0:T(128)S(6)} %copy.16.index_ref, s32[1]{0:T(128)S(6)} %copy.17.count_ref, ...), custom_call_target="tpu_custom_call", output_to_operand_aliasing={{4}: (5, {})} | custom-call | tf_op jit(solution)/shard_map/prep_own/pallas_call | solution.py:402
  9.9 0.2 collective-permute-start.1
  10.1 0.0 copy-done.9
  10.1 0.3 collective-permute-start.4
  10.3 0.0 copy-done.6
  10.3 0.2 collective-permute-start.6
  10.5 0.0 copy-done.8
  10.5 1.7 %collective-permute-start.7 = (bf16[96,640]{1,0:T(8,128)(2,1)S(1)}, bf16[96,640]{1,0:T(8,128)(2,1)S(1)}, u32[]{:S(2)}, u32[]{:S(2)}) collective-permute-start(bf16[96,640]{1,0:T(8,128)(2,1)S(1)} %copy-done.8), channel_id=1, source_target_pairs={{0,1},{1,0},{2,3},{3,2},{4,5},{5,4},{6,7},{7,6},{8,9},{9,8},{10,11... | collective-permute-start | bytes 368648 | tf_op jit(solution)/shard_map/ppermute | solution.py:432
  12.2 3.5 %collective-permute-done.2.x_ref = bf16[288,640]{1,0:T(8,128)(2,1)S(1)} collective-permute-done((bf16[288,640]{1,0:T(8,128)(2,1)}, bf16[288,640]{1,0:T(8,128)(2,1)S(1)}, u32[]{:S(2)}, u32[]{:S(2)}) %collective-permute-start.2) | collective-permute-done | bytes 368672 | tf_op jit(solution)/shard_map/ppermute | solution.py:430
  15.7 0.3 kv_norm_kernel.1.refs_3_
  16.0 0.0 copy-start
  16.0 0.1 collective-permute-start.3
  16.1 0.9 %collective-permute-done.4.x_ref = bf16[48,640]{1,0:T(8,128)(2,1)S(1)} collective-permute-done((bf16[48,640]{1,0:T(8,128)(2,1)S(1)}, bf16[48,640]{1,0:T(8,128)(2,1)S(1)}, u32[]{:S(2)}, u32[]{:S(2)}) %collective-permute-start.4) | collective-permute-done | bytes 61472 | tf_op jit(solution)/shard_map/ppermute | solution.py:432
  17.0 0.2 q_norm_kernel.2.refs_0_
  17.2 0.5 %collective-permute-done.3.refs_4_ = bf16[288,640]{1,0:T(8,128)(2,1)S(1)} collective-permute-done((bf16[288,640]{1,0:T(8,128)(2,1)S(1)}, bf16[288,640]{1,0:T(8,128)(2,1)S(1)}, u32[]{:S(2)}, u32[]{:S(2)}) %collective-permute-start.3) | collective-permute-done | bytes 368672 | tf_op jit(solution)/shard_map/ppermute | solution.py:437
  17.8 0.0 collective-permute-done.1.refs_2_
  17.8 0.0 copy-done
  17.8 1.3 %attend.2 = (bf16[48,1280]{1,0:T(8,128)(2,1)S(1)}, bf16[48,640]{1,0:T(8,128)(2,1)S(1)}) custom-call(bf16[48,640]{1,0:T(8,128)(2,1)S(1)} %q_norm_kernel.2.refs_0_, bf16[384,640]{1,0:T(8,128)(2,1)S(1)} %get-tuple-element.22.refs_1_, bf16[384,640]{1,0:T(8,128)(2,1)S(1)} %collective-permute-done.1.refs_2_, bf16[288,640]{1,0:T(8,128)(2,1)S(1)} %kv_norm_kernel.1.refs_3_, ...), custom_call_target="tpu_custom_call" | custom-call | tf_op jit(solution)/shard_map/attend/pallas_call | solution.py:442
  19.0 2.0 %collective-permute-start.5 = (bf16[48,1280]{1,0:T(8,128)(2,1)S(1)}, bf16[48,1280]{1,0:T(8,128)(2,1)S(1)}, u32[]{:S(2)}, u32[]{:S(2)}) collective-permute-start(bf16[48,1280]{1,0:T(8,128)(2,1)S(1)} %get-tuple-element.27), channel_id=1, source_target_pairs={{0,1},{1,0},{2,3},{3,2},{4,5},{5,4},{6,7},{7,6},{8,9},{9,8},{10,11... | collective-permute-start | bytes 368648 | tf_op jit(solution)/shard_map/ppermute | solution.py:453
  21.0 0.0 collective-permute-done.7.x_ref
  21.0 0.2 q_norm_kernel.3.refs_0_
  21.3 0.5 %rest.1 = bf16[48,1152]{1,0:T(8,128)(2,1)S(1)} custom-call(bf16[48,640]{1,0:T(8,128)(2,1)S(1)} %get-tuple-element.30.attended_ref, bf16[1216,640]{1,0:T(8,128)(2,1)S(1)} %bitcast.7, bf16[1216,640]{1,0:T(8,128)(2,1)S(1)} %get-tuple-element.25.refs_6_.theirs_ref), custom_call_target="tpu_custom_call" | custom-call | tf_op jit(solution)/shard_map/rest/pallas_call | solution.py:454
  21.8 0.0 copy-start.5
  21.8 0.0 copy-start.7
  21.8 0.2 collective-permute-start.9
  22.0 1.9 %attend.3 = bf16[96,2432]{1,0:T(8,128)(2,1)S(1)} custom-call(bf16[96,640]{1,0:T(8,128)(2,1)S(1)} %q_norm_kernel.3.refs_0_, bf16[384,640]{1,0:T(8,128)(2,1)S(1)} %get-tuple-element.22.refs_1_, bf16[384,640]{1,0:T(8,128)(2,1)S(1)} %collective-permute-done.1.refs_2_, bf16[288,640]{1,0:T(8,128)(2,1)S(1)} %kv_norm_kernel.1.refs_3_, ...), custom_call_target="tpu_custom_call" | custom-call | tf_op jit(solution)/shard_map/attend/pallas_call | solution.py:442
  23.9 2.0 %collective-permute-start.8 = (bf16[96,2432]{1,0:T(8,128)(2,1)S(1)}, bf16[96,2432]{1,0:T(8,128)(2,1)S(1)}, u32[]{:S(2)}, u32[]{:S(2)}) collective-permute-start(bf16[96,2432]{1,0:T(8,128)(2,1)S(1)} %attend.3), channel_id=1, source_target_pairs={{0,1},{1,0},{2,3},{3,2},{4,5},{5,4},{6,7},{7,6},{8,9},{9,8},{10,11... | collective-permute-start | bytes 1400840 | tf_op jit(solution)/shard_map/ppermute | solution.py:465
  25.9 0.0 collective-permute-done.6.refs_11_
  25.9 0.0 collective-permute-done.5.refs_9_
  25.9 0.0 copy-done.5
  25.9 0.0 copy-done.7
  25.9 0.0 copy-start.2
  25.9 2.5 %own.1 = (f32[144,2432]{1,0:T(8,128)S(1)}, f32[3,2432]{1,0:T(4,128)S(1)}, bf16[64,2432]{1,0:T(8,128)(2,1)S(1)}) custom-call(bf16[144,640]{1,0:T(8,128)(2,1)S(1)} %get-tuple-element.21.refs_0_, bf16[384,640]{1,0:T(8,128)(2,1)S(1)} %get-tuple-element.22.refs_1_, bf16[384,640]{1,0:T(8,128)(2,1)S(1)} %collective-permute-done.1.refs_2_, ...), custom_call_target="tpu_custom_call" | custom-call | flops 60000002048 | bytes 180000000 | tf_op jit(solution)/shard_map/own/pallas_call | solution.py:466
  28.4 0.0 collective-permute-done.9.rest_ref
  28.5 0.0 copy-done.2
  28.5 0.9 %final.2 = (f32[24,384]{1,0:T(8,128)S(1)}, f32[24,384]{1,0:T(8,128)S(1)}) custom-call(f32[1,384]{1,0:T(1,128)S(1)} %get-tuple-element.20.euler_ref, f32[144,2432]{1,0:T(8,128)S(1)} %get-tuple-element.28.mixed_ref, bf16[48,1152]{1,0:T(8,128)(2,1)S(1)} %collective-permute-done.9.rest_ref, f32[3,2432]{1,0:T(4,128)S(1)} %get-tuple-element.32.mod_ref, ...), custom_call_target="tpu_custom_call" | custom-call | tf_op jit(solution)/shard_map/final/pallas_call | solution.py:491
  29.3 7.7 %collective-permute-done.8.rest_ref = bf16[96,2432]{1,0:T(8,128)(2,1)S(1)} collective-permute-done((bf16[96,2432]{1,0:T(8,128)(2,1)S(1)}, bf16[96,2432]{1,0:T(8,128)(2,1)S(1)}, u32[]{:S(2)}, u32[]{:S(2)}) %collective-permute-start.8) | collective-permute-done | bytes 466976 | tf_op jit(solution)/shard_map/ppermute | solution.py:465
  37.0 1.7 %final.3 = (f32[24,384]{1,0:T(8,128)}, f32[24,384]{1,0:T(8,128)}) custom-call(f32[1,384]{1,0:T(1,128)S(1)} %get-tuple-element.20.euler_ref, f32[144,2432]{1,0:T(8,128)S(1)} %get-tuple-element.28.mixed_ref, bf16[96,2432]{1,0:T(8,128)(2,1)S(1)} %collective-permute-done.8.rest_ref, f32[3,2432]{1,0:T(4,128)S(1)} %get-tuple-element.32.mod_ref, ...), custom_call_target="tpu_custom_call" | custom-call | tf_op jit(solution)/shard_map/final/pallas_call | solution.py:491
  (3 shorter events, 0.0 us)
Async XLA Ops:
  0.6 6.7 %copy-start.1 = (bf16[12,12,3,1280]{3,2,1,0:T(4,128)(2,1)S(1)}, bf16[12,12,3,1280]{3,2,1,0:T(4,128)(2,1)}, u32[]{:S(2)}) copy-start(bf16[12,12,3,1280]{3,2,1,0:T(4,128)(2,1)} %param.12) | copy-start | bytes 3317764
  0.6 6.7 %collective-permute-start = (bf16[1216,640]{1,0:T(8,128)(2,1)}, bf16[1216,640]{1,0:T(8,128)(2,1)S(1)}, u32[]{:S(2)}, u32[]{:S(2)}) collective-permute-start(bf16[1216,640]{1,0:T(8,128)(2,1)} %bitcast.5), channel_id=1, source_target_pairs={{0,2},{2,0},{1,3},{3,1},{4,6},{6,4},{5,7},{7,5},{8,10},{10,8},{9,1... | collective-permute-start | bytes 4669448 | tf_op jit(solution)/shard_map/ppermute | solution.py:400
  3.4 12.3 %collective-permute-start.2 = (bf16[288,640]{1,0:T(8,128)(2,1)}, bf16[288,640]{1,0:T(8,128)(2,1)S(1)}, u32[]{:S(2)}, u32[]{:S(2)}) collective-permute-start(bf16[288,640]{1,0:T(8,128)(2,1)} %get-tuple-element.23), channel_id=1, source_target_pairs={{0,1},{1,0},{2,3},{3,2},{4,5},{5,4},{6,7},{7,6},{8,9},{9,8},{10,11... | collective-permute-start | bytes 1105928 | tf_op jit(solution)/shard_map/ppermute | solution.py:430
  7.4 0.9 %copy-start.3 = (bf16[48,2,640]{2,1,0:T(2,128)(2,1)S(1)}, bf16[48,2,640]{2,1,0:T(2,128)(2,1)}, u32[]{:S(2)}) copy-start(bf16[48,2,640]{2,1,0:T(2,128)(2,1)} %text_ref.1) | copy-start | bytes 368644
  8.3 0.7 %copy-start.4 = (f32[3,64]{1,0:T(4,128)S(1)}, f32[3,64]{1,0:T(4,128)}, u32[]{:S(2)}) copy-start(f32[3,64]{1,0:T(4,128)} %get-tuple-element.19.gains) | copy-start | bytes 2308
  9.0 1.1 %copy-start.9 = (bf16[48,640]{1,0:T(8,128)(2,1)S(1)}, bf16[48,640]{1,0:T(8,128)(2,1)}, u32[]{:S(2)}) copy-start(bf16[48,640]{1,0:T(8,128)(2,1)} %get-tuple-element.26) | copy-start | bytes 184324
  9.0 1.4 %copy-start.6 = (bf16[64,1216]{1,0:T(8,128)(2,1)S(1)}, bf16[64,1216]{1,0:T(8,128)(2,1)}, u32[]{:S(2)}) copy-start(bf16[64,1216]{1,0:T(8,128)(2,1)} %refs_10_.1) | copy-start | bytes 466948
  9.0 1.5 %copy-start.8 = (bf16[96,640]{1,0:T(8,128)(2,1)S(1)}, bf16[96,640]{1,0:T(8,128)(2,1)}, u32[]{:S(2)}) copy-start(bf16[96,640]{1,0:T(8,128)(2,1)} %get-tuple-element.29) | copy-start | bytes 368644
  9.9 7.9 %collective-permute-start.1 = (bf16[384,640]{1,0:T(8,128)(2,1)S(1)}, bf16[384,640]{1,0:T(8,128)(2,1)S(1)}, u32[]{:S(2)}, u32[]{:S(2)}) collective-permute-start(bf16[384,640]{1,0:T(8,128)(2,1)S(1)} %get-tuple-element.22.refs_1_), channel_id=1, source_target_pairs={{0,2},{2,0},{1,3},{3,1},{4,6},{6,4},{5,7},{7,5},{8,10},{10,8},{9,1... | collective-permute-start | bytes 1474568 | tf_op jit(solution)/shard_map/ppermute | solution.py:437
  10.1 6.9 %collective-permute-start.4 = (bf16[48,640]{1,0:T(8,128)(2,1)S(1)}, bf16[48,640]{1,0:T(8,128)(2,1)S(1)}, u32[]{:S(2)}, u32[]{:S(2)}) collective-permute-start(bf16[48,640]{1,0:T(8,128)(2,1)S(1)} %copy-done.9), channel_id=1, source_target_pairs={{0,1},{1,0},{2,3},{3,2},{4,5},{5,4},{6,7},{7,6},{8,9},{9,8},{10,11... | collective-permute-start | bytes 184328 | tf_op jit(solution)/shard_map/ppermute | solution.py:432
  10.3 15.6 %collective-permute-start.6 = (bf16[64,1216]{1,0:T(8,128)(2,1)S(1)}, bf16[64,1216]{1,0:T(8,128)(2,1)S(1)}, u32[]{:S(2)}, u32[]{:S(2)}) collective-permute-start(bf16[64,1216]{1,0:T(8,128)(2,1)S(1)} %copy-done.6), channel_id=1, source_target_pairs={{0,2},{2,0},{1,3},{3,1},{4,6},{6,4},{5,7},{7,5},{8,10},{10,8},{9,1... | collective-permute-start | bytes 466952 | tf_op jit(solution)/shard_map/ppermute | solution.py:401
  10.5 10.5 %collective-permute-start.7 = (bf16[96,640]{1,0:T(8,128)(2,1)S(1)}, bf16[96,640]{1,0:T(8,128)(2,1)S(1)}, u32[]{:S(2)}, u32[]{:S(2)}) collective-permute-start(bf16[96,640]{1,0:T(8,128)(2,1)S(1)} %copy-done.8), channel_id=1, source_target_pairs={{0,1},{1,0},{2,3},{3,2},{4,5},{5,4},{6,7},{7,6},{8,9},{9,8},{10,11... | collective-permute-start | bytes 368648 | tf_op jit(solution)/shard_map/ppermute | solution.py:432
  16.0 1.8 %copy-start = (bf16[640,1216]{0,1:T(8,128)(2,1)S(1)}, bf16[640,1216]{0,1:T(8,128)(2,1)}, u32[]{:S(2)}) copy-start(bf16[640,1216]{0,1:T(8,128)(2,1)} %param.17) | copy-start | bytes 4669444
  16.0 1.8 %collective-permute-start.3 = (bf16[288,640]{1,0:T(8,128)(2,1)S(1)}, bf16[288,640]{1,0:T(8,128)(2,1)S(1)}, u32[]{:S(2)}, u32[]{:S(2)}) collective-permute-start(bf16[288,640]{1,0:T(8,128)(2,1)S(1)} %kv_norm_kernel.1.refs_3_), channel_id=1, source_target_pairs={{0,2},{2,0},{1,3},{3,1},{4,6},{6,4},{5,7},{7,5},{8,10},{10,8},{9,1... | collective-permute-start | bytes 1105928 | tf_op jit(solution)/shard_map/ppermute | solution.py:437
  19.0 6.9 %collective-permute-start.5 = (bf16[48,1280]{1,0:T(8,128)(2,1)S(1)}, bf16[48,1280]{1,0:T(8,128)(2,1)S(1)}, u32[]{:S(2)}, u32[]{:S(2)}) collective-permute-start(bf16[48,1280]{1,0:T(8,128)(2,1)S(1)} %get-tuple-element.27), channel_id=1, source_target_pairs={{0,1},{1,0},{2,3},{3,2},{4,5},{5,4},{6,7},{7,6},{8,9},{9,8},{10,11... | collective-permute-start | bytes 368648 | tf_op jit(solution)/shard_map/ppermute | solution.py:453
  21.8 4.1 %copy-start.5 = (bf16[12,12,2432]{2,1,0:T(8,128)(2,1)S(1)}, bf16[12,12,2432]{2,1,0:T(8,128)(2,1)}, u32[]{:S(2)}) copy-start(bf16[12,12,2432]{2,1,0:T(8,128)(2,1)} %refs_7_.1) | copy-start | bytes 2101252
  21.8 4.1 %copy-start.7 = (f32[3,2432]{1,0:T(4,128)S(1)}, f32[3,2432]{1,0:T(4,128)}, u32[]{:S(2)}) copy-start(f32[3,2432]{1,0:T(4,128)} %refs_8_.1) | copy-start | bytes 87556
  21.8 6.6 %collective-permute-start.9 = (bf16[48,1152]{1,0:T(8,128)(2,1)S(1)}, bf16[48,1152]{1,0:T(8,128)(2,1)S(1)}, u32[]{:S(2)}, u32[]{:S(2)}) collective-permute-start(bf16[48,1152]{1,0:T(8,128)(2,1)S(1)} %rest.1), channel_id=1, source_target_pairs={{0,1},{1,0},{2,3},{3,2},{4,5},{5,4},{6,7},{7,6},{8,9},{9,8},{10,11... | collective-permute-start | bytes 331784 | tf_op jit(solution)/shard_map/ppermute | solution.py:462
  23.9 13.1 %collective-permute-start.8 = (bf16[96,2432]{1,0:T(8,128)(2,1)S(1)}, bf16[96,2432]{1,0:T(8,128)(2,1)S(1)}, u32[]{:S(2)}, u32[]{:S(2)}) collective-permute-start(bf16[96,2432]{1,0:T(8,128)(2,1)S(1)} %attend.3), channel_id=1, source_target_pairs={{0,1},{1,0},{2,3},{3,2},{4,5},{5,4},{6,7},{7,6},{8,9},{9,8},{10,11... | collective-permute-start | bytes 1400840 | tf_op jit(solution)/shard_map/ppermute | solution.py:465
  25.9 2.5 %copy-start.2 = (f32[24,384]{1,0:T(8,128)S(1)}, f32[24,384]{1,0:T(8,128)}, u32[]{:S(2)}) copy-start(f32[24,384]{1,0:T(8,128)} %latent_ref.3) | copy-start | bytes 110596

commit v4 on v3

--- a/solution.py
+++ b/solution.py
@@ -17,7 +17,7 @@
 EPS = 1e-06
 VMEM_LIMIT = 16 * 1024 * 1024
 VMEM_MOST = 60 * 1024 * 1024
-LOADS = 9
+LOADS = 3
 FIRST = 1280
 STEP = 640
 SWAP = [(0, 1), (1, 0)]
@@ -83,14 +83,17 @@
     return ref.at[:rows], ref.at[rows:]
 
 
+def three(ref, tokens):
+    return ref.at[:tokens], ref.at[tokens : 2 * tokens], ref.at[2 * tokens :]
+
+
 def split_kernel(
     x_ref,
     gain_q_ref,
     gain_k_ref,
     gain_t_ref,
-    q_first_ref,
+    first_ref,
     q_second_ref,
-    kv_ref,
     gains,
     held,
     sems,
@@ -103,11 +106,12 @@
     ]
     for copy in gain_copies:
         copy.start()
+    tokens = held.shape[0]
+    k_ref, v_ref, q_first_ref = three(first_ref, tokens)
     cut = q_first_ref.shape[0]
-    k_ref, v_ref = halves(kv_ref)
     for rows, copy in blocks:
         copy.wait()
-        q, k, v = held[rows].astype(jnp.float32).transpose(1, 0, 2).astype(jnp.bfloat16)
+        q, k, v = held[rows].transpose(1, 0, 2)
         k_ref[rows] = k
         v_ref[rows] = v
         if rows.stop <= cut:
@@ -118,26 +122,30 @@
         copy.wait()
 
 
-def q_norm_kernel(x_ref, gains, out_ref):
-    (out_ref[...],) = head_norms([(x_ref[...].astype(jnp.float32), gains[0:1])])
-
-
-def kv_norm_kernel(x_ref, gains, out_ref):
-    (k_ref, v_ref), (k_out, v_out) = halves(x_ref), halves(out_ref)
-    v_out[...] = v_ref[...]
-    (k_out[...],) = head_norms([(k_ref[...].astype(jnp.float32), gains[1:2])])
+def q_norm(x_ref, gains):
+    (q,) = head_norms([(x_ref[...].astype(jnp.float32), gains[0:1])])
+    return q
+
+
+def norm_kernel(x_ref, gains, kv_ref, q_ref):
+    k, v, q = three(x_ref, kv_ref.shape[0] // 2)
+    k_out, v_out = halves(kv_ref)
+    v_out[...] = v[...]
+    k_out[...], q_ref[...] = head_norms(
+        [(k[...].astype(jnp.float32), gains[1:2]), (q[...].astype(jnp.float32), gains[0:1])]
+    )
 
 
 def keys_and_values(refs):
-    pairs = [halves(ref) for ref in refs]
+    k_own, v_own, k_row, v_row, *joined = refs
+    pairs = [(k_own, v_own), (k_row, v_row)] + [halves(ref) for ref in joined]
     return [keys for keys, _ in pairs], [values for _, values in pairs]
 
 
 def prep_own_kernel(
-    index_ref, count_ref, x_ref, text_ref, gains, _, kv_ref, q_ref, gains_out, euler_ref, __
+    index_ref, count_ref, x_ref, text_ref, gains, _, k_ref, v_ref, q_ref, gains_out, euler_ref, __
 ):
     tokens, width = q_ref.shape
-    k_ref, v_ref = halves(kv_ref)
     gains_out[...] = gains[...]
     now = jnp.full(euler_ref.shape, index_ref[0], jnp.int32)
     then = now + jnp.full(euler_ref.shape, count_ref[0], jnp.int32)
@@ -156,7 +164,7 @@
     )
 
 
-def attend(q, keys_refs, values_refs, attended_ref):
+def attend(q, keys_refs, values_refs, store):
     tokens, width = q.shape
     first = lax.broadcasted_iota(jnp.int32, (tokens, LANES), 1) < HEAD
     scale = math.log2(math.e) / math.sqrt(HEAD)
@@ -185,7 +193,7 @@
         )
         weighted = jnp.where(first, out[:tokens, :LANES], out[tokens:, :LANES])
         total = jnp.where(first, out[:tokens, LANES:], out[tokens:, LANES:])
-        attended_ref[:, lanes] = (weighted / total).astype(jnp.bfloat16)
+        store(lanes, weighted, total)
 
     ahead = scores_of(0)
     for at in range(0, width, LANES):
@@ -213,9 +221,43 @@
         store(at, to, parts[0] if len(parts) == 1 else jnp.concatenate(parts, axis=1))
 
 
-def attend_kernel(*refs):
-    q_ref, weight_refs, (out_ref, attended) = refs[0], refs[5:7], refs[7:]
-    attend(q_ref[...], *keys_and_values(refs[1:5]), attended)
+def divide_into(ref):
+    def store(lanes, weighted, total):
+        ref[:, lanes] = (weighted / total).astype(jnp.bfloat16)
+
+    return store
+
+
+def part_kernel(q_ref, *refs):
+    sum_ref, total_ref = refs[5:]
+
+    def store(lanes, weighted, total):
+        sum_ref[:, lanes] = weighted
+        total_ref[:, lanes] = total
+
+    attend(q_ref[...], *keys_and_values(refs[:5]), store)
+
+
+def first_kernel(
+    q_ref, last_ref, sum_ref, total_ref, mine_ref, theirs_ref, out_ref, attended
+):
+    finish = divide_into(attended)
+
+    def store(lanes, weighted, total):
+        finish(lanes, weighted + sum_ref[:, lanes], total + total_ref[:, lanes])
+
+    keys, values = halves(last_ref)
+    attend(q_ref[...], [keys], [values], store)
+
+    def keep(at, to, product):
+        out_ref[:, at:to] = product
+
+    project(attended[...], (mine_ref, theirs_ref), 0, out_ref.shape[1], keep)
+
+
+def second_kernel(*refs):
+    x_ref, gains, weight_refs, (out_ref, attended) = refs[0], refs[1], refs[8:10], refs[10:]
+    attend(q_norm(x_ref, gains), *keys_and_values(refs[2:8]), divide_into(attended))
 
     def keep(at, to, product):
         out_ref[:, at:to] = product
@@ -239,10 +281,10 @@
 
 
 def own_kernel(*refs):
-    q_ref, weight_refs = refs[0], refs[5:7]
-    hidden_ref, mod_ref, got_ref, mine_ref, theirs_ref = refs[7:12]
-    out_ref, mod_out, finals_ref, attended = refs[12:]
-    attend(q_ref[...], *keys_and_values(refs[1:5]), attended)
+    q_ref, weight_refs = refs[0], refs[7:9]
+    hidden_ref, mod_ref, got_ref, mine_ref, theirs_ref = refs[9:14]
+    out_ref, mod_out, finals_ref, attended = refs[14:]
+    attend(q_ref[...], *keys_and_values(refs[1:7]), divide_into(attended))
     is_first = lax.axis_index("row") == 0
     tile_rows, tile_cols, features = hidden_ref.shape
     mod_out[...] = in_order(mod_ref[...], is_first)
@@ -386,12 +428,15 @@
     loads = pltpu.SemaphoreType.DMA((LOADS,))
     cut = tile_rows // 3 * tile_cols
     chunks = ((0, cut), (cut, tokens))
-    *q_raw, kv_raw, gains = pl.pallas_call(
+    first_raw, second_raw, gains = pl.pallas_call(
         split_kernel,
-        out_shape=tuple(shape((upto - start, width)) for start, upto in chunks)
-        + (shape((2 * tokens, width)), shape((len(gains), HEAD), jnp.float32)),
+        out_shape=(
+            shape((2 * tokens + cut, width)),
+            shape((tokens - cut, width)),
+            shape((len(gains), HEAD), jnp.float32),
+        ),
         in_specs=[HBM] * 4,
-        out_specs=(VMEM,) * 4,
+        out_specs=(VMEM,) * 3,
         scratch_shapes=[held, loads, pltpu.SemaphoreType.DMA((len(gains),))],
         compiler_params=params(VMEM_MOST),
         name="split",
@@ -399,57 +444,52 @@
 
     weight_got = lax.ppermute(weight_half, "row", SWAP)
     final_got = lax.ppermute(final_weight, "row", SWAP)
-    kv_own, q_own, gains_on, euler, weight_theirs = pl.pallas_call(
+    k_own, v_own, q_own, gains_on, euler, weight_theirs = pl.pallas_call(
         prep_own_kernel,
         out_shape=(
-            shape((2 * (tokens + words), width)),
+            shape((tokens + words, width)),
+            shape((tokens + words, width)),
             block,
             shape(gains.shape, jnp.float32),
             shape((1, latent.shape[1]), jnp.float32),
             shape(weight_got.shape),
         ),
         in_specs=[SMEM, SMEM, VMEM, VMEM, VMEM, ANY],
-        out_specs=(VMEM,) * 4 + (ANY,),
-        input_output_aliases={5: 4},
+        out_specs=(VMEM,) * 5 + (ANY,),
+        input_output_aliases={5: 5},
         compiler_params=params(),
         name="prep_own",
     )(step_index, step_count, x, text_kv, gains, weight_got)
     weights = (weight_half, weight_theirs)
 
-    def normed(kernel, got, duration):
-        return pl.pallas_call(
-            kernel,
-            out_shape=shape(got.shape),
-            in_specs=[VMEM, VMEM],
-            out_specs=VMEM,
-            compiler_params=params(),
-            cost_estimate=lasting(duration),
-            name=kernel.__name__,
-        )(got, gains_on)
-
-    kv_got = normed(kv_norm_kernel, lax.ppermute(kv_raw, "col", SWAP), 0)
-    q_got = [
-        normed(q_norm_kernel, lax.ppermute(raw, "col", SWAP), duration)
-        for raw, duration in zip(q_raw, (4.2, 1))
-    ]
-    pairs = []
-    for kv in (kv_own, kv_got):
-        pairs += [kv, lax.ppermute(kv, "row", SWAP)]
-
-    def attended(q, projected, scratch):
-        rows = q.shape[0]
-        out_shape = (shape((rows, projected)),) + (() if scratch else (shape((rows, width)),))
-        return pl.pallas_call(
-            attend_kernel,
-            out_shape=out_shape,
-            in_specs=[VMEM] * 7,
-            out_specs=(VMEM,) * len(out_shape),
-            scratch_shapes=[pltpu.VMEM((rows, width), jnp.bfloat16)] if scratch else (),
-            compiler_params=params(),
-            name="attend",
-        )(q, *pairs, *weights)
-
-    first, heads = attended(q_got[0], FIRST, False)
+    kv_got, q_first = pl.pallas_call(
+        norm_kernel,
+        out_shape=(shape((2 * tokens, width)), shape((cut, width))),
+        in_specs=[VMEM] * 2,
+        out_specs=(VMEM,) * 2,
+        compiler_params=params(),
+        name="norm",
+    )(lax.ppermute(first_raw, "col", SWAP), gains_on)
+    q_second = lax.ppermute(second_raw, "col", SWAP)
+    k_row, v_row, kv_last = (lax.ppermute(x, "row", SWAP) for x in (k_own, v_own, kv_got))
+    pairs = (k_own, v_own, k_row, v_row, kv_got, kv_last)
+    sums = pl.pallas_call(
+        part_kernel,
+        out_shape=(shape((cut, width), jnp.float32),) * 2,
+        in_specs=[VMEM] * 6,
+        out_specs=(VMEM,) * 2,
+        compiler_params=params(),
+        cost_estimate=lasting(4.5),
+        name="part",
+    )(q_first, *pairs[:5])
+    first, heads = pl.pallas_call(
+        first_kernel,
+        out_shape=(shape((cut, FIRST)), shape((cut, width))),
+        in_specs=[VMEM] * 6,
+        out_specs=(VMEM,) * 2,
+        compiler_params=params(),
+        name="first",
+    )(q_first, kv_last, *sums, *weights)
     first_got = lax.ppermute(first, "col", SWAP)
     rest = pl.pallas_call(
         rest_kernel,
@@ -460,8 +500,16 @@
         name="rest",
     )(heads, *weights)
     rest_got = lax.ppermute(rest, "col", SWAP)
-    second_q, rest = lax.optimization_barrier((q_got[1], rest))
-    (second,) = attended(second_q, features, True)
+    q_second, rest = lax.optimization_barrier((q_second, rest))
+    second = pl.pallas_call(
+        second_kernel,
+        out_shape=shape((tokens - cut, features)),
+        in_specs=[VMEM] * 10,
+        out_specs=VMEM,
+        scratch_shapes=[pltpu.VMEM((tokens - cut, width), jnp.bfloat16)],
+        compiler_params=params(),
+        name="second",
+    )(q_second, gains_on, *pairs, *weights)
     second_got = lax.ppermute(second, "col", SWAP)
     mixed, mods, finals = pl.pallas_call(
         own_kernel,
@@ -470,7 +518,7 @@
             shape(modulation.shape, jnp.float32),
             shape((final_weight.shape[0], features)),
         ),
-        in_specs=[VMEM] * 12,
+        in_specs=[VMEM] * 14,
         out_specs=(VMEM,) * 3,
         scratch_shapes=[pltpu.VMEM((tokens, width), jnp.bfloat16)],
         compiler_params=params(),

time: 38.9 us -> 40.1 us (1.031)
  waiting for transfers between devices: 12.7 us -> 15 us
  starting transfers between devices: 9.72 us -> 8.39 us
    ppermute x5, waiting for transfers between devices: 4.99 us -> 7.12 us  [the longest x1 6.17 us: on_device(): lax.ppermute(first_raw, 'col', SWAP)]
    ppermute x5, starting transfers between devices: 4.91 us -> 3.6 us  [the longest x1 2.69 us: on_device(): lax.ppermute(first_raw, 'col', SWAP)]
    pallas_call x7 -> x6, Pallas kernels: 6.98 us -> 7.17 us  [the longest x1 2.12 us: on_device(): pl.pallas_call(split_kernel, out_shape=(shape((2 * tokens + cut, width)),...]
    unnamed x20 -> x18, local copies, waits for them, and re-layouts: 1.62 us -> 1.62 us
  transfers between devices with their start and end apart: 10 -> 10, of which waited for: 4 -> 3; matrix products, arithmetic and copies ran while one was open for 0% -> 0% of each run, Pallas kernels for 28% -> 28%
where the time goes in v4:
time: 40.1 us; the launch traced here: 39.8 us
  waiting for transfers between devices  15 us (37%)
  Pallas kernels  12.8 us (32%)
  starting transfers between devices  8.39 us (21%)
  between operations  2.12 us (5%)
  local copies, waits for them, and re-layouts  1.62 us (4%)
    ppermute x1, waiting for transfers between devices, on_device(): second_got = lax.ppermute(second, 'col', SWAP)  7.84 us
    ppermute x1, waiting for transfers between devices, on_device(): lax.ppermute(first_raw, 'col', SWAP)  6.17 us
    ppermute x1, starting transfers between devices, on_device(): lax.ppermute(first_raw, 'col', SWAP)  2.69 us
    pallas_call x2, Pallas kernels, on_device(): pl.pallas_call(functools.partial(final_kernel, start), out_shape=(shape(l...  2.57 us
    pallas_call x1, Pallas kernels, on_device(): pl.pallas_call(own_kernel, out_shape=(shape((tokens, features), jnp.float...  2.48 us
    pallas_call x1, Pallas kernels, on_device(): pl.pallas_call(split_kernel, out_shape=(shape((2 * tokens + cut, width)),...  2.12 us
    pallas_call x1, Pallas kernels, on_device(): pl.pallas_call(second_kernel, out_shape=shape((tokens - cut, features)),...  2.08 us
    ppermute x1, starting transfers between devices, on_device(): second_got = lax.ppermute(second, 'col', SWAP)  2.02 us
  transfers between devices with their start and end apart: 10, of which 3 were waited for; matrix products, arithmetic and copies ran while one was open for 0% of the time, Pallas kernels for 28%

profile of v4, /device:TPU:0, one launch (start us, length us, event | category | flops | bytes accessed | tf_op | source)
XLA Modules:
  0.0 39.8 jit_solution(8458723778642905078)
XLA Ops:
  0.6 0.0 copy-start.1
  0.6 0.5 %collective-permute-start = (bf16[1216,640]{1,0:T(8,128)(2,1)}, bf16[1216,640]{1,0:T(8,128)(2,1)S(1)}, u32[]{:S(2)}, u32[]{:S(2)}) collective-permute-start(bf16[1216,640]{1,0:T(8,128)(2,1)} %bitcast.5), channel_id=1, source_target_pairs={{0,2},{2,0},{1,3},{3,1},{4,6},{6,4},{5,7},{7,5},{8,10},{10,8},{9,1... | collective-permute-start | bytes 4669448 | tf_op jit(solution)/shard_map/ppermute | solution.py:445
  1.2 2.1 %split.1 = (bf16[336,640]{1,0:T(8,128)(2,1)}, bf16[96,640]{1,0:T(8,128)(2,1)}, f32[3,64]{1,0:T(4,128)}) custom-call(bf16[144,3,1280]{2,1,0:T(4,128)(2,1)} %bitcast.10, f32[1,64]{1,0:T(1,128)} %bitcast.12, f32[1,64]{1,0:T(1,128)} %bitcast.13, f32[1,64]{1,0:T(1,128)} %bitcast.14), custom_call_target="tpu_custom_call" | custom-call | tf_op jit(solution)/shard_map/split/pallas_call | solution.py:431
  3.3 2.7 %collective-permute-start.3 = (bf16[336,640]{1,0:T(8,128)(2,1)}, bf16[336,640]{1,0:T(8,128)(2,1)S(1)}, u32[]{:S(2)}, u32[]{:S(2)}) collective-permute-start(bf16[336,640]{1,0:T(8,128)(2,1)} %get-tuple-element.28), channel_id=1, source_target_pairs={{0,1},{1,0},{2,3},{3,2},{4,5},{5,4},{6,7},{7,6},{8,9},{9,8},{10,11... | collective-permute-start | bytes 1290248 | tf_op jit(solution)/shard_map/ppermute | solution.py:472
  7.3 0.0 collective-permute-done._
  7.3 0.0 copy-done.1
  7.3 0.0 copy-start.3
  7.3 0.9 %copy-done.3 = bf16[48,2,640]{2,1,0:T(2,128)(2,1)S(1)} copy-done((bf16[48,2,640]{2,1,0:T(2,128)(2,1)S(1)}, bf16[48,2,640]{2,1,0:T(2,128)(2,1)}, u32[]{:S(2)}) %copy-start.3) | copy-done | bytes 122904
  8.2 0.0 copy-start.4
  8.2 0.7 %copy-done.4 = f32[3,64]{1,0:T(4,128)S(1)} copy-done((f32[3,64]{1,0:T(4,128)S(1)}, f32[3,64]{1,0:T(4,128)}, u32[]{:S(2)}) %copy-start.4) | copy-done | bytes 792
  8.9 0.0 copy-start.6
  8.9 0.0 copy-start.8
  8.9 0.9 %prep_own.1 = (bf16[192,640]{1,0:T(8,128)(2,1)S(1)}, bf16[192,640]{1,0:T(8,128)(2,1)S(1)}, bf16[144,640]{1,0:T(8,128)(2,1)S(1)}, f32[3,64]{1,0:T(4,128)S(1)}, f3...) custom-call(s32[1]{0:T(128)S(6)} %copy.16.index_ref, s32[1]{0:T(128)S(6)} %copy.17.count_ref, ...), custom_call_target="tpu_custom_call", output_to_operand_aliasing={{5}: (5, {})} | custom-call | tf_op jit(solution)/shard_map/prep_own/pallas_call | solution.py:447
  9.8 0.2 collective-permute-start.1
  10.0 0.4 collective-permute-start.2
  10.4 0.0 copy-done.6
  10.4 0.1 collective-permute-start.6
  10.5 0.0 copy-done.8
  10.5 0.3 collective-permute-start.7
  10.8 6.2 %collective-permute-done.3.x_ref = bf16[336,640]{1,0:T(8,128)(2,1)S(1)} collective-permute-done((bf16[336,640]{1,0:T(8,128)(2,1)}, bf16[336,640]{1,0:T(8,128)(2,1)S(1)}, u32[]{:S(2)}, u32[]{:S(2)}) %collective-permute-start.3) | collective-permute-done | bytes 430112 | tf_op jit(solution)/shard_map/ppermute | solution.py:472
  16.9 0.3 norm.1
  17.3 0.1 collective-permute-start.4
  17.4 0.0 collective-permute-done.1.refs_2_.refs_3_.refs_4_
  17.4 0.0 collective-permute-done.2.refs_3_.refs_4_.refs_5_
  17.4 0.0 copy-start
  17.4 0.7 %part.1 = (f32[48,640]{1,0:T(8,128)S(1)}, f32[48,640]{1,0:T(8,128)S(1)}) custom-call(bf16[48,640]{1,0:T(8,128)(2,1)S(1)} %get-tuple-element.32.q_ref, bf16[192,640]{1,0:T(8,128)(2,1)S(1)} %get-tuple-element.26.refs_0_.refs_1_.refs_2_, bf16[192,640]{1,0:T(8,128)(2,1)S(1)} %get-tuple-element.27.refs_1_.refs_2_.refs_3_, ...), custom_call_target="tpu_custom_call" | custom-call | flops 4499999744 | bytes 13500000 | tf_op jit(solution)/shard_map/part/pallas_call | solution.py:476
  18.1 0.9 %collective-permute-done.4.last_ref.refs_6_.refs_7_ = bf16[288,640]{1,0:T(8,128)(2,1)S(1)} collective-permute-done((bf16[288,640]{1,0:T(8,128)(2,1)S(1)}, bf16[288,640]{1,0:T(8,128)(2,1)S(1)}, u32[]{:S(2)}, u32[]{:S(2)}) %collective-permute-start.4) | collective-permute-done | bytes 368672 | tf_op jit(solution)/shard_map/ppermute | solution.py:474
  19.0 0.0 copy-done
  19.0 1.1 %first.1 = (bf16[48,1280]{1,0:T(8,128)(2,1)S(1)}, bf16[48,640]{1,0:T(8,128)(2,1)S(1)}) custom-call(bf16[48,640]{1,0:T(8,128)(2,1)S(1)} %get-tuple-element.32.q_ref, bf16[288,640]{1,0:T(8,128)(2,1)S(1)} %collective-permute-done.4.last_ref.refs_6_.refs_7_, f32[48,640]{1,0:T(8,128)S(1)} %get-tuple-element.33.sum_ref, ...), custom_call_target="tpu_custom_call" | custom-call | tf_op jit(solution)/shard_map/first/pallas_call | solution.py:485
  20.1 2.0 %collective-permute-start.5 = (bf16[48,1280]{1,0:T(8,128)(2,1)S(1)}, bf16[48,1280]{1,0:T(8,128)(2,1)S(1)}, u32[]{:S(2)}, u32[]{:S(2)}) collective-permute-start(bf16[48,1280]{1,0:T(8,128)(2,1)S(1)} %get-tuple-element.35), channel_id=1, source_target_pairs={{0,1},{1,0},{2,3},{3,2},{4,5},{5,4},{6,7},{7,6},{8,9},{9,8},{10,11... | collective-permute-start | bytes 368648 | tf_op jit(solution)/shard_map/ppermute | solution.py:493
  22.1 0.5 %rest.1 = bf16[48,1152]{1,0:T(8,128)(2,1)S(1)} custom-call(bf16[48,640]{1,0:T(8,128)(2,1)S(1)} %get-tuple-element.38.attended_ref, bf16[1216,640]{1,0:T(8,128)(2,1)S(1)} %bitcast.7, bf16[1216,640]{1,0:T(8,128)(2,1)S(1)} %get-tuple-element.31.theirs_ref.refs_8_.refs_9_), custom_call_target="tpu_custom_call" | custom-call | tf_op jit(solution)/shard_map/rest/pallas_call | solution.py:494
  22.6 0.0 copy-start.5
  22.6 0.0 copy-start.7
  22.6 0.1 collective-permute-start.9
  22.8 0.0 collective-permute-done.7.refs_0_
  22.8 2.1 %second.1 = bf16[96,2432]{1,0:T(8,128)(2,1)S(1)} custom-call(bf16[96,640]{1,0:T(8,128)(2,1)S(1)} %collective-permute-done.7.refs_0_, f32[3,64]{1,0:T(4,128)S(1)} %get-tuple-element.29.gains.refs_1_, bf16[192,640]{1,0:T(8,128)(2,1)S(1)} %get-tuple-element.26.refs_0_.refs_1_.refs_2_, bf16[192,640]{1,0:T(8,128)(2,1)S(1)} %get-tuple-element.27.refs_1_.refs_2_.refs_3_, ...), custom_call_target="tpu_custom_call" | custom-call | tf_op jit(solution)/shard_map/second/pallas_call | solution.py:504
  24.9 2.0 %collective-permute-start.8 = (bf16[96,2432]{1,0:T(8,128)(2,1)S(1)}, bf16[96,2432]{1,0:T(8,128)(2,1)S(1)}, u32[]{:S(2)}, u32[]{:S(2)}) collective-permute-start(bf16[96,2432]{1,0:T(8,128)(2,1)S(1)} %second.1), channel_id=1, source_target_pairs={{0,1},{1,0},{2,3},{3,2},{4,5},{5,4},{6,7},{7,6},{8,9},{9,8},{10,11... | collective-permute-start | bytes 1400840 | tf_op jit(solution)/shard_map/ppermute | solution.py:513
  26.9 0.0 collective-permute-done.6.refs_13_
  26.9 0.0 collective-permute-done.5.refs_11_
  26.9 0.0 copy-done.5
  26.9 0.0 copy-done.7
  26.9 0.0 copy-start.2
  26.9 2.5 %own.1 = (f32[144,2432]{1,0:T(8,128)S(1)}, f32[3,2432]{1,0:T(4,128)S(1)}, bf16[64,2432]{1,0:T(8,128)(2,1)S(1)}) custom-call(bf16[144,640]{1,0:T(8,128)(2,1)S(1)} %get-tuple-element.25.refs_0_, bf16[192,640]{1,0:T(8,128)(2,1)S(1)} %get-tuple-element.26.refs_0_.refs_1_.refs_2_, bf16[192,640]{1,0:T(8,128)(2,1)S(1)} %get-tuple-element.27.refs_1_.refs_2_.refs_3_, ...), custom_call_target="tpu_custom_call" | custom-call | flops 60000002048 | bytes 180000000 | tf_op jit(solution)/shard_map/own/pallas_call | solution.py:514
  29.4 0.0 collective-permute-done.9.rest_ref
  29.4 0.0 copy-done.2
  29.4 0.9 %final.2 = (f32[24,384]{1,0:T(8,128)S(1)}, f32[24,384]{1,0:T(8,128)S(1)}) custom-call(f32[1,384]{1,0:T(1,128)S(1)} %get-tuple-element.24.euler_ref, f32[144,2432]{1,0:T(8,128)S(1)} %get-tuple-element.36.mixed_ref, bf16[48,1152]{1,0:T(8,128)(2,1)S(1)} %collective-permute-done.9.rest_ref, f32[3,2432]{1,0:T(4,128)S(1)} %get-tuple-element.40.mod_ref, ...), custom_call_target="tpu_custom_call" | custom-call | tf_op jit(solution)/shard_map/final/pallas_call | solution.py:539
  30.3 7.8 %collective-permute-done.8.rest_ref = bf16[96,2432]{1,0:T(8,128)(2,1)S(1)} collective-permute-done((bf16[96,2432]{1,0:T(8,128)(2,1)S(1)}, bf16[96,2432]{1,0:T(8,128)(2,1)S(1)}, u32[]{:S(2)}, u32[]{:S(2)}) %collective-permute-start.8) | collective-permute-done | bytes 466976 | tf_op jit(solution)/shard_map/ppermute | solution.py:513
  38.2 1.7 %final.3 = (f32[24,384]{1,0:T(8,128)}, f32[24,384]{1,0:T(8,128)}) custom-call(f32[1,384]{1,0:T(1,128)S(1)} %get-tuple-element.24.euler_ref, f32[144,2432]{1,0:T(8,128)S(1)} %get-tuple-element.36.mixed_ref, bf16[96,2432]{1,0:T(8,128)(2,1)S(1)} %collective-permute-done.8.rest_ref, f32[3,2432]{1,0:T(4,128)S(1)} %get-tuple-element.40.mod_ref, ...), custom_call_target="tpu_custom_call" | custom-call | tf_op jit(solution)/shard_map/final/pallas_call | solution.py:539
Async XLA Ops:
  0.6 6.7 %copy-start.1 = (bf16[12,12,3,1280]{3,2,1,0:T(4,128)(2,1)S(1)}, bf16[12,12,3,1280]{3,2,1,0:T(4,128)(2,1)}, u32[]{:S(2)}) copy-start(bf16[12,12,3,1280]{3,2,1,0:T(4,128)(2,1)} %param.12) | copy-start | bytes 3317764
  0.6 6.6 %collective-permute-start = (bf16[1216,640]{1,0:T(8,128)(2,1)}, bf16[1216,640]{1,0:T(8,128)(2,1)S(1)}, u32[]{:S(2)}, u32[]{:S(2)}) collective-permute-start(bf16[1216,640]{1,0:T(8,128)(2,1)} %bitcast.5), channel_id=1, source_target_pairs={{0,2},{2,0},{1,3},{3,1},{4,6},{6,4},{5,7},{7,5},{8,10},{10,8},{9,1... | collective-permute-start | bytes 4669448 | tf_op jit(solution)/shard_map/ppermute | solution.py:445
  3.3 13.7 %collective-permute-start.3 = (bf16[336,640]{1,0:T(8,128)(2,1)}, bf16[336,640]{1,0:T(8,128)(2,1)S(1)}, u32[]{:S(2)}, u32[]{:S(2)}) collective-permute-start(bf16[336,640]{1,0:T(8,128)(2,1)} %get-tuple-element.28), channel_id=1, source_target_pairs={{0,1},{1,0},{2,3},{3,2},{4,5},{5,4},{6,7},{7,6},{8,9},{9,8},{10,11... | collective-permute-start | bytes 1290248 | tf_op jit(solution)/shard_map/ppermute | solution.py:472
  7.3 0.9 %copy-start.3 = (bf16[48,2,640]{2,1,0:T(2,128)(2,1)S(1)}, bf16[48,2,640]{2,1,0:T(2,128)(2,1)}, u32[]{:S(2)}) copy-start(bf16[48,2,640]{2,1,0:T(2,128)(2,1)} %text_ref.1) | copy-start | bytes 368644
  8.2 0.7 %copy-start.4 = (f32[3,64]{1,0:T(4,128)S(1)}, f32[3,64]{1,0:T(4,128)}, u32[]{:S(2)}) copy-start(f32[3,64]{1,0:T(4,128)} %get-tuple-element.23.gains) | copy-start | bytes 2308
  8.9 1.5 %copy-start.6 = (bf16[64,1216]{1,0:T(8,128)(2,1)S(1)}, bf16[64,1216]{1,0:T(8,128)(2,1)}, u32[]{:S(2)}) copy-start(bf16[64,1216]{1,0:T(8,128)(2,1)} %refs_12_.1) | copy-start | bytes 466948
  8.9 1.6 %copy-start.8 = (bf16[96,640]{1,0:T(8,128)(2,1)S(1)}, bf16[96,640]{1,0:T(8,128)(2,1)}, u32[]{:S(2)}) copy-start(bf16[96,640]{1,0:T(8,128)(2,1)} %get-tuple-element.37) | copy-start | bytes 368644
  9.8 7.6 %collective-permute-start.1 = (bf16[192,640]{1,0:T(8,128)(2,1)S(1)}, bf16[192,640]{1,0:T(8,128)(2,1)S(1)}, u32[]{:S(2)}, u32[]{:S(2)}) collective-permute-start(bf16[192,640]{1,0:T(8,128)(2,1)S(1)} %get-tuple-element.26.refs_0_.refs_1_.refs_2_), channel_id=1, source_target_pairs={{0,2},{2,0},{1,3},{3,1},{4,6},{6,4},{5,7},{7,5},{8,10},{10,8},{9,1... | collective-permute-start | bytes 737288 | tf_op jit(solution)/shard_map/ppermute | solution.py:474
  10.0 7.4 %collective-permute-start.2 = (bf16[192,640]{1,0:T(8,128)(2,1)S(1)}, bf16[192,640]{1,0:T(8,128)(2,1)S(1)}, u32[]{:S(2)}, u32[]{:S(2)}) collective-permute-start(bf16[192,640]{1,0:T(8,128)(2,1)S(1)} %get-tuple-element.27.refs_1_.refs_2_.refs_3_), channel_id=1, source_target_pairs={{0,2},{2,0},{1,3},{3,1},{4,6},{6,4},{5,7},{7,5},{8,10},{10,8},{9,1... | collective-permute-start | bytes 737288 | tf_op jit(solution)/shard_map/ppermute | solution.py:474
  10.4 16.5 %collective-permute-start.6 = (bf16[64,1216]{1,0:T(8,128)(2,1)S(1)}, bf16[64,1216]{1,0:T(8,128)(2,1)S(1)}, u32[]{:S(2)}, u32[]{:S(2)}) collective-permute-start(bf16[64,1216]{1,0:T(8,128)(2,1)S(1)} %copy-done.6), channel_id=1, source_target_pairs={{0,2},{2,0},{1,3},{3,1},{4,6},{6,4},{5,7},{7,5},{8,10},{10,8},{9,1... | collective-permute-start | bytes 466952 | tf_op jit(solution)/shard_map/ppermute | solution.py:446
  10.5 12.3 %collective-permute-start.7 = (bf16[96,640]{1,0:T(8,128)(2,1)S(1)}, bf16[96,640]{1,0:T(8,128)(2,1)S(1)}, u32[]{:S(2)}, u32[]{:S(2)}) collective-permute-start(bf16[96,640]{1,0:T(8,128)(2,1)S(1)} %copy-done.8), channel_id=1, source_target_pairs={{0,1},{1,0},{2,3},{3,2},{4,5},{5,4},{6,7},{7,6},{8,9},{9,8},{10,11... | collective-permute-start | bytes 368648 | tf_op jit(solution)/shard_map/ppermute | solution.py:473
  17.3 1.8 %collective-permute-start.4 = (bf16[288,640]{1,0:T(8,128)(2,1)S(1)}, bf16[288,640]{1,0:T(8,128)(2,1)S(1)}, u32[]{:S(2)}, u32[]{:S(2)}) collective-permute-start(bf16[288,640]{1,0:T(8,128)(2,1)S(1)} %get-tuple-element.30.refs_4_.refs_5_.refs_6_), channel_id=1, source_target_pairs={{0,2},{2,0},{1,3},{3,1},{4,6},{6,4},{5,7},{7,5},{8,10},{10,8},{9,1... | collective-permute-start | bytes 1105928 | tf_op jit(solution)/shard_map/ppermute | solution.py:474
  17.4 1.7 %copy-start = (bf16[640,1216]{0,1:T(8,128)(2,1)S(1)}, bf16[640,1216]{0,1:T(8,128)(2,1)}, u32[]{:S(2)}) copy-start(bf16[640,1216]{0,1:T(8,128)(2,1)} %param.17) | copy-start | bytes 4669444
  20.1 6.8 %collective-permute-start.5 = (bf16[48,1280]{1,0:T(8,128)(2,1)S(1)}, bf16[48,1280]{1,0:T(8,128)(2,1)S(1)}, u32[]{:S(2)}, u32[]{:S(2)}) collective-permute-start(bf16[48,1280]{1,0:T(8,128)(2,1)S(1)} %get-tuple-element.35), channel_id=1, source_target_pairs={{0,1},{1,0},{2,3},{3,2},{4,5},{5,4},{6,7},{7,6},{8,9},{9,8},{10,11... | collective-permute-start | bytes 368648 | tf_op jit(solution)/shard_map/ppermute | solution.py:493
  22.6 4.3 %copy-start.5 = (bf16[12,12,2432]{2,1,0:T(8,128)(2,1)S(1)}, bf16[12,12,2432]{2,1,0:T(8,128)(2,1)}, u32[]{:S(2)}) copy-start(bf16[12,12,2432]{2,1,0:T(8,128)(2,1)} %refs_9_.1) | copy-start | bytes 2101252
  22.6 4.3 %copy-start.7 = (f32[3,2432]{1,0:T(4,128)S(1)}, f32[3,2432]{1,0:T(4,128)}, u32[]{:S(2)}) copy-start(f32[3,2432]{1,0:T(4,128)} %refs_10_.1) | copy-start | bytes 87556
  22.6 6.8 %collective-permute-start.9 = (bf16[48,1152]{1,0:T(8,128)(2,1)S(1)}, bf16[48,1152]{1,0:T(8,128)(2,1)S(1)}, u32[]{:S(2)}, u32[]{:S(2)}) collective-permute-start(bf16[48,1152]{1,0:T(8,128)(2,1)S(1)} %rest.1), channel_id=1, source_target_pairs={{0,1},{1,0},{2,3},{3,2},{4,5},{5,4},{6,7},{7,6},{8,9},{9,8},{10,11... | collective-permute-start | bytes 331784 | tf_op jit(solution)/shard_map/ppermute | solution.py:502
  24.9 13.3 %collective-permute-start.8 = (bf16[96,2432]{1,0:T(8,128)(2,1)S(1)}, bf16[96,2432]{1,0:T(8,128)(2,1)S(1)}, u32[]{:S(2)}, u32[]{:S(2)}) collective-permute-start(bf16[96,2432]{1,0:T(8,128)(2,1)S(1)} %second.1), channel_id=1, source_target_pairs={{0,1},{1,0},{2,3},{3,2},{4,5},{5,4},{6,7},{7,6},{8,9},{9,8},{10,11... | collective-permute-start | bytes 1400840 | tf_op jit(solution)/shard_map/ppermute | solution.py:513
  26.9 2.5 %copy-start.2 = (f32[24,384]{1,0:T(8,128)S(1)}, f32[24,384]{1,0:T(8,128)}, u32[]{:S(2)}) copy-start(f32[24,384]{1,0:T(8,128)} %latent_ref.3) | copy-start | bytes 110596

commit v5 on v3

--- a/solution.py
+++ b/solution.py
@@ -16,9 +16,8 @@
 LANES = 128
 EPS = 1e-06
 VMEM_LIMIT = 16 * 1024 * 1024
-VMEM_MOST = 60 * 1024 * 1024
-LOADS = 9
-FIRST = 1280
+VMEM_MOST = 52 * 1024 * 1024
+LOADS = 3
 STEP = 640
 SWAP = [(0, 1), (1, 0)]
 
@@ -85,36 +84,29 @@
 
 def split_kernel(
     x_ref,
-    gain_q_ref,
-    gain_k_ref,
-    gain_t_ref,
     q_first_ref,
     q_second_ref,
     kv_ref,
-    gains,
+    own_ref,
     held,
     sems,
-    gain_sems,
+    own_sems,
 ):
-    blocks = load_half(x_ref, held, sems, 1 - lax.axis_index("col"))
-    gain_copies = [
-        pltpu.make_async_copy(ref, gains.at[at : at + 1], gain_sems.at[at])
-        for at, ref in enumerate((gain_q_ref, gain_k_ref, gain_t_ref))
-    ]
-    for copy in gain_copies:
-        copy.start()
+    column = lax.axis_index("col")
+    blocks = load_half(x_ref, held, sems, 1 - column)
+    own_blocks = load_half(x_ref, own_ref, own_sems, column)
     cut = q_first_ref.shape[0]
     k_ref, v_ref = halves(kv_ref)
     for rows, copy in blocks:
         copy.wait()
-        q, k, v = held[rows].astype(jnp.float32).transpose(1, 0, 2).astype(jnp.bfloat16)
+        q, k, v = held[rows].transpose(1, 0, 2)
         k_ref[rows] = k
         v_ref[rows] = v
         if rows.stop <= cut:
             q_first_ref[rows] = q
         else:
             q_second_ref[rows.start - cut : rows.stop - cut] = q
-    for copy in gain_copies:
+    for _, copy in own_blocks:
         copy.wait()
 
 
@@ -134,18 +126,30 @@
 
 
 def prep_own_kernel(
-    index_ref, count_ref, x_ref, text_ref, gains, _, kv_ref, q_ref, gains_out, euler_ref, __
+    index_ref,
+    count_ref,
+    x_ref,
+    text_ref,
+    gain_q_ref,
+    gain_k_ref,
+    gain_t_ref,
+    _,
+    kv_ref,
+    q_ref,
+    gains,
+    euler_ref,
+    __,
 ):
     tokens, width = q_ref.shape
     k_ref, v_ref = halves(kv_ref)
-    gains_out[...] = gains[...]
+    for at, ref in enumerate((gain_q_ref, gain_k_ref, gain_t_ref)):
+        gains[at : at + 1] = ref[...]
     now = jnp.full(euler_ref.shape, index_ref[0], jnp.int32)
     then = now + jnp.full(euler_ref.shape, count_ref[0], jnp.int32)
     euler_ref[...] = noise_level(then) - noise_level(now)
     text = text_ref[...].astype(jnp.float32).transpose(1, 0, 2)
     v_ref[tokens:] = text[1].astype(jnp.bfloat16)
-    at = pl.multiple_of(lax.axis_index("col") * width, LANES)
-    q, k, v = x_ref[:, :, pl.ds(at, width)].transpose(1, 0, 2)
+    q, k, v = x_ref[...].transpose(1, 0, 2)
     v_ref[:tokens] = v
     k_ref[:tokens], k_ref[tokens:], q_ref[...] = head_norms(
         [
@@ -223,16 +227,6 @@
     project(attended[...], weight_refs, 0, out_ref.shape[1], keep)
 
 
-def rest_kernel(attended_ref, mine_ref, theirs_ref, out_ref):
-    features = 2 * mine_ref.shape[0]
-    start = features - out_ref.shape[1]
-
-    def keep(at, to, product):
-        out_ref[:, at - start : to - start] = product
-
-    project(attended_ref[...], (mine_ref, theirs_ref), start, features, keep)
-
-
 def in_order(x, is_first):
     half = x.shape[1] // 2
     return jnp.where(is_first, x, jnp.concatenate([x[:, half:], x[:, :half]], axis=1))
@@ -255,8 +249,8 @@
         out_ref[:, at:to] += mod_out[2:3, at:to] * product.astype(jnp.float32)
 
     project(attended[...], weight_refs, 0, features, keep)
-    upto, to = got_ref.shape
-    out_ref[:upto, :to] += mod_out[2:3, :to] * got_ref[...].astype(jnp.float32)
+    upto = got_ref.shape[0]
+    out_ref[:upto] += mod_out[2:3] * got_ref[...].astype(jnp.float32)
     finals_ref[...] = jnp.concatenate(
         [mine_ref[...].astype(jnp.float32), theirs_ref[...].astype(jnp.float32)], axis=1
     ).astype(jnp.bfloat16)
@@ -293,27 +287,17 @@
     return total
 
 
-def final_kernel(
-    start,
-    euler_ref,
-    mixed_ref,
-    rest_ref,
-    mod_ref,
-    final_ref,
-    latent_ref,
-    *refs,
-):
+def final_kernel(start, upto, euler_ref, mixed_ref, mod_ref, final_ref, latent_ref, *refs):
     velocity_ref, next_ref = refs[-2:]
-    tokens = rest_ref.shape[0]
+    got_ref = refs[0] if len(refs) > 2 else None
+    tokens = upto - start
     step = 48
     parts = []
     for at in range(0, tokens, step):
         rows = slice(start + at, start + at + step)
-        had = mixed_ref.shape[1] - rest_ref.shape[1]
         mixed = mixed_ref[rows]
-        got = rest_ref[at : at + step].astype(jnp.float32)
-        added = mixed[:, had:] + mod_ref[2:3, had:] * got
-        mixed = jnp.concatenate([mixed[:, :had], added], axis=1) if had else added
+        if got_ref is not None:
+            mixed += mod_ref[2:3] * got_ref[at : at + step].astype(jnp.float32)
         mean = jnp.mean(mixed, axis=-1, keepdims=True)
         centered = mixed - mean
         var = jnp.mean(centered * centered, axis=-1, keepdims=True)
@@ -332,8 +316,9 @@
     velocity = to_pixels(jnp.concatenate(parts, axis=0), tile_cols)
     first = start // tile_cols * PATCH
     pixels = slice(first, first + velocity.shape[0])
-    for before_ref, after_ref in zip(refs[:-2], refs[-2:]):
-        after_ref[:first] = before_ref[:first]
+    if got_ref is not None:
+        for before_ref, after_ref in zip(refs[1:3], refs[3:]):
+            after_ref[:first] = before_ref[:first]
     velocity_ref[pixels] = velocity
     next_ref[pixels] = latent_ref[pixels] + euler_ref[...] * velocity
 
@@ -386,16 +371,19 @@
     loads = pltpu.SemaphoreType.DMA((LOADS,))
     cut = tile_rows // 3 * tile_cols
     chunks = ((0, cut), (cut, tokens))
-    *q_raw, kv_raw, gains = pl.pallas_call(
+    *q_raw, kv_raw, own_raw = pl.pallas_call(
         split_kernel,
         out_shape=tuple(shape((upto - start, width)) for start, upto in chunks)
-        + (shape((2 * tokens, width)), shape((len(gains), HEAD), jnp.float32)),
-        in_specs=[HBM] * 4,
+        + (
+            shape((2 * tokens, width)),
+            shape((tokens, 3, width)),
+        ),
+        in_specs=[HBM],
         out_specs=(VMEM,) * 4,
-        scratch_shapes=[held, loads, pltpu.SemaphoreType.DMA((len(gains),))],
+        scratch_shapes=[held, loads, loads],
         compiler_params=params(VMEM_MOST),
         name="split",
-    )(x, *gains)
+    )(x)
 
     weight_got = lax.ppermute(weight_half, "row", SWAP)
     final_got = lax.ppermute(final_weight, "row", SWAP)
@@ -404,16 +392,16 @@
         out_shape=(
             shape((2 * (tokens + words), width)),
             block,
-            shape(gains.shape, jnp.float32),
+            shape((len(gains), HEAD), jnp.float32),
             shape((1, latent.shape[1]), jnp.float32),
             shape(weight_got.shape),
         ),
-        in_specs=[SMEM, SMEM, VMEM, VMEM, VMEM, ANY],
+        in_specs=[SMEM] * 2 + [VMEM] * 5 + [ANY],
         out_specs=(VMEM,) * 4 + (ANY,),
-        input_output_aliases={5: 4},
+        input_output_aliases={7: 4},
         compiler_params=params(),
         name="prep_own",
-    )(step_index, step_count, x, text_kv, gains, weight_got)
+    )(step_index, step_count, own_raw, text_kv, *gains, weight_got)
     weights = (weight_half, weight_theirs)
 
     def normed(kernel, got, duration):
@@ -430,39 +418,25 @@
     kv_got = normed(kv_norm_kernel, lax.ppermute(kv_raw, "col", SWAP), 0)
     q_got = [
         normed(q_norm_kernel, lax.ppermute(raw, "col", SWAP), duration)
-        for raw, duration in zip(q_raw, (4.2, 1))
+        for raw, duration in zip(q_raw, (4.2, 4))
     ]
     pairs = []
     for kv in (kv_own, kv_got):
         pairs += [kv, lax.ppermute(kv, "row", SWAP)]
 
-    def attended(q, projected, scratch):
+    def group(q):
         rows = q.shape[0]
-        out_shape = (shape((rows, projected)),) + (() if scratch else (shape((rows, width)),))
         return pl.pallas_call(
             attend_kernel,
-            out_shape=out_shape,
+            out_shape=shape((rows, features)),
             in_specs=[VMEM] * 7,
-            out_specs=(VMEM,) * len(out_shape),
-            scratch_shapes=[pltpu.VMEM((rows, width), jnp.bfloat16)] if scratch else (),
+            out_specs=VMEM,
+            scratch_shapes=[pltpu.VMEM((rows, width), jnp.bfloat16)],
             compiler_params=params(),
-            name="attend",
+            name="group",
         )(q, *pairs, *weights)
 
-    first, heads = attended(q_got[0], FIRST, False)
-    first_got = lax.ppermute(first, "col", SWAP)
-    rest = pl.pallas_call(
-        rest_kernel,
-        out_shape=shape((cut, features - FIRST)),
-        in_specs=[VMEM] * 3,
-        out_specs=VMEM,
-        compiler_params=params(),
-        name="rest",
-    )(heads, *weights)
-    rest_got = lax.ppermute(rest, "col", SWAP)
-    second_q, rest = lax.optimization_barrier((q_got[1], rest))
-    (second,) = attended(second_q, features, True)
-    second_got = lax.ppermute(second, "col", SWAP)
+    first_got, second_got = (lax.ppermute(group(q), "col", SWAP) for q in q_got)
     mixed, mods, finals = pl.pallas_call(
         own_kernel,
         out_shape=(
@@ -487,15 +461,15 @@
         final_got,
     )
     results = ()
-    for (start, _), got in ((chunks[0], rest_got), (chunks[1], second_got)):
+    for (start, upto), got in zip(chunks, ((), (second_got,))):
         results = pl.pallas_call(
-            functools.partial(final_kernel, start),
+            functools.partial(final_kernel, start, upto),
             out_shape=(shape(latent.shape, jnp.float32),) * 2,
-            in_specs=[VMEM] * (6 + len(results)),
+            in_specs=[VMEM] * (5 + len(got) + len(results)),
             out_specs=(VMEM, VMEM),
             compiler_params=params(),
             name="final",
-        )(euler, mixed, got, mods, finals, latent, *results)
+        )(euler, mixed, mods, finals, latent, *got, *results)
     return results
 
 

time: 38.9 us -> 38.4 us (0.987)
  starting transfers between devices: 9.72 us -> 7.68 us
  waiting for transfers between devices: 12.7 us -> 14.7 us
  Pallas kernels: 12.6 us -> 11.8 us
    ppermute x3 -> x2, waiting for transfers between devices: 7.67 us -> 10.3 us  [on_device(): first_got, second_got = (lax.ppermute(group(q), 'col', SWAP) for q in q_got)]
    ppermute x3 -> x2, starting transfers between devices: 4.13 us -> 2.16 us  [on_device(): first_got, second_got = (lax.ppermute(group(q), 'col', SWAP) for q in q_got)]
    pallas_call x1, Pallas kernels: 2.2 us -> 1.54 us  [on_device(): pl.pallas_call(split_kernel, out_shape=tuple((shape((upto - start, width)...]
    ppermute x1, waiting for transfers between devices: 3.51 us -> 2.93 us  [on_device(): kv_got = normed(kv_norm_kernel, lax.ppermute(kv_raw, 'col', SWAP), 0)]
    unnamed x20 -> x18, local copies, waits for them, and re-layouts: 1.62 us -> 1.99 us
    pallas_call x5 -> x4, Pallas kernels: 6.27 us -> 6.15 us  [the longest x2 3.61 us: group(): pl.pallas_call(attend_kernel, out_shape=shape((rows, features)), in_specs...]
  transfers between devices with their start and end apart: 10 -> 9, of which waited for: 4 -> 5; matrix products, arithmetic and copies ran while one was open for 0% -> 0% of each run, Pallas kernels for 28% -> 26%
where the time goes in v5:
time: 38.4 us; the launch traced here: 38.2 us
  waiting for transfers between devices  14.7 us (38%)
  Pallas kernels  11.8 us (31%)
  starting transfers between devices  7.68 us (20%)
  between operations  2.09 us (5%)
  local copies, waits for them, and re-layouts  1.99 us (5%)
    ppermute x2, waiting for transfers between devices, on_device(): first_got, second_got = (lax.ppermute(group(q), 'col', SWAP) for q in q_got)  10.3 us
    pallas_call x2, Pallas kernels, group(): pl.pallas_call(attend_kernel, out_shape=shape((rows, features)), in_specs...  3.61 us
    ppermute x1, waiting for transfers between devices, on_device(): kv_got = normed(kv_norm_kernel, lax.ppermute(kv_raw, 'col', SWAP), 0)  2.93 us
    ppermute x1, starting transfers between devices, on_device(): kv_got = normed(kv_norm_kernel, lax.ppermute(kv_raw, 'col', SWAP), 0)  2.61 us
    pallas_call x2, Pallas kernels, on_device(): pl.pallas_call(functools.partial(final_kernel, start, upto), out_shape=(s...  2.55 us
    pallas_call x1, Pallas kernels, on_device(): pl.pallas_call(own_kernel, out_shape=(shape((tokens, features), jnp.float...  2.48 us
    ppermute x2, starting transfers between devices, on_device(): first_got, second_got = (lax.ppermute(group(q), 'col', SWAP) for q in q_got)  2.16 us
    unnamed x18, local copies, waits for them, and re-layouts  1.99 us
  transfers between devices with their start and end apart: 9, of which 5 were waited for; matrix products, arithmetic and copies ran while one was open for 0% of the time, Pallas kernels for 26%

profile of v5, /device:TPU:0, one launch (start us, length us, event | category | flops | bytes accessed | tf_op | source)
XLA Modules:
  0.0 38.2 jit_solution(14201366023176160057)
XLA Ops:
  0.6 0.0 copy-start.2
  0.6 0.5 %collective-permute-start = (bf16[1216,640]{1,0:T(8,128)(2,1)}, bf16[1216,640]{1,0:T(8,128)(2,1)S(1)}, u32[]{:S(2)}, u32[]{:S(2)}) collective-permute-start(bf16[1216,640]{1,0:T(8,128)(2,1)} %bitcast.5), channel_id=1, source_target_pairs={{0,2},{2,0},{1,3},{3,1},{4,6},{6,4},{5,7},{7,5},{8,10},{10,8},{9,1... | collective-permute-start | bytes 4669448 | tf_op jit(solution)/shard_map/ppermute | solution.py:388
  1.2 0.0 copy-start.7
  1.2 1.5 %split.1 = (bf16[48,640]{1,0:T(8,128)(2,1)S(1)}, bf16[96,640]{1,0:T(8,128)(2,1)S(1)}, bf16[288,640]{1,0:T(8,128)(2,1)S(1)}, bf16[144,3,640]{2,1,0:T(4,128)(2,1)S(1)}) custom-call(bf16[144,3,1280]{2,1,0:T(4,128)(2,1)} %bitcast.12), custom_call_target="tpu_custom_call" | custom-call | tf_op jit(solution)/shard_map/split/pallas_call | solution.py:374
  2.7 2.6 %collective-permute-start.2 = (bf16[288,640]{1,0:T(8,128)(2,1)S(1)}, bf16[288,640]{1,0:T(8,128)(2,1)S(1)}, u32[]{:S(2)}, u32[]{:S(2)}) collective-permute-start(bf16[288,640]{1,0:T(8,128)(2,1)S(1)} %get-tuple-element.20), channel_id=1, source_target_pairs={{0,1},{1,0},{2,3},{3,2},{4,5},{5,4},{6,7},{7,6},{8,9},{9,8},{10,11... | collective-permute-start | bytes 1105928 | tf_op jit(solution)/shard_map/ppermute | solution.py:418
  6.6 0.0 collective-permute-done._
  6.6 0.0 copy-done.2
  6.6 0.0 copy-start.3
  6.6 0.6 %copy-done.3 = f32[64]{0:T(128)S(1)} copy-done((f32[64]{0:T(128)S(1)}, f32[64]{0:T(128)}, u32[]{:S(2)}) %copy-start.3) | copy-done | bytes 280
  7.3 0.0 copy-start.4
  7.3 0.7 %copy-done.4 = f32[64]{0:T(128)S(1)} copy-done((f32[64]{0:T(128)S(1)}, f32[64]{0:T(128)}, u32[]{:S(2)}) %copy-start.4) | copy-done | bytes 280
  8.0 0.0 copy-start.5
  8.0 0.7 %copy-done.5 = f32[64]{0:T(128)S(1)} copy-done((f32[64]{0:T(128)S(1)}, f32[64]{0:T(128)}, u32[]{:S(2)}) %copy-start.5) | copy-done | bytes 280
  8.6 0.9 %prep_own.1 = (bf16[384,640]{1,0:T(8,128)(2,1)S(1)}, bf16[144,640]{1,0:T(8,128)(2,1)S(1)}, f32[3,64]{1,0:T(4,128)S(1)}, f32[1,384]{1,0:T(1,128)S(1)}, bf16[1216,640]{1,0:T(8,128)(2,1)S(1)}) custom-call(s32[1]{0:T(128)S(6)} %copy.16.index_ref, s32[1]{0:T(128)S(6)} %copy.17.count_ref, ...), custom_call_target="tpu_custom_call", output_to_operand_aliasing={{4}: (7, {})} | custom-call | tf_op jit(solution)/shard_map/prep_own/pallas_call | solution.py:390
  9.5 0.3 collective-permute-start.1
  9.8 0.6 %collective-permute-start.4 = (bf16[48,640]{1,0:T(8,128)(2,1)S(1)}, bf16[48,640]{1,0:T(8,128)(2,1)S(1)}, u32[]{:S(2)}, u32[]{:S(2)}) collective-permute-start(bf16[48,640]{1,0:T(8,128)(2,1)S(1)} %get-tuple-element.23), channel_id=1, source_target_pairs={{0,1},{1,0},{2,3},{3,2},{4,5},{5,4},{6,7},{7,6},{8,9},{9,8},{10,11... | collective-permute-start | bytes 184328 | tf_op jit(solution)/shard_map/ppermute | solution.py:420
  10.4 0.0 copy-done.7
  10.4 0.1 collective-permute-start.6
  10.4 1.4 %collective-permute-start.7 = (bf16[96,640]{1,0:T(8,128)(2,1)S(1)}, bf16[96,640]{1,0:T(8,128)(2,1)S(1)}, u32[]{:S(2)}, u32[]{:S(2)}) collective-permute-start(bf16[96,640]{1,0:T(8,128)(2,1)S(1)} %get-tuple-element.27), channel_id=1, source_target_pairs={{0,1},{1,0},{2,3},{3,2},{4,5},{5,4},{6,7},{7,6},{8,9},{9,8},{10,11... | collective-permute-start | bytes 368648 | tf_op jit(solution)/shard_map/ppermute | solution.py:420
  11.8 2.9 %collective-permute-done.2.x_ref = bf16[288,640]{1,0:T(8,128)(2,1)S(1)} collective-permute-done((bf16[288,640]{1,0:T(8,128)(2,1)S(1)}, bf16[288,640]{1,0:T(8,128)(2,1)S(1)}, u32[]{:S(2)}, u32[]{:S(2)}) %collective-permute-start.2) | collective-permute-done | bytes 368672 | tf_op jit(solution)/shard_map/ppermute | solution.py:418
  14.8 0.3 kv_norm_kernel.1.refs_3_
  15.0 0.0 copy-start
  15.1 0.1 collective-permute-start.3
  15.1 0.9 %collective-permute-done.4.x_ref = bf16[48,640]{1,0:T(8,128)(2,1)S(1)} collective-permute-done((bf16[48,640]{1,0:T(8,128)(2,1)S(1)}, bf16[48,640]{1,0:T(8,128)(2,1)S(1)}, u32[]{:S(2)}, u32[]{:S(2)}) %collective-permute-start.4) | collective-permute-done | bytes 61472 | tf_op jit(solution)/shard_map/ppermute | solution.py:420
  16.1 0.2 q_norm_kernel.2.refs_0_
  16.3 0.5 %collective-permute-done.3.refs_4_ = bf16[288,640]{1,0:T(8,128)(2,1)S(1)} collective-permute-done((bf16[288,640]{1,0:T(8,128)(2,1)S(1)}, bf16[288,640]{1,0:T(8,128)(2,1)S(1)}, u32[]{:S(2)}, u32[]{:S(2)}) %collective-permute-start.3) | collective-permute-done | bytes 368672 | tf_op jit(solution)/shard_map/ppermute | solution.py:425
  16.8 0.0 collective-permute-done.1.refs_2_
  16.8 0.0 copy-done
  16.8 1.7 %group.2 = bf16[48,2432]{1,0:T(8,128)(2,1)S(1)} custom-call(bf16[48,640]{1,0:T(8,128)(2,1)S(1)} %q_norm_kernel.2.refs_0_, bf16[384,640]{1,0:T(8,128)(2,1)S(1)} %get-tuple-element.19.refs_1_, bf16[384,640]{1,0:T(8,128)(2,1)S(1)} %collective-permute-done.1.refs_2_, bf16[288,640]{1,0:T(8,128)(2,1)S(1)} %kv_norm_kernel.1.refs_3_, ...), custom_call_target="tpu_custom_call" | custom-call | tf_op jit(solution)/shard_map/group/pallas_call | solution.py:429
  18.6 2.0 %collective-permute-start.5 = (bf16[48,2432]{1,0:T(8,128)(2,1)S(1)}, bf16[48,2432]{1,0:T(8,128)(2,1)S(1)}, u32[]{:S(2)}, u32[]{:S(2)}) collective-permute-start(bf16[48,2432]{1,0:T(8,128)(2,1)S(1)} %group.2), channel_id=1, source_target_pairs={{0,1},{1,0},{2,3},{3,2},{4,5},{5,4},{6,7},{7,6},{8,9},{9,8},{10,11... | collective-permute-start | bytes 700424 | tf_op jit(solution)/shard_map/ppermute | solution.py:439
  20.6 0.0 collective-permute-done.7.x_ref
  20.6 0.2 q_norm_kernel.3.refs_0_
  20.8 0.0 copy-start.6
  20.8 0.0 copy-start.8
  20.9 1.9 %group.3 = bf16[96,2432]{1,0:T(8,128)(2,1)S(1)} custom-call(bf16[96,640]{1,0:T(8,128)(2,1)S(1)} %q_norm_kernel.3.refs_0_, bf16[384,640]{1,0:T(8,128)(2,1)S(1)} %get-tuple-element.19.refs_1_, bf16[384,640]{1,0:T(8,128)(2,1)S(1)} %collective-permute-done.1.refs_2_, bf16[288,640]{1,0:T(8,128)(2,1)S(1)} %kv_norm_kernel.1.refs_3_, ...), custom_call_target="tpu_custom_call" | custom-call | tf_op jit(solution)/shard_map/group/pallas_call | solution.py:429
  22.7 0.1 collective-permute-start.8
  22.9 0.0 collective-permute-done.6.refs_11_
  22.9 4.2 %collective-permute-done.5.refs_9_ = bf16[48,2432]{1,0:T(8,128)(2,1)S(1)} collective-permute-done((bf16[48,2432]{1,0:T(8,128)(2,1)S(1)}, bf16[48,2432]{1,0:T(8,128)(2,1)S(1)}, u32[]{:S(2)}, u32[]{:S(2)}) %collective-permute-start.5) | collective-permute-done | bytes 233504 | tf_op jit(solution)/shard_map/ppermute | solution.py:439
  27.1 0.0 copy-done.6
  27.1 0.0 copy-done.8
  27.1 0.0 copy-start.1
  27.1 2.5 %own.1 = (f32[144,2432]{1,0:T(8,128)S(1)}, f32[3,2432]{1,0:T(4,128)S(1)}, bf16[64,2432]{1,0:T(8,128)(2,1)S(1)}) custom-call(bf16[144,640]{1,0:T(8,128)(2,1)S(1)} %get-tuple-element.18.refs_0_, bf16[384,640]{1,0:T(8,128)(2,1)S(1)} %get-tuple-element.19.refs_1_, bf16[384,640]{1,0:T(8,128)(2,1)S(1)} %collective-permute-done.1.refs_2_, ...), custom_call_target="tpu_custom_call" | custom-call | flops 60000002048 | bytes 180000000 | tf_op jit(solution)/shard_map/own/pallas_call | solution.py:440
  29.6 0.0 copy-done.1
  29.6 0.9 %final.2 = (f32[24,384]{1,0:T(8,128)S(1)}, f32[24,384]{1,0:T(8,128)S(1)}) custom-call(f32[1,384]{1,0:T(1,128)S(1)} %get-tuple-element.17.euler_ref, f32[144,2432]{1,0:T(8,128)S(1)} %get-tuple-element.24.mixed_ref, f32[3,2432]{1,0:T(4,128)S(1)} %get-tuple-element.25.mod_ref, bf16[64,2432]{1,0:T(8,128)(2,1)S(1)} %get-tuple-element.26.final_ref, ...), custom_call_target="tpu_custom_call" | custom-call | tf_op jit(solution)/shard_map/final/pallas_call | solution.py:465
  30.5 6.1 %collective-permute-done.8.refs_0_ = bf16[96,2432]{1,0:T(8,128)(2,1)S(1)} collective-permute-done((bf16[96,2432]{1,0:T(8,128)(2,1)S(1)}, bf16[96,2432]{1,0:T(8,128)(2,1)S(1)}, u32[]{:S(2)}, u32[]{:S(2)}) %collective-permute-start.8) | collective-permute-done | bytes 466976 | tf_op jit(solution)/shard_map/ppermute | solution.py:439
  36.6 1.7 %final.3 = (f32[24,384]{1,0:T(8,128)}, f32[24,384]{1,0:T(8,128)}) custom-call(f32[1,384]{1,0:T(1,128)S(1)} %get-tuple-element.17.euler_ref, f32[144,2432]{1,0:T(8,128)S(1)} %get-tuple-element.24.mixed_ref, f32[3,2432]{1,0:T(4,128)S(1)} %get-tuple-element.25.mod_ref, bf16[64,2432]{1,0:T(8,128)(2,1)S(1)} %get-tuple-element.26.final_ref, ...), custom_call_target="tpu_custom_call" | custom-call | tf_op jit(solution)/shard_map/final/pallas_call | solution.py:465
Async XLA Ops:
  0.6 6.0 %copy-start.2 = (bf16[48,2,640]{2,1,0:T(2,128)(2,1)S(1)}, bf16[48,2,640]{2,1,0:T(2,128)(2,1)}, u32[]{:S(2)}) copy-start(bf16[48,2,640]{2,1,0:T(2,128)(2,1)} %text_ref.1) | copy-start | bytes 368644
  0.6 6.0 %collective-permute-start = (bf16[1216,640]{1,0:T(8,128)(2,1)}, bf16[1216,640]{1,0:T(8,128)(2,1)S(1)}, u32[]{:S(2)}, u32[]{:S(2)}) collective-permute-start(bf16[1216,640]{1,0:T(8,128)(2,1)} %bitcast.5), channel_id=1, source_target_pairs={{0,2},{2,0},{1,3},{3,1},{4,6},{6,4},{5,7},{7,5},{8,10},{10,8},{9,1... | collective-permute-start | bytes 4669448 | tf_op jit(solution)/shard_map/ppermute | solution.py:388
  1.2 9.2 %copy-start.7 = (bf16[64,1216]{1,0:T(8,128)(2,1)S(1)}, bf16[64,1216]{1,0:T(8,128)(2,1)}, u32[]{:S(2)}) copy-start(bf16[64,1216]{1,0:T(8,128)(2,1)} %refs_10_.1) | copy-start | bytes 466948
  2.7 12.1 %collective-permute-start.2 = (bf16[288,640]{1,0:T(8,128)(2,1)S(1)}, bf16[288,640]{1,0:T(8,128)(2,1)S(1)}, u32[]{:S(2)}, u32[]{:S(2)}) collective-permute-start(bf16[288,640]{1,0:T(8,128)(2,1)S(1)} %get-tuple-element.20), channel_id=1, source_target_pairs={{0,1},{1,0},{2,3},{3,2},{4,5},{5,4},{6,7},{7,6},{8,9},{9,8},{10,11... | collective-permute-start | bytes 1105928 | tf_op jit(solution)/shard_map/ppermute | solution.py:418
  6.6 0.7 %copy-start.3 = (f32[64]{0:T(128)S(1)}, f32[64]{0:T(128)}, u32[]{:S(2)}) copy-start(f32[64]{0:T(128)} %param.14) | copy-start | bytes 772
  7.3 0.7 %copy-start.4 = (f32[64]{0:T(128)S(1)}, f32[64]{0:T(128)}, u32[]{:S(2)}) copy-start(f32[64]{0:T(128)} %param.15) | copy-start | bytes 772
  8.0 0.7 %copy-start.5 = (f32[64]{0:T(128)S(1)}, f32[64]{0:T(128)}, u32[]{:S(2)}) copy-start(f32[64]{0:T(128)} %param.16) | copy-start | bytes 772
  9.5 7.3 %collective-permute-start.1 = (bf16[384,640]{1,0:T(8,128)(2,1)S(1)}, bf16[384,640]{1,0:T(8,128)(2,1)S(1)}, u32[]{:S(2)}, u32[]{:S(2)}) collective-permute-start(bf16[384,640]{1,0:T(8,128)(2,1)S(1)} %get-tuple-element.19.refs_1_), channel_id=1, source_target_pairs={{0,2},{2,0},{1,3},{3,1},{4,6},{6,4},{5,7},{7,5},{8,10},{10,8},{9,1... | collective-permute-start | bytes 1474568 | tf_op jit(solution)/shard_map/ppermute | solution.py:425
  9.8 6.3 %collective-permute-start.4 = (bf16[48,640]{1,0:T(8,128)(2,1)S(1)}, bf16[48,640]{1,0:T(8,128)(2,1)S(1)}, u32[]{:S(2)}, u32[]{:S(2)}) collective-permute-start(bf16[48,640]{1,0:T(8,128)(2,1)S(1)} %get-tuple-element.23), channel_id=1, source_target_pairs={{0,1},{1,0},{2,3},{3,2},{4,5},{5,4},{6,7},{7,6},{8,9},{9,8},{10,11... | collective-permute-start | bytes 184328 | tf_op jit(solution)/shard_map/ppermute | solution.py:420
  10.4 12.5 %collective-permute-start.6 = (bf16[64,1216]{1,0:T(8,128)(2,1)S(1)}, bf16[64,1216]{1,0:T(8,128)(2,1)S(1)}, u32[]{:S(2)}, u32[]{:S(2)}) collective-permute-start(bf16[64,1216]{1,0:T(8,128)(2,1)S(1)} %copy-done.7), channel_id=1, source_target_pairs={{0,2},{2,0},{1,3},{3,1},{4,6},{6,4},{5,7},{7,5},{8,10},{10,8},{9,1... | collective-permute-start | bytes 466952 | tf_op jit(solution)/shard_map/ppermute | solution.py:389
  10.4 10.1 %collective-permute-start.7 = (bf16[96,640]{1,0:T(8,128)(2,1)S(1)}, bf16[96,640]{1,0:T(8,128)(2,1)S(1)}, u32[]{:S(2)}, u32[]{:S(2)}) collective-permute-start(bf16[96,640]{1,0:T(8,128)(2,1)S(1)} %get-tuple-element.27), channel_id=1, source_target_pairs={{0,1},{1,0},{2,3},{3,2},{4,5},{5,4},{6,7},{7,6},{8,9},{9,8},{10,11... | collective-permute-start | bytes 368648 | tf_op jit(solution)/shard_map/ppermute | solution.py:420
  15.0 1.8 %copy-start = (bf16[640,1216]{0,1:T(8,128)(2,1)S(1)}, bf16[640,1216]{0,1:T(8,128)(2,1)}, u32[]{:S(2)}) copy-start(bf16[640,1216]{0,1:T(8,128)(2,1)} %param.17) | copy-start | bytes 4669444
  15.1 1.8 %collective-permute-start.3 = (bf16[288,640]{1,0:T(8,128)(2,1)S(1)}, bf16[288,640]{1,0:T(8,128)(2,1)S(1)}, u32[]{:S(2)}, u32[]{:S(2)}) collective-permute-start(bf16[288,640]{1,0:T(8,128)(2,1)S(1)} %kv_norm_kernel.1.refs_3_), channel_id=1, source_target_pairs={{0,2},{2,0},{1,3},{3,1},{4,6},{6,4},{5,7},{7,5},{8,10},{10,8},{9,1... | collective-permute-start | bytes 1105928 | tf_op jit(solution)/shard_map/ppermute | solution.py:425
  18.6 8.6 %collective-permute-start.5 = (bf16[48,2432]{1,0:T(8,128)(2,1)S(1)}, bf16[48,2432]{1,0:T(8,128)(2,1)S(1)}, u32[]{:S(2)}, u32[]{:S(2)}) collective-permute-start(bf16[48,2432]{1,0:T(8,128)(2,1)S(1)} %group.2), channel_id=1, source_target_pairs={{0,1},{1,0},{2,3},{3,2},{4,5},{5,4},{6,7},{7,6},{8,9},{9,8},{10,11... | collective-permute-start | bytes 700424 | tf_op jit(solution)/shard_map/ppermute | solution.py:439
  20.8 6.3 %copy-start.6 = (bf16[12,12,2432]{2,1,0:T(8,128)(2,1)S(1)}, bf16[12,12,2432]{2,1,0:T(8,128)(2,1)}, u32[]{:S(2)}) copy-start(bf16[12,12,2432]{2,1,0:T(8,128)(2,1)} %refs_7_.1) | copy-start | bytes 2101252
  20.8 6.3 %copy-start.8 = (f32[3,2432]{1,0:T(4,128)S(1)}, f32[3,2432]{1,0:T(4,128)}, u32[]{:S(2)}) copy-start(f32[3,2432]{1,0:T(4,128)} %refs_8_.1) | copy-start | bytes 87556
  22.7 13.8 %collective-permute-start.8 = (bf16[96,2432]{1,0:T(8,128)(2,1)S(1)}, bf16[96,2432]{1,0:T(8,128)(2,1)S(1)}, u32[]{:S(2)}, u32[]{:S(2)}) collective-permute-start(bf16[96,2432]{1,0:T(8,128)(2,1)S(1)} %group.3), channel_id=1, source_target_pairs={{0,1},{1,0},{2,3},{3,2},{4,5},{5,4},{6,7},{7,6},{8,9},{9,8},{10,11... | collective-permute-start | bytes 1400840 | tf_op jit(solution)/shard_map/ppermute | solution.py:439
  27.1 2.5 %copy-start.1 = (f32[24,384]{1,0:T(8,128)S(1)}, f32[24,384]{1,0:T(8,128)}, u32[]{:S(2)}) copy-start(f32[24,384]{1,0:T(8,128)} %latent_ref.3) | copy-start | bytes 110596

commit v6 on v5

--- a/solution.py
+++ b/solution.py
@@ -18,6 +18,7 @@
 VMEM_LIMIT = 16 * 1024 * 1024
 VMEM_MOST = 52 * 1024 * 1024
 LOADS = 3
+FIRST = 1280
 STEP = 640
 SWAP = [(0, 1), (1, 0)]
 
@@ -227,6 +228,16 @@
     project(attended[...], weight_refs, 0, out_ref.shape[1], keep)
 
 
+def rest_kernel(attended_ref, mine_ref, theirs_ref, out_ref):
+    features = 2 * mine_ref.shape[0]
+    start = features - out_ref.shape[1]
+
+    def keep(at, to, product):
+        out_ref[:, at - start : to - start] = product
+
+    project(attended_ref[...], (mine_ref, theirs_ref), start, features, keep)
+
+
 def in_order(x, is_first):
     half = x.shape[1] // 2
     return jnp.where(is_first, x, jnp.concatenate([x[:, half:], x[:, :half]], axis=1))
@@ -249,8 +260,8 @@
         out_ref[:, at:to] += mod_out[2:3, at:to] * product.astype(jnp.float32)
 
     project(attended[...], weight_refs, 0, features, keep)
-    upto = got_ref.shape[0]
-    out_ref[:upto] += mod_out[2:3] * got_ref[...].astype(jnp.float32)
+    upto, to = got_ref.shape
+    out_ref[:upto, :to] += mod_out[2:3, :to] * got_ref[...].astype(jnp.float32)
     finals_ref[...] = jnp.concatenate(
         [mine_ref[...].astype(jnp.float32), theirs_ref[...].astype(jnp.float32)], axis=1
     ).astype(jnp.bfloat16)
@@ -287,17 +298,18 @@
     return total
 
 
-def final_kernel(start, upto, euler_ref, mixed_ref, mod_ref, final_ref, latent_ref, *refs):
+def final_kernel(start, euler_ref, mixed_ref, got_ref, mod_ref, final_ref, latent_ref, *refs):
     velocity_ref, next_ref = refs[-2:]
-    got_ref = refs[0] if len(refs) > 2 else None
-    tokens = upto - start
+    tokens = got_ref.shape[0]
     step = 48
+    had = mixed_ref.shape[1] - got_ref.shape[1]
     parts = []
     for at in range(0, tokens, step):
         rows = slice(start + at, start + at + step)
-        mixed = mixed_ref[rows]
-        if got_ref is not None:
-            mixed += mod_ref[2:3] * got_ref[at : at + step].astype(jnp.float32)
+        got = got_ref[at : at + step].astype(jnp.float32)
+        mixed = mixed_ref[rows, had:] + mod_ref[2:3, had:] * got
+        if had:
+            mixed = jnp.concatenate([mixed_ref[rows, :had], mixed], axis=1)
         mean = jnp.mean(mixed, axis=-1, keepdims=True)
         centered = mixed - mean
         var = jnp.mean(centered * centered, axis=-1, keepdims=True)
@@ -316,9 +328,8 @@
     velocity = to_pixels(jnp.concatenate(parts, axis=0), tile_cols)
     first = start // tile_cols * PATCH
     pixels = slice(first, first + velocity.shape[0])
-    if got_ref is not None:
-        for before_ref, after_ref in zip(refs[1:3], refs[3:]):
-            after_ref[:first] = before_ref[:first]
+    for before_ref, after_ref in zip(refs[:-2], refs[-2:]):
+        after_ref[:first] = before_ref[:first]
     velocity_ref[pixels] = velocity
     next_ref[pixels] = latent_ref[pixels] + euler_ref[...] * velocity
 
@@ -424,19 +435,31 @@
     for kv in (kv_own, kv_got):
         pairs += [kv, lax.ppermute(kv, "row", SWAP)]
 
-    def group(q):
+    def group(q, sent):
         rows = q.shape[0]
         return pl.pallas_call(
             attend_kernel,
-            out_shape=shape((rows, features)),
+            out_shape=(shape((rows, sent)), shape((rows, width))),
             in_specs=[VMEM] * 7,
-            out_specs=VMEM,
-            scratch_shapes=[pltpu.VMEM((rows, width), jnp.bfloat16)],
+            out_specs=(VMEM, VMEM),
             compiler_params=params(),
             name="group",
         )(q, *pairs, *weights)
 
-    first_got, second_got = (lax.ppermute(group(q), "col", SWAP) for q in q_got)
+    first, heads = group(q_got[0], FIRST)
+    first_got = lax.ppermute(first, "col", SWAP)
+    rest = pl.pallas_call(
+        rest_kernel,
+        out_shape=shape((cut, features - FIRST)),
+        in_specs=[VMEM] * 3,
+        out_specs=VMEM,
+        compiler_params=params(),
+        name="rest",
+    )(heads, *weights)
+    rest_got = lax.ppermute(rest, "col", SWAP)
+    second_q, rest = lax.optimization_barrier((q_got[1], rest))
+    second, _ = group(second_q, features)
+    second_got = lax.ppermute(second, "col", SWAP)
     mixed, mods, finals = pl.pallas_call(
         own_kernel,
         out_shape=(
@@ -461,15 +484,15 @@
         final_got,
     )
     results = ()
-    for (start, upto), got in zip(chunks, ((), (second_got,))):
+    for (start, _), got in zip(chunks, (rest_got, second_got)):
         results = pl.pallas_call(
-            functools.partial(final_kernel, start, upto),
+            functools.partial(final_kernel, start),
             out_shape=(shape(latent.shape, jnp.float32),) * 2,
-            in_specs=[VMEM] * (5 + len(got) + len(results)),
+            in_specs=[VMEM] * (6 + len(results)),
             out_specs=(VMEM, VMEM),
             compiler_params=params(),
             name="final",
-        )(euler, mixed, mods, finals, latent, *got, *results)
+        )(euler, mixed, got, mods, finals, latent, *results)
     return results
 
 

time: 38.4 us -> 37.9 us (0.987)
  waiting for transfers between devices: 14.7 us -> 11.6 us
  starting transfers between devices: 7.68 us -> 9.58 us
  Pallas kernels: 11.8 us -> 12.4 us
    ppermute x2 -> x3, waiting for transfers between devices: 10.3 us -> 7.23 us  [the longest x1 7.23 us: on_device(): second_got = lax.ppermute(second, 'col', SWAP)]
    ppermute x2 -> x3, starting transfers between devices: 2.16 us -> 4.06 us  [the longest x1 1.97 us: on_device(): first_got = lax.ppermute(first, 'col', SWAP)]
    pallas_call x4 -> x5, Pallas kernels: 6.15 us -> 6.75 us  [the longest x2 3.67 us: group(): pl.pallas_call(attend_kernel, out_shape=(shape((rows, sent)), shape((rows...]
  transfers between devices with their start and end apart: 9 -> 10, of which waited for: 5 -> 4; matrix products, arithmetic and copies ran while one was open for 0% -> 0% of each run, Pallas kernels for 26% -> 28%
where the time goes in v6:
time: 37.9 us; the launch traced here: 37.7 us
  Pallas kernels  12.4 us (33%)
  waiting for transfers between devices  11.6 us (31%)
  starting transfers between devices  9.58 us (25%)
  between operations  2.11 us (6%)
  local copies, waits for them, and re-layouts  1.99 us (5%)
    ppermute x1, waiting for transfers between devices, on_device(): second_got = lax.ppermute(second, 'col', SWAP)  7.23 us
    pallas_call x2, Pallas kernels, group(): pl.pallas_call(attend_kernel, out_shape=(shape((rows, sent)), shape((rows...  3.67 us
    ppermute x1, waiting for transfers between devices, on_device(): kv_got = normed(kv_norm_kernel, lax.ppermute(kv_raw, 'col', SWAP), 0)  2.93 us
    ppermute x1, starting transfers between devices, on_device(): kv_got = normed(kv_norm_kernel, lax.ppermute(kv_raw, 'col', SWAP), 0)  2.61 us
    pallas_call x2, Pallas kernels, on_device(): pl.pallas_call(functools.partial(final_kernel, start), out_shape=(shape(l...  2.56 us
    pallas_call x1, Pallas kernels, on_device(): pl.pallas_call(own_kernel, out_shape=(shape((tokens, features), jnp.float...  2.51 us
    unnamed x18, local copies, waits for them, and re-layouts  1.99 us
    ppermute x2, starting transfers between devices, on_device(): lax.ppermute(raw, 'col', SWAP)  1.98 us
  transfers between devices with their start and end apart: 10, of which 4 were waited for; matrix products, arithmetic and copies ran while one was open for 0% of the time, Pallas kernels for 28%

profile of v6, /device:TPU:0, one launch (start us, length us, event | category | flops | bytes accessed | tf_op | source)
XLA Modules:
  0.0 37.7 jit_solution(4343159882549326936)
XLA Ops:
  0.6 0.0 copy-start.2
  0.6 0.5 %collective-permute-start = (bf16[1216,640]{1,0:T(8,128)(2,1)}, bf16[1216,640]{1,0:T(8,128)(2,1)S(1)}, u32[]{:S(2)}, u32[]{:S(2)}) collective-permute-start(bf16[1216,640]{1,0:T(8,128)(2,1)} %bitcast.5), channel_id=1, source_target_pairs={{0,2},{2,0},{1,3},{3,1},{4,6},{6,4},{5,7},{7,5},{8,10},{10,8},{9,1... | collective-permute-start | bytes 4669448 | tf_op jit(solution)/shard_map/ppermute | solution.py:399
  1.2 0.0 copy-start.7
  1.2 1.5 %split.1 = (bf16[48,640]{1,0:T(8,128)(2,1)S(1)}, bf16[96,640]{1,0:T(8,128)(2,1)S(1)}, bf16[288,640]{1,0:T(8,128)(2,1)S(1)}, bf16[144,3,640]{2,1,0:T(4,128)(2,1)S(1)}) custom-call(bf16[144,3,1280]{2,1,0:T(4,128)(2,1)} %bitcast.13), custom_call_target="tpu_custom_call" | custom-call | tf_op jit(solution)/shard_map/split/pallas_call | solution.py:385
  2.7 2.6 %collective-permute-start.2 = (bf16[288,640]{1,0:T(8,128)(2,1)S(1)}, bf16[288,640]{1,0:T(8,128)(2,1)S(1)}, u32[]{:S(2)}, u32[]{:S(2)}) collective-permute-start(bf16[288,640]{1,0:T(8,128)(2,1)S(1)} %get-tuple-element.24), channel_id=1, source_target_pairs={{0,1},{1,0},{2,3},{3,2},{4,5},{5,4},{6,7},{7,6},{8,9},{9,8},{10,11... | collective-permute-start | bytes 1105928 | tf_op jit(solution)/shard_map/ppermute | solution.py:429
  6.6 0.0 collective-permute-done._
  6.6 0.0 copy-done.2
  6.6 0.0 copy-start.3
  6.6 0.6 %copy-done.3 = f32[64]{0:T(128)S(1)} copy-done((f32[64]{0:T(128)S(1)}, f32[64]{0:T(128)}, u32[]{:S(2)}) %copy-start.3) | copy-done | bytes 280
  7.3 0.0 copy-start.4
  7.3 0.7 %copy-done.4 = f32[64]{0:T(128)S(1)} copy-done((f32[64]{0:T(128)S(1)}, f32[64]{0:T(128)}, u32[]{:S(2)}) %copy-start.4) | copy-done | bytes 280
  8.0 0.7 %copy-done.5 = f32[64]{0:T(128)S(1)} copy-done((f32[64]{0:T(128)S(1)}, f32[64]{0:T(128)}, u32[]{:S(2)}) %copy-start.5) | copy-done | bytes 280
  8.6 0.9 %prep_own.1 = (bf16[384,640]{1,0:T(8,128)(2,1)S(1)}, bf16[144,640]{1,0:T(8,128)(2,1)S(1)}, f32[3,64]{1,0:T(4,128)S(1)}, f32[1,384]{1,0:T(1,128)S(1)}, bf16[1216,640]{1,0:T(8,128)(2,1)S(1)}) custom-call(s32[1]{0:T(128)S(6)} %copy.16.index_ref, s32[1]{0:T(128)S(6)} %copy.17.count_ref, ...), custom_call_target="tpu_custom_call", output_to_operand_aliasing={{4}: (7, {})} | custom-call | tf_op jit(solution)/shard_map/prep_own/pallas_call | solution.py:401
  9.5 0.3 collective-permute-start.1
  9.8 0.6 %collective-permute-start.4 = (bf16[48,640]{1,0:T(8,128)(2,1)S(1)}, bf16[48,640]{1,0:T(8,128)(2,1)S(1)}, u32[]{:S(2)}, u32[]{:S(2)}) collective-permute-start(bf16[48,640]{1,0:T(8,128)(2,1)S(1)} %get-tuple-element.27), channel_id=1, source_target_pairs={{0,1},{1,0},{2,3},{3,2},{4,5},{5,4},{6,7},{7,6},{8,9},{9,8},{10,11... | collective-permute-start | bytes 184328 | tf_op jit(solution)/shard_map/ppermute | solution.py:431
  10.4 0.0 copy-done.7
  10.4 0.1 collective-permute-start.6
  10.4 1.4 %collective-permute-start.7 = (bf16[96,640]{1,0:T(8,128)(2,1)S(1)}, bf16[96,640]{1,0:T(8,128)(2,1)S(1)}, u32[]{:S(2)}, u32[]{:S(2)}) collective-permute-start(bf16[96,640]{1,0:T(8,128)(2,1)S(1)} %get-tuple-element.30), channel_id=1, source_target_pairs={{0,1},{1,0},{2,3},{3,2},{4,5},{5,4},{6,7},{7,6},{8,9},{9,8},{10,11... | collective-permute-start | bytes 368648 | tf_op jit(solution)/shard_map/ppermute | solution.py:431
  11.8 2.9 %collective-permute-done.2.x_ref = bf16[288,640]{1,0:T(8,128)(2,1)S(1)} collective-permute-done((bf16[288,640]{1,0:T(8,128)(2,1)S(1)}, bf16[288,640]{1,0:T(8,128)(2,1)S(1)}, u32[]{:S(2)}, u32[]{:S(2)}) %collective-permute-start.2) | collective-permute-done | bytes 368672 | tf_op jit(solution)/shard_map/ppermute | solution.py:429
  14.8 0.3 kv_norm_kernel.1.refs_3_
  15.0 0.0 copy-start
  15.1 0.1 collective-permute-start.3
  15.1 0.9 %collective-permute-done.4.x_ref = bf16[48,640]{1,0:T(8,128)(2,1)S(1)} collective-permute-done((bf16[48,640]{1,0:T(8,128)(2,1)S(1)}, bf16[48,640]{1,0:T(8,128)(2,1)S(1)}, u32[]{:S(2)}, u32[]{:S(2)}) %collective-permute-start.4) | collective-permute-done | bytes 61472 | tf_op jit(solution)/shard_map/ppermute | solution.py:431
  16.1 0.2 q_norm_kernel.2.refs_0_
  16.3 0.5 %collective-permute-done.3.refs_4_ = bf16[288,640]{1,0:T(8,128)(2,1)S(1)} collective-permute-done((bf16[288,640]{1,0:T(8,128)(2,1)S(1)}, bf16[288,640]{1,0:T(8,128)(2,1)S(1)}, u32[]{:S(2)}, u32[]{:S(2)}) %collective-permute-start.3) | collective-permute-done | bytes 368672 | tf_op jit(solution)/shard_map/ppermute | solution.py:436
  16.8 0.0 collective-permute-done.1.refs_2_
  16.8 0.0 copy-done
  16.8 1.3 %group.2 = (bf16[48,1280]{1,0:T(8,128)(2,1)S(1)}, bf16[48,640]{1,0:T(8,128)(2,1)S(1)}) custom-call(bf16[48,640]{1,0:T(8,128)(2,1)S(1)} %q_norm_kernel.2.refs_0_, bf16[384,640]{1,0:T(8,128)(2,1)S(1)} %get-tuple-element.23.refs_1_, bf16[384,640]{1,0:T(8,128)(2,1)S(1)} %collective-permute-done.1.refs_2_, bf16[288,640]{1,0:T(8,128)(2,1)S(1)} %kv_norm_kernel.1.refs_3_, ...), custom_call_target="tpu_custom_call" | custom-call | tf_op jit(solution)/shard_map/group/pallas_call | solution.py:440
  18.1 2.0 %collective-permute-start.5 = (bf16[48,1280]{1,0:T(8,128)(2,1)S(1)}, bf16[48,1280]{1,0:T(8,128)(2,1)S(1)}, u32[]{:S(2)}, u32[]{:S(2)}) collective-permute-start(bf16[48,1280]{1,0:T(8,128)(2,1)S(1)} %get-tuple-element.28), channel_id=1, source_target_pairs={{0,1},{1,0},{2,3},{3,2},{4,5},{5,4},{6,7},{7,6},{8,9},{9,8},{10,11... | collective-permute-start | bytes 368648 | tf_op jit(solution)/shard_map/ppermute | solution.py:450
  20.1 0.0 collective-permute-done.7.x_ref
  20.1 0.2 q_norm_kernel.3.refs_0_
  20.3 0.5 %rest.1 = bf16[48,1152]{1,0:T(8,128)(2,1)S(1)} custom-call(bf16[48,640]{1,0:T(8,128)(2,1)S(1)} %get-tuple-element.31.attended_ref, bf16[1216,640]{1,0:T(8,128)(2,1)S(1)} %bitcast.7, bf16[1216,640]{1,0:T(8,128)(2,1)S(1)} %get-tuple-element.26.refs_6_.theirs_ref), custom_call_target="tpu_custom_call" | custom-call | tf_op jit(solution)/shard_map/rest/pallas_call | solution.py:451
  20.9 0.0 copy-start.6
  20.9 0.0 copy-start.8
  20.9 0.2 collective-permute-start.9
  21.1 2.4 %group.3 = (bf16[96,2432]{1,0:T(8,128)(2,1)S(1)}, bf16[96,640]{1,0:T(8,128)(2,1)}) custom-call(bf16[96,640]{1,0:T(8,128)(2,1)S(1)} %q_norm_kernel.3.refs_0_, bf16[384,640]{1,0:T(8,128)(2,1)S(1)} %get-tuple-element.23.refs_1_, bf16[384,640]{1,0:T(8,128)(2,1)S(1)} %collective-permute-done.1.refs_2_, bf16[288,640]{1,0:T(8,128)(2,1)S(1)} %kv_norm_kernel.1.refs_3_, ...), custom_call_target="tpu_custom_call" | custom-call | tf_op jit(solution)/shard_map/group/pallas_call | solution.py:440
  23.5 1.9 %collective-permute-start.8 = (bf16[96,2432]{1,0:T(8,128)(2,1)S(1)}, bf16[96,2432]{1,0:T(8,128)(2,1)S(1)}, u32[]{:S(2)}, u32[]{:S(2)}) collective-permute-start(bf16[96,2432]{1,0:T(8,128)(2,1)S(1)} %get-tuple-element.33), channel_id=1, source_target_pairs={{0,1},{1,0},{2,3},{3,2},{4,5},{5,4},{6,7},{7,6},{8,9},{9,8},{10,11... | collective-permute-start | bytes 1400840 | tf_op jit(solution)/shard_map/ppermute | solution.py:462
  25.4 0.0 collective-permute-done.6.refs_11_
  25.4 0.0 collective-permute-done.5.refs_9_
  25.4 0.0 copy-done.6
  25.4 0.0 copy-done.8
  25.4 0.0 copy-start.1
  25.4 2.5 %own.1 = (f32[144,2432]{1,0:T(8,128)S(1)}, f32[3,2432]{1,0:T(4,128)S(1)}, bf16[64,2432]{1,0:T(8,128)(2,1)S(1)}) custom-call(bf16[144,640]{1,0:T(8,128)(2,1)S(1)} %get-tuple-element.22.refs_0_, bf16[384,640]{1,0:T(8,128)(2,1)S(1)} %get-tuple-element.23.refs_1_, bf16[384,640]{1,0:T(8,128)(2,1)S(1)} %collective-permute-done.1.refs_2_, ...), custom_call_target="tpu_custom_call" | custom-call | flops 60000002048 | bytes 180000000 | tf_op jit(solution)/shard_map/own/pallas_call | solution.py:463
  27.9 0.0 collective-permute-done.9.got_ref
  27.9 0.0 copy-done.1
  27.9 0.9 %final.2 = (f32[24,384]{1,0:T(8,128)S(1)}, f32[24,384]{1,0:T(8,128)S(1)}) custom-call(f32[1,384]{1,0:T(1,128)S(1)} %get-tuple-element.21.euler_ref, f32[144,2432]{1,0:T(8,128)S(1)} %get-tuple-element.29.mixed_ref, bf16[48,1152]{1,0:T(8,128)(2,1)S(1)} %collective-permute-done.9.got_ref, f32[3,2432]{1,0:T(4,128)S(1)} %get-tuple-element.34.mod_ref, ...), custom_call_target="tpu_custom_call" | custom-call | tf_op jit(solution)/shard_map/final/pallas_call | solution.py:488
  28.8 7.2 %collective-permute-done.8.got_ref = bf16[96,2432]{1,0:T(8,128)(2,1)S(1)} collective-permute-done((bf16[96,2432]{1,0:T(8,128)(2,1)S(1)}, bf16[96,2432]{1,0:T(8,128)(2,1)S(1)}, u32[]{:S(2)}, u32[]{:S(2)}) %collective-permute-start.8) | collective-permute-done | bytes 466976 | tf_op jit(solution)/shard_map/ppermute | solution.py:462
  36.1 1.7 %final.3 = (f32[24,384]{1,0:T(8,128)}, f32[24,384]{1,0:T(8,128)}) custom-call(f32[1,384]{1,0:T(1,128)S(1)} %get-tuple-element.21.euler_ref, f32[144,2432]{1,0:T(8,128)S(1)} %get-tuple-element.29.mixed_ref, bf16[96,2432]{1,0:T(8,128)(2,1)S(1)} %collective-permute-done.8.got_ref, f32[3,2432]{1,0:T(4,128)S(1)} %get-tuple-element.34.mod_ref, ...), custom_call_target="tpu_custom_call" | custom-call | tf_op jit(solution)/shard_map/final/pallas_call | solution.py:488
  (1 shorter events, 0.0 us)
Async XLA Ops:
  0.6 6.0 %copy-start.2 = (bf16[48,2,640]{2,1,0:T(2,128)(2,1)S(1)}, bf16[48,2,640]{2,1,0:T(2,128)(2,1)}, u32[]{:S(2)}) copy-start(bf16[48,2,640]{2,1,0:T(2,128)(2,1)} %text_ref.1) | copy-start | bytes 368644
  0.6 6.0 %collective-permute-start = (bf16[1216,640]{1,0:T(8,128)(2,1)}, bf16[1216,640]{1,0:T(8,128)(2,1)S(1)}, u32[]{:S(2)}, u32[]{:S(2)}) collective-permute-start(bf16[1216,640]{1,0:T(8,128)(2,1)} %bitcast.5), channel_id=1, source_target_pairs={{0,2},{2,0},{1,3},{3,1},{4,6},{6,4},{5,7},{7,5},{8,10},{10,8},{9,1... | collective-permute-start | bytes 4669448 | tf_op jit(solution)/shard_map/ppermute | solution.py:399
  1.2 9.2 %copy-start.7 = (bf16[64,1216]{1,0:T(8,128)(2,1)S(1)}, bf16[64,1216]{1,0:T(8,128)(2,1)}, u32[]{:S(2)}) copy-start(bf16[64,1216]{1,0:T(8,128)(2,1)} %refs_10_.1) | copy-start | bytes 466948
  2.7 12.1 %collective-permute-start.2 = (bf16[288,640]{1,0:T(8,128)(2,1)S(1)}, bf16[288,640]{1,0:T(8,128)(2,1)S(1)}, u32[]{:S(2)}, u32[]{:S(2)}) collective-permute-start(bf16[288,640]{1,0:T(8,128)(2,1)S(1)} %get-tuple-element.24), channel_id=1, source_target_pairs={{0,1},{1,0},{2,3},{3,2},{4,5},{5,4},{6,7},{7,6},{8,9},{9,8},{10,11... | collective-permute-start | bytes 1105928 | tf_op jit(solution)/shard_map/ppermute | solution.py:429
  6.6 0.7 %copy-start.3 = (f32[64]{0:T(128)S(1)}, f32[64]{0:T(128)}, u32[]{:S(2)}) copy-start(f32[64]{0:T(128)} %param.14) | copy-start | bytes 772
  7.3 0.7 %copy-start.4 = (f32[64]{0:T(128)S(1)}, f32[64]{0:T(128)}, u32[]{:S(2)}) copy-start(f32[64]{0:T(128)} %param.15) | copy-start | bytes 772
  8.0 0.7 %copy-start.5 = (f32[64]{0:T(128)S(1)}, f32[64]{0:T(128)}, u32[]{:S(2)}) copy-start(f32[64]{0:T(128)} %param.16) | copy-start | bytes 772
  9.5 7.3 %collective-permute-start.1 = (bf16[384,640]{1,0:T(8,128)(2,1)S(1)}, bf16[384,640]{1,0:T(8,128)(2,1)S(1)}, u32[]{:S(2)}, u32[]{:S(2)}) collective-permute-start(bf16[384,640]{1,0:T(8,128)(2,1)S(1)} %get-tuple-element.23.refs_1_), channel_id=1, source_target_pairs={{0,2},{2,0},{1,3},{3,1},{4,6},{6,4},{5,7},{7,5},{8,10},{10,8},{9,1... | collective-permute-start | bytes 1474568 | tf_op jit(solution)/shard_map/ppermute | solution.py:436
  9.8 6.3 %collective-permute-start.4 = (bf16[48,640]{1,0:T(8,128)(2,1)S(1)}, bf16[48,640]{1,0:T(8,128)(2,1)S(1)}, u32[]{:S(2)}, u32[]{:S(2)}) collective-permute-start(bf16[48,640]{1,0:T(8,128)(2,1)S(1)} %get-tuple-element.27), channel_id=1, source_target_pairs={{0,1},{1,0},{2,3},{3,2},{4,5},{5,4},{6,7},{7,6},{8,9},{9,8},{10,11... | collective-permute-start | bytes 184328 | tf_op jit(solution)/shard_map/ppermute | solution.py:431
  10.4 15.0 %collective-permute-start.6 = (bf16[64,1216]{1,0:T(8,128)(2,1)S(1)}, bf16[64,1216]{1,0:T(8,128)(2,1)S(1)}, u32[]{:S(2)}, u32[]{:S(2)}) collective-permute-start(bf16[64,1216]{1,0:T(8,128)(2,1)S(1)} %copy-done.7), channel_id=1, source_target_pairs={{0,2},{2,0},{1,3},{3,1},{4,6},{6,4},{5,7},{7,5},{8,10},{10,8},{9,1... | collective-permute-start | bytes 466952 | tf_op jit(solution)/shard_map/ppermute | solution.py:400
  10.4 9.6 %collective-permute-start.7 = (bf16[96,640]{1,0:T(8,128)(2,1)S(1)}, bf16[96,640]{1,0:T(8,128)(2,1)S(1)}, u32[]{:S(2)}, u32[]{:S(2)}) collective-permute-start(bf16[96,640]{1,0:T(8,128)(2,1)S(1)} %get-tuple-element.30), channel_id=1, source_target_pairs={{0,1},{1,0},{2,3},{3,2},{4,5},{5,4},{6,7},{7,6},{8,9},{9,8},{10,11... | collective-permute-start | bytes 368648 | tf_op jit(solution)/shard_map/ppermute | solution.py:431
  15.0 1.8 %copy-start = (bf16[640,1216]{0,1:T(8,128)(2,1)S(1)}, bf16[640,1216]{0,1:T(8,128)(2,1)}, u32[]{:S(2)}) copy-start(bf16[640,1216]{0,1:T(8,128)(2,1)} %param.17) | copy-start | bytes 4669444
  15.1 1.8 %collective-permute-start.3 = (bf16[288,640]{1,0:T(8,128)(2,1)S(1)}, bf16[288,640]{1,0:T(8,128)(2,1)S(1)}, u32[]{:S(2)}, u32[]{:S(2)}) collective-permute-start(bf16[288,640]{1,0:T(8,128)(2,1)S(1)} %kv_norm_kernel.1.refs_3_), channel_id=1, source_target_pairs={{0,2},{2,0},{1,3},{3,1},{4,6},{6,4},{5,7},{7,5},{8,10},{10,8},{9,1... | collective-permute-start | bytes 1105928 | tf_op jit(solution)/shard_map/ppermute | solution.py:436
  18.1 7.3 %collective-permute-start.5 = (bf16[48,1280]{1,0:T(8,128)(2,1)S(1)}, bf16[48,1280]{1,0:T(8,128)(2,1)S(1)}, u32[]{:S(2)}, u32[]{:S(2)}) collective-permute-start(bf16[48,1280]{1,0:T(8,128)(2,1)S(1)} %get-tuple-element.28), channel_id=1, source_target_pairs={{0,1},{1,0},{2,3},{3,2},{4,5},{5,4},{6,7},{7,6},{8,9},{9,8},{10,11... | collective-permute-start | bytes 368648 | tf_op jit(solution)/shard_map/ppermute | solution.py:450
  20.9 4.5 %copy-start.6 = (bf16[12,12,2432]{2,1,0:T(8,128)(2,1)S(1)}, bf16[12,12,2432]{2,1,0:T(8,128)(2,1)}, u32[]{:S(2)}) copy-start(bf16[12,12,2432]{2,1,0:T(8,128)(2,1)} %refs_7_.1) | copy-start | bytes 2101252
  20.9 4.5 %copy-start.8 = (f32[3,2432]{1,0:T(4,128)S(1)}, f32[3,2432]{1,0:T(4,128)}, u32[]{:S(2)}) copy-start(f32[3,2432]{1,0:T(4,128)} %refs_8_.1) | copy-start | bytes 87556
  20.9 7.0 %collective-permute-start.9 = (bf16[48,1152]{1,0:T(8,128)(2,1)S(1)}, bf16[48,1152]{1,0:T(8,128)(2,1)S(1)}, u32[]{:S(2)}, u32[]{:S(2)}) collective-permute-start(bf16[48,1152]{1,0:T(8,128)(2,1)S(1)} %rest.1), channel_id=1, source_target_pairs={{0,1},{1,0},{2,3},{3,2},{4,5},{5,4},{6,7},{7,6},{8,9},{9,8},{10,11... | collective-permute-start | bytes 331784 | tf_op jit(solution)/shard_map/ppermute | solution.py:459
  23.5 12.5 %collective-permute-start.8 = (bf16[96,2432]{1,0:T(8,128)(2,1)S(1)}, bf16[96,2432]{1,0:T(8,128)(2,1)S(1)}, u32[]{:S(2)}, u32[]{:S(2)}) collective-permute-start(bf16[96,2432]{1,0:T(8,128)(2,1)S(1)} %get-tuple-element.33), channel_id=1, source_target_pairs={{0,1},{1,0},{2,3},{3,2},{4,5},{5,4},{6,7},{7,6},{8,9},{9,8},{10,11... | collective-permute-start | bytes 1400840 | tf_op jit(solution)/shard_map/ppermute | solution.py:462
  25.4 2.5 %copy-start.1 = (f32[24,384]{1,0:T(8,128)S(1)}, f32[24,384]{1,0:T(8,128)}, u32[]{:S(2)}) copy-start(f32[24,384]{1,0:T(8,128)} %latent_ref.3) | copy-start | bytes 110596

commit v7 on v4

--- a/solution.py
+++ b/solution.py
@@ -16,7 +16,7 @@
 LANES = 128
 EPS = 1e-06
 VMEM_LIMIT = 16 * 1024 * 1024
-VMEM_MOST = 60 * 1024 * 1024
+VMEM_MOST = 52 * 1024 * 1024
 LOADS = 3
 FIRST = 1280
 STEP = 640
@@ -89,23 +89,16 @@
 
 def split_kernel(
     x_ref,
-    gain_q_ref,
-    gain_k_ref,
-    gain_t_ref,
     first_ref,
     q_second_ref,
-    gains,
+    own_ref,
     held,
     sems,
-    gain_sems,
+    own_sems,
 ):
-    blocks = load_half(x_ref, held, sems, 1 - lax.axis_index("col"))
-    gain_copies = [
-        pltpu.make_async_copy(ref, gains.at[at : at + 1], gain_sems.at[at])
-        for at, ref in enumerate((gain_q_ref, gain_k_ref, gain_t_ref))
-    ]
-    for copy in gain_copies:
-        copy.start()
+    column = lax.axis_index("col")
+    blocks = load_half(x_ref, held, sems, 1 - column)
+    own_blocks = load_half(x_ref, own_ref, own_sems, column)
     tokens = held.shape[0]
     k_ref, v_ref, q_first_ref = three(first_ref, tokens)
     cut = q_first_ref.shape[0]
@@ -118,7 +111,7 @@
             q_first_ref[rows] = q
         else:
             q_second_ref[rows.start - cut : rows.stop - cut] = q
-    for copy in gain_copies:
+    for _, copy in own_blocks:
         copy.wait()
 
 
@@ -143,17 +136,30 @@
 
 
 def prep_own_kernel(
-    index_ref, count_ref, x_ref, text_ref, gains, _, k_ref, v_ref, q_ref, gains_out, euler_ref, __
+    index_ref,
+    count_ref,
+    x_ref,
+    text_ref,
+    gain_q_ref,
+    gain_k_ref,
+    gain_t_ref,
+    _,
+    k_ref,
+    v_ref,
+    q_ref,
+    gains,
+    euler_ref,
+    __,
 ):
     tokens, width = q_ref.shape
-    gains_out[...] = gains[...]
+    for at, ref in enumerate((gain_q_ref, gain_k_ref, gain_t_ref)):
+        gains[at : at + 1] = ref[...]
     now = jnp.full(euler_ref.shape, index_ref[0], jnp.int32)
     then = now + jnp.full(euler_ref.shape, count_ref[0], jnp.int32)
     euler_ref[...] = noise_level(then) - noise_level(now)
     text = text_ref[...].astype(jnp.float32).transpose(1, 0, 2)
     v_ref[tokens:] = text[1].astype(jnp.bfloat16)
-    at = pl.multiple_of(lax.axis_index("col") * width, LANES)
-    q, k, v = x_ref[:, :, pl.ds(at, width)].transpose(1, 0, 2)
+    q, k, v = x_ref[...].transpose(1, 0, 2)
     v_ref[:tokens] = v
     k_ref[:tokens], k_ref[tokens:], q_ref[...] = head_norms(
         [
@@ -228,14 +234,16 @@
     return store
 
 
-def part_kernel(q_ref, *refs):
-    sum_ref, total_ref = refs[5:]
-
+def keep_sums(sum_ref, total_ref):
     def store(lanes, weighted, total):
         sum_ref[:, lanes] = weighted
         total_ref[:, lanes] = total
 
-    attend(q_ref[...], *keys_and_values(refs[:5]), store)
+    return store
+
+
+def part_kernel(q_ref, *refs):
+    attend(q_ref[...], *keys_and_values(refs[:5]), keep_sums(*refs[5:]))
 
 
 def first_kernel(
@@ -280,28 +288,52 @@
     return jnp.where(is_first, x, jnp.concatenate([x[:, half:], x[:, :half]], axis=1))
 
 
-def own_kernel(*refs):
-    q_ref, weight_refs = refs[0], refs[7:9]
-    hidden_ref, mod_ref, got_ref, mine_ref, theirs_ref = refs[9:14]
-    out_ref, mod_out, finals_ref, attended = refs[14:]
-    attend(q_ref[...], *keys_and_values(refs[1:7]), divide_into(attended))
+def early_kernel(*refs):
+    q_ref, gains, hidden_ref, mod_ref, mine_ref, theirs_ref = refs[0], *refs[5:10]
+    sum_ref, total_ref, mixed_ref, gains_out, mod_out, finals_ref, _ = refs[11:]
+    attend(q_ref[...], *keys_and_values(refs[1:5]), keep_sums(sum_ref, total_ref))
+    gains_out[...] = gains[...]
     is_first = lax.axis_index("row") == 0
-    tile_rows, tile_cols, features = hidden_ref.shape
     mod_out[...] = in_order(mod_ref[...], is_first)
-    out_ref[...] = in_order(
-        jnp.concatenate([hidden_ref[row].astype(jnp.float32) for row in range(tile_rows)], axis=0),
+    mixed_ref[...] = in_order(
+        jnp.concatenate(
+            [hidden_ref[row].astype(jnp.float32) for row in range(hidden_ref.shape[0])], axis=0
+        ),
         is_first,
     )
-
-    def keep(at, to, product):
-        out_ref[:, at:to] += mod_out[2:3, at:to] * product.astype(jnp.float32)
-
-    project(attended[...], weight_refs, 0, features, keep)
-    upto, to = got_ref.shape
-    out_ref[:upto, :to] += mod_out[2:3, :to] * got_ref[...].astype(jnp.float32)
     finals_ref[...] = jnp.concatenate(
         [mine_ref[...].astype(jnp.float32), theirs_ref[...].astype(jnp.float32)], axis=1
     ).astype(jnp.bfloat16)
+
+
+def own_kernel(
+    q_ref,
+    got_ref,
+    last_ref,
+    sum_ref,
+    total_ref,
+    mine_ref,
+    theirs_ref,
+    mixed_ref,
+    mod_ref,
+    first_ref,
+    out_ref,
+    attended,
+):
+    finish = divide_into(attended)
+
+    def store(lanes, weighted, total):
+        finish(lanes, weighted + sum_ref[:, lanes], total + total_ref[:, lanes])
+
+    pairs = [halves(got_ref), halves(last_ref)]
+    attend(q_ref[...], [keys for keys, _ in pairs], [values for _, values in pairs], store)
+
+    def keep(at, to, product):
+        out_ref[:, at:to] = mixed_ref[:, at:to] + mod_ref[2:3, at:to] * product.astype(jnp.float32)
+
+    project(attended[...], (mine_ref, theirs_ref), 0, out_ref.shape[1], keep)
+    upto, to = first_ref.shape
+    out_ref[:upto, :to] += mod_ref[2:3, :to] * first_ref[...].astype(jnp.float32)
 
 
 def one_hot(dims, condition):
@@ -428,40 +460,58 @@
     loads = pltpu.SemaphoreType.DMA((LOADS,))
     cut = tile_rows // 3 * tile_cols
     chunks = ((0, cut), (cut, tokens))
-    first_raw, second_raw, gains = pl.pallas_call(
+    first_raw, second_raw, own_raw = pl.pallas_call(
         split_kernel,
         out_shape=(
             shape((2 * tokens + cut, width)),
             shape((tokens - cut, width)),
-            shape((len(gains), HEAD), jnp.float32),
+            shape((tokens, 3, width)),
         ),
-        in_specs=[HBM] * 4,
+        in_specs=[HBM],
         out_specs=(VMEM,) * 3,
-        scratch_shapes=[held, loads, pltpu.SemaphoreType.DMA((len(gains),))],
+        scratch_shapes=[held, loads, loads],
         compiler_params=params(VMEM_MOST),
         name="split",
-    )(x, *gains)
-
+    )(x)
     weight_got = lax.ppermute(weight_half, "row", SWAP)
     final_got = lax.ppermute(final_weight, "row", SWAP)
-    k_own, v_own, q_own, gains_on, euler, weight_theirs = pl.pallas_call(
+    k_own, v_own, q_own, gains, euler, weight_theirs = pl.pallas_call(
         prep_own_kernel,
         out_shape=(
             shape((tokens + words, width)),
             shape((tokens + words, width)),
             block,
-            shape(gains.shape, jnp.float32),
+            shape((len(gains), HEAD), jnp.float32),
             shape((1, latent.shape[1]), jnp.float32),
             shape(weight_got.shape),
         ),
-        in_specs=[SMEM, SMEM, VMEM, VMEM, VMEM, ANY],
+        in_specs=[SMEM] * 2 + [VMEM] * 5 + [ANY],
         out_specs=(VMEM,) * 5 + (ANY,),
-        input_output_aliases={5: 5},
+        input_output_aliases={7: 5},
         compiler_params=params(),
         name="prep_own",
-    )(step_index, step_count, x, text_kv, gains, weight_got)
+    )(step_index, step_count, own_raw, text_kv, *gains, weight_got)
     weights = (weight_half, weight_theirs)
-
+    k_row, v_row = (lax.ppermute(x, "row", SWAP) for x in (k_own, v_own))
+    nearby = (k_own, v_own, k_row, v_row)
+    own_sum, own_total, mixed, gains, mods, finals, second_raw = pl.pallas_call(
+        early_kernel,
+        out_shape=(
+            shape((tokens, width), jnp.float32),
+            shape((tokens, width), jnp.float32),
+            shape((tokens, features), jnp.float32),
+            shape(gains.shape, jnp.float32),
+            shape(modulation.shape, jnp.float32),
+            shape((final_weight.shape[0], features)),
+            shape(second_raw.shape),
+        ),
+        in_specs=[VMEM] * 10 + [ANY],
+        out_specs=(VMEM,) * 6 + (ANY,),
+        input_output_aliases={10: 6},
+        compiler_params=params(),
+        name="early",
+    )(q_own, *nearby, gains, hidden, modulation, final_weight, final_got, second_raw)
+    q_second = lax.ppermute(second_raw, "col", SWAP)
     kv_got, q_first = pl.pallas_call(
         norm_kernel,
         out_shape=(shape((2 * tokens, width)), shape((cut, width))),
@@ -469,10 +519,8 @@
         out_specs=(VMEM,) * 2,
         compiler_params=params(),
         name="norm",
-    )(lax.ppermute(first_raw, "col", SWAP), gains_on)
-    q_second = lax.ppermute(second_raw, "col", SWAP)
-    k_row, v_row, kv_last = (lax.ppermute(x, "row", SWAP) for x in (k_own, v_own, kv_got))
-    pairs = (k_own, v_own, k_row, v_row, kv_got, kv_last)
+    )(lax.ppermute(first_raw, "col", SWAP), gains)
+    kv_last = lax.ppermute(kv_got, "row", SWAP)
     sums = pl.pallas_call(
         part_kernel,
         out_shape=(shape((cut, width), jnp.float32),) * 2,
@@ -481,7 +529,7 @@
         compiler_params=params(),
         cost_estimate=lasting(4.5),
         name="part",
-    )(q_first, *pairs[:5])
+    )(q_first, *nearby, kv_got)
     first, heads = pl.pallas_call(
         first_kernel,
         out_shape=(shape((cut, FIRST)), shape((cut, width))),
@@ -509,31 +557,18 @@
         scratch_shapes=[pltpu.VMEM((tokens - cut, width), jnp.bfloat16)],
         compiler_params=params(),
         name="second",
-    )(q_second, gains_on, *pairs, *weights)
+    )(q_second, gains, *nearby, kv_got, kv_last, *weights)
     second_got = lax.ppermute(second, "col", SWAP)
-    mixed, mods, finals = pl.pallas_call(
+    mixed = pl.pallas_call(
         own_kernel,
-        out_shape=(
-            shape((tokens, features), jnp.float32),
-            shape(modulation.shape, jnp.float32),
-            shape((final_weight.shape[0], features)),
-        ),
-        in_specs=[VMEM] * 14,
-        out_specs=(VMEM,) * 3,
+        out_shape=shape(mixed.shape, jnp.float32),
+        in_specs=[VMEM] * 10,
+        out_specs=VMEM,
         scratch_shapes=[pltpu.VMEM((tokens, width), jnp.bfloat16)],
         compiler_params=params(),
         cost_estimate=lasting(60),
         name="own",
-    )(
-        q_own,
-        *pairs,
-        *weights,
-        hidden,
-        modulation,
-        first_got,
-        final_weight,
-        final_got,
-    )
+    )(q_own, kv_got, kv_last, own_sum, own_total, *weights, mixed, mods, first_got)
     results = ()
     for (start, _), got in ((chunks[0], rest_got), (chunks[1], second_got)):
         results = pl.pallas_call(

time: 40.1 us -> 39.1 us (0.975)
  waiting for transfers between devices: 15 us -> 13.5 us
    ppermute x1, waiting for transfers between devices: 6.17 us -> 2.67 us  [on_device(): lax.ppermute(first_raw, 'col', SWAP)]
    ppermute x1, waiting for transfers between devices: 0.01 us -> 1.38 us  [on_device(): final_got = lax.ppermute(final_weight, 'row', SWAP)]
    ppermute x1, waiting for transfers between devices: 7.84 us -> 8.5 us  [on_device(): second_got = lax.ppermute(second, 'col', SWAP)]
    pallas_call x1, Pallas kernels: 2.12 us -> 1.51 us  [on_device(): pl.pallas_call(split_kernel, out_shape=(shape((2 * tokens + cut, width)),...]
    ppermute x1, starting transfers between devices: 0.26 us -> 0.7 us  [on_device(): q_second = lax.ppermute(second_raw, 'col', SWAP)]
    pallas_call x1 -> x2, Pallas kernels: 2.48 us -> 2.88 us  [the longest x1 1.87 us: on_device(): pl.pallas_call(own_kernel, out_shape=shape(mixed.shape, jnp.float32), in_...]
  transfers between devices with their start and end apart: 10 -> 10, of which waited for: 3 -> 4; matrix products, arithmetic and copies ran while one was open for 0% -> 0% of each run, Pallas kernels for 28% -> 28%
where the time goes in v7:
time: 39.1 us; the launch traced here: 38.9 us
  waiting for transfers between devices  13.5 us (35%)
  Pallas kernels  12.5 us (32%)
  starting transfers between devices  8.78 us (22%)
  between operations  2.12 us (5%)
  local copies, waits for them, and re-layouts  1.99 us (5%)
    ppermute x1, waiting for transfers between devices, on_device(): second_got = lax.ppermute(second, 'col', SWAP)  8.5 us
    ppermute x1, waiting for transfers between devices, on_device(): lax.ppermute(first_raw, 'col', SWAP)  2.67 us
    ppermute x1, starting transfers between devices, on_device(): lax.ppermute(first_raw, 'col', SWAP)  2.61 us
    pallas_call x2, Pallas kernels, on_device(): pl.pallas_call(functools.partial(final_kernel, start), out_shape=(shape(l...  2.56 us
    pallas_call x1, Pallas kernels, on_device(): pl.pallas_call(second_kernel, out_shape=shape((tokens - cut, features)),...  2.08 us
    ppermute x1, starting transfers between devices, on_device(): second_got = lax.ppermute(second, 'col', SWAP)  2.01 us
    unnamed x18, local copies, waits for them, and re-layouts  1.99 us
    ppermute x1, starting transfers between devices, on_device(): first_got = lax.ppermute(first, 'col', SWAP)  1.95 us
  transfers between devices with their start and end apart: 10, of which 4 were waited for; matrix products, arithmetic and copies ran while one was open for 0% of the time, Pallas kernels for 28%

profile of v7, /device:TPU:0, one launch (start us, length us, event | category | flops | bytes accessed | tf_op | source)
XLA Modules:
  0.0 38.9 jit_solution(5160773374653020085)
XLA Ops:
  0.6 0.0 copy-start.4
  0.6 0.5 %collective-permute-start = (bf16[1216,640]{1,0:T(8,128)(2,1)}, bf16[1216,640]{1,0:T(8,128)(2,1)S(1)}, u32[]{:S(2)}, u32[]{:S(2)}) collective-permute-start(bf16[1216,640]{1,0:T(8,128)(2,1)} %bitcast.5), channel_id=1, source_target_pairs={{0,2},{2,0},{1,3},{3,1},{4,6},{6,4},{5,7},{7,5},{8,10},{10,8},{9,1... | collective-permute-start | bytes 4669448 | tf_op jit(solution)/shard_map/ppermute | solution.py:476
  1.2 1.5 %split.1 = (bf16[336,640]{1,0:T(8,128)(2,1)S(1)}, bf16[96,640]{1,0:T(8,128)(2,1)S(1)}, bf16[144,3,640]{2,1,0:T(4,128)(2,1)S(1)}) custom-call(bf16[144,3,1280]{2,1,0:T(4,128)(2,1)} %bitcast.13), custom_call_target="tpu_custom_call" | custom-call | tf_op jit(solution)/shard_map/split/pallas_call | solution.py:463
  2.7 0.0 copy-start.2
  2.7 0.0 copy-start.1
  2.7 0.0 copy-start.5
  2.7 2.6 %collective-permute-start.1 = (bf16[336,640]{1,0:T(8,128)(2,1)S(1)}, bf16[336,640]{1,0:T(8,128)(2,1)S(1)}, u32[]{:S(2)}, u32[]{:S(2)}) collective-permute-start(bf16[336,640]{1,0:T(8,128)(2,1)S(1)} %get-tuple-element.30), channel_id=1, source_target_pairs={{0,1},{1,0},{2,3},{3,2},{4,5},{5,4},{6,7},{7,6},{8,9},{9,8},{10,11... | collective-permute-start | bytes 1290248 | tf_op jit(solution)/shard_map/ppermute | solution.py:522
  6.6 0.0 collective-permute-done._
  6.6 0.0 copy-done.4
  6.6 0.0 copy-start.6
  6.6 0.6 %copy-done.6 = f32[64]{0:T(128)S(1)} copy-done((f32[64]{0:T(128)S(1)}, f32[64]{0:T(128)}, u32[]{:S(2)}) %copy-start.6) | copy-done | bytes 280
  7.3 0.0 copy-start.7
  7.3 0.7 %copy-done.7 = f32[64]{0:T(128)S(1)} copy-done((f32[64]{0:T(128)S(1)}, f32[64]{0:T(128)}, u32[]{:S(2)}) %copy-start.7) | copy-done | bytes 280
  7.9 0.0 copy-start.8
  8.0 0.7 %copy-done.8 = f32[64]{0:T(128)S(1)} copy-done((f32[64]{0:T(128)S(1)}, f32[64]{0:T(128)}, u32[]{:S(2)}) %copy-start.8) | copy-done | bytes 280
  8.6 0.9 %prep_own.1 = (bf16[192,640]{1,0:T(8,128)(2,1)S(1)}, bf16[192,640]{1,0:T(8,128)(2,1)S(1)}, bf16[144,640]{1,0:T(8,128)(2,1)S(1)}, f32[3,64]{1,0:T(4,128)S(1)}, f3...) custom-call(s32[1]{0:T(128)S(6)} %copy.18.index_ref, s32[1]{0:T(128)S(6)} %copy.19.count_ref, ...), custom_call_target="tpu_custom_call", output_to_operand_aliasing={{5}: (7, {})} | custom-call | tf_op jit(solution)/shard_map/prep_own/pallas_call | solution.py:478
  9.5 0.3 collective-permute-start.2
  9.8 0.3 collective-permute-start.3
  10.1 0.0 copy-done.2
  10.1 0.2 collective-permute-start.4
  10.3 1.4 %collective-permute-done.4.refs_9_ = bf16[64,1216]{1,0:T(8,128)(2,1)S(1)} collective-permute-done((bf16[64,1216]{1,0:T(8,128)(2,1)S(1)}, bf16[64,1216]{1,0:T(8,128)(2,1)S(1)}, u32[]{:S(2)}, u32[]{:S(2)}) %collective-permute-start.4) | collective-permute-done | bytes 155680 | tf_op jit(solution)/shard_map/ppermute | solution.py:477
  11.7 0.0 collective-permute-done.2.refs_3_.refs_2_.refs_4_
  11.7 0.0 collective-permute-done.3.refs_4_.refs_3_.refs_5_
  11.7 0.0 copy-done.1
  11.7 0.0 copy-done.5
  11.7 1.0 %early.1 = (f32[144,640]{1,0:T(8,128)S(1)}, f32[144,640]{1,0:T(8,128)S(1)}, f32[144,2432]{1,0:T(8,128)S(1)}, f32[3,64]{1,0:T(4,128)S(1)}, f32[3,2432]{1,0:T(4,12...) custom-call(bf16[144,640]{1,0:T(8,128)(2,1)S(1)} %get-tuple-element.29.refs_0_, ...), custom_call_target="tpu_custom_call", output_to_operand_aliasing={{6}: (10, {})} | custom-call | tf_op jit(solution)/shard_map/early/pallas_call | solution.py:497
  12.7 0.7 %collective-permute-start.7 = (bf16[96,640]{1,0:T(8,128)(2,1)S(1)}, bf16[96,640]{1,0:T(8,128)(2,1)S(1)}, u32[]{:S(2)}, u32[]{:S(2)}) collective-permute-start(bf16[96,640]{1,0:T(8,128)(2,1)S(1)} %get-tuple-element.46), channel_id=1, source_target_pairs={{0,1},{1,0},{2,3},{3,2},{4,5},{5,4},{6,7},{7,6},{8,9},{9,8},{10,11... | collective-permute-start | bytes 368648 | tf_op jit(solution)/shard_map/ppermute | solution.py:514
  13.4 2.7 %collective-permute-done.1.x_ref = bf16[336,640]{1,0:T(8,128)(2,1)S(1)} collective-permute-done((bf16[336,640]{1,0:T(8,128)(2,1)S(1)}, bf16[336,640]{1,0:T(8,128)(2,1)S(1)}, u32[]{:S(2)}, u32[]{:S(2)}) %collective-permute-start.1) | collective-permute-done | bytes 430112 | tf_op jit(solution)/shard_map/ppermute | solution.py:522
  16.1 0.3 norm.1
  16.4 0.1 collective-permute-start.5
  16.5 0.0 copy-start
  16.5 0.7 %part.1 = (f32[48,640]{1,0:T(8,128)S(1)}, f32[48,640]{1,0:T(8,128)S(1)}) custom-call(bf16[48,640]{1,0:T(8,128)(2,1)S(1)} %get-tuple-element.42.q_ref, bf16[192,640]{1,0:T(8,128)(2,1)S(1)} %get-tuple-element.31.refs_1_.refs_0_.refs_2_, bf16[192,640]{1,0:T(8,128)(2,1)S(1)} %get-tuple-element.32.refs_2_.refs_1_.refs_3_, ...), custom_call_target="tpu_custom_call" | custom-call | flops 4499999744 | bytes 13500000 | tf_op jit(solution)/shard_map/part/pallas_call | solution.py:524
  17.2 1.0 %collective-permute-done.5.last_ref.refs_7_ = bf16[288,640]{1,0:T(8,128)(2,1)S(1)} collective-permute-done((bf16[288,640]{1,0:T(8,128)(2,1)S(1)}, bf16[288,640]{1,0:T(8,128)(2,1)S(1)}, u32[]{:S(2)}, u32[]{:S(2)}) %collective-permute-start.5) | collective-permute-done | bytes 368672 | tf_op jit(solution)/shard_map/ppermute | solution.py:523
  18.2 0.0 copy-done
  18.2 1.1 %first.1 = (bf16[48,1280]{1,0:T(8,128)(2,1)S(1)}, bf16[48,640]{1,0:T(8,128)(2,1)S(1)}) custom-call(bf16[48,640]{1,0:T(8,128)(2,1)S(1)} %get-tuple-element.42.q_ref, bf16[288,640]{1,0:T(8,128)(2,1)S(1)} %collective-permute-done.5.last_ref.refs_7_, f32[48,640]{1,0:T(8,128)S(1)} %get-tuple-element.43.sum_ref, f32[48,640]{1,0:T(8,128)S(1)} %get-tuple-element.44.total_ref, ...), custom_call_target="tpu_custom_call" | custom-call | tf_op jit(solution)/shard_map/first/pallas_call | solution.py:533
  19.2 2.0 %collective-permute-start.6 = (bf16[48,1280]{1,0:T(8,128)(2,1)S(1)}, bf16[48,1280]{1,0:T(8,128)(2,1)S(1)}, u32[]{:S(2)}, u32[]{:S(2)}) collective-permute-start(bf16[48,1280]{1,0:T(8,128)(2,1)S(1)} %get-tuple-element.45), channel_id=1, source_target_pairs={{0,1},{1,0},{2,3},{3,2},{4,5},{5,4},{6,7},{7,6},{8,9},{9,8},{10,11... | collective-permute-start | bytes 368648 | tf_op jit(solution)/shard_map/ppermute | solution.py:541
  21.2 0.5 %rest.1 = bf16[48,1152]{1,0:T(8,128)(2,1)S(1)} custom-call(bf16[48,640]{1,0:T(8,128)(2,1)S(1)} %get-tuple-element.47.attended_ref, bf16[1216,640]{1,0:T(8,128)(2,1)S(1)} %bitcast.7, bf16[1216,640]{1,0:T(8,128)(2,1)S(1)} %get-tuple-element.39.theirs_ref.refs_9_), custom_call_target="tpu_custom_call" | custom-call | tf_op jit(solution)/shard_map/rest/pallas_call | solution.py:542
  21.7 0.2 collective-permute-start.9
  21.9 0.0 collective-permute-done.7.refs_0_
  21.9 2.1 %second.1 = bf16[96,2432]{1,0:T(8,128)(2,1)S(1)} custom-call(bf16[96,640]{1,0:T(8,128)(2,1)S(1)} %collective-permute-done.7.refs_0_, f32[3,64]{1,0:T(4,128)S(1)} %get-tuple-element.35.gains.refs_1_, bf16[192,640]{1,0:T(8,128)(2,1)S(1)} %get-tuple-element.31.refs_1_.refs_0_.refs_2_, bf16[192,640]{1,0:T(8,128)(2,1)S(1)} %get-tuple-element.32.refs_2_.refs_1_.refs_3_, ...), custom_call_target="tpu_custom_call" | custom-call | tf_op jit(solution)/shard_map/second/pallas_call | solution.py:552
  24.0 2.0 %collective-permute-start.8 = (bf16[96,2432]{1,0:T(8,128)(2,1)S(1)}, bf16[96,2432]{1,0:T(8,128)(2,1)S(1)}, u32[]{:S(2)}, u32[]{:S(2)}) collective-permute-start(bf16[96,2432]{1,0:T(8,128)(2,1)S(1)} %second.1), channel_id=1, source_target_pairs={{0,1},{1,0},{2,3},{3,2},{4,5},{5,4},{6,7},{7,6},{8,9},{9,8},{10,11... | collective-permute-start | bytes 1400840 | tf_op jit(solution)/shard_map/ppermute | solution.py:561
  26.0 0.0 collective-permute-done.6.first_ref
  26.0 1.9 %own.1.mixed_ref = f32[144,2432]{1,0:T(8,128)S(1)} custom-call(bf16[144,640]{1,0:T(8,128)(2,1)S(1)} %get-tuple-element.29.refs_0_.q_ref, bf16[288,640]{1,0:T(8,128)(2,1)S(1)} %get-tuple-element.36.refs_4_.got_ref.refs_6_, bf16[288,640]{1,0:T(8,128)(2,1)S(1)} %collective-permute-done.5.last_ref.refs_7_, f32[144,640]{1,0:T(8,128)S(1)} %get-tuple-element.37.sum_ref, ...), custom_call_target="tpu_custom_call" | custom-call | flops 60000002048 | bytes 180000000 | tf_op jit(solution)/shard_map/own/pallas_call | solution.py:562
  27.9 0.0 collective-permute-done.9.rest_ref
  27.9 0.0 copy-done.3
  27.9 0.9 %final.2 = (f32[24,384]{1,0:T(8,128)S(1)}, f32[24,384]{1,0:T(8,128)S(1)}) custom-call(f32[1,384]{1,0:T(1,128)S(1)} %get-tuple-element.28.euler_ref, f32[144,2432]{1,0:T(8,128)S(1)} %own.1.mixed_ref, bf16[48,1152]{1,0:T(8,128)(2,1)S(1)} %collective-permute-done.9.rest_ref, f32[3,2432]{1,0:T(4,128)S(1)} %get-tuple-element.41.mod_ref, ...), custom_call_target="tpu_custom_call" | custom-call | tf_op jit(solution)/shard_map/final/pallas_call | solution.py:574
  28.8 8.5 %collective-permute-done.8.rest_ref = bf16[96,2432]{1,0:T(8,128)(2,1)S(1)} collective-permute-done((bf16[96,2432]{1,0:T(8,128)(2,1)S(1)}, bf16[96,2432]{1,0:T(8,128)(2,1)S(1)}, u32[]{:S(2)}, u32[]{:S(2)}) %collective-permute-start.8) | collective-permute-done | bytes 466976 | tf_op jit(solution)/shard_map/ppermute | solution.py:561
  37.3 1.7 %final.3 = (f32[24,384]{1,0:T(8,128)}, f32[24,384]{1,0:T(8,128)}) custom-call(f32[1,384]{1,0:T(1,128)S(1)} %get-tuple-element.28.euler_ref, f32[144,2432]{1,0:T(8,128)S(1)} %own.1.mixed_ref, bf16[96,2432]{1,0:T(8,128)(2,1)S(1)} %collective-permute-done.8.rest_ref, f32[3,2432]{1,0:T(4,128)S(1)} %get-tuple-element.41.mod_ref, ...), custom_call_target="tpu_custom_call" | custom-call | tf_op jit(solution)/shard_map/final/pallas_call | solution.py:574
  (1 shorter events, 0.0 us)
Async XLA Ops:
  0.6 6.0 %copy-start.4 = (bf16[48,2,640]{2,1,0:T(2,128)(2,1)S(1)}, bf16[48,2,640]{2,1,0:T(2,128)(2,1)}, u32[]{:S(2)}) copy-start(bf16[48,2,640]{2,1,0:T(2,128)(2,1)} %text_ref.1) | copy-start | bytes 368644
  0.6 6.0 %collective-permute-start = (bf16[1216,640]{1,0:T(8,128)(2,1)}, bf16[1216,640]{1,0:T(8,128)(2,1)S(1)}, u32[]{:S(2)}, u32[]{:S(2)}) collective-permute-start(bf16[1216,640]{1,0:T(8,128)(2,1)} %bitcast.5), channel_id=1, source_target_pairs={{0,2},{2,0},{1,3},{3,1},{4,6},{6,4},{5,7},{7,5},{8,10},{10,8},{9,1... | collective-permute-start | bytes 4669448 | tf_op jit(solution)/shard_map/ppermute | solution.py:476
  2.7 7.4 %copy-start.2 = (bf16[64,1216]{1,0:T(8,128)(2,1)S(1)}, bf16[64,1216]{1,0:T(8,128)(2,1)}, u32[]{:S(2)}) copy-start(bf16[64,1216]{1,0:T(8,128)(2,1)} %refs_8_.1) | copy-start | bytes 466948
  2.7 9.0 %copy-start.1 = (bf16[12,12,2432]{2,1,0:T(8,128)(2,1)S(1)}, bf16[12,12,2432]{2,1,0:T(8,128)(2,1)}, u32[]{:S(2)}) copy-start(bf16[12,12,2432]{2,1,0:T(8,128)(2,1)} %refs_6_.1) | copy-start | bytes 2101252
  2.7 9.0 %copy-start.5 = (f32[3,2432]{1,0:T(4,128)S(1)}, f32[3,2432]{1,0:T(4,128)}, u32[]{:S(2)}) copy-start(f32[3,2432]{1,0:T(4,128)} %refs_7_.1) | copy-start | bytes 87556
  2.7 13.4 %collective-permute-start.1 = (bf16[336,640]{1,0:T(8,128)(2,1)S(1)}, bf16[336,640]{1,0:T(8,128)(2,1)S(1)}, u32[]{:S(2)}, u32[]{:S(2)}) collective-permute-start(bf16[336,640]{1,0:T(8,128)(2,1)S(1)} %get-tuple-element.30), channel_id=1, source_target_pairs={{0,1},{1,0},{2,3},{3,2},{4,5},{5,4},{6,7},{7,6},{8,9},{9,8},{10,11... | collective-permute-start | bytes 1290248 | tf_op jit(solution)/shard_map/ppermute | solution.py:522
  6.6 0.7 %copy-start.6 = (f32[64]{0:T(128)S(1)}, f32[64]{0:T(128)}, u32[]{:S(2)}) copy-start(f32[64]{0:T(128)} %param.14) | copy-start | bytes 772
  7.3 0.7 %copy-start.7 = (f32[64]{0:T(128)S(1)}, f32[64]{0:T(128)}, u32[]{:S(2)}) copy-start(f32[64]{0:T(128)} %param.15) | copy-start | bytes 772
  7.9 0.7 %copy-start.8 = (f32[64]{0:T(128)S(1)}, f32[64]{0:T(128)}, u32[]{:S(2)}) copy-start(f32[64]{0:T(128)} %param.16) | copy-start | bytes 772
  9.5 2.2 %collective-permute-start.2 = (bf16[192,640]{1,0:T(8,128)(2,1)S(1)}, bf16[192,640]{1,0:T(8,128)(2,1)S(1)}, u32[]{:S(2)}, u32[]{:S(2)}) collective-permute-start(bf16[192,640]{1,0:T(8,128)(2,1)S(1)} %get-tuple-element.31.refs_1_.refs_0_.refs_2_), channel_id=1, source_target_pairs={{0,2},{2,0},{1,3},{3,1},{4,6},{6,4},{5,7},{7,5},{8,10},{10,8},{9,1... | collective-permute-start | bytes 737288 | tf_op jit(solution)/shard_map/ppermute | solution.py:495
  9.8 1.9 %collective-permute-start.3 = (bf16[192,640]{1,0:T(8,128)(2,1)S(1)}, bf16[192,640]{1,0:T(8,128)(2,1)S(1)}, u32[]{:S(2)}, u32[]{:S(2)}) collective-permute-start(bf16[192,640]{1,0:T(8,128)(2,1)S(1)} %get-tuple-element.32.refs_2_.refs_1_.refs_3_), channel_id=1, source_target_pairs={{0,2},{2,0},{1,3},{3,1},{4,6},{6,4},{5,7},{7,5},{8,10},{10,8},{9,1... | collective-permute-start | bytes 737288 | tf_op jit(solution)/shard_map/ppermute | solution.py:495
  10.1 1.6 %collective-permute-start.4 = (bf16[64,1216]{1,0:T(8,128)(2,1)S(1)}, bf16[64,1216]{1,0:T(8,128)(2,1)S(1)}, u32[]{:S(2)}, u32[]{:S(2)}) collective-permute-start(bf16[64,1216]{1,0:T(8,128)(2,1)S(1)} %copy-done.2), channel_id=1, source_target_pairs={{0,2},{2,0},{1,3},{3,1},{4,6},{6,4},{5,7},{7,5},{8,10},{10,8},{9,1... | collective-permute-start | bytes 466952 | tf_op jit(solution)/shard_map/ppermute | solution.py:477
  12.7 9.2 %collective-permute-start.7 = (bf16[96,640]{1,0:T(8,128)(2,1)S(1)}, bf16[96,640]{1,0:T(8,128)(2,1)S(1)}, u32[]{:S(2)}, u32[]{:S(2)}) collective-permute-start(bf16[96,640]{1,0:T(8,128)(2,1)S(1)} %get-tuple-element.46), channel_id=1, source_target_pairs={{0,1},{1,0},{2,3},{3,2},{4,5},{5,4},{6,7},{7,6},{8,9},{9,8},{10,11... | collective-permute-start | bytes 368648 | tf_op jit(solution)/shard_map/ppermute | solution.py:514
  16.4 1.8 %collective-permute-start.5 = (bf16[288,640]{1,0:T(8,128)(2,1)S(1)}, bf16[288,640]{1,0:T(8,128)(2,1)S(1)}, u32[]{:S(2)}, u32[]{:S(2)}) collective-permute-start(bf16[288,640]{1,0:T(8,128)(2,1)S(1)} %get-tuple-element.36.refs_4_.got_ref.refs_6_), channel_id=1, source_target_pairs={{0,2},{2,0},{1,3},{3,1},{4,6},{6,4},{5,7},{7,5},{8,10},{10,8},{9,1... | collective-permute-start | bytes 1105928 | tf_op jit(solution)/shard_map/ppermute | solution.py:523
  16.5 1.7 %copy-start = (bf16[640,1216]{0,1:T(8,128)(2,1)S(1)}, bf16[640,1216]{0,1:T(8,128)(2,1)}, u32[]{:S(2)}) copy-start(bf16[640,1216]{0,1:T(8,128)(2,1)} %param.17) | copy-start | bytes 4669444
  19.2 6.8 %collective-permute-start.6 = (bf16[48,1280]{1,0:T(8,128)(2,1)S(1)}, bf16[48,1280]{1,0:T(8,128)(2,1)S(1)}, u32[]{:S(2)}, u32[]{:S(2)}) collective-permute-start(bf16[48,1280]{1,0:T(8,128)(2,1)S(1)} %get-tuple-element.45), channel_id=1, source_target_pairs={{0,1},{1,0},{2,3},{3,2},{4,5},{5,4},{6,7},{7,6},{8,9},{9,8},{10,11... | collective-permute-start | bytes 368648 | tf_op jit(solution)/shard_map/ppermute | solution.py:541
  21.7 6.1 %collective-permute-start.9 = (bf16[48,1152]{1,0:T(8,128)(2,1)S(1)}, bf16[48,1152]{1,0:T(8,128)(2,1)S(1)}, u32[]{:S(2)}, u32[]{:S(2)}) collective-permute-start(bf16[48,1152]{1,0:T(8,128)(2,1)S(1)} %rest.1), channel_id=1, source_target_pairs={{0,1},{1,0},{2,3},{3,2},{4,5},{5,4},{6,7},{7,6},{8,9},{9,8},{10,11... | collective-permute-start | bytes 331784 | tf_op jit(solution)/shard_map/ppermute | solution.py:550
  24.0 13.3 %collective-permute-start.8 = (bf16[96,2432]{1,0:T(8,128)(2,1)S(1)}, bf16[96,2432]{1,0:T(8,128)(2,1)S(1)}, u32[]{:S(2)}, u32[]{:S(2)}) collective-permute-start(bf16[96,2432]{1,0:T(8,128)(2,1)S(1)} %second.1), channel_id=1, source_target_pairs={{0,1},{1,0},{2,3},{3,2},{4,5},{5,4},{6,7},{7,6},{8,9},{9,8},{10,11... | collective-permute-start | bytes 1400840 | tf_op jit(solution)/shard_map/ppermute | solution.py:561
  26.0 1.9 %copy-start.3 = (f32[24,384]{1,0:T(8,128)S(1)}, f32[24,384]{1,0:T(8,128)}, u32[]{:S(2)}) copy-start(f32[24,384]{1,0:T(8,128)} %latent_ref.3) | copy-start | bytes 110596

commit v8 on v7

--- a/solution.py
+++ b/solution.py
@@ -83,13 +83,10 @@
     return ref.at[:rows], ref.at[rows:]
 
 
-def three(ref, tokens):
-    return ref.at[:tokens], ref.at[tokens : 2 * tokens], ref.at[2 * tokens :]
-
-
 def split_kernel(
     x_ref,
-    first_ref,
+    kv_ref,
+    q_first_ref,
     q_second_ref,
     own_ref,
     held,
@@ -99,8 +96,7 @@
     column = lax.axis_index("col")
     blocks = load_half(x_ref, held, sems, 1 - column)
     own_blocks = load_half(x_ref, own_ref, own_sems, column)
-    tokens = held.shape[0]
-    k_ref, v_ref, q_first_ref = three(first_ref, tokens)
+    k_ref, v_ref = halves(kv_ref)
     cut = q_first_ref.shape[0]
     for rows, copy in blocks:
         copy.wait()
@@ -120,13 +116,10 @@
     return q
 
 
-def norm_kernel(x_ref, gains, kv_ref, q_ref):
-    k, v, q = three(x_ref, kv_ref.shape[0] // 2)
-    k_out, v_out = halves(kv_ref)
+def norm_kernel(x_ref, gains, kv_ref):
+    (k, v), (k_out, v_out) = halves(x_ref), halves(kv_ref)
     v_out[...] = v[...]
-    k_out[...], q_ref[...] = head_norms(
-        [(k[...].astype(jnp.float32), gains[1:2]), (q[...].astype(jnp.float32), gains[0:1])]
-    )
+    (k_out[...],) = head_norms([(k[...].astype(jnp.float32), gains[1:2])])
 
 
 def keys_and_values(refs):
@@ -242,8 +235,10 @@
     return store
 
 
-def part_kernel(q_ref, *refs):
-    attend(q_ref[...], *keys_and_values(refs[:5]), keep_sums(*refs[5:]))
+def part_kernel(x_ref, gains, *refs):
+    q_ref, sum_ref, total_ref = refs[5:]
+    q_ref[...] = q_norm(x_ref, gains)
+    attend(q_ref[...], *keys_and_values(refs[:5]), keep_sums(sum_ref, total_ref))
 
 
 def first_kernel(
@@ -290,7 +285,7 @@
 
 def early_kernel(*refs):
     q_ref, gains, hidden_ref, mod_ref, mine_ref, theirs_ref = refs[0], *refs[5:10]
-    sum_ref, total_ref, mixed_ref, gains_out, mod_out, finals_ref, _ = refs[11:]
+    sum_ref, total_ref, mixed_ref, gains_out, mod_out, finals_ref = refs[12:18]
     attend(q_ref[...], *keys_and_values(refs[1:5]), keep_sums(sum_ref, total_ref))
     gains_out[...] = gains[...]
     is_first = lax.axis_index("row") == 0
@@ -460,15 +455,16 @@
     loads = pltpu.SemaphoreType.DMA((LOADS,))
     cut = tile_rows // 3 * tile_cols
     chunks = ((0, cut), (cut, tokens))
-    first_raw, second_raw, own_raw = pl.pallas_call(
+    kv_raw, first_raw, second_raw, own_raw = pl.pallas_call(
         split_kernel,
         out_shape=(
-            shape((2 * tokens + cut, width)),
+            shape((2 * tokens, width)),
+            shape((cut, width)),
             shape((tokens - cut, width)),
             shape((tokens, 3, width)),
         ),
         in_specs=[HBM],
-        out_specs=(VMEM,) * 3,
+        out_specs=(VMEM,) * 4,
         scratch_shapes=[held, loads, loads],
         compiler_params=params(VMEM_MOST),
         name="split",
@@ -494,7 +490,7 @@
     weights = (weight_half, weight_theirs)
     k_row, v_row = (lax.ppermute(x, "row", SWAP) for x in (k_own, v_own))
     nearby = (k_own, v_own, k_row, v_row)
-    own_sum, own_total, mixed, gains, mods, finals, second_raw = pl.pallas_call(
+    own_sum, own_total, mixed, gains, mods, finals, *q_raw = pl.pallas_call(
         early_kernel,
         out_shape=(
             shape((tokens, width), jnp.float32),
@@ -503,33 +499,34 @@
             shape(gains.shape, jnp.float32),
             shape(modulation.shape, jnp.float32),
             shape((final_weight.shape[0], features)),
+            shape(first_raw.shape),
             shape(second_raw.shape),
         ),
-        in_specs=[VMEM] * 10 + [ANY],
-        out_specs=(VMEM,) * 6 + (ANY,),
-        input_output_aliases={10: 6},
+        in_specs=[VMEM] * 10 + [ANY] * 2,
+        out_specs=(VMEM,) * 6 + (ANY,) * 2,
+        input_output_aliases={10: 6, 11: 7},
         compiler_params=params(),
         name="early",
-    )(q_own, *nearby, gains, hidden, modulation, final_weight, final_got, second_raw)
-    q_second = lax.ppermute(second_raw, "col", SWAP)
-    kv_got, q_first = pl.pallas_call(
+    )(q_own, *nearby, gains, hidden, modulation, final_weight, final_got, first_raw, second_raw)
+    q_first, q_second = (lax.ppermute(raw, "col", SWAP) for raw in q_raw)
+    kv_got = pl.pallas_call(
         norm_kernel,
-        out_shape=(shape((2 * tokens, width)), shape((cut, width))),
+        out_shape=shape((2 * tokens, width)),
         in_specs=[VMEM] * 2,
-        out_specs=(VMEM,) * 2,
+        out_specs=VMEM,
         compiler_params=params(),
         name="norm",
-    )(lax.ppermute(first_raw, "col", SWAP), gains)
+    )(lax.ppermute(kv_raw, "col", SWAP), gains)
     kv_last = lax.ppermute(kv_got, "row", SWAP)
-    sums = pl.pallas_call(
+    q_first, *sums = pl.pallas_call(
         part_kernel,
-        out_shape=(shape((cut, width), jnp.float32),) * 2,
-        in_specs=[VMEM] * 6,
-        out_specs=(VMEM,) * 2,
+        out_shape=(shape((cut, width)),) + (shape((cut, width), jnp.float32),) * 2,
+        in_specs=[VMEM] * 7,
+        out_specs=(VMEM,) * 3,
         compiler_params=params(),
         cost_estimate=lasting(4.5),
         name="part",
-    )(q_first, *nearby, kv_got)
+    )(q_first, gains, *nearby, kv_got)
     first, heads = pl.pallas_call(
         first_kernel,
         out_shape=(shape((cut, FIRST)), shape((cut, width))),

time: 39.1 us -> 38.1 us (0.974)
  waiting for transfers between devices: 13.5 us -> 12.6 us
    ppermute x1, starting transfers between devices: 1.95 us -> 0.34 us  [on_device(): first_got = lax.ppermute(first, 'col', SWAP)]
    ppermute x1, starting transfers between devices: 0.15 us -> 1.77 us  [on_device(): rest_got = lax.ppermute(rest, 'col', SWAP)]
    ppermute x1, starting transfers between devices: 2.01 us -> 0.39 us  [on_device(): second_got = lax.ppermute(second, 'col', SWAP)]
    ppermute x2 -> x3, starting transfers between devices: 3.3 us -> 4.7 us  [the longest x1 2.61 us: on_device(): lax.ppermute(kv_raw, 'col', SWAP)]
    ppermute x1, waiting for transfers between devices: 0.96 us -> 0.01 us  [on_device(): kv_last = lax.ppermute(kv_got, 'row', SWAP)]
    ppermute x1, waiting for transfers between devices: 8.5 us -> 7.87 us  [on_device(): second_got = lax.ppermute(second, 'col', SWAP)]
    ppermute x1, waiting for transfers between devices: 0.01 us -> 0.49 us  [on_device(): rest_got = lax.ppermute(rest, 'col', SWAP)]
    ppermute x2 -> x3, waiting for transfers between devices: 2.67 us -> 2.44 us  [the longest x2 2.44 us: on_device(): q_first, q_second = (lax.ppermute(raw, 'col', SWAP) for raw in q_raw)]
  transfers between devices with their start and end apart: 10 -> 11, of which waited for: 4 -> 5; matrix products, arithmetic and copies ran while one was open for 0% -> 0% of each run, Pallas kernels for 28% -> 29%
where the time goes in v8:
time: 38.1 us; the launch traced here: 37.9 us
  Pallas kernels  12.7 us (33%)
  waiting for transfers between devices  12.6 us (33%)
  starting transfers between devices  8.56 us (22%)
  between operations  2.12 us (6%)
  local copies, waits for them, and re-layouts  1.99 us (5%)
    ppermute x1, waiting for transfers between devices, on_device(): second_got = lax.ppermute(second, 'col', SWAP)  7.87 us
    ppermute x1, starting transfers between devices, on_device(): lax.ppermute(kv_raw, 'col', SWAP)  2.61 us
    pallas_call x2, Pallas kernels, on_device(): pl.pallas_call(functools.partial(final_kernel, start), out_shape=(shape(l...  2.53 us
    ppermute x2, waiting for transfers between devices, on_device(): q_first, q_second = (lax.ppermute(raw, 'col', SWAP) for raw in q_raw)  2.44 us
    ppermute x2, starting transfers between devices, on_device(): q_first, q_second = (lax.ppermute(raw, 'col', SWAP) for raw in q_raw)  2.09 us
    pallas_call x1, Pallas kernels, on_device(): pl.pallas_call(second_kernel, out_shape=shape((tokens - cut, features)),...  2.07 us
    unnamed x18, local copies, waits for them, and re-layouts  1.99 us
    pallas_call x1, Pallas kernels, on_device(): pl.pallas_call(own_kernel, out_shape=shape(mixed.shape, jnp.float32), in_...  1.87 us
  transfers between devices with their start and end apart: 11, of which 5 were waited for; matrix products, arithmetic and copies ran while one was open for 0% of the time, Pallas kernels for 29%

profile of v8, /device:TPU:0, one launch (start us, length us, event | category | flops | bytes accessed | tf_op | source)
XLA Modules:
  0.0 37.9 jit_solution(17516190158165810096)
XLA Ops:
  0.6 0.0 copy-start.4
  0.6 0.5 %collective-permute-start = (bf16[1216,640]{1,0:T(8,128)(2,1)}, bf16[1216,640]{1,0:T(8,128)(2,1)S(1)}, u32[]{:S(2)}, u32[]{:S(2)}) collective-permute-start(bf16[1216,640]{1,0:T(8,128)(2,1)} %bitcast.5), channel_id=1, source_target_pairs={{0,2},{2,0},{1,3},{3,1},{4,6},{6,4},{5,7},{7,5},{8,10},{10,8},{9,1... | collective-permute-start | bytes 4669448 | tf_op jit(solution)/shard_map/ppermute | solution.py:472
  1.2 1.5 %split.1 = (bf16[288,640]{1,0:T(8,128)(2,1)S(1)}, bf16[48,640]{1,0:T(8,128)(2,1)S(1)}, bf16[96,640]{1,0:T(8,128)(2,1)S(1)}, bf16[144,3,640]{2,1,0:T(4,128)(2,1)S(1)}) custom-call(bf16[144,3,1280]{2,1,0:T(4,128)(2,1)} %bitcast.13), custom_call_target="tpu_custom_call" | custom-call | tf_op jit(solution)/shard_map/split/pallas_call | solution.py:458
  2.7 0.0 copy-start.2
  2.7 0.0 copy-start.1
  2.7 0.0 copy-start.5
  2.7 2.6 %collective-permute-start.1 = (bf16[288,640]{1,0:T(8,128)(2,1)S(1)}, bf16[288,640]{1,0:T(8,128)(2,1)S(1)}, u32[]{:S(2)}, u32[]{:S(2)}) collective-permute-start(bf16[288,640]{1,0:T(8,128)(2,1)S(1)} %get-tuple-element.31), channel_id=1, source_target_pairs={{0,1},{1,0},{2,3},{3,2},{4,5},{5,4},{6,7},{7,6},{8,9},{9,8},{10,11... | collective-permute-start | bytes 1105928 | tf_op jit(solution)/shard_map/ppermute | solution.py:519
  6.6 0.0 collective-permute-done._
  6.6 0.0 copy-done.4
  6.6 0.0 copy-start.6
  6.6 0.6 %copy-done.6 = f32[64]{0:T(128)S(1)} copy-done((f32[64]{0:T(128)S(1)}, f32[64]{0:T(128)}, u32[]{:S(2)}) %copy-start.6) | copy-done | bytes 280
  7.3 0.7 %copy-done.7 = f32[64]{0:T(128)S(1)} copy-done((f32[64]{0:T(128)S(1)}, f32[64]{0:T(128)}, u32[]{:S(2)}) %copy-start.7) | copy-done | bytes 280
  8.0 0.7 %copy-done.8 = f32[64]{0:T(128)S(1)} copy-done((f32[64]{0:T(128)S(1)}, f32[64]{0:T(128)}, u32[]{:S(2)}) %copy-start.8) | copy-done | bytes 280
  8.6 0.9 %prep_own.1 = (bf16[192,640]{1,0:T(8,128)(2,1)S(1)}, bf16[192,640]{1,0:T(8,128)(2,1)S(1)}, bf16[144,640]{1,0:T(8,128)(2,1)S(1)}, f32[3,64]{1,0:T(4,128)S(1)}, f3...) custom-call(s32[1]{0:T(128)S(6)} %copy.20.index_ref, s32[1]{0:T(128)S(6)} %copy.21.count_ref, ...), custom_call_target="tpu_custom_call", output_to_operand_aliasing={{5}: (7, {})} | custom-call | tf_op jit(solution)/shard_map/prep_own/pallas_call | solution.py:474
  9.5 0.3 collective-permute-start.2
  9.8 0.3 collective-permute-start.3
  10.1 0.0 copy-done.2
  10.1 0.2 collective-permute-start.4
  10.3 1.4 %collective-permute-done.4.refs_9_ = bf16[64,1216]{1,0:T(8,128)(2,1)S(1)} collective-permute-done((bf16[64,1216]{1,0:T(8,128)(2,1)S(1)}, bf16[64,1216]{1,0:T(8,128)(2,1)S(1)}, u32[]{:S(2)}, u32[]{:S(2)}) %collective-permute-start.4) | collective-permute-done | bytes 155680 | tf_op jit(solution)/shard_map/ppermute | solution.py:473
  11.7 0.0 collective-permute-done.2.refs_3_.refs_2_.refs_4_
  11.7 0.0 collective-permute-done.3.refs_4_.refs_3_.refs_5_
  11.7 0.0 copy-done.1
  11.7 0.0 copy-done.5
  11.7 1.0 %early.1 = (f32[144,640]{1,0:T(8,128)S(1)}, f32[144,640]{1,0:T(8,128)S(1)}, f32[144,2432]{1,0:T(8,128)S(1)}, f32[3,64]{1,0:T(4,128)S(1)}, f32[3,2432]{1,0:T(4,12...) custom-call(bf16[144,640]{1,0:T(8,128)(2,1)S(1)} %get-tuple-element., ...), custom_call_target="tpu_custom_call", output_to_operand_aliasing={{6}: (10, {}), {7}: (11, {})} | custom-call | tf_op jit(solution)/shard_map/early/pallas_call | solution.py:493
  12.7 0.7 %collective-permute-start.6 = (bf16[48,640]{1,0:T(8,128)(2,1)S(1)}, bf16[48,640]{1,0:T(8,128)(2,1)S(1)}, u32[]{:S(2)}, u32[]{:S(2)}) collective-permute-start(bf16[48,640]{1,0:T(8,128)(2,1)S(1)} %get-tuple-element.43), channel_id=1, source_target_pairs={{0,1},{1,0},{2,3},{3,2},{4,5},{5,4},{6,7},{7,6},{8,9},{9,8},{10,11... | collective-permute-start | bytes 184328 | tf_op jit(solution)/shard_map/ppermute | solution.py:511
  13.4 1.4 %collective-permute-start.8 = (bf16[96,640]{1,0:T(8,128)(2,1)S(1)}, bf16[96,640]{1,0:T(8,128)(2,1)S(1)}, u32[]{:S(2)}, u32[]{:S(2)}) collective-permute-start(bf16[96,640]{1,0:T(8,128)(2,1)S(1)} %get-tuple-element.48), channel_id=1, source_target_pairs={{0,1},{1,0},{2,3},{3,2},{4,5},{5,4},{6,7},{7,6},{8,9},{9,8},{10,11... | collective-permute-start | bytes 368648 | tf_op jit(solution)/shard_map/ppermute | solution.py:511
  14.8 0.0 collective-permute-done.1.x_ref
  14.8 0.3 norm.1.refs_4_.got_ref.refs_6_
  15.1 0.0 copy-start
  15.1 0.1 collective-permute-start.5
  15.2 2.4 %collective-permute-done.6.x_ref = bf16[48,640]{1,0:T(8,128)(2,1)S(1)} collective-permute-done((bf16[48,640]{1,0:T(8,128)(2,1)S(1)}, bf16[48,640]{1,0:T(8,128)(2,1)S(1)}, u32[]{:S(2)}, u32[]{:S(2)}) %collective-permute-start.6) | collective-permute-done | bytes 61472 | tf_op jit(solution)/shard_map/ppermute | solution.py:511
  17.6 0.9 %part.1 = (bf16[48,640]{1,0:T(8,128)(2,1)S(1)}, f32[48,640]{1,0:T(8,128)S(1)}, f32[48,640]{1,0:T(8,128)S(1)}) custom-call(bf16[48,640]{1,0:T(8,128)(2,1)S(1)} %collective-permute-done.6.x_ref, f32[3,64]{1,0:T(4,128)S(1)} %get-tuple-element.37.gains.refs_1_, bf16[192,640]{1,0:T(8,128)(2,1)S(1)} %get-tuple-element.32.refs_1_.refs_0_.refs_2_, ...), custom_call_target="tpu_custom_call" | custom-call | flops 4499999744 | bytes 13500000 | tf_op jit(solution)/shard_map/part/pallas_call | solution.py:521
  18.5 0.0 collective-permute-done.5.last_ref.refs_7_
  18.5 0.0 copy-done
  18.5 1.1 %first.1 = (bf16[48,1280]{1,0:T(8,128)(2,1)S(1)}, bf16[48,640]{1,0:T(8,128)(2,1)S(1)}) custom-call(bf16[48,640]{1,0:T(8,128)(2,1)S(1)} %get-tuple-element.44.q_ref, bf16[288,640]{1,0:T(8,128)(2,1)S(1)} %collective-permute-done.5.last_ref.refs_7_, f32[48,640]{1,0:T(8,128)S(1)} %get-tuple-element.45.sum_ref, f32[48,640]{1,0:T(8,128)S(1)} %get-tuple-element.46.total_ref, ...), custom_call_target="tpu_custom_call" | custom-call | tf_op jit(solution)/shard_map/first/pallas_call | solution.py:530
  19.6 0.3 collective-permute-start.7
  19.9 0.5 %rest.1 = bf16[48,1152]{1,0:T(8,128)(2,1)S(1)} custom-call(bf16[48,640]{1,0:T(8,128)(2,1)S(1)} %get-tuple-element.49.attended_ref, bf16[1216,640]{1,0:T(8,128)(2,1)S(1)} %bitcast.7, bf16[1216,640]{1,0:T(8,128)(2,1)S(1)} %get-tuple-element.40.theirs_ref.refs_9_), custom_call_target="tpu_custom_call" | custom-call | tf_op jit(solution)/shard_map/rest/pallas_call | solution.py:539
  20.5 1.8 %collective-permute-start.10 = (bf16[48,1152]{1,0:T(8,128)(2,1)S(1)}, bf16[48,1152]{1,0:T(8,128)(2,1)S(1)}, u32[]{:S(2)}, u32[]{:S(2)}) collective-permute-start(bf16[48,1152]{1,0:T(8,128)(2,1)S(1)} %rest.1), channel_id=1, source_target_pairs={{0,1},{1,0},{2,3},{3,2},{4,5},{5,4},{6,7},{7,6},{8,9},{9,8},{10,11... | collective-permute-start | bytes 331784 | tf_op jit(solution)/shard_map/ppermute | solution.py:547
  22.3 0.0 collective-permute-done.8.refs_0_
  22.3 2.1 %second.1 = bf16[96,2432]{1,0:T(8,128)(2,1)S(1)} custom-call(bf16[96,640]{1,0:T(8,128)(2,1)S(1)} %collective-permute-done.8.refs_0_, f32[3,64]{1,0:T(4,128)S(1)} %get-tuple-element.37.gains.refs_1_, bf16[192,640]{1,0:T(8,128)(2,1)S(1)} %get-tuple-element.32.refs_1_.refs_0_.refs_2_, bf16[192,640]{1,0:T(8,128)(2,1)S(1)} %get-tuple-element.33.refs_2_.refs_1_.refs_3_, ...), custom_call_target="tpu_custom_call" | custom-call | tf_op jit(solution)/shard_map/second/pallas_call | solution.py:549
  24.3 0.4 %collective-permute-start.9 = (bf16[96,2432]{1,0:T(8,128)(2,1)S(1)}, bf16[96,2432]{1,0:T(8,128)(2,1)S(1)}, u32[]{:S(2)}, u32[]{:S(2)}) collective-permute-start(bf16[96,2432]{1,0:T(8,128)(2,1)S(1)} %second.1), channel_id=1, source_target_pairs={{0,1},{1,0},{2,3},{3,2},{4,5},{5,4},{6,7},{7,6},{8,9},{9,8},{10,11... | collective-permute-start | bytes 1400840 | tf_op jit(solution)/shard_map/ppermute | solution.py:558
  24.7 0.4 %collective-permute-done.7.first_ref = bf16[48,1280]{1,0:T(8,128)(2,1)S(1)} collective-permute-done((bf16[48,1280]{1,0:T(8,128)(2,1)S(1)}, bf16[48,1280]{1,0:T(8,128)(2,1)S(1)}, u32[]{:S(2)}, u32[]{:S(2)}) %collective-permute-start.7) | collective-permute-done | bytes 122912 | tf_op jit(solution)/shard_map/ppermute | solution.py:538
  25.1 1.9 %own.1.mixed_ref = f32[144,2432]{1,0:T(8,128)S(1)} custom-call(bf16[144,640]{1,0:T(8,128)(2,1)S(1)} %get-tuple-element.30.refs_0_.q_ref, bf16[288,640]{1,0:T(8,128)(2,1)S(1)} %norm.1.refs_4_.got_ref.refs_6_, bf16[288,640]{1,0:T(8,128)(2,1)S(1)} %collective-permute-done.5.last_ref.refs_7_, f32[144,640]{1,0:T(8,128)S(1)} %get-tuple-element.38.sum_ref, ...), custom_call_target="tpu_custom_call" | custom-call | flops 60000002048 | bytes 180000000 | tf_op jit(solution)/shard_map/own/pallas_call | solution.py:559
  27.0 0.5 %collective-permute-done.10.rest_ref = bf16[48,1152]{1,0:T(8,128)(2,1)S(1)} collective-permute-done((bf16[48,1152]{1,0:T(8,128)(2,1)S(1)}, bf16[48,1152]{1,0:T(8,128)(2,1)S(1)}, u32[]{:S(2)}, u32[]{:S(2)}) %collective-permute-start.10) | collective-permute-done | bytes 110624 | tf_op jit(solution)/shard_map/ppermute | solution.py:547
  27.5 0.0 copy-done.3
  27.5 0.9 %final.2 = (f32[24,384]{1,0:T(8,128)S(1)}, f32[24,384]{1,0:T(8,128)S(1)}) custom-call(f32[1,384]{1,0:T(1,128)S(1)} %get-tuple-element.29.euler_ref, f32[144,2432]{1,0:T(8,128)S(1)} %own.1.mixed_ref, bf16[48,1152]{1,0:T(8,128)(2,1)S(1)} %collective-permute-done.10.rest_ref, f32[3,2432]{1,0:T(4,128)S(1)} %get-tuple-element.42.mod_ref, ...), custom_call_target="tpu_custom_call" | custom-call | tf_op jit(solution)/shard_map/final/pallas_call | solution.py:571
  28.4 7.9 %collective-permute-done.9.rest_ref = bf16[96,2432]{1,0:T(8,128)(2,1)S(1)} collective-permute-done((bf16[96,2432]{1,0:T(8,128)(2,1)S(1)}, bf16[96,2432]{1,0:T(8,128)(2,1)S(1)}, u32[]{:S(2)}, u32[]{:S(2)}) %collective-permute-start.9) | collective-permute-done | bytes 466976 | tf_op jit(solution)/shard_map/ppermute | solution.py:558
  36.2 1.7 %final.3 = (f32[24,384]{1,0:T(8,128)}, f32[24,384]{1,0:T(8,128)}) custom-call(f32[1,384]{1,0:T(1,128)S(1)} %get-tuple-element.29.euler_ref, f32[144,2432]{1,0:T(8,128)S(1)} %own.1.mixed_ref, bf16[96,2432]{1,0:T(8,128)(2,1)S(1)} %collective-permute-done.9.rest_ref, f32[3,2432]{1,0:T(4,128)S(1)} %get-tuple-element.42.mod_ref, ...), custom_call_target="tpu_custom_call" | custom-call | tf_op jit(solution)/shard_map/final/pallas_call | solution.py:571
  (3 shorter events, 0.0 us)
Async XLA Ops:
  0.6 6.0 %copy-start.4 = (bf16[48,2,640]{2,1,0:T(2,128)(2,1)S(1)}, bf16[48,2,640]{2,1,0:T(2,128)(2,1)}, u32[]{:S(2)}) copy-start(bf16[48,2,640]{2,1,0:T(2,128)(2,1)} %text_ref.1) | copy-start | bytes 368644
  0.6 6.0 %collective-permute-start = (bf16[1216,640]{1,0:T(8,128)(2,1)}, bf16[1216,640]{1,0:T(8,128)(2,1)S(1)}, u32[]{:S(2)}, u32[]{:S(2)}) collective-permute-start(bf16[1216,640]{1,0:T(8,128)(2,1)} %bitcast.5), channel_id=1, source_target_pairs={{0,2},{2,0},{1,3},{3,1},{4,6},{6,4},{5,7},{7,5},{8,10},{10,8},{9,1... | collective-permute-start | bytes 4669448 | tf_op jit(solution)/shard_map/ppermute | solution.py:472
  2.7 7.4 %copy-start.2 = (bf16[64,1216]{1,0:T(8,128)(2,1)S(1)}, bf16[64,1216]{1,0:T(8,128)(2,1)}, u32[]{:S(2)}) copy-start(bf16[64,1216]{1,0:T(8,128)(2,1)} %refs_8_.1) | copy-start | bytes 466948
  2.7 9.0 %copy-start.1 = (bf16[12,12,2432]{2,1,0:T(8,128)(2,1)S(1)}, bf16[12,12,2432]{2,1,0:T(8,128)(2,1)}, u32[]{:S(2)}) copy-start(bf16[12,12,2432]{2,1,0:T(8,128)(2,1)} %refs_6_.1) | copy-start | bytes 2101252
  2.7 9.0 %copy-start.5 = (f32[3,2432]{1,0:T(4,128)S(1)}, f32[3,2432]{1,0:T(4,128)}, u32[]{:S(2)}) copy-start(f32[3,2432]{1,0:T(4,128)} %refs_7_.1) | copy-start | bytes 87556
  2.7 12.1 %collective-permute-start.1 = (bf16[288,640]{1,0:T(8,128)(2,1)S(1)}, bf16[288,640]{1,0:T(8,128)(2,1)S(1)}, u32[]{:S(2)}, u32[]{:S(2)}) collective-permute-start(bf16[288,640]{1,0:T(8,128)(2,1)S(1)} %get-tuple-element.31), channel_id=1, source_target_pairs={{0,1},{1,0},{2,3},{3,2},{4,5},{5,4},{6,7},{7,6},{8,9},{9,8},{10,11... | collective-permute-start | bytes 1105928 | tf_op jit(solution)/shard_map/ppermute | solution.py:519
  6.6 0.7 %copy-start.6 = (f32[64]{0:T(128)S(1)}, f32[64]{0:T(128)}, u32[]{:S(2)}) copy-start(f32[64]{0:T(128)} %param.14) | copy-start | bytes 772
  7.3 0.7 %copy-start.7 = (f32[64]{0:T(128)S(1)}, f32[64]{0:T(128)}, u32[]{:S(2)}) copy-start(f32[64]{0:T(128)} %param.15) | copy-start | bytes 772
  7.9 0.7 %copy-start.8 = (f32[64]{0:T(128)S(1)}, f32[64]{0:T(128)}, u32[]{:S(2)}) copy-start(f32[64]{0:T(128)} %param.16) | copy-start | bytes 772
  9.5 2.2 %collective-permute-start.2 = (bf16[192,640]{1,0:T(8,128)(2,1)S(1)}, bf16[192,640]{1,0:T(8,128)(2,1)S(1)}, u32[]{:S(2)}, u32[]{:S(2)}) collective-permute-start(bf16[192,640]{1,0:T(8,128)(2,1)S(1)} %get-tuple-element.32.refs_1_.refs_0_.refs_2_), channel_id=1, source_target_pairs={{0,2},{2,0},{1,3},{3,1},{4,6},{6,4},{5,7},{7,5},{8,10},{10,8},{9,1... | collective-permute-start | bytes 737288 | tf_op jit(solution)/shard_map/ppermute | solution.py:491
  9.8 1.9 %collective-permute-start.3 = (bf16[192,640]{1,0:T(8,128)(2,1)S(1)}, bf16[192,640]{1,0:T(8,128)(2,1)S(1)}, u32[]{:S(2)}, u32[]{:S(2)}) collective-permute-start(bf16[192,640]{1,0:T(8,128)(2,1)S(1)} %get-tuple-element.33.refs_2_.refs_1_.refs_3_), channel_id=1, source_target_pairs={{0,2},{2,0},{1,3},{3,1},{4,6},{6,4},{5,7},{7,5},{8,10},{10,8},{9,1... | collective-permute-start | bytes 737288 | tf_op jit(solution)/shard_map/ppermute | solution.py:491
  10.1 1.6 %collective-permute-start.4 = (bf16[64,1216]{1,0:T(8,128)(2,1)S(1)}, bf16[64,1216]{1,0:T(8,128)(2,1)S(1)}, u32[]{:S(2)}, u32[]{:S(2)}) collective-permute-start(bf16[64,1216]{1,0:T(8,128)(2,1)S(1)} %copy-done.2), channel_id=1, source_target_pairs={{0,2},{2,0},{1,3},{3,1},{4,6},{6,4},{5,7},{7,5},{8,10},{10,8},{9,1... | collective-permute-start | bytes 466952 | tf_op jit(solution)/shard_map/ppermute | solution.py:473
  12.7 4.9 %collective-permute-start.6 = (bf16[48,640]{1,0:T(8,128)(2,1)S(1)}, bf16[48,640]{1,0:T(8,128)(2,1)S(1)}, u32[]{:S(2)}, u32[]{:S(2)}) collective-permute-start(bf16[48,640]{1,0:T(8,128)(2,1)S(1)} %get-tuple-element.43), channel_id=1, source_target_pairs={{0,1},{1,0},{2,3},{3,2},{4,5},{5,4},{6,7},{7,6},{8,9},{9,8},{10,11... | collective-permute-start | bytes 184328 | tf_op jit(solution)/shard_map/ppermute | solution.py:511
  13.4 8.9 %collective-permute-start.8 = (bf16[96,640]{1,0:T(8,128)(2,1)S(1)}, bf16[96,640]{1,0:T(8,128)(2,1)S(1)}, u32[]{:S(2)}, u32[]{:S(2)}) collective-permute-start(bf16[96,640]{1,0:T(8,128)(2,1)S(1)} %get-tuple-element.48), channel_id=1, source_target_pairs={{0,1},{1,0},{2,3},{3,2},{4,5},{5,4},{6,7},{7,6},{8,9},{9,8},{10,11... | collective-permute-start | bytes 368648 | tf_op jit(solution)/shard_map/ppermute | solution.py:511
  15.1 3.4 %copy-start = (bf16[640,1216]{0,1:T(8,128)(2,1)S(1)}, bf16[640,1216]{0,1:T(8,128)(2,1)}, u32[]{:S(2)}) copy-start(bf16[640,1216]{0,1:T(8,128)(2,1)} %param.17) | copy-start | bytes 4669444
  15.1 3.4 %collective-permute-start.5 = (bf16[288,640]{1,0:T(8,128)(2,1)S(1)}, bf16[288,640]{1,0:T(8,128)(2,1)S(1)}, u32[]{:S(2)}, u32[]{:S(2)}) collective-permute-start(bf16[288,640]{1,0:T(8,128)(2,1)S(1)} %norm.1.refs_4_.got_ref.refs_6_), channel_id=1, source_target_pairs={{0,2},{2,0},{1,3},{3,1},{4,6},{6,4},{5,7},{7,5},{8,10},{10,8},{9,1... | collective-permute-start | bytes 1105928 | tf_op jit(solution)/shard_map/ppermute | solution.py:520
  19.6 5.5 %collective-permute-start.7 = (bf16[48,1280]{1,0:T(8,128)(2,1)S(1)}, bf16[48,1280]{1,0:T(8,128)(2,1)S(1)}, u32[]{:S(2)}, u32[]{:S(2)}) collective-permute-start(bf16[48,1280]{1,0:T(8,128)(2,1)S(1)} %get-tuple-element.47), channel_id=1, source_target_pairs={{0,1},{1,0},{2,3},{3,2},{4,5},{5,4},{6,7},{7,6},{8,9},{9,8},{10,11... | collective-permute-start | bytes 368648 | tf_op jit(solution)/shard_map/ppermute | solution.py:538
  20.5 7.0 %collective-permute-start.10 = (bf16[48,1152]{1,0:T(8,128)(2,1)S(1)}, bf16[48,1152]{1,0:T(8,128)(2,1)S(1)}, u32[]{:S(2)}, u32[]{:S(2)}) collective-permute-start(bf16[48,1152]{1,0:T(8,128)(2,1)S(1)} %rest.1), channel_id=1, source_target_pairs={{0,1},{1,0},{2,3},{3,2},{4,5},{5,4},{6,7},{7,6},{8,9},{9,8},{10,11... | collective-permute-start | bytes 331784 | tf_op jit(solution)/shard_map/ppermute | solution.py:547
  24.3 11.9 %collective-permute-start.9 = (bf16[96,2432]{1,0:T(8,128)(2,1)S(1)}, bf16[96,2432]{1,0:T(8,128)(2,1)S(1)}, u32[]{:S(2)}, u32[]{:S(2)}) collective-permute-start(bf16[96,2432]{1,0:T(8,128)(2,1)S(1)} %second.1), channel_id=1, source_target_pairs={{0,1},{1,0},{2,3},{3,2},{4,5},{5,4},{6,7},{7,6},{8,9},{9,8},{10,11... | collective-permute-start | bytes 1400840 | tf_op jit(solution)/shard_map/ppermute | solution.py:558
  25.1 2.4 %copy-start.3 = (f32[24,384]{1,0:T(8,128)S(1)}, f32[24,384]{1,0:T(8,128)}, u32[]{:S(2)}) copy-start(f32[24,384]{1,0:T(8,128)} %latent_ref.3) | copy-start | bytes 110596

commit v9 on v8

--- a/solution.py
+++ b/solution.py
@@ -285,7 +285,7 @@
 
 def early_kernel(*refs):
     q_ref, gains, hidden_ref, mod_ref, mine_ref, theirs_ref = refs[0], *refs[5:10]
-    sum_ref, total_ref, mixed_ref, gains_out, mod_out, finals_ref = refs[12:18]
+    sum_ref, total_ref, mixed_ref, gains_out, mod_out, finals_ref = refs[11:17]
     attend(q_ref[...], *keys_and_values(refs[1:5]), keep_sums(sum_ref, total_ref))
     gains_out[...] = gains[...]
     is_first = lax.axis_index("row") == 0
@@ -490,7 +490,7 @@
     weights = (weight_half, weight_theirs)
     k_row, v_row = (lax.ppermute(x, "row", SWAP) for x in (k_own, v_own))
     nearby = (k_own, v_own, k_row, v_row)
-    own_sum, own_total, mixed, gains, mods, finals, *q_raw = pl.pallas_call(
+    own_sum, own_total, mixed, gains, mods, finals, second_raw = pl.pallas_call(
         early_kernel,
         out_shape=(
             shape((tokens, width), jnp.float32),
@@ -499,16 +499,15 @@
             shape(gains.shape, jnp.float32),
             shape(modulation.shape, jnp.float32),
             shape((final_weight.shape[0], features)),
-            shape(first_raw.shape),
             shape(second_raw.shape),
         ),
-        in_specs=[VMEM] * 10 + [ANY] * 2,
-        out_specs=(VMEM,) * 6 + (ANY,) * 2,
-        input_output_aliases={10: 6, 11: 7},
+        in_specs=[VMEM] * 10 + [ANY],
+        out_specs=(VMEM,) * 6 + (ANY,),
+        input_output_aliases={10: 6},
         compiler_params=params(),
         name="early",
-    )(q_own, *nearby, gains, hidden, modulation, final_weight, final_got, first_raw, second_raw)
-    q_first, q_second = (lax.ppermute(raw, "col", SWAP) for raw in q_raw)
+    )(q_own, *nearby, gains, hidden, modulation, final_weight, final_got, second_raw)
+    q_first, q_second = (lax.ppermute(raw, "col", SWAP) for raw in (first_raw, second_raw))
     kv_got = pl.pallas_call(
         norm_kernel,
         out_shape=shape((2 * tokens, width)),

time: 38.1 us -> 37.7 us (0.990)
  waiting for transfers between devices: 12.6 us -> 11.3 us
  starting transfers between devices: 8.56 us -> 9.39 us
    ppermute x1, starting transfers between devices: 1.77 us -> 0.15 us  [on_device(): rest_got = lax.ppermute(rest, 'col', SWAP)]
    ppermute x1, starting transfers between devices: 0.34 us -> 1.95 us  [on_device(): first_got = lax.ppermute(first, 'col', SWAP)]
    ppermute x1, starting transfers between devices: 0.39 us -> 2 us  [on_device(): second_got = lax.ppermute(second, 'col', SWAP)]
    ppermute x2, waiting for transfers between devices: 2.44 us -> 0.94 us  [on_device(): lax.ppermute(raw, 'col', SWAP)]
    ppermute x1, waiting for transfers between devices: 0.01 us -> 1.33 us  [on_device(): lax.ppermute(kv_raw, 'col', SWAP)]
    ppermute x2, starting transfers between devices: 2.09 us -> 1.3 us  [on_device(): lax.ppermute(raw, 'col', SWAP)]
    ppermute x1, waiting for transfers between devices: 1.38 us -> 0.8 us  [on_device(): final_got = lax.ppermute(final_weight, 'row', SWAP)]
    ppermute x1, waiting for transfers between devices: 0.49 us -> 0.01 us  [on_device(): rest_got = lax.ppermute(rest, 'col', SWAP)]
  transfers between devices with their start and end apart: 11 -> 11, of which waited for: 5 -> 4; matrix products, arithmetic and copies ran while one was open for 0% -> 0% of each run, Pallas kernels for 29% -> 29%
where the time goes in v9:
time: 37.7 us; the launch traced here: 37.5 us
  Pallas kernels  12.7 us (34%)
  waiting for transfers between devices  11.3 us (30%)
  starting transfers between devices  9.39 us (25%)
  between operations  2.13 us (6%)
  local copies, waits for them, and re-layouts  1.99 us (5%)
    ppermute x1, waiting for transfers between devices, on_device(): second_got = lax.ppermute(second, 'col', SWAP)  8.26 us
    ppermute x1, starting transfers between devices, on_device(): lax.ppermute(kv_raw, 'col', SWAP)  2.61 us
    pallas_call x2, Pallas kernels, on_device(): pl.pallas_call(functools.partial(final_kernel, start), out_shape=(shape(l...  2.56 us
    pallas_call x1, Pallas kernels, on_device(): pl.pallas_call(second_kernel, out_shape=shape((tokens - cut, features)),...  2.08 us
    ppermute x1, starting transfers between devices, on_device(): second_got = lax.ppermute(second, 'col', SWAP)  2 us
    unnamed x18, local copies, waits for them, and re-layouts  1.99 us
    ppermute x1, starting transfers between devices, on_device(): first_got = lax.ppermute(first, 'col', SWAP)  1.95 us
    pallas_call x1, Pallas kernels, on_device(): pl.pallas_call(own_kernel, out_shape=shape(mixed.shape, jnp.float32), in_...  1.87 us
  transfers between devices with their start and end apart: 11, of which 4 were waited for; matrix products, arithmetic and copies ran while one was open for 0% of the time, Pallas kernels for 29%

profile of v9, /device:TPU:0, one launch (start us, length us, event | category | flops | bytes accessed | tf_op | source)
XLA Modules:
  0.0 37.5 jit_solution(6652416657473907287)
XLA Ops:
  0.6 0.0 copy-start.4
  0.6 0.5 %collective-permute-start = (bf16[1216,640]{1,0:T(8,128)(2,1)}, bf16[1216,640]{1,0:T(8,128)(2,1)S(1)}, u32[]{:S(2)}, u32[]{:S(2)}) collective-permute-start(bf16[1216,640]{1,0:T(8,128)(2,1)} %bitcast.5), channel_id=1, source_target_pairs={{0,2},{2,0},{1,3},{3,1},{4,6},{6,4},{5,7},{7,5},{8,10},{10,8},{9,1... | collective-permute-start | bytes 4669448 | tf_op jit(solution)/shard_map/ppermute | solution.py:472
  1.2 1.5 %split.1 = (bf16[288,640]{1,0:T(8,128)(2,1)S(1)}, bf16[48,640]{1,0:T(8,128)(2,1)S(1)}, bf16[96,640]{1,0:T(8,128)(2,1)S(1)}, bf16[144,3,640]{2,1,0:T(4,128)(2,1)S(1)}) custom-call(bf16[144,3,1280]{2,1,0:T(4,128)(2,1)} %bitcast.13), custom_call_target="tpu_custom_call" | custom-call | tf_op jit(solution)/shard_map/split/pallas_call | solution.py:458
  2.7 0.0 copy-start.2
  2.7 0.0 copy-start.1
  2.7 0.0 copy-start.5
  2.7 2.6 %collective-permute-start.1 = (bf16[288,640]{1,0:T(8,128)(2,1)S(1)}, bf16[288,640]{1,0:T(8,128)(2,1)S(1)}, u32[]{:S(2)}, u32[]{:S(2)}) collective-permute-start(bf16[288,640]{1,0:T(8,128)(2,1)S(1)} %get-tuple-element.30), channel_id=1, source_target_pairs={{0,1},{1,0},{2,3},{3,2},{4,5},{5,4},{6,7},{7,6},{8,9},{9,8},{10,11... | collective-permute-start | bytes 1105928 | tf_op jit(solution)/shard_map/ppermute | solution.py:518
  6.6 0.0 collective-permute-done._
  6.6 0.0 copy-done.4
  6.6 0.0 copy-start.6
  6.6 0.6 %copy-done.6 = f32[64]{0:T(128)S(1)} copy-done((f32[64]{0:T(128)S(1)}, f32[64]{0:T(128)}, u32[]{:S(2)}) %copy-start.6) | copy-done | bytes 280
  7.3 0.7 %copy-done.7 = f32[64]{0:T(128)S(1)} copy-done((f32[64]{0:T(128)S(1)}, f32[64]{0:T(128)}, u32[]{:S(2)}) %copy-start.7) | copy-done | bytes 280
  8.0 0.7 %copy-done.8 = f32[64]{0:T(128)S(1)} copy-done((f32[64]{0:T(128)S(1)}, f32[64]{0:T(128)}, u32[]{:S(2)}) %copy-start.8) | copy-done | bytes 280
  8.6 0.9 %prep_own.1 = (bf16[192,640]{1,0:T(8,128)(2,1)S(1)}, bf16[192,640]{1,0:T(8,128)(2,1)S(1)}, bf16[144,640]{1,0:T(8,128)(2,1)S(1)}, f32[3,64]{1,0:T(4,128)S(1)}, f3...) custom-call(s32[1]{0:T(128)S(6)} %copy.18.index_ref, s32[1]{0:T(128)S(6)} %copy.19.count_ref, ...), custom_call_target="tpu_custom_call", output_to_operand_aliasing={{5}: (7, {})} | custom-call | tf_op jit(solution)/shard_map/prep_own/pallas_call | solution.py:474
  9.5 0.3 collective-permute-start.2
  9.8 0.3 collective-permute-start.3
  10.1 0.0 copy-done.2
  10.1 0.2 collective-permute-start.4
  10.3 0.6 %collective-permute-start.6 = (bf16[48,640]{1,0:T(8,128)(2,1)S(1)}, bf16[48,640]{1,0:T(8,128)(2,1)S(1)}, u32[]{:S(2)}, u32[]{:S(2)}) collective-permute-start(bf16[48,640]{1,0:T(8,128)(2,1)S(1)} %get-tuple-element.41), channel_id=1, source_target_pairs={{0,1},{1,0},{2,3},{3,2},{4,5},{5,4},{6,7},{7,6},{8,9},{9,8},{10,11... | collective-permute-start | bytes 184328 | tf_op jit(solution)/shard_map/ppermute | solution.py:510
  10.9 0.8 %collective-permute-done.4.refs_9_ = bf16[64,1216]{1,0:T(8,128)(2,1)S(1)} collective-permute-done((bf16[64,1216]{1,0:T(8,128)(2,1)S(1)}, bf16[64,1216]{1,0:T(8,128)(2,1)S(1)}, u32[]{:S(2)}, u32[]{:S(2)}) %collective-permute-start.4) | collective-permute-done | bytes 155680 | tf_op jit(solution)/shard_map/ppermute | solution.py:473
  11.7 0.0 collective-permute-done.2.refs_3_.refs_2_.refs_4_
  11.7 0.0 collective-permute-done.3.refs_4_.refs_3_.refs_5_
  11.7 0.0 copy-done.1
  11.7 0.0 copy-done.5
  11.7 1.0 %early.1 = (f32[144,640]{1,0:T(8,128)S(1)}, f32[144,640]{1,0:T(8,128)S(1)}, f32[144,2432]{1,0:T(8,128)S(1)}, f32[3,64]{1,0:T(4,128)S(1)}, f32[3,2432]{1,0:T(4,12...) custom-call(bf16[144,640]{1,0:T(8,128)(2,1)S(1)} %get-tuple-element.29.refs_0_, ...), custom_call_target="tpu_custom_call", output_to_operand_aliasing={{6}: (10, {})} | custom-call | tf_op jit(solution)/shard_map/early/pallas_call | solution.py:493
  12.7 0.7 %collective-permute-start.8 = (bf16[96,640]{1,0:T(8,128)(2,1)S(1)}, bf16[96,640]{1,0:T(8,128)(2,1)S(1)}, u32[]{:S(2)}, u32[]{:S(2)}) collective-permute-start(bf16[96,640]{1,0:T(8,128)(2,1)S(1)} %get-tuple-element.46), channel_id=1, source_target_pairs={{0,1},{1,0},{2,3},{3,2},{4,5},{5,4},{6,7},{7,6},{8,9},{9,8},{10,11... | collective-permute-start | bytes 368648 | tf_op jit(solution)/shard_map/ppermute | solution.py:510
  13.4 1.3 %collective-permute-done.1.x_ref = bf16[288,640]{1,0:T(8,128)(2,1)S(1)} collective-permute-done((bf16[288,640]{1,0:T(8,128)(2,1)S(1)}, bf16[288,640]{1,0:T(8,128)(2,1)S(1)}, u32[]{:S(2)}, u32[]{:S(2)}) %collective-permute-start.1) | collective-permute-done | bytes 368672 | tf_op jit(solution)/shard_map/ppermute | solution.py:518
  14.8 0.3 norm.1.refs_4_.got_ref.refs_6_
  15.0 0.0 copy-start
  15.1 0.1 collective-permute-start.5
  15.1 0.9 %collective-permute-done.6.x_ref = bf16[48,640]{1,0:T(8,128)(2,1)S(1)} collective-permute-done((bf16[48,640]{1,0:T(8,128)(2,1)S(1)}, bf16[48,640]{1,0:T(8,128)(2,1)S(1)}, u32[]{:S(2)}, u32[]{:S(2)}) %collective-permute-start.6) | collective-permute-done | bytes 61472 | tf_op jit(solution)/shard_map/ppermute | solution.py:510
  16.1 0.9 %part.1 = (bf16[48,640]{1,0:T(8,128)(2,1)S(1)}, f32[48,640]{1,0:T(8,128)S(1)}, f32[48,640]{1,0:T(8,128)S(1)}) custom-call(bf16[48,640]{1,0:T(8,128)(2,1)S(1)} %collective-permute-done.6.x_ref, f32[3,64]{1,0:T(4,128)S(1)} %get-tuple-element.35.gains.refs_1_, bf16[192,640]{1,0:T(8,128)(2,1)S(1)} %get-tuple-element.31.refs_1_.refs_0_.refs_2_, ...), custom_call_target="tpu_custom_call" | custom-call | flops 4499999744 | bytes 13500000 | tf_op jit(solution)/shard_map/part/pallas_call | solution.py:520
  17.0 0.0 collective-permute-done.5.last_ref.refs_7_
  17.0 0.0 copy-done
  17.0 1.1 %first.1 = (bf16[48,1280]{1,0:T(8,128)(2,1)S(1)}, bf16[48,640]{1,0:T(8,128)(2,1)S(1)}) custom-call(bf16[48,640]{1,0:T(8,128)(2,1)S(1)} %get-tuple-element.42.q_ref, bf16[288,640]{1,0:T(8,128)(2,1)S(1)} %collective-permute-done.5.last_ref.refs_7_, f32[48,640]{1,0:T(8,128)S(1)} %get-tuple-element.43.sum_ref, f32[48,640]{1,0:T(8,128)S(1)} %get-tuple-element.44.total_ref, ...), custom_call_target="tpu_custom_call" | custom-call | tf_op jit(solution)/shard_map/first/pallas_call | solution.py:529
  18.1 2.0 %collective-permute-start.7 = (bf16[48,1280]{1,0:T(8,128)(2,1)S(1)}, bf16[48,1280]{1,0:T(8,128)(2,1)S(1)}, u32[]{:S(2)}, u32[]{:S(2)}) collective-permute-start(bf16[48,1280]{1,0:T(8,128)(2,1)S(1)} %get-tuple-element.45), channel_id=1, source_target_pairs={{0,1},{1,0},{2,3},{3,2},{4,5},{5,4},{6,7},{7,6},{8,9},{9,8},{10,11... | collective-permute-start | bytes 368648 | tf_op jit(solution)/shard_map/ppermute | solution.py:537
  20.0 0.5 %rest.1 = bf16[48,1152]{1,0:T(8,128)(2,1)S(1)} custom-call(bf16[48,640]{1,0:T(8,128)(2,1)S(1)} %get-tuple-element.47.attended_ref, bf16[1216,640]{1,0:T(8,128)(2,1)S(1)} %bitcast.7, bf16[1216,640]{1,0:T(8,128)(2,1)S(1)} %get-tuple-element.38.theirs_ref.refs_9_), custom_call_target="tpu_custom_call" | custom-call | tf_op jit(solution)/shard_map/rest/pallas_call | solution.py:538
  20.6 0.2 collective-permute-start.10
  20.7 0.0 collective-permute-done.8.refs_0_
  20.7 2.1 %second.1 = bf16[96,2432]{1,0:T(8,128)(2,1)S(1)} custom-call(bf16[96,640]{1,0:T(8,128)(2,1)S(1)} %collective-permute-done.8.refs_0_, f32[3,64]{1,0:T(4,128)S(1)} %get-tuple-element.35.gains.refs_1_, bf16[192,640]{1,0:T(8,128)(2,1)S(1)} %get-tuple-element.31.refs_1_.refs_0_.refs_2_, bf16[192,640]{1,0:T(8,128)(2,1)S(1)} %get-tuple-element.32.refs_2_.refs_1_.refs_3_, ...), custom_call_target="tpu_custom_call" | custom-call | tf_op jit(solution)/shard_map/second/pallas_call | solution.py:548
  22.8 2.0 %collective-permute-start.9 = (bf16[96,2432]{1,0:T(8,128)(2,1)S(1)}, bf16[96,2432]{1,0:T(8,128)(2,1)S(1)}, u32[]{:S(2)}, u32[]{:S(2)}) collective-permute-start(bf16[96,2432]{1,0:T(8,128)(2,1)S(1)} %second.1), channel_id=1, source_target_pairs={{0,1},{1,0},{2,3},{3,2},{4,5},{5,4},{6,7},{7,6},{8,9},{9,8},{10,11... | collective-permute-start | bytes 1400840 | tf_op jit(solution)/shard_map/ppermute | solution.py:557
  24.8 0.0 collective-permute-done.7.first_ref
  24.8 1.9 %own.1.mixed_ref = f32[144,2432]{1,0:T(8,128)S(1)} custom-call(bf16[144,640]{1,0:T(8,128)(2,1)S(1)} %get-tuple-element.29.refs_0_.q_ref, bf16[288,640]{1,0:T(8,128)(2,1)S(1)} %norm.1.refs_4_.got_ref.refs_6_, bf16[288,640]{1,0:T(8,128)(2,1)S(1)} %collective-permute-done.5.last_ref.refs_7_, f32[144,640]{1,0:T(8,128)S(1)} %get-tuple-element.36.sum_ref, ...), custom_call_target="tpu_custom_call" | custom-call | flops 60000002048 | bytes 180000000 | tf_op jit(solution)/shard_map/own/pallas_call | solution.py:558
  26.7 0.0 collective-permute-done.10.rest_ref
  26.7 0.0 copy-done.3
  26.7 0.9 %final.2 = (f32[24,384]{1,0:T(8,128)S(1)}, f32[24,384]{1,0:T(8,128)S(1)}) custom-call(f32[1,384]{1,0:T(1,128)S(1)} %get-tuple-element.28.euler_ref, f32[144,2432]{1,0:T(8,128)S(1)} %own.1.mixed_ref, bf16[48,1152]{1,0:T(8,128)(2,1)S(1)} %collective-permute-done.10.rest_ref, f32[3,2432]{1,0:T(4,128)S(1)} %get-tuple-element.40.mod_ref, ...), custom_call_target="tpu_custom_call" | custom-call | tf_op jit(solution)/shard_map/final/pallas_call | solution.py:570
  27.6 8.3 %collective-permute-done.9.rest_ref = bf16[96,2432]{1,0:T(8,128)(2,1)S(1)} collective-permute-done((bf16[96,2432]{1,0:T(8,128)(2,1)S(1)}, bf16[96,2432]{1,0:T(8,128)(2,1)S(1)}, u32[]{:S(2)}, u32[]{:S(2)}) %collective-permute-start.9) | collective-permute-done | bytes 466976 | tf_op jit(solution)/shard_map/ppermute | solution.py:557
  35.8 1.7 %final.3 = (f32[24,384]{1,0:T(8,128)}, f32[24,384]{1,0:T(8,128)}) custom-call(f32[1,384]{1,0:T(1,128)S(1)} %get-tuple-element.28.euler_ref, f32[144,2432]{1,0:T(8,128)S(1)} %own.1.mixed_ref, bf16[96,2432]{1,0:T(8,128)(2,1)S(1)} %collective-permute-done.9.rest_ref, f32[3,2432]{1,0:T(4,128)S(1)} %get-tuple-element.40.mod_ref, ...), custom_call_target="tpu_custom_call" | custom-call | tf_op jit(solution)/shard_map/final/pallas_call | solution.py:570
  (3 shorter events, 0.0 us)
Async XLA Ops:
  0.6 6.0 %copy-start.4 = (bf16[48,2,640]{2,1,0:T(2,128)(2,1)S(1)}, bf16[48,2,640]{2,1,0:T(2,128)(2,1)}, u32[]{:S(2)}) copy-start(bf16[48,2,640]{2,1,0:T(2,128)(2,1)} %text_ref.1) | copy-start | bytes 368644
  0.6 6.0 %collective-permute-start = (bf16[1216,640]{1,0:T(8,128)(2,1)}, bf16[1216,640]{1,0:T(8,128)(2,1)S(1)}, u32[]{:S(2)}, u32[]{:S(2)}) collective-permute-start(bf16[1216,640]{1,0:T(8,128)(2,1)} %bitcast.5), channel_id=1, source_target_pairs={{0,2},{2,0},{1,3},{3,1},{4,6},{6,4},{5,7},{7,5},{8,10},{10,8},{9,1... | collective-permute-start | bytes 4669448 | tf_op jit(solution)/shard_map/ppermute | solution.py:472
  2.7 7.4 %copy-start.2 = (bf16[64,1216]{1,0:T(8,128)(2,1)S(1)}, bf16[64,1216]{1,0:T(8,128)(2,1)}, u32[]{:S(2)}) copy-start(bf16[64,1216]{1,0:T(8,128)(2,1)} %refs_8_.1) | copy-start | bytes 466948
  2.7 9.0 %copy-start.1 = (bf16[12,12,2432]{2,1,0:T(8,128)(2,1)S(1)}, bf16[12,12,2432]{2,1,0:T(8,128)(2,1)}, u32[]{:S(2)}) copy-start(bf16[12,12,2432]{2,1,0:T(8,128)(2,1)} %refs_6_.1) | copy-start | bytes 2101252
  2.7 9.0 %copy-start.5 = (f32[3,2432]{1,0:T(4,128)S(1)}, f32[3,2432]{1,0:T(4,128)}, u32[]{:S(2)}) copy-start(f32[3,2432]{1,0:T(4,128)} %refs_7_.1) | copy-start | bytes 87556
  2.7 12.0 %collective-permute-start.1 = (bf16[288,640]{1,0:T(8,128)(2,1)S(1)}, bf16[288,640]{1,0:T(8,128)(2,1)S(1)}, u32[]{:S(2)}, u32[]{:S(2)}) collective-permute-start(bf16[288,640]{1,0:T(8,128)(2,1)S(1)} %get-tuple-element.30), channel_id=1, source_target_pairs={{0,1},{1,0},{2,3},{3,2},{4,5},{5,4},{6,7},{7,6},{8,9},{9,8},{10,11... | collective-permute-start | bytes 1105928 | tf_op jit(solution)/shard_map/ppermute | solution.py:518
  6.6 0.7 %copy-start.6 = (f32[64]{0:T(128)S(1)}, f32[64]{0:T(128)}, u32[]{:S(2)}) copy-start(f32[64]{0:T(128)} %param.14) | copy-start | bytes 772
  7.3 0.7 %copy-start.7 = (f32[64]{0:T(128)S(1)}, f32[64]{0:T(128)}, u32[]{:S(2)}) copy-start(f32[64]{0:T(128)} %param.15) | copy-start | bytes 772
  7.9 0.7 %copy-start.8 = (f32[64]{0:T(128)S(1)}, f32[64]{0:T(128)}, u32[]{:S(2)}) copy-start(f32[64]{0:T(128)} %param.16) | copy-start | bytes 772
  9.5 2.2 %collective-permute-start.2 = (bf16[192,640]{1,0:T(8,128)(2,1)S(1)}, bf16[192,640]{1,0:T(8,128)(2,1)S(1)}, u32[]{:S(2)}, u32[]{:S(2)}) collective-permute-start(bf16[192,640]{1,0:T(8,128)(2,1)S(1)} %get-tuple-element.31.refs_1_.refs_0_.refs_2_), channel_id=1, source_target_pairs={{0,2},{2,0},{1,3},{3,1},{4,6},{6,4},{5,7},{7,5},{8,10},{10,8},{9,1... | collective-permute-start | bytes 737288 | tf_op jit(solution)/shard_map/ppermute | solution.py:491
  9.8 1.9 %collective-permute-start.3 = (bf16[192,640]{1,0:T(8,128)(2,1)S(1)}, bf16[192,640]{1,0:T(8,128)(2,1)S(1)}, u32[]{:S(2)}, u32[]{:S(2)}) collective-permute-start(bf16[192,640]{1,0:T(8,128)(2,1)S(1)} %get-tuple-element.32.refs_2_.refs_1_.refs_3_), channel_id=1, source_target_pairs={{0,2},{2,0},{1,3},{3,1},{4,6},{6,4},{5,7},{7,5},{8,10},{10,8},{9,1... | collective-permute-start | bytes 737288 | tf_op jit(solution)/shard_map/ppermute | solution.py:491
  10.1 1.6 %collective-permute-start.4 = (bf16[64,1216]{1,0:T(8,128)(2,1)S(1)}, bf16[64,1216]{1,0:T(8,128)(2,1)S(1)}, u32[]{:S(2)}, u32[]{:S(2)}) collective-permute-start(bf16[64,1216]{1,0:T(8,128)(2,1)S(1)} %copy-done.2), channel_id=1, source_target_pairs={{0,2},{2,0},{1,3},{3,1},{4,6},{6,4},{5,7},{7,5},{8,10},{10,8},{9,1... | collective-permute-start | bytes 466952 | tf_op jit(solution)/shard_map/ppermute | solution.py:473
  10.3 5.8 %collective-permute-start.6 = (bf16[48,640]{1,0:T(8,128)(2,1)S(1)}, bf16[48,640]{1,0:T(8,128)(2,1)S(1)}, u32[]{:S(2)}, u32[]{:S(2)}) collective-permute-start(bf16[48,640]{1,0:T(8,128)(2,1)S(1)} %get-tuple-element.41), channel_id=1, source_target_pairs={{0,1},{1,0},{2,3},{3,2},{4,5},{5,4},{6,7},{7,6},{8,9},{9,8},{10,11... | collective-permute-start | bytes 184328 | tf_op jit(solution)/shard_map/ppermute | solution.py:510
  12.7 8.0 %collective-permute-start.8 = (bf16[96,640]{1,0:T(8,128)(2,1)S(1)}, bf16[96,640]{1,0:T(8,128)(2,1)S(1)}, u32[]{:S(2)}, u32[]{:S(2)}) collective-permute-start(bf16[96,640]{1,0:T(8,128)(2,1)S(1)} %get-tuple-element.46), channel_id=1, source_target_pairs={{0,1},{1,0},{2,3},{3,2},{4,5},{5,4},{6,7},{7,6},{8,9},{9,8},{10,11... | collective-permute-start | bytes 368648 | tf_op jit(solution)/shard_map/ppermute | solution.py:510
  15.0 1.9 %copy-start = (bf16[640,1216]{0,1:T(8,128)(2,1)S(1)}, bf16[640,1216]{0,1:T(8,128)(2,1)}, u32[]{:S(2)}) copy-start(bf16[640,1216]{0,1:T(8,128)(2,1)} %param.17) | copy-start | bytes 4669444
  15.1 1.9 %collective-permute-start.5 = (bf16[288,640]{1,0:T(8,128)(2,1)S(1)}, bf16[288,640]{1,0:T(8,128)(2,1)S(1)}, u32[]{:S(2)}, u32[]{:S(2)}) collective-permute-start(bf16[288,640]{1,0:T(8,128)(2,1)S(1)} %norm.1.refs_4_.got_ref.refs_6_), channel_id=1, source_target_pairs={{0,2},{2,0},{1,3},{3,1},{4,6},{6,4},{5,7},{7,5},{8,10},{10,8},{9,1... | collective-permute-start | bytes 1105928 | tf_op jit(solution)/shard_map/ppermute | solution.py:519
  18.1 6.7 %collective-permute-start.7 = (bf16[48,1280]{1,0:T(8,128)(2,1)S(1)}, bf16[48,1280]{1,0:T(8,128)(2,1)S(1)}, u32[]{:S(2)}, u32[]{:S(2)}) collective-permute-start(bf16[48,1280]{1,0:T(8,128)(2,1)S(1)} %get-tuple-element.45), channel_id=1, source_target_pairs={{0,1},{1,0},{2,3},{3,2},{4,5},{5,4},{6,7},{7,6},{8,9},{9,8},{10,11... | collective-permute-start | bytes 368648 | tf_op jit(solution)/shard_map/ppermute | solution.py:537
  20.6 6.1 %collective-permute-start.10 = (bf16[48,1152]{1,0:T(8,128)(2,1)S(1)}, bf16[48,1152]{1,0:T(8,128)(2,1)S(1)}, u32[]{:S(2)}, u32[]{:S(2)}) collective-permute-start(bf16[48,1152]{1,0:T(8,128)(2,1)S(1)} %rest.1), channel_id=1, source_target_pairs={{0,1},{1,0},{2,3},{3,2},{4,5},{5,4},{6,7},{7,6},{8,9},{9,8},{10,11... | collective-permute-start | bytes 331784 | tf_op jit(solution)/shard_map/ppermute | solution.py:546
  22.8 13.1 %collective-permute-start.9 = (bf16[96,2432]{1,0:T(8,128)(2,1)S(1)}, bf16[96,2432]{1,0:T(8,128)(2,1)S(1)}, u32[]{:S(2)}, u32[]{:S(2)}) collective-permute-start(bf16[96,2432]{1,0:T(8,128)(2,1)S(1)} %second.1), channel_id=1, source_target_pairs={{0,1},{1,0},{2,3},{3,2},{4,5},{5,4},{6,7},{7,6},{8,9},{9,8},{10,11... | collective-permute-start | bytes 1400840 | tf_op jit(solution)/shard_map/ppermute | solution.py:557
  24.8 1.9 %copy-start.3 = (f32[24,384]{1,0:T(8,128)S(1)}, f32[24,384]{1,0:T(8,128)}, u32[]{:S(2)}) copy-start(f32[24,384]{1,0:T(8,128)} %latent_ref.3) | copy-start | bytes 110596

commit v10 on v9

--- a/solution.py
+++ b/solution.py
@@ -331,37 +331,6 @@
     out_ref[:upto, :to] += mod_ref[2:3, :to] * first_ref[...].astype(jnp.float32)
 
 
-def one_hot(dims, condition):
-    row = lax.broadcasted_iota(jnp.int32, dims, 0)
-    col = lax.broadcasted_iota(jnp.int32, dims, 1)
-    return jnp.where(condition(row, col), 1.0, 0.0).astype(jnp.bfloat16)
-
-
-def to_pixels(velocity, tile_cols):
-    tokens, values = velocity.shape
-    side = values // PATCH
-    out_rows, out_lanes = tokens // tile_cols * PATCH, tile_cols * side
-    terms, rest = [], velocity
-    for _ in range(3):
-        term = rest.astype(jnp.bfloat16)
-        rest = rest - term.astype(jnp.float32)
-        terms.append(term)
-    terms = jnp.concatenate(terms, axis=0)
-    row = lax.broadcasted_iota(jnp.int32, (3 * tokens, out_lanes), 0)
-    col = lax.broadcasted_iota(jnp.int32, (3 * tokens, out_lanes), 1)
-    here = col // side == row % tile_cols
-    total = jnp.zeros((out_rows, out_lanes), jnp.float32)
-    for at in range(PATCH):
-        spread = one_hot((values, out_lanes), lambda r, c: r == c % side + at * side)
-        wide = jnp.dot(terms, spread, preferred_element_type=jnp.float32)
-        wide = jnp.where(here, wide, 0.0).astype(jnp.bfloat16)
-        pick = one_hot(
-            (out_rows, 3 * tokens), lambda r, c: r == c % tokens // tile_cols * PATCH + at
-        )
-        total += jnp.dot(pick, wide, preferred_element_type=jnp.float32)
-    return total
-
-
 def final_kernel(
     start,
     euler_ref,
@@ -372,7 +341,7 @@
     latent_ref,
     *refs,
 ):
-    velocity_ref, next_ref = refs[-2:]
+    velocity_ref, next_ref, values_ref, pixels_ref = refs[-4:]
     tokens = rest_ref.shape[0]
     step = 48
     parts = []
@@ -397,14 +366,26 @@
                 preferred_element_type=jnp.float32,
             )
         )
-    tile_cols = latent_ref.shape[1] // (final_ref.shape[0] // PATCH)
-    velocity = to_pixels(jnp.concatenate(parts, axis=0), tile_cols)
+    values = final_ref.shape[0]
+    values_ref[:tokens, :values] = jnp.concatenate(parts, axis=0)
+    side = values // PATCH
+    tile_cols = latent_ref.shape[1] // side
+    rows = tokens // tile_cols
+    columns = [values_ref[pl.ds(at, rows, stride=tile_cols), :] for at in range(tile_cols)]
+    for at in range(PATCH):
+        wide = jnp.concatenate([column[:, at * side : (at + 1) * side] for column in columns], axis=1)
+        for tile in range(pixels_ref.shape[0]):
+            lanes = slice(tile * LANES, (tile + 1) * LANES)
+            pixels_ref[tile, pl.ds(at, rows, stride=PATCH), :] = wide[:, lanes]
     first = start // tile_cols * PATCH
-    pixels = slice(first, first + velocity.shape[0])
-    for before_ref, after_ref in zip(refs[:-2], refs[-2:]):
+    pixels = slice(first, first + rows * PATCH)
+    for before_ref, after_ref in zip(refs[:-4], refs[-4:-2]):
         after_ref[:first] = before_ref[:first]
-    velocity_ref[pixels] = velocity
-    next_ref[pixels] = latent_ref[pixels] + euler_ref[...] * velocity
+    for tile in range(pixels_ref.shape[0]):
+        lanes = slice(tile * LANES, (tile + 1) * LANES)
+        velocity = pixels_ref[tile, : rows * PATCH]
+        velocity_ref[pixels, lanes] = velocity
+        next_ref[pixels, lanes] = latent_ref[pixels, lanes] + euler_ref[:, lanes] * velocity
 
 
 def params(limit=VMEM_LIMIT):
@@ -565,6 +546,7 @@
         cost_estimate=lasting(60),
         name="own",
     )(q_own, kv_got, kv_last, own_sum, own_total, *weights, mixed, mods, first_got)
+    room = -(-tile_rows // 8) * 8 + 8
     results = ()
     for (start, _), got in ((chunks[0], rest_got), (chunks[1], second_got)):
         results = pl.pallas_call(
@@ -572,6 +554,10 @@
             out_shape=(shape(latent.shape, jnp.float32),) * 2,
             in_specs=[VMEM] * (6 + len(results)),
             out_specs=(VMEM, VMEM),
+            scratch_shapes=[
+                pltpu.VMEM((room * tile_cols, LANES), jnp.float32),
+                pltpu.VMEM((latent.shape[1] // LANES, room * PATCH, LANES), jnp.float32),
+            ],
             compiler_params=params(),
             name="final",
         )(euler, mixed, got, mods, finals, latent, *results)

time: 37.7 us -> 37.4 us (level)
  Pallas kernels: 12.7 us -> 12 us
  waiting for transfers between devices: 11.3 us -> 11.7 us
    pallas_call x2, Pallas kernels: 2.56 us -> 1.91 us  [on_device(): pl.pallas_call(functools.partial(final_kernel, start), out_shape=(shape(l...]
where the time goes in v10:
time: 37.4 us; the launch traced here: 37.2 us
  Pallas kernels  12 us (32%)
  waiting for transfers between devices  11.7 us (31%)
  starting transfers between devices  9.39 us (25%)
  between operations  2.14 us (6%)
  local copies, waits for them, and re-layouts  1.99 us (5%)
    ppermute x1, waiting for transfers between devices, on_device(): second_got = lax.ppermute(second, 'col', SWAP)  8.58 us
    ppermute x1, starting transfers between devices, on_device(): lax.ppermute(kv_raw, 'col', SWAP)  2.61 us
    pallas_call x1, Pallas kernels, on_device(): pl.pallas_call(second_kernel, out_shape=shape((tokens - cut, features)),...  2.08 us
    ppermute x1, starting transfers between devices, on_device(): second_got = lax.ppermute(second, 'col', SWAP)  2 us
    unnamed x18, local copies, waits for them, and re-layouts  1.99 us
    ppermute x1, starting transfers between devices, on_device(): first_got = lax.ppermute(first, 'col', SWAP)  1.95 us
    pallas_call x2, Pallas kernels, on_device(): pl.pallas_call(functools.partial(final_kernel, start), out_shape=(shape(l...  1.91 us
    pallas_call x1, Pallas kernels, on_device(): pl.pallas_call(own_kernel, out_shape=shape(mixed.shape, jnp.float32), in_...  1.87 us
  transfers between devices with their start and end apart: 11, of which 4 were waited for; matrix products, arithmetic and copies ran while one was open for 0% of the time, Pallas kernels for 29%

profile of v10, /device:TPU:0, one launch (start us, length us, event | category | flops | bytes accessed | tf_op | source)
XLA Modules:
  0.0 37.2 jit_solution(16090889739400092674)
XLA Ops:
  0.6 0.0 copy-start.4
  0.6 0.5 %collective-permute-start = (bf16[1216,640]{1,0:T(8,128)(2,1)}, bf16[1216,640]{1,0:T(8,128)(2,1)S(1)}, u32[]{:S(2)}, u32[]{:S(2)}) collective-permute-start(bf16[1216,640]{1,0:T(8,128)(2,1)} %bitcast.5), channel_id=1, source_target_pairs={{0,2},{2,0},{1,3},{3,1},{4,6},{6,4},{5,7},{7,5},{8,10},{10,8},{9,1... | collective-permute-start | bytes 4669448 | tf_op jit(solution)/shard_map/ppermute | solution.py:453
  1.2 1.5 %split.1 = (bf16[288,640]{1,0:T(8,128)(2,1)S(1)}, bf16[48,640]{1,0:T(8,128)(2,1)S(1)}, bf16[96,640]{1,0:T(8,128)(2,1)S(1)}, bf16[144,3,640]{2,1,0:T(4,128)(2,1)S(1)}) custom-call(bf16[144,3,1280]{2,1,0:T(4,128)(2,1)} %bitcast.13), custom_call_target="tpu_custom_call" | custom-call | tf_op jit(solution)/shard_map/split/pallas_call | solution.py:439
  2.7 0.0 copy-start.2
  2.7 0.0 copy-start.1
  2.7 0.0 copy-start.5
  2.7 2.6 %collective-permute-start.1 = (bf16[288,640]{1,0:T(8,128)(2,1)S(1)}, bf16[288,640]{1,0:T(8,128)(2,1)S(1)}, u32[]{:S(2)}, u32[]{:S(2)}) collective-permute-start(bf16[288,640]{1,0:T(8,128)(2,1)S(1)} %get-tuple-element.30), channel_id=1, source_target_pairs={{0,1},{1,0},{2,3},{3,2},{4,5},{5,4},{6,7},{7,6},{8,9},{9,8},{10,11... | collective-permute-start | bytes 1105928 | tf_op jit(solution)/shard_map/ppermute | solution.py:499
  6.6 0.0 collective-permute-done._
  6.6 0.0 copy-done.4
  6.6 0.0 copy-start.6
  6.6 0.6 %copy-done.6 = f32[64]{0:T(128)S(1)} copy-done((f32[64]{0:T(128)S(1)}, f32[64]{0:T(128)}, u32[]{:S(2)}) %copy-start.6) | copy-done | bytes 280
  7.3 0.7 %copy-done.7 = f32[64]{0:T(128)S(1)} copy-done((f32[64]{0:T(128)S(1)}, f32[64]{0:T(128)}, u32[]{:S(2)}) %copy-start.7) | copy-done | bytes 280
  8.0 0.7 %copy-done.8 = f32[64]{0:T(128)S(1)} copy-done((f32[64]{0:T(128)S(1)}, f32[64]{0:T(128)}, u32[]{:S(2)}) %copy-start.8) | copy-done | bytes 280
  8.6 0.9 %prep_own.1 = (bf16[192,640]{1,0:T(8,128)(2,1)S(1)}, bf16[192,640]{1,0:T(8,128)(2,1)S(1)}, bf16[144,640]{1,0:T(8,128)(2,1)S(1)}, f32[3,64]{1,0:T(4,128)S(1)}, f3...) custom-call(s32[1]{0:T(128)S(6)} %copy.18.index_ref, s32[1]{0:T(128)S(6)} %copy.19.count_ref, ...), custom_call_target="tpu_custom_call", output_to_operand_aliasing={{5}: (7, {})} | custom-call | tf_op jit(solution)/shard_map/prep_own/pallas_call | solution.py:455
  9.5 0.3 collective-permute-start.2
  9.8 0.3 collective-permute-start.3
  10.1 0.0 copy-done.2
  10.1 0.2 collective-permute-start.4
  10.3 0.6 %collective-permute-start.6 = (bf16[48,640]{1,0:T(8,128)(2,1)S(1)}, bf16[48,640]{1,0:T(8,128)(2,1)S(1)}, u32[]{:S(2)}, u32[]{:S(2)}) collective-permute-start(bf16[48,640]{1,0:T(8,128)(2,1)S(1)} %get-tuple-element.41), channel_id=1, source_target_pairs={{0,1},{1,0},{2,3},{3,2},{4,5},{5,4},{6,7},{7,6},{8,9},{9,8},{10,11... | collective-permute-start | bytes 184328 | tf_op jit(solution)/shard_map/ppermute | solution.py:491
  10.9 0.8 %collective-permute-done.4.refs_9_ = bf16[64,1216]{1,0:T(8,128)(2,1)S(1)} collective-permute-done((bf16[64,1216]{1,0:T(8,128)(2,1)S(1)}, bf16[64,1216]{1,0:T(8,128)(2,1)S(1)}, u32[]{:S(2)}, u32[]{:S(2)}) %collective-permute-start.4) | collective-permute-done | bytes 155680 | tf_op jit(solution)/shard_map/ppermute | solution.py:454
  11.7 0.0 collective-permute-done.2.refs_3_.refs_2_.refs_4_
  11.7 0.0 collective-permute-done.3.refs_4_.refs_3_.refs_5_
  11.7 0.0 copy-done.1
  11.7 0.0 copy-done.5
  11.7 1.0 %early.1 = (f32[144,640]{1,0:T(8,128)S(1)}, f32[144,640]{1,0:T(8,128)S(1)}, f32[144,2432]{1,0:T(8,128)S(1)}, f32[3,64]{1,0:T(4,128)S(1)}, f32[3,2432]{1,0:T(4,12...) custom-call(bf16[144,640]{1,0:T(8,128)(2,1)S(1)} %get-tuple-element.29.refs_0_, ...), custom_call_target="tpu_custom_call", output_to_operand_aliasing={{6}: (10, {})} | custom-call | tf_op jit(solution)/shard_map/early/pallas_call | solution.py:474
  12.7 0.7 %collective-permute-start.8 = (bf16[96,640]{1,0:T(8,128)(2,1)S(1)}, bf16[96,640]{1,0:T(8,128)(2,1)S(1)}, u32[]{:S(2)}, u32[]{:S(2)}) collective-permute-start(bf16[96,640]{1,0:T(8,128)(2,1)S(1)} %get-tuple-element.46), channel_id=1, source_target_pairs={{0,1},{1,0},{2,3},{3,2},{4,5},{5,4},{6,7},{7,6},{8,9},{9,8},{10,11... | collective-permute-start | bytes 368648 | tf_op jit(solution)/shard_map/ppermute | solution.py:491
  13.4 1.3 %collective-permute-done.1.x_ref = bf16[288,640]{1,0:T(8,128)(2,1)S(1)} collective-permute-done((bf16[288,640]{1,0:T(8,128)(2,1)S(1)}, bf16[288,640]{1,0:T(8,128)(2,1)S(1)}, u32[]{:S(2)}, u32[]{:S(2)}) %collective-permute-start.1) | collective-permute-done | bytes 368672 | tf_op jit(solution)/shard_map/ppermute | solution.py:499
  14.8 0.3 norm.1.refs_4_.got_ref.refs_6_
  15.0 0.0 copy-start
  15.1 0.1 collective-permute-start.5
  15.1 0.9 %collective-permute-done.6.x_ref = bf16[48,640]{1,0:T(8,128)(2,1)S(1)} collective-permute-done((bf16[48,640]{1,0:T(8,128)(2,1)S(1)}, bf16[48,640]{1,0:T(8,128)(2,1)S(1)}, u32[]{:S(2)}, u32[]{:S(2)}) %collective-permute-start.6) | collective-permute-done | bytes 61472 | tf_op jit(solution)/shard_map/ppermute | solution.py:491
  16.1 0.9 %part.1 = (bf16[48,640]{1,0:T(8,128)(2,1)S(1)}, f32[48,640]{1,0:T(8,128)S(1)}, f32[48,640]{1,0:T(8,128)S(1)}) custom-call(bf16[48,640]{1,0:T(8,128)(2,1)S(1)} %collective-permute-done.6.x_ref, f32[3,64]{1,0:T(4,128)S(1)} %get-tuple-element.35.gains.refs_1_, bf16[192,640]{1,0:T(8,128)(2,1)S(1)} %get-tuple-element.31.refs_1_.refs_0_.refs_2_, ...), custom_call_target="tpu_custom_call" | custom-call | flops 4499999744 | bytes 13500000 | tf_op jit(solution)/shard_map/part/pallas_call | solution.py:501
  17.0 0.0 collective-permute-done.5.last_ref.refs_7_
  17.0 0.0 copy-done
  17.0 1.1 %first.1 = (bf16[48,1280]{1,0:T(8,128)(2,1)S(1)}, bf16[48,640]{1,0:T(8,128)(2,1)S(1)}) custom-call(bf16[48,640]{1,0:T(8,128)(2,1)S(1)} %get-tuple-element.42.q_ref, bf16[288,640]{1,0:T(8,128)(2,1)S(1)} %collective-permute-done.5.last_ref.refs_7_, f32[48,640]{1,0:T(8,128)S(1)} %get-tuple-element.43.sum_ref, f32[48,640]{1,0:T(8,128)S(1)} %get-tuple-element.44.total_ref, ...), custom_call_target="tpu_custom_call" | custom-call | tf_op jit(solution)/shard_map/first/pallas_call | solution.py:510
  18.1 2.0 %collective-permute-start.7 = (bf16[48,1280]{1,0:T(8,128)(2,1)S(1)}, bf16[48,1280]{1,0:T(8,128)(2,1)S(1)}, u32[]{:S(2)}, u32[]{:S(2)}) collective-permute-start(bf16[48,1280]{1,0:T(8,128)(2,1)S(1)} %get-tuple-element.45), channel_id=1, source_target_pairs={{0,1},{1,0},{2,3},{3,2},{4,5},{5,4},{6,7},{7,6},{8,9},{9,8},{10,11... | collective-permute-start | bytes 368648 | tf_op jit(solution)/shard_map/ppermute | solution.py:518
  20.0 0.5 %rest.1 = bf16[48,1152]{1,0:T(8,128)(2,1)S(1)} custom-call(bf16[48,640]{1,0:T(8,128)(2,1)S(1)} %get-tuple-element.47.attended_ref, bf16[1216,640]{1,0:T(8,128)(2,1)S(1)} %bitcast.7, bf16[1216,640]{1,0:T(8,128)(2,1)S(1)} %get-tuple-element.38.theirs_ref.refs_9_), custom_call_target="tpu_custom_call" | custom-call | tf_op jit(solution)/shard_map/rest/pallas_call | solution.py:519
  20.6 0.2 collective-permute-start.10
  20.7 0.0 collective-permute-done.8.refs_0_
  20.7 2.1 %second.1 = bf16[96,2432]{1,0:T(8,128)(2,1)S(1)} custom-call(bf16[96,640]{1,0:T(8,128)(2,1)S(1)} %collective-permute-done.8.refs_0_, f32[3,64]{1,0:T(4,128)S(1)} %get-tuple-element.35.gains.refs_1_, bf16[192,640]{1,0:T(8,128)(2,1)S(1)} %get-tuple-element.31.refs_1_.refs_0_.refs_2_, bf16[192,640]{1,0:T(8,128)(2,1)S(1)} %get-tuple-element.32.refs_2_.refs_1_.refs_3_, ...), custom_call_target="tpu_custom_call" | custom-call | tf_op jit(solution)/shard_map/second/pallas_call | solution.py:529
  22.8 2.0 %collective-permute-start.9 = (bf16[96,2432]{1,0:T(8,128)(2,1)S(1)}, bf16[96,2432]{1,0:T(8,128)(2,1)S(1)}, u32[]{:S(2)}, u32[]{:S(2)}) collective-permute-start(bf16[96,2432]{1,0:T(8,128)(2,1)S(1)} %second.1), channel_id=1, source_target_pairs={{0,1},{1,0},{2,3},{3,2},{4,5},{5,4},{6,7},{7,6},{8,9},{9,8},{10,11... | collective-permute-start | bytes 1400840 | tf_op jit(solution)/shard_map/ppermute | solution.py:538
  24.8 0.0 collective-permute-done.7.first_ref
  24.8 1.9 %own.1.mixed_ref = f32[144,2432]{1,0:T(8,128)S(1)} custom-call(bf16[144,640]{1,0:T(8,128)(2,1)S(1)} %get-tuple-element.29.refs_0_.q_ref, bf16[288,640]{1,0:T(8,128)(2,1)S(1)} %norm.1.refs_4_.got_ref.refs_6_, bf16[288,640]{1,0:T(8,128)(2,1)S(1)} %collective-permute-done.5.last_ref.refs_7_, f32[144,640]{1,0:T(8,128)S(1)} %get-tuple-element.36.sum_ref, ...), custom_call_target="tpu_custom_call" | custom-call | flops 60000002048 | bytes 180000000 | tf_op jit(solution)/shard_map/own/pallas_call | solution.py:539
  26.7 0.0 collective-permute-done.10.rest_ref
  26.7 0.0 copy-done.3
  26.7 0.6 %final.2 = (f32[24,384]{1,0:T(8,128)S(1)}, f32[24,384]{1,0:T(8,128)S(1)}) custom-call(f32[1,384]{1,0:T(1,128)S(1)} %get-tuple-element.28.euler_ref, f32[144,2432]{1,0:T(8,128)S(1)} %own.1.mixed_ref, bf16[48,1152]{1,0:T(8,128)(2,1)S(1)} %collective-permute-done.10.rest_ref, f32[3,2432]{1,0:T(4,128)S(1)} %get-tuple-element.40.mod_ref, ...), custom_call_target="tpu_custom_call" | custom-call | tf_op jit(solution)/shard_map/final/pallas_call | solution.py:552
  27.3 8.6 %collective-permute-done.9.rest_ref = bf16[96,2432]{1,0:T(8,128)(2,1)S(1)} collective-permute-done((bf16[96,2432]{1,0:T(8,128)(2,1)S(1)}, bf16[96,2432]{1,0:T(8,128)(2,1)S(1)}, u32[]{:S(2)}, u32[]{:S(2)}) %collective-permute-start.9) | collective-permute-done | bytes 466976 | tf_op jit(solution)/shard_map/ppermute | solution.py:538
  35.8 1.3 %final.3 = (f32[24,384]{1,0:T(8,128)}, f32[24,384]{1,0:T(8,128)}) custom-call(f32[1,384]{1,0:T(1,128)S(1)} %get-tuple-element.28.euler_ref, f32[144,2432]{1,0:T(8,128)S(1)} %own.1.mixed_ref, bf16[96,2432]{1,0:T(8,128)(2,1)S(1)} %collective-permute-done.9.rest_ref, f32[3,2432]{1,0:T(4,128)S(1)} %get-tuple-element.40.mod_ref, ...), custom_call_target="tpu_custom_call" | custom-call | tf_op jit(solution)/shard_map/final/pallas_call | solution.py:552
  (3 shorter events, 0.0 us)
Async XLA Ops:
  0.6 6.0 %copy-start.4 = (bf16[48,2,640]{2,1,0:T(2,128)(2,1)S(1)}, bf16[48,2,640]{2,1,0:T(2,128)(2,1)}, u32[]{:S(2)}) copy-start(bf16[48,2,640]{2,1,0:T(2,128)(2,1)} %text_ref.1) | copy-start | bytes 368644
  0.6 6.0 %collective-permute-start = (bf16[1216,640]{1,0:T(8,128)(2,1)}, bf16[1216,640]{1,0:T(8,128)(2,1)S(1)}, u32[]{:S(2)}, u32[]{:S(2)}) collective-permute-start(bf16[1216,640]{1,0:T(8,128)(2,1)} %bitcast.5), channel_id=1, source_target_pairs={{0,2},{2,0},{1,3},{3,1},{4,6},{6,4},{5,7},{7,5},{8,10},{10,8},{9,1... | collective-permute-start | bytes 4669448 | tf_op jit(solution)/shard_map/ppermute | solution.py:453
  2.7 7.4 %copy-start.2 = (bf16[64,1216]{1,0:T(8,128)(2,1)S(1)}, bf16[64,1216]{1,0:T(8,128)(2,1)}, u32[]{:S(2)}) copy-start(bf16[64,1216]{1,0:T(8,128)(2,1)} %refs_8_.1) | copy-start | bytes 466948
  2.7 9.0 %copy-start.1 = (bf16[12,12,2432]{2,1,0:T(8,128)(2,1)S(1)}, bf16[12,12,2432]{2,1,0:T(8,128)(2,1)}, u32[]{:S(2)}) copy-start(bf16[12,12,2432]{2,1,0:T(8,128)(2,1)} %refs_6_.1) | copy-start | bytes 2101252
  2.7 9.0 %copy-start.5 = (f32[3,2432]{1,0:T(4,128)S(1)}, f32[3,2432]{1,0:T(4,128)}, u32[]{:S(2)}) copy-start(f32[3,2432]{1,0:T(4,128)} %refs_7_.1) | copy-start | bytes 87556
  2.7 12.0 %collective-permute-start.1 = (bf16[288,640]{1,0:T(8,128)(2,1)S(1)}, bf16[288,640]{1,0:T(8,128)(2,1)S(1)}, u32[]{:S(2)}, u32[]{:S(2)}) collective-permute-start(bf16[288,640]{1,0:T(8,128)(2,1)S(1)} %get-tuple-element.30), channel_id=1, source_target_pairs={{0,1},{1,0},{2,3},{3,2},{4,5},{5,4},{6,7},{7,6},{8,9},{9,8},{10,11... | collective-permute-start | bytes 1105928 | tf_op jit(solution)/shard_map/ppermute | solution.py:499
  6.6 0.7 %copy-start.6 = (f32[64]{0:T(128)S(1)}, f32[64]{0:T(128)}, u32[]{:S(2)}) copy-start(f32[64]{0:T(128)} %param.14) | copy-start | bytes 772
  7.3 0.7 %copy-start.7 = (f32[64]{0:T(128)S(1)}, f32[64]{0:T(128)}, u32[]{:S(2)}) copy-start(f32[64]{0:T(128)} %param.15) | copy-start | bytes 772
  7.9 0.7 %copy-start.8 = (f32[64]{0:T(128)S(1)}, f32[64]{0:T(128)}, u32[]{:S(2)}) copy-start(f32[64]{0:T(128)} %param.16) | copy-start | bytes 772
  9.5 2.2 %collective-permute-start.2 = (bf16[192,640]{1,0:T(8,128)(2,1)S(1)}, bf16[192,640]{1,0:T(8,128)(2,1)S(1)}, u32[]{:S(2)}, u32[]{:S(2)}) collective-permute-start(bf16[192,640]{1,0:T(8,128)(2,1)S(1)} %get-tuple-element.31.refs_1_.refs_0_.refs_2_), channel_id=1, source_target_pairs={{0,2},{2,0},{1,3},{3,1},{4,6},{6,4},{5,7},{7,5},{8,10},{10,8},{9,1... | collective-permute-start | bytes 737288 | tf_op jit(solution)/shard_map/ppermute | solution.py:472
  9.8 1.9 %collective-permute-start.3 = (bf16[192,640]{1,0:T(8,128)(2,1)S(1)}, bf16[192,640]{1,0:T(8,128)(2,1)S(1)}, u32[]{:S(2)}, u32[]{:S(2)}) collective-permute-start(bf16[192,640]{1,0:T(8,128)(2,1)S(1)} %get-tuple-element.32.refs_2_.refs_1_.refs_3_), channel_id=1, source_target_pairs={{0,2},{2,0},{1,3},{3,1},{4,6},{6,4},{5,7},{7,5},{8,10},{10,8},{9,1... | collective-permute-start | bytes 737288 | tf_op jit(solution)/shard_map/ppermute | solution.py:472
  10.1 1.6 %collective-permute-start.4 = (bf16[64,1216]{1,0:T(8,128)(2,1)S(1)}, bf16[64,1216]{1,0:T(8,128)(2,1)S(1)}, u32[]{:S(2)}, u32[]{:S(2)}) collective-permute-start(bf16[64,1216]{1,0:T(8,128)(2,1)S(1)} %copy-done.2), channel_id=1, source_target_pairs={{0,2},{2,0},{1,3},{3,1},{4,6},{6,4},{5,7},{7,5},{8,10},{10,8},{9,1... | collective-permute-start | bytes 466952 | tf_op jit(solution)/shard_map/ppermute | solution.py:454
  10.3 5.8 %collective-permute-start.6 = (bf16[48,640]{1,0:T(8,128)(2,1)S(1)}, bf16[48,640]{1,0:T(8,128)(2,1)S(1)}, u32[]{:S(2)}, u32[]{:S(2)}) collective-permute-start(bf16[48,640]{1,0:T(8,128)(2,1)S(1)} %get-tuple-element.41), channel_id=1, source_target_pairs={{0,1},{1,0},{2,3},{3,2},{4,5},{5,4},{6,7},{7,6},{8,9},{9,8},{10,11... | collective-permute-start | bytes 184328 | tf_op jit(solution)/shard_map/ppermute | solution.py:491
  12.7 8.0 %collective-permute-start.8 = (bf16[96,640]{1,0:T(8,128)(2,1)S(1)}, bf16[96,640]{1,0:T(8,128)(2,1)S(1)}, u32[]{:S(2)}, u32[]{:S(2)}) collective-permute-start(bf16[96,640]{1,0:T(8,128)(2,1)S(1)} %get-tuple-element.46), channel_id=1, source_target_pairs={{0,1},{1,0},{2,3},{3,2},{4,5},{5,4},{6,7},{7,6},{8,9},{9,8},{10,11... | collective-permute-start | bytes 368648 | tf_op jit(solution)/shard_map/ppermute | solution.py:491
  15.0 1.9 %copy-start = (bf16[640,1216]{0,1:T(8,128)(2,1)S(1)}, bf16[640,1216]{0,1:T(8,128)(2,1)}, u32[]{:S(2)}) copy-start(bf16[640,1216]{0,1:T(8,128)(2,1)} %param.17) | copy-start | bytes 4669444
  15.1 1.9 %collective-permute-start.5 = (bf16[288,640]{1,0:T(8,128)(2,1)S(1)}, bf16[288,640]{1,0:T(8,128)(2,1)S(1)}, u32[]{:S(2)}, u32[]{:S(2)}) collective-permute-start(bf16[288,640]{1,0:T(8,128)(2,1)S(1)} %norm.1.refs_4_.got_ref.refs_6_), channel_id=1, source_target_pairs={{0,2},{2,0},{1,3},{3,1},{4,6},{6,4},{5,7},{7,5},{8,10},{10,8},{9,1... | collective-permute-start | bytes 1105928 | tf_op jit(solution)/shard_map/ppermute | solution.py:500
  18.1 6.7 %collective-permute-start.7 = (bf16[48,1280]{1,0:T(8,128)(2,1)S(1)}, bf16[48,1280]{1,0:T(8,128)(2,1)S(1)}, u32[]{:S(2)}, u32[]{:S(2)}) collective-permute-start(bf16[48,1280]{1,0:T(8,128)(2,1)S(1)} %get-tuple-element.45), channel_id=1, source_target_pairs={{0,1},{1,0},{2,3},{3,2},{4,5},{5,4},{6,7},{7,6},{8,9},{9,8},{10,11... | collective-permute-start | bytes 368648 | tf_op jit(solution)/shard_map/ppermute | solution.py:518
  20.6 6.1 %collective-permute-start.10 = (bf16[48,1152]{1,0:T(8,128)(2,1)S(1)}, bf16[48,1152]{1,0:T(8,128)(2,1)S(1)}, u32[]{:S(2)}, u32[]{:S(2)}) collective-permute-start(bf16[48,1152]{1,0:T(8,128)(2,1)S(1)} %rest.1), channel_id=1, source_target_pairs={{0,1},{1,0},{2,3},{3,2},{4,5},{5,4},{6,7},{7,6},{8,9},{9,8},{10,11... | collective-permute-start | bytes 331784 | tf_op jit(solution)/shard_map/ppermute | solution.py:527
  22.8 13.1 %collective-permute-start.9 = (bf16[96,2432]{1,0:T(8,128)(2,1)S(1)}, bf16[96,2432]{1,0:T(8,128)(2,1)S(1)}, u32[]{:S(2)}, u32[]{:S(2)}) collective-permute-start(bf16[96,2432]{1,0:T(8,128)(2,1)S(1)} %second.1), channel_id=1, source_target_pairs={{0,1},{1,0},{2,3},{3,2},{4,5},{5,4},{6,7},{7,6},{8,9},{9,8},{10,11... | collective-permute-start | bytes 1400840 | tf_op jit(solution)/shard_map/ppermute | solution.py:538
  24.8 1.9 %copy-start.3 = (f32[24,384]{1,0:T(8,128)S(1)}, f32[24,384]{1,0:T(8,128)}, u32[]{:S(2)}) copy-start(f32[24,384]{1,0:T(8,128)} %latent_ref.3) | copy-start | bytes 110596

commit v11 on v10

--- a/solution.py
+++ b/solution.py
@@ -16,7 +16,8 @@
 LANES = 128
 EPS = 1e-06
 VMEM_LIMIT = 16 * 1024 * 1024
-VMEM_MOST = 52 * 1024 * 1024
+VMEM_MOST = 53 * 1024 * 1024
+VMEM_OWN = 52 * 1024 * 1024
 LOADS = 3
 FIRST = 1280
 STEP = 640
@@ -88,14 +89,10 @@
     kv_ref,
     q_first_ref,
     q_second_ref,
-    own_ref,
     held,
     sems,
-    own_sems,
 ):
-    column = lax.axis_index("col")
-    blocks = load_half(x_ref, held, sems, 1 - column)
-    own_blocks = load_half(x_ref, own_ref, own_sems, column)
+    blocks = load_half(x_ref, held, sems, 1 - lax.axis_index("col"))
     k_ref, v_ref = halves(kv_ref)
     cut = q_first_ref.shape[0]
     for rows, copy in blocks:
@@ -107,8 +104,6 @@
             q_first_ref[rows] = q
         else:
             q_second_ref[rows.start - cut : rows.stop - cut] = q
-    for _, copy in own_blocks:
-        copy.wait()
 
 
 def q_norm(x_ref, gains):
@@ -133,26 +128,26 @@
     count_ref,
     x_ref,
     text_ref,
-    gain_q_ref,
-    gain_k_ref,
-    gain_t_ref,
-    _,
+    gains_in,
     k_ref,
     v_ref,
     q_ref,
     gains,
     euler_ref,
-    __,
+    held,
+    sems,
 ):
+    blocks = load_half(x_ref, held, sems, lax.axis_index("col"))
     tokens, width = q_ref.shape
-    for at, ref in enumerate((gain_q_ref, gain_k_ref, gain_t_ref)):
-        gains[at : at + 1] = ref[...]
+    gains[...] = gains_in[...]
     now = jnp.full(euler_ref.shape, index_ref[0], jnp.int32)
     then = now + jnp.full(euler_ref.shape, count_ref[0], jnp.int32)
     euler_ref[...] = noise_level(then) - noise_level(now)
     text = text_ref[...].astype(jnp.float32).transpose(1, 0, 2)
     v_ref[tokens:] = text[1].astype(jnp.bfloat16)
-    q, k, v = x_ref[...].transpose(1, 0, 2)
+    for _, copy in blocks:
+        copy.wait()
+    q, k, v = held[...].transpose(1, 0, 2)
     v_ref[:tokens] = v
     k_ref[:tokens], k_ref[tokens:], q_ref[...] = head_norms(
         [
@@ -427,7 +422,7 @@
     words = text_kv.shape[0]
     width = all_width // lax.axis_size("col")
     features = hidden.shape[2]
-    gains = [gain.reshape(1, HEAD) for gain in (gain_query, gain_key, gain_text)]
+    gains = jnp.stack([gain_query, gain_key, gain_text])
     x = image_qkv.reshape(tokens, 3, all_width)
     weight_half = out_weight.T
     held = pltpu.VMEM((tokens, 3, width), jnp.bfloat16)
@@ -436,39 +431,37 @@
     loads = pltpu.SemaphoreType.DMA((LOADS,))
     cut = tile_rows // 3 * tile_cols
     chunks = ((0, cut), (cut, tokens))
-    kv_raw, first_raw, second_raw, own_raw = pl.pallas_call(
+    kv_raw, first_raw, second_raw = pl.pallas_call(
         split_kernel,
         out_shape=(
             shape((2 * tokens, width)),
             shape((cut, width)),
             shape((tokens - cut, width)),
-            shape((tokens, 3, width)),
         ),
         in_specs=[HBM],
-        out_specs=(VMEM,) * 4,
-        scratch_shapes=[held, loads, loads],
+        out_specs=(VMEM,) * 3,
+        scratch_shapes=[held, loads],
         compiler_params=params(VMEM_MOST),
         name="split",
     )(x)
     weight_got = lax.ppermute(weight_half, "row", SWAP)
     final_got = lax.ppermute(final_weight, "row", SWAP)
-    k_own, v_own, q_own, gains, euler, weight_theirs = pl.pallas_call(
+    k_own, v_own, q_own, gains, euler = pl.pallas_call(
         prep_own_kernel,
         out_shape=(
             shape((tokens + words, width)),
             shape((tokens + words, width)),
             block,
-            shape((len(gains), HEAD), jnp.float32),
+            shape(gains.shape, jnp.float32),
             shape((1, latent.shape[1]), jnp.float32),
-            shape(weight_got.shape),
         ),
-        in_specs=[SMEM] * 2 + [VMEM] * 5 + [ANY],
-        out_specs=(VMEM,) * 5 + (ANY,),
-        input_output_aliases={7: 5},
-        compiler_params=params(),
+        in_specs=[SMEM] * 2 + [HBM] + [VMEM] * 2,
+        out_specs=(VMEM,) * 5,
+        scratch_shapes=[held, loads],
+        compiler_params=params(VMEM_OWN),
         name="prep_own",
-    )(step_index, step_count, own_raw, text_kv, *gains, weight_got)
-    weights = (weight_half, weight_theirs)
+    )(step_index, step_count, x, text_kv, gains)
+    weights = (weight_half, weight_got)
     k_row, v_row = (lax.ppermute(x, "row", SWAP) for x in (k_own, v_own))
     nearby = (k_own, v_own, k_row, v_row)
     own_sum, own_total, mixed, gains, mods, finals, second_raw = pl.pallas_call(

time: 37.4 us -> 37.3 us (level)
  local copies, waits for them, and re-layouts: 1.99 us -> 0.04 us
  Pallas kernels: 12 us -> 13 us
  starting transfers between devices: 9.39 us -> 10.2 us
    unnamed x18, local copies, waits for them, and re-layouts: 1.99 us -> 0.04 us
    pallas_call x1, Pallas kernels: 0.89 us -> 2.05 us  [on_device(): pl.pallas_call(prep_own_kernel, out_shape=(shape((tokens + words, width))...]
    ppermute x2, starting transfers between devices: 1.3 us -> 2.09 us  [on_device(): lax.ppermute(raw, 'col', SWAP)]
    ppermute x1, waiting for transfers between devices: 0.8 us -> 1.4 us  [on_device(): final_got = lax.ppermute(final_weight, 'row', SWAP)]
    ppermute x1, waiting for transfers between devices: 1.33 us -> 0.73 us  [on_device(): lax.ppermute(kv_raw, 'col', SWAP)]
  transfers between devices with their start and end apart: 11 -> 11, of which waited for: 4 -> 4; matrix products, arithmetic and copies ran while one was open for 0% -> 0% of each run, Pallas kernels for 29% -> 31%
where the time goes in v11:
time: 37.3 us; the launch traced here: 37.1 us
  Pallas kernels  13 us (35%)
  waiting for transfers between devices  11.6 us (31%)
  starting transfers between devices  10.2 us (27%)
  between operations  2.17 us (6%)
    ppermute x1, waiting for transfers between devices, on_device(): second_got = lax.ppermute(second, 'col', SWAP)  8.56 us
    ppermute x1, starting transfers between devices, on_device(): lax.ppermute(kv_raw, 'col', SWAP)  2.63 us
    ppermute x2, starting transfers between devices, on_device(): lax.ppermute(raw, 'col', SWAP)  2.09 us
    pallas_call x1, Pallas kernels, on_device(): pl.pallas_call(second_kernel, out_shape=shape((tokens - cut, features)),...  2.07 us
    pallas_call x1, Pallas kernels, on_device(): pl.pallas_call(prep_own_kernel, out_shape=(shape((tokens + words, width))...  2.05 us
    ppermute x1, starting transfers between devices, on_device(): second_got = lax.ppermute(second, 'col', SWAP)  2.03 us
    ppermute x1, starting transfers between devices, on_device(): first_got = lax.ppermute(first, 'col', SWAP)  1.97 us
    pallas_call x2, Pallas kernels, on_device(): pl.pallas_call(functools.partial(final_kernel, start), out_shape=(shape(l...  1.93 us
  transfers between devices with their start and end apart: 11, of which 4 were waited for; matrix products, arithmetic and copies ran while one was open for 0% of the time, Pallas kernels for 31%

profile of v11, /device:TPU:0, one launch (start us, length us, event | category | flops | bytes accessed | tf_op | source)
XLA Modules:
  0.0 37.1 jit_solution(16696528177860629772)
XLA Ops:
  0.6 0.0 copy-start.6
  0.6 0.0 copy-start.7
  0.7 0.0 copy-start.8
  0.7 0.0 copy-start.4
  0.7 0.5 %collective-permute-start.5 = (bf16[1216,640]{1,0:T(8,128)(2,1)}, bf16[1216,640]{1,0:T(8,128)(2,1)S(1)}, u32[]{:S(2)}, u32[]{:S(2)}) collective-permute-start(bf16[1216,640]{1,0:T(8,128)(2,1)} %bitcast.5), channel_id=1, source_target_pairs={{0,2},{2,0},{1,3},{3,1},{4,6},{6,4},{5,7},{7,5},{8,10},{10,8},{9,1... | collective-permute-start | bytes 4669448 | tf_op jit(solution)/shard_map/ppermute | solution.py:447
  1.2 0.0 copy-start.2
  1.2 1.3 %split.1 = (bf16[288,640]{1,0:T(8,128)(2,1)S(1)}, bf16[48,640]{1,0:T(8,128)(2,1)S(1)}, bf16[96,640]{1,0:T(8,128)(2,1)S(1)}) custom-call(bf16[144,3,1280]{2,1,0:T(4,128)(2,1)} %bitcast.10), custom_call_target="tpu_custom_call" | custom-call | tf_op jit(solution)/shard_map/split/pallas_call | solution.py:434
  2.5 2.6 %collective-permute-start = (bf16[288,640]{1,0:T(8,128)(2,1)S(1)}, bf16[288,640]{1,0:T(8,128)(2,1)S(1)}, u32[]{:S(2)}, u32[]{:S(2)}) collective-permute-start(bf16[288,640]{1,0:T(8,128)(2,1)S(1)} %get-tuple-element.27), channel_id=1, source_target_pairs={{0,1},{1,0},{2,3},{3,2},{4,5},{5,4},{6,7},{7,6},{8,9},{9,8},{10,11... | collective-permute-start | bytes 1105928 | tf_op jit(solution)/shard_map/ppermute | solution.py:492
  6.5 0.0 copy-done.6
  6.5 0.0 copy-done.7
  6.5 0.0 copy-done.8
  6.5 0.0 copy-done.4
  6.5 2.0 %prep_own.1 = (bf16[192,640]{1,0:T(8,128)(2,1)S(1)}, bf16[192,640]{1,0:T(8,128)(2,1)S(1)}, bf16[144,640]{1,0:T(8,128)(2,1)S(1)}, f32[3,64]{1,0:T(4,128)S(1)}, f32[1,384]{1,0:T(1,128)S(1)}) custom-call(s32[1]{0:T(128)S(6)} %copy.16.index_ref, s32[1]{0:T(128)S(6)} %copy.17.count_ref, bf16[144,3,1280]{2,1,0:T(4,128)(2,1)} %bitcast.11, ...), custom_call_target="tpu_custom_call" | custom-call | tf_op jit(solution)/shard_map/prep_own/pallas_call | solution.py:449
  8.6 0.2 collective-permute-start.1
  8.8 0.3 collective-permute-start.2
  9.2 0.0 copy-done.2
  9.2 0.2 collective-permute-start.3
  9.3 1.4 %collective-permute-done.3.refs_9_ = bf16[64,1216]{1,0:T(8,128)(2,1)S(1)} collective-permute-done((bf16[64,1216]{1,0:T(8,128)(2,1)S(1)}, bf16[64,1216]{1,0:T(8,128)(2,1)S(1)}, u32[]{:S(2)}, u32[]{:S(2)}) %collective-permute-start.3) | collective-permute-done | bytes 155680 | tf_op jit(solution)/shard_map/ppermute | solution.py:448
  10.7 0.1 collective-permute-start.6
  10.9 0.0 collective-permute-done.1.refs_3_.refs_2_.refs_4_
  10.9 0.0 collective-permute-done.2.refs_4_.refs_3_.refs_5_
  10.9 0.0 copy-done.1
  10.9 0.0 copy-done.5
  10.9 1.0 %early.1 = (f32[144,640]{1,0:T(8,128)S(1)}, f32[144,640]{1,0:T(8,128)S(1)}, f32[144,2432]{1,0:T(8,128)S(1)}, f32[3,64]{1,0:T(4,128)S(1)}, f32[3,2432]{1,0:T(4,12...) custom-call(bf16[144,640]{1,0:T(8,128)(2,1)S(1)} %get-tuple-element.26.refs_0_, ...), custom_call_target="tpu_custom_call", output_to_operand_aliasing={{6}: (10, {})} | custom-call | tf_op jit(solution)/shard_map/early/pallas_call | solution.py:467
  11.9 2.0 %collective-permute-start.8 = (bf16[96,640]{1,0:T(8,128)(2,1)S(1)}, bf16[96,640]{1,0:T(8,128)(2,1)S(1)}, u32[]{:S(2)}, u32[]{:S(2)}) collective-permute-start(bf16[96,640]{1,0:T(8,128)(2,1)S(1)} %get-tuple-element.42), channel_id=1, source_target_pairs={{0,1},{1,0},{2,3},{3,2},{4,5},{5,4},{6,7},{7,6},{8,9},{9,8},{10,11... | collective-permute-start | bytes 368648 | tf_op jit(solution)/shard_map/ppermute | solution.py:484
  13.9 0.7 %collective-permute-done.x_ref = bf16[288,640]{1,0:T(8,128)(2,1)S(1)} collective-permute-done((bf16[288,640]{1,0:T(8,128)(2,1)S(1)}, bf16[288,640]{1,0:T(8,128)(2,1)S(1)}, u32[]{:S(2)}, u32[]{:S(2)}) %collective-permute-start) | collective-permute-done | bytes 368672 | tf_op jit(solution)/shard_map/ppermute | solution.py:492
  14.6 0.3 norm.1.refs_4_.got_ref.refs_6_
  14.9 0.0 copy-start
  14.9 0.1 collective-permute-start.4
  15.0 0.9 %collective-permute-done.6.x_ref = bf16[48,640]{1,0:T(8,128)(2,1)S(1)} collective-permute-done((bf16[48,640]{1,0:T(8,128)(2,1)S(1)}, bf16[48,640]{1,0:T(8,128)(2,1)S(1)}, u32[]{:S(2)}, u32[]{:S(2)}) %collective-permute-start.6) | collective-permute-done | bytes 61472 | tf_op jit(solution)/shard_map/ppermute | solution.py:484
  15.9 0.9 %part.1 = (bf16[48,640]{1,0:T(8,128)(2,1)S(1)}, f32[48,640]{1,0:T(8,128)S(1)}, f32[48,640]{1,0:T(8,128)S(1)}) custom-call(bf16[48,640]{1,0:T(8,128)(2,1)S(1)} %collective-permute-done.6.x_ref, f32[3,64]{1,0:T(4,128)S(1)} %get-tuple-element.32.gains.refs_1_, bf16[192,640]{1,0:T(8,128)(2,1)S(1)} %get-tuple-element.28.refs_1_.refs_0_.refs_2_, ...), custom_call_target="tpu_custom_call" | custom-call | flops 4499999744 | bytes 13500000 | tf_op jit(solution)/shard_map/part/pallas_call | solution.py:494
  16.8 0.0 collective-permute-done.4.last_ref.refs_7_
  16.8 0.0 collective-permute-done.5.theirs_ref.refs_9_
  16.8 0.0 copy-done
  16.8 1.1 %first.1 = (bf16[48,1280]{1,0:T(8,128)(2,1)S(1)}, bf16[48,640]{1,0:T(8,128)(2,1)S(1)}) custom-call(bf16[48,640]{1,0:T(8,128)(2,1)S(1)} %get-tuple-element.38.q_ref, bf16[288,640]{1,0:T(8,128)(2,1)S(1)} %collective-permute-done.4.last_ref.refs_7_, f32[48,640]{1,0:T(8,128)S(1)} %get-tuple-element.39.sum_ref, f32[48,640]{1,0:T(8,128)S(1)} %get-tuple-element.40.total_ref, ...), custom_call_target="tpu_custom_call" | custom-call | tf_op jit(solution)/shard_map/first/pallas_call | solution.py:503
  17.9 2.0 %collective-permute-start.7 = (bf16[48,1280]{1,0:T(8,128)(2,1)S(1)}, bf16[48,1280]{1,0:T(8,128)(2,1)S(1)}, u32[]{:S(2)}, u32[]{:S(2)}) collective-permute-start(bf16[48,1280]{1,0:T(8,128)(2,1)S(1)} %get-tuple-element.41), channel_id=1, source_target_pairs={{0,1},{1,0},{2,3},{3,2},{4,5},{5,4},{6,7},{7,6},{8,9},{9,8},{10,11... | collective-permute-start | bytes 368648 | tf_op jit(solution)/shard_map/ppermute | solution.py:511
  19.9 0.5 %rest.1 = bf16[48,1152]{1,0:T(8,128)(2,1)S(1)} custom-call(bf16[48,640]{1,0:T(8,128)(2,1)S(1)} %get-tuple-element.43.attended_ref, bf16[1216,640]{1,0:T(8,128)(2,1)S(1)} %bitcast.7, bf16[1216,640]{1,0:T(8,128)(2,1)S(1)} %collective-permute-done.5.theirs_ref.refs_9_), custom_call_target="tpu_custom_call" | custom-call | tf_op jit(solution)/shard_map/rest/pallas_call | solution.py:512
  20.4 0.1 collective-permute-start.10
  20.6 0.0 collective-permute-done.8.refs_0_
  20.6 2.1 %second.1 = bf16[96,2432]{1,0:T(8,128)(2,1)S(1)} custom-call(bf16[96,640]{1,0:T(8,128)(2,1)S(1)} %collective-permute-done.8.refs_0_, f32[3,64]{1,0:T(4,128)S(1)} %get-tuple-element.32.gains.refs_1_, bf16[192,640]{1,0:T(8,128)(2,1)S(1)} %get-tuple-element.28.refs_1_.refs_0_.refs_2_, bf16[192,640]{1,0:T(8,128)(2,1)S(1)} %get-tuple-element.29.refs_2_.refs_1_.refs_3_, ...), custom_call_target="tpu_custom_call" | custom-call | tf_op jit(solution)/shard_map/second/pallas_call | solution.py:522
  22.7 2.0 %collective-permute-start.9 = (bf16[96,2432]{1,0:T(8,128)(2,1)S(1)}, bf16[96,2432]{1,0:T(8,128)(2,1)S(1)}, u32[]{:S(2)}, u32[]{:S(2)}) collective-permute-start(bf16[96,2432]{1,0:T(8,128)(2,1)S(1)} %second.1), channel_id=1, source_target_pairs={{0,1},{1,0},{2,3},{3,2},{4,5},{5,4},{6,7},{7,6},{8,9},{9,8},{10,11... | collective-permute-start | bytes 1400840 | tf_op jit(solution)/shard_map/ppermute | solution.py:531
  24.7 0.0 collective-permute-done.7.first_ref
  24.7 1.9 %own.1.mixed_ref = f32[144,2432]{1,0:T(8,128)S(1)} custom-call(bf16[144,640]{1,0:T(8,128)(2,1)S(1)} %get-tuple-element.26.refs_0_.q_ref, bf16[288,640]{1,0:T(8,128)(2,1)S(1)} %norm.1.refs_4_.got_ref.refs_6_, bf16[288,640]{1,0:T(8,128)(2,1)S(1)} %collective-permute-done.4.last_ref.refs_7_, f32[144,640]{1,0:T(8,128)S(1)} %get-tuple-element.33.sum_ref, ...), custom_call_target="tpu_custom_call" | custom-call | flops 60000002048 | bytes 180000000 | tf_op jit(solution)/shard_map/own/pallas_call | solution.py:532
  26.6 0.0 collective-permute-done.10.rest_ref
  26.6 0.0 copy-done.3
  26.6 0.6 %final.2 = (f32[24,384]{1,0:T(8,128)S(1)}, f32[24,384]{1,0:T(8,128)S(1)}) custom-call(f32[1,384]{1,0:T(1,128)S(1)} %get-tuple-element.25.euler_ref, f32[144,2432]{1,0:T(8,128)S(1)} %own.1.mixed_ref, bf16[48,1152]{1,0:T(8,128)(2,1)S(1)} %collective-permute-done.10.rest_ref, f32[3,2432]{1,0:T(4,128)S(1)} %get-tuple-element.36.mod_ref, ...), custom_call_target="tpu_custom_call" | custom-call | tf_op jit(solution)/shard_map/final/pallas_call | solution.py:545
  27.2 8.6 %collective-permute-done.9.rest_ref = bf16[96,2432]{1,0:T(8,128)(2,1)S(1)} collective-permute-done((bf16[96,2432]{1,0:T(8,128)(2,1)S(1)}, bf16[96,2432]{1,0:T(8,128)(2,1)S(1)}, u32[]{:S(2)}, u32[]{:S(2)}) %collective-permute-start.9) | collective-permute-done | bytes 466976 | tf_op jit(solution)/shard_map/ppermute | solution.py:531
  35.7 1.4 %final.3 = (f32[24,384]{1,0:T(8,128)}, f32[24,384]{1,0:T(8,128)}) custom-call(f32[1,384]{1,0:T(1,128)S(1)} %get-tuple-element.25.euler_ref, f32[144,2432]{1,0:T(8,128)S(1)} %own.1.mixed_ref, bf16[96,2432]{1,0:T(8,128)(2,1)S(1)} %collective-permute-done.9.rest_ref, f32[3,2432]{1,0:T(4,128)S(1)} %get-tuple-element.36.mod_ref, ...), custom_call_target="tpu_custom_call" | custom-call | tf_op jit(solution)/shard_map/final/pallas_call | solution.py:545
  (4 shorter events, 0.0 us)
Async XLA Ops:
  0.6 5.8 %copy-start.6 = (f32[64]{0:T(128)S(1)}, f32[64]{0:T(128)}, u32[]{:S(2)}) copy-start(f32[64]{0:T(128)} %param.16) | copy-start | bytes 772
  0.6 5.8 %copy-start.7 = (f32[64]{0:T(128)S(1)}, f32[64]{0:T(128)}, u32[]{:S(2)}) copy-start(f32[64]{0:T(128)} %param.15) | copy-start | bytes 772
  0.7 5.8 %copy-start.8 = (f32[64]{0:T(128)S(1)}, f32[64]{0:T(128)}, u32[]{:S(2)}) copy-start(f32[64]{0:T(128)} %param.14) | copy-start | bytes 772
  0.7 5.9 %copy-start.4 = (bf16[48,2,640]{2,1,0:T(2,128)(2,1)S(1)}, bf16[48,2,640]{2,1,0:T(2,128)(2,1)}, u32[]{:S(2)}) copy-start(bf16[48,2,640]{2,1,0:T(2,128)(2,1)} %text_ref.1) | copy-start | bytes 368644
  0.7 16.2 %collective-permute-start.5 = (bf16[1216,640]{1,0:T(8,128)(2,1)}, bf16[1216,640]{1,0:T(8,128)(2,1)S(1)}, u32[]{:S(2)}, u32[]{:S(2)}) collective-permute-start(bf16[1216,640]{1,0:T(8,128)(2,1)} %bitcast.5), channel_id=1, source_target_pairs={{0,2},{2,0},{1,3},{3,1},{4,6},{6,4},{5,7},{7,5},{8,10},{10,8},{9,1... | collective-permute-start | bytes 4669448 | tf_op jit(solution)/shard_map/ppermute | solution.py:447
  1.2 8.0 %copy-start.2 = (bf16[64,1216]{1,0:T(8,128)(2,1)S(1)}, bf16[64,1216]{1,0:T(8,128)(2,1)}, u32[]{:S(2)}) copy-start(bf16[64,1216]{1,0:T(8,128)(2,1)} %refs_8_.1) | copy-start | bytes 466948
  1.2 9.7 %copy-start.1 = (bf16[12,12,2432]{2,1,0:T(8,128)(2,1)S(1)}, bf16[12,12,2432]{2,1,0:T(8,128)(2,1)}, u32[]{:S(2)}) copy-start(bf16[12,12,2432]{2,1,0:T(8,128)(2,1)} %refs_6_.1) | copy-start | bytes 2101252
  1.2 9.7 %copy-start.5 = (f32[3,2432]{1,0:T(4,128)S(1)}, f32[3,2432]{1,0:T(4,128)}, u32[]{:S(2)}) copy-start(f32[3,2432]{1,0:T(4,128)} %refs_7_.1) | copy-start | bytes 87556
  2.5 12.1 %collective-permute-start = (bf16[288,640]{1,0:T(8,128)(2,1)S(1)}, bf16[288,640]{1,0:T(8,128)(2,1)S(1)}, u32[]{:S(2)}, u32[]{:S(2)}) collective-permute-start(bf16[288,640]{1,0:T(8,128)(2,1)S(1)} %get-tuple-element.27), channel_id=1, source_target_pairs={{0,1},{1,0},{2,3},{3,2},{4,5},{5,4},{6,7},{7,6},{8,9},{9,8},{10,11... | collective-permute-start | bytes 1105928 | tf_op jit(solution)/shard_map/ppermute | solution.py:492
  8.6 2.3 %collective-permute-start.1 = (bf16[192,640]{1,0:T(8,128)(2,1)S(1)}, bf16[192,640]{1,0:T(8,128)(2,1)S(1)}, u32[]{:S(2)}, u32[]{:S(2)}) collective-permute-start(bf16[192,640]{1,0:T(8,128)(2,1)S(1)} %get-tuple-element.28.refs_1_.refs_0_.refs_2_), channel_id=1, source_target_pairs={{0,2},{2,0},{1,3},{3,1},{4,6},{6,4},{5,7},{7,5},{8,10},{10,8},{9,1... | collective-permute-start | bytes 737288 | tf_op jit(solution)/shard_map/ppermute | solution.py:465
  8.8 2.0 %collective-permute-start.2 = (bf16[192,640]{1,0:T(8,128)(2,1)S(1)}, bf16[192,640]{1,0:T(8,128)(2,1)S(1)}, u32[]{:S(2)}, u32[]{:S(2)}) collective-permute-start(bf16[192,640]{1,0:T(8,128)(2,1)S(1)} %get-tuple-element.29.refs_2_.refs_1_.refs_3_), channel_id=1, source_target_pairs={{0,2},{2,0},{1,3},{3,1},{4,6},{6,4},{5,7},{7,5},{8,10},{10,8},{9,1... | collective-permute-start | bytes 737288 | tf_op jit(solution)/shard_map/ppermute | solution.py:465
  9.2 1.6 %collective-permute-start.3 = (bf16[64,1216]{1,0:T(8,128)(2,1)S(1)}, bf16[64,1216]{1,0:T(8,128)(2,1)S(1)}, u32[]{:S(2)}, u32[]{:S(2)}) collective-permute-start(bf16[64,1216]{1,0:T(8,128)(2,1)S(1)} %copy-done.2), channel_id=1, source_target_pairs={{0,2},{2,0},{1,3},{3,1},{4,6},{6,4},{5,7},{7,5},{8,10},{10,8},{9,1... | collective-permute-start | bytes 466952 | tf_op jit(solution)/shard_map/ppermute | solution.py:448
  10.7 5.2 %collective-permute-start.6 = (bf16[48,640]{1,0:T(8,128)(2,1)S(1)}, bf16[48,640]{1,0:T(8,128)(2,1)S(1)}, u32[]{:S(2)}, u32[]{:S(2)}) collective-permute-start(bf16[48,640]{1,0:T(8,128)(2,1)S(1)} %get-tuple-element.37), channel_id=1, source_target_pairs={{0,1},{1,0},{2,3},{3,2},{4,5},{5,4},{6,7},{7,6},{8,9},{9,8},{10,11... | collective-permute-start | bytes 184328 | tf_op jit(solution)/shard_map/ppermute | solution.py:484
  11.9 8.7 %collective-permute-start.8 = (bf16[96,640]{1,0:T(8,128)(2,1)S(1)}, bf16[96,640]{1,0:T(8,128)(2,1)S(1)}, u32[]{:S(2)}, u32[]{:S(2)}) collective-permute-start(bf16[96,640]{1,0:T(8,128)(2,1)S(1)} %get-tuple-element.42), channel_id=1, source_target_pairs={{0,1},{1,0},{2,3},{3,2},{4,5},{5,4},{6,7},{7,6},{8,9},{9,8},{10,11... | collective-permute-start | bytes 368648 | tf_op jit(solution)/shard_map/ppermute | solution.py:484
  14.9 1.9 %copy-start = (bf16[640,1216]{0,1:T(8,128)(2,1)S(1)}, bf16[640,1216]{0,1:T(8,128)(2,1)}, u32[]{:S(2)}) copy-start(bf16[640,1216]{0,1:T(8,128)(2,1)} %param.17) | copy-start | bytes 4669444
  14.9 1.9 %collective-permute-start.4 = (bf16[288,640]{1,0:T(8,128)(2,1)S(1)}, bf16[288,640]{1,0:T(8,128)(2,1)S(1)}, u32[]{:S(2)}, u32[]{:S(2)}) collective-permute-start(bf16[288,640]{1,0:T(8,128)(2,1)S(1)} %norm.1.refs_4_.got_ref.refs_6_), channel_id=1, source_target_pairs={{0,2},{2,0},{1,3},{3,1},{4,6},{6,4},{5,7},{7,5},{8,10},{10,8},{9,1... | collective-permute-start | bytes 1105928 | tf_op jit(solution)/shard_map/ppermute | solution.py:493
  17.9 6.8 %collective-permute-start.7 = (bf16[48,1280]{1,0:T(8,128)(2,1)S(1)}, bf16[48,1280]{1,0:T(8,128)(2,1)S(1)}, u32[]{:S(2)}, u32[]{:S(2)}) collective-permute-start(bf16[48,1280]{1,0:T(8,128)(2,1)S(1)} %get-tuple-element.41), channel_id=1, source_target_pairs={{0,1},{1,0},{2,3},{3,2},{4,5},{5,4},{6,7},{7,6},{8,9},{9,8},{10,11... | collective-permute-start | bytes 368648 | tf_op jit(solution)/shard_map/ppermute | solution.py:511
  20.4 6.1 %collective-permute-start.10 = (bf16[48,1152]{1,0:T(8,128)(2,1)S(1)}, bf16[48,1152]{1,0:T(8,128)(2,1)S(1)}, u32[]{:S(2)}, u32[]{:S(2)}) collective-permute-start(bf16[48,1152]{1,0:T(8,128)(2,1)S(1)} %rest.1), channel_id=1, source_target_pairs={{0,1},{1,0},{2,3},{3,2},{4,5},{5,4},{6,7},{7,6},{8,9},{9,8},{10,11... | collective-permute-start | bytes 331784 | tf_op jit(solution)/shard_map/ppermute | solution.py:520
  22.7 13.1 %collective-permute-start.9 = (bf16[96,2432]{1,0:T(8,128)(2,1)S(1)}, bf16[96,2432]{1,0:T(8,128)(2,1)S(1)}, u32[]{:S(2)}, u32[]{:S(2)}) collective-permute-start(bf16[96,2432]{1,0:T(8,128)(2,1)S(1)} %second.1), channel_id=1, source_target_pairs={{0,1},{1,0},{2,3},{3,2},{4,5},{5,4},{6,7},{7,6},{8,9},{9,8},{10,11... | collective-permute-start | bytes 1400840 | tf_op jit(solution)/shard_map/ppermute | solution.py:531
  24.7 1.9 %copy-start.3 = (f32[24,384]{1,0:T(8,128)S(1)}, f32[24,384]{1,0:T(8,128)}, u32[]{:S(2)}) copy-start(f32[24,384]{1,0:T(8,128)} %latent_ref.3) | copy-start | bytes 110596

commit v12 on v11

--- a/solution.py
+++ b/solution.py
@@ -338,7 +338,7 @@
 ):
     velocity_ref, next_ref, values_ref, pixels_ref = refs[-4:]
     tokens = rest_ref.shape[0]
-    step = 48
+    step = 16
     parts = []
     for at in range(0, tokens, step):
         rows = slice(start + at, start + at + step)
@@ -353,16 +353,15 @@
         normed = (
             centered * lax.rsqrt(var + EPS) * (1.0 + mod_ref[1:2]) + mod_ref[0:1]
         ).astype(jnp.bfloat16)
-        parts.append(
-            lax.dot_general(
-                normed,
-                final_ref[...],
-                (((1,), (1,)), ((), ())),
-                preferred_element_type=jnp.float32,
-            )
-        )
+        parts.append(normed)
+    velocity = lax.dot_general(
+        jnp.concatenate(parts, axis=0),
+        final_ref[...],
+        (((1,), (1,)), ((), ())),
+        preferred_element_type=jnp.float32,
+    )
     values = final_ref.shape[0]
-    values_ref[:tokens, :values] = jnp.concatenate(parts, axis=0)
+    values_ref[:tokens, :values] = velocity
     side = values // PATCH
     tile_cols = latent_ref.shape[1] // side
     rows = tokens // tile_cols
@@ -378,9 +377,9 @@
         after_ref[:first] = before_ref[:first]
     for tile in range(pixels_ref.shape[0]):
         lanes = slice(tile * LANES, (tile + 1) * LANES)
-        velocity = pixels_ref[tile, : rows * PATCH]
-        velocity_ref[pixels, lanes] = velocity
-        next_ref[pixels, lanes] = latent_ref[pixels, lanes] + euler_ref[:, lanes] * velocity
+        placed = pixels_ref[tile, : rows * PATCH]
+        velocity_ref[pixels, lanes] = placed
+        next_ref[pixels, lanes] = latent_ref[pixels, lanes] + euler_ref[:, lanes] * placed
 
 
 def params(limit=VMEM_LIMIT):

time: 37.3 us -> 37.2 us (level)
  no operation moved by 1% of the time
where the time goes in v12:
time: 37.2 us; the launch traced here: 37.1 us
  Pallas kernels  13 us (35%)
  waiting for transfers between devices  11.6 us (31%)
  starting transfers between devices  10.2 us (27%)
  between operations  2.17 us (6%)
    ppermute x1, waiting for transfers between devices, on_device(): second_got = lax.ppermute(second, 'col', SWAP)  8.55 us
    ppermute x1, starting transfers between devices, on_device(): lax.ppermute(kv_raw, 'col', SWAP)  2.63 us
    ppermute x2, starting transfers between devices, on_device(): lax.ppermute(raw, 'col', SWAP)  2.09 us
    pallas_call x1, Pallas kernels, on_device(): pl.pallas_call(second_kernel, out_shape=shape((tokens - cut, features)),...  2.07 us
    pallas_call x1, Pallas kernels, on_device(): pl.pallas_call(prep_own_kernel, out_shape=(shape((tokens + words, width))...  2.05 us
    ppermute x1, starting transfers between devices, on_device(): second_got = lax.ppermute(second, 'col', SWAP)  2.03 us
    ppermute x1, starting transfers between devices, on_device(): first_got = lax.ppermute(first, 'col', SWAP)  1.97 us
    pallas_call x2, Pallas kernels, on_device(): pl.pallas_call(functools.partial(final_kernel, start), out_shape=(shape(l...  1.91 us
  transfers between devices with their start and end apart: 11, of which 4 were waited for; matrix products, arithmetic and copies ran while one was open for 0% of the time, Pallas kernels for 31%

profile of v12, /device:TPU:0, one launch (start us, length us, event | category | flops | bytes accessed | tf_op | source)
XLA Modules:
  0.0 37.1 jit_solution(6066230297324755510)
XLA Ops:
  0.6 0.0 copy-start.6
  0.6 0.0 copy-start.7
  0.7 0.0 copy-start.8
  0.7 0.0 copy-start.4
  0.7 0.5 %collective-permute-start.5 = (bf16[1216,640]{1,0:T(8,128)(2,1)}, bf16[1216,640]{1,0:T(8,128)(2,1)S(1)}, u32[]{:S(2)}, u32[]{:S(2)}) collective-permute-start(bf16[1216,640]{1,0:T(8,128)(2,1)} %bitcast.5), channel_id=1, source_target_pairs={{0,2},{2,0},{1,3},{3,1},{4,6},{6,4},{5,7},{7,5},{8,10},{10,8},{9,1... | collective-permute-start | bytes 4669448 | tf_op jit(solution)/shard_map/ppermute | solution.py:446
  1.2 0.0 copy-start.2
  1.2 1.3 %split.1 = (bf16[288,640]{1,0:T(8,128)(2,1)S(1)}, bf16[48,640]{1,0:T(8,128)(2,1)S(1)}, bf16[96,640]{1,0:T(8,128)(2,1)S(1)}) custom-call(bf16[144,3,1280]{2,1,0:T(4,128)(2,1)} %bitcast.10), custom_call_target="tpu_custom_call" | custom-call | tf_op jit(solution)/shard_map/split/pallas_call | solution.py:433
  2.5 2.6 %collective-permute-start = (bf16[288,640]{1,0:T(8,128)(2,1)S(1)}, bf16[288,640]{1,0:T(8,128)(2,1)S(1)}, u32[]{:S(2)}, u32[]{:S(2)}) collective-permute-start(bf16[288,640]{1,0:T(8,128)(2,1)S(1)} %get-tuple-element.27), channel_id=1, source_target_pairs={{0,1},{1,0},{2,3},{3,2},{4,5},{5,4},{6,7},{7,6},{8,9},{9,8},{10,11... | collective-permute-start | bytes 1105928 | tf_op jit(solution)/shard_map/ppermute | solution.py:491
  6.5 0.0 copy-done.6
  6.5 0.0 copy-done.7
  6.5 0.0 copy-done.8
  6.5 0.0 copy-done.4
  6.5 2.0 %prep_own.1 = (bf16[192,640]{1,0:T(8,128)(2,1)S(1)}, bf16[192,640]{1,0:T(8,128)(2,1)S(1)}, bf16[144,640]{1,0:T(8,128)(2,1)S(1)}, f32[3,64]{1,0:T(4,128)S(1)}, f32[1,384]{1,0:T(1,128)S(1)}) custom-call(s32[1]{0:T(128)S(6)} %copy.16.index_ref, s32[1]{0:T(128)S(6)} %copy.17.count_ref, bf16[144,3,1280]{2,1,0:T(4,128)(2,1)} %bitcast.11, ...), custom_call_target="tpu_custom_call" | custom-call | tf_op jit(solution)/shard_map/prep_own/pallas_call | solution.py:448
  8.6 0.2 collective-permute-start.1
  8.8 0.3 collective-permute-start.2
  9.2 0.0 copy-done.2
  9.2 0.2 collective-permute-start.3
  9.3 1.4 %collective-permute-done.3.refs_9_ = bf16[64,1216]{1,0:T(8,128)(2,1)S(1)} collective-permute-done((bf16[64,1216]{1,0:T(8,128)(2,1)S(1)}, bf16[64,1216]{1,0:T(8,128)(2,1)S(1)}, u32[]{:S(2)}, u32[]{:S(2)}) %collective-permute-start.3) | collective-permute-done | bytes 155680 | tf_op jit(solution)/shard_map/ppermute | solution.py:447
  10.7 0.1 collective-permute-start.6
  10.9 0.0 collective-permute-done.1.refs_3_.refs_2_.refs_4_
  10.9 0.0 collective-permute-done.2.refs_4_.refs_3_.refs_5_
  10.9 0.0 copy-done.1
  10.9 0.0 copy-done.5
  10.9 1.0 %early.1 = (f32[144,640]{1,0:T(8,128)S(1)}, f32[144,640]{1,0:T(8,128)S(1)}, f32[144,2432]{1,0:T(8,128)S(1)}, f32[3,64]{1,0:T(4,128)S(1)}, f32[3,2432]{1,0:T(4,12...) custom-call(bf16[144,640]{1,0:T(8,128)(2,1)S(1)} %get-tuple-element.26.refs_0_, ...), custom_call_target="tpu_custom_call", output_to_operand_aliasing={{6}: (10, {})} | custom-call | tf_op jit(solution)/shard_map/early/pallas_call | solution.py:466
  11.9 2.0 %collective-permute-start.8 = (bf16[96,640]{1,0:T(8,128)(2,1)S(1)}, bf16[96,640]{1,0:T(8,128)(2,1)S(1)}, u32[]{:S(2)}, u32[]{:S(2)}) collective-permute-start(bf16[96,640]{1,0:T(8,128)(2,1)S(1)} %get-tuple-element.42), channel_id=1, source_target_pairs={{0,1},{1,0},{2,3},{3,2},{4,5},{5,4},{6,7},{7,6},{8,9},{9,8},{10,11... | collective-permute-start | bytes 368648 | tf_op jit(solution)/shard_map/ppermute | solution.py:483
  13.9 0.7 %collective-permute-done.x_ref = bf16[288,640]{1,0:T(8,128)(2,1)S(1)} collective-permute-done((bf16[288,640]{1,0:T(8,128)(2,1)S(1)}, bf16[288,640]{1,0:T(8,128)(2,1)S(1)}, u32[]{:S(2)}, u32[]{:S(2)}) %collective-permute-start) | collective-permute-done | bytes 368672 | tf_op jit(solution)/shard_map/ppermute | solution.py:491
  14.6 0.3 norm.1.refs_4_.got_ref.refs_6_
  14.9 0.0 copy-start
  14.9 0.1 collective-permute-start.4
  15.0 0.9 %collective-permute-done.6.x_ref = bf16[48,640]{1,0:T(8,128)(2,1)S(1)} collective-permute-done((bf16[48,640]{1,0:T(8,128)(2,1)S(1)}, bf16[48,640]{1,0:T(8,128)(2,1)S(1)}, u32[]{:S(2)}, u32[]{:S(2)}) %collective-permute-start.6) | collective-permute-done | bytes 61472 | tf_op jit(solution)/shard_map/ppermute | solution.py:483
  15.9 0.9 %part.1 = (bf16[48,640]{1,0:T(8,128)(2,1)S(1)}, f32[48,640]{1,0:T(8,128)S(1)}, f32[48,640]{1,0:T(8,128)S(1)}) custom-call(bf16[48,640]{1,0:T(8,128)(2,1)S(1)} %collective-permute-done.6.x_ref, f32[3,64]{1,0:T(4,128)S(1)} %get-tuple-element.32.gains.refs_1_, bf16[192,640]{1,0:T(8,128)(2,1)S(1)} %get-tuple-element.28.refs_1_.refs_0_.refs_2_, ...), custom_call_target="tpu_custom_call" | custom-call | flops 4499999744 | bytes 13500000 | tf_op jit(solution)/shard_map/part/pallas_call | solution.py:493
  16.8 0.0 collective-permute-done.4.last_ref.refs_7_
  16.8 0.0 collective-permute-done.5.theirs_ref.refs_9_
  16.8 0.0 copy-done
  16.8 1.1 %first.1 = (bf16[48,1280]{1,0:T(8,128)(2,1)S(1)}, bf16[48,640]{1,0:T(8,128)(2,1)S(1)}) custom-call(bf16[48,640]{1,0:T(8,128)(2,1)S(1)} %get-tuple-element.38.q_ref, bf16[288,640]{1,0:T(8,128)(2,1)S(1)} %collective-permute-done.4.last_ref.refs_7_, f32[48,640]{1,0:T(8,128)S(1)} %get-tuple-element.39.sum_ref, f32[48,640]{1,0:T(8,128)S(1)} %get-tuple-element.40.total_ref, ...), custom_call_target="tpu_custom_call" | custom-call | tf_op jit(solution)/shard_map/first/pallas_call | solution.py:502
  17.9 2.0 %collective-permute-start.7 = (bf16[48,1280]{1,0:T(8,128)(2,1)S(1)}, bf16[48,1280]{1,0:T(8,128)(2,1)S(1)}, u32[]{:S(2)}, u32[]{:S(2)}) collective-permute-start(bf16[48,1280]{1,0:T(8,128)(2,1)S(1)} %get-tuple-element.41), channel_id=1, source_target_pairs={{0,1},{1,0},{2,3},{3,2},{4,5},{5,4},{6,7},{7,6},{8,9},{9,8},{10,11... | collective-permute-start | bytes 368648 | tf_op jit(solution)/shard_map/ppermute | solution.py:510
  19.9 0.5 %rest.1 = bf16[48,1152]{1,0:T(8,128)(2,1)S(1)} custom-call(bf16[48,640]{1,0:T(8,128)(2,1)S(1)} %get-tuple-element.43.attended_ref, bf16[1216,640]{1,0:T(8,128)(2,1)S(1)} %bitcast.7, bf16[1216,640]{1,0:T(8,128)(2,1)S(1)} %collective-permute-done.5.theirs_ref.refs_9_), custom_call_target="tpu_custom_call" | custom-call | tf_op jit(solution)/shard_map/rest/pallas_call | solution.py:511
  20.4 0.1 collective-permute-start.10
  20.6 0.0 collective-permute-done.8.refs_0_
  20.6 2.1 %second.1 = bf16[96,2432]{1,0:T(8,128)(2,1)S(1)} custom-call(bf16[96,640]{1,0:T(8,128)(2,1)S(1)} %collective-permute-done.8.refs_0_, f32[3,64]{1,0:T(4,128)S(1)} %get-tuple-element.32.gains.refs_1_, bf16[192,640]{1,0:T(8,128)(2,1)S(1)} %get-tuple-element.28.refs_1_.refs_0_.refs_2_, bf16[192,640]{1,0:T(8,128)(2,1)S(1)} %get-tuple-element.29.refs_2_.refs_1_.refs_3_, ...), custom_call_target="tpu_custom_call" | custom-call | tf_op jit(solution)/shard_map/second/pallas_call | solution.py:521
  22.7 2.0 %collective-permute-start.9 = (bf16[96,2432]{1,0:T(8,128)(2,1)S(1)}, bf16[96,2432]{1,0:T(8,128)(2,1)S(1)}, u32[]{:S(2)}, u32[]{:S(2)}) collective-permute-start(bf16[96,2432]{1,0:T(8,128)(2,1)S(1)} %second.1), channel_id=1, source_target_pairs={{0,1},{1,0},{2,3},{3,2},{4,5},{5,4},{6,7},{7,6},{8,9},{9,8},{10,11... | collective-permute-start | bytes 1400840 | tf_op jit(solution)/shard_map/ppermute | solution.py:530
  24.7 0.0 collective-permute-done.7.first_ref
  24.7 1.9 %own.1.mixed_ref = f32[144,2432]{1,0:T(8,128)S(1)} custom-call(bf16[144,640]{1,0:T(8,128)(2,1)S(1)} %get-tuple-element.26.refs_0_.q_ref, bf16[288,640]{1,0:T(8,128)(2,1)S(1)} %norm.1.refs_4_.got_ref.refs_6_, bf16[288,640]{1,0:T(8,128)(2,1)S(1)} %collective-permute-done.4.last_ref.refs_7_, f32[144,640]{1,0:T(8,128)S(1)} %get-tuple-element.33.sum_ref, ...), custom_call_target="tpu_custom_call" | custom-call | flops 60000002048 | bytes 180000000 | tf_op jit(solution)/shard_map/own/pallas_call | solution.py:531
  26.6 0.0 collective-permute-done.10.rest_ref
  26.6 0.0 copy-done.3
  26.6 0.6 %final.2 = (f32[24,384]{1,0:T(8,128)S(1)}, f32[24,384]{1,0:T(8,128)S(1)}) custom-call(f32[1,384]{1,0:T(1,128)S(1)} %get-tuple-element.25.euler_ref, f32[144,2432]{1,0:T(8,128)S(1)} %own.1.mixed_ref, bf16[48,1152]{1,0:T(8,128)(2,1)S(1)} %collective-permute-done.10.rest_ref, f32[3,2432]{1,0:T(4,128)S(1)} %get-tuple-element.36.mod_ref, ...), custom_call_target="tpu_custom_call" | custom-call | tf_op jit(solution)/shard_map/final/pallas_call | solution.py:544
  27.2 8.6 %collective-permute-done.9.rest_ref = bf16[96,2432]{1,0:T(8,128)(2,1)S(1)} collective-permute-done((bf16[96,2432]{1,0:T(8,128)(2,1)S(1)}, bf16[96,2432]{1,0:T(8,128)(2,1)S(1)}, u32[]{:S(2)}, u32[]{:S(2)}) %collective-permute-start.9) | collective-permute-done | bytes 466976 | tf_op jit(solution)/shard_map/ppermute | solution.py:530
  35.7 1.3 %final.3 = (f32[24,384]{1,0:T(8,128)}, f32[24,384]{1,0:T(8,128)}) custom-call(f32[1,384]{1,0:T(1,128)S(1)} %get-tuple-element.25.euler_ref, f32[144,2432]{1,0:T(8,128)S(1)} %own.1.mixed_ref, bf16[96,2432]{1,0:T(8,128)(2,1)S(1)} %collective-permute-done.9.rest_ref, f32[3,2432]{1,0:T(4,128)S(1)} %get-tuple-element.36.mod_ref, ...), custom_call_target="tpu_custom_call" | custom-call | tf_op jit(solution)/shard_map/final/pallas_call | solution.py:544
  (4 shorter events, 0.0 us)
Async XLA Ops:
  0.6 5.8 %copy-start.6 = (f32[64]{0:T(128)S(1)}, f32[64]{0:T(128)}, u32[]{:S(2)}) copy-start(f32[64]{0:T(128)} %param.16) | copy-start | bytes 772
  0.6 5.8 %copy-start.7 = (f32[64]{0:T(128)S(1)}, f32[64]{0:T(128)}, u32[]{:S(2)}) copy-start(f32[64]{0:T(128)} %param.15) | copy-start | bytes 772
  0.7 5.8 %copy-start.8 = (f32[64]{0:T(128)S(1)}, f32[64]{0:T(128)}, u32[]{:S(2)}) copy-start(f32[64]{0:T(128)} %param.14) | copy-start | bytes 772
  0.7 5.9 %copy-start.4 = (bf16[48,2,640]{2,1,0:T(2,128)(2,1)S(1)}, bf16[48,2,640]{2,1,0:T(2,128)(2,1)}, u32[]{:S(2)}) copy-start(bf16[48,2,640]{2,1,0:T(2,128)(2,1)} %text_ref.1) | copy-start | bytes 368644
  0.7 16.2 %collective-permute-start.5 = (bf16[1216,640]{1,0:T(8,128)(2,1)}, bf16[1216,640]{1,0:T(8,128)(2,1)S(1)}, u32[]{:S(2)}, u32[]{:S(2)}) collective-permute-start(bf16[1216,640]{1,0:T(8,128)(2,1)} %bitcast.5), channel_id=1, source_target_pairs={{0,2},{2,0},{1,3},{3,1},{4,6},{6,4},{5,7},{7,5},{8,10},{10,8},{9,1... | collective-permute-start | bytes 4669448 | tf_op jit(solution)/shard_map/ppermute | solution.py:446
  1.2 8.0 %copy-start.2 = (bf16[64,1216]{1,0:T(8,128)(2,1)S(1)}, bf16[64,1216]{1,0:T(8,128)(2,1)}, u32[]{:S(2)}) copy-start(bf16[64,1216]{1,0:T(8,128)(2,1)} %refs_8_.1) | copy-start | bytes 466948
  1.2 9.7 %copy-start.1 = (bf16[12,12,2432]{2,1,0:T(8,128)(2,1)S(1)}, bf16[12,12,2432]{2,1,0:T(8,128)(2,1)}, u32[]{:S(2)}) copy-start(bf16[12,12,2432]{2,1,0:T(8,128)(2,1)} %refs_6_.1) | copy-start | bytes 2101252
  1.2 9.7 %copy-start.5 = (f32[3,2432]{1,0:T(4,128)S(1)}, f32[3,2432]{1,0:T(4,128)}, u32[]{:S(2)}) copy-start(f32[3,2432]{1,0:T(4,128)} %refs_7_.1) | copy-start | bytes 87556
  2.5 12.1 %collective-permute-start = (bf16[288,640]{1,0:T(8,128)(2,1)S(1)}, bf16[288,640]{1,0:T(8,128)(2,1)S(1)}, u32[]{:S(2)}, u32[]{:S(2)}) collective-permute-start(bf16[288,640]{1,0:T(8,128)(2,1)S(1)} %get-tuple-element.27), channel_id=1, source_target_pairs={{0,1},{1,0},{2,3},{3,2},{4,5},{5,4},{6,7},{7,6},{8,9},{9,8},{10,11... | collective-permute-start | bytes 1105928 | tf_op jit(solution)/shard_map/ppermute | solution.py:491
  8.6 2.3 %collective-permute-start.1 = (bf16[192,640]{1,0:T(8,128)(2,1)S(1)}, bf16[192,640]{1,0:T(8,128)(2,1)S(1)}, u32[]{:S(2)}, u32[]{:S(2)}) collective-permute-start(bf16[192,640]{1,0:T(8,128)(2,1)S(1)} %get-tuple-element.28.refs_1_.refs_0_.refs_2_), channel_id=1, source_target_pairs={{0,2},{2,0},{1,3},{3,1},{4,6},{6,4},{5,7},{7,5},{8,10},{10,8},{9,1... | collective-permute-start | bytes 737288 | tf_op jit(solution)/shard_map/ppermute | solution.py:464
  8.8 2.0 %collective-permute-start.2 = (bf16[192,640]{1,0:T(8,128)(2,1)S(1)}, bf16[192,640]{1,0:T(8,128)(2,1)S(1)}, u32[]{:S(2)}, u32[]{:S(2)}) collective-permute-start(bf16[192,640]{1,0:T(8,128)(2,1)S(1)} %get-tuple-element.29.refs_2_.refs_1_.refs_3_), channel_id=1, source_target_pairs={{0,2},{2,0},{1,3},{3,1},{4,6},{6,4},{5,7},{7,5},{8,10},{10,8},{9,1... | collective-permute-start | bytes 737288 | tf_op jit(solution)/shard_map/ppermute | solution.py:464
  9.2 1.6 %collective-permute-start.3 = (bf16[64,1216]{1,0:T(8,128)(2,1)S(1)}, bf16[64,1216]{1,0:T(8,128)(2,1)S(1)}, u32[]{:S(2)}, u32[]{:S(2)}) collective-permute-start(bf16[64,1216]{1,0:T(8,128)(2,1)S(1)} %copy-done.2), channel_id=1, source_target_pairs={{0,2},{2,0},{1,3},{3,1},{4,6},{6,4},{5,7},{7,5},{8,10},{10,8},{9,1... | collective-permute-start | bytes 466952 | tf_op jit(solution)/shard_map/ppermute | solution.py:447
  10.7 5.2 %collective-permute-start.6 = (bf16[48,640]{1,0:T(8,128)(2,1)S(1)}, bf16[48,640]{1,0:T(8,128)(2,1)S(1)}, u32[]{:S(2)}, u32[]{:S(2)}) collective-permute-start(bf16[48,640]{1,0:T(8,128)(2,1)S(1)} %get-tuple-element.37), channel_id=1, source_target_pairs={{0,1},{1,0},{2,3},{3,2},{4,5},{5,4},{6,7},{7,6},{8,9},{9,8},{10,11... | collective-permute-start | bytes 184328 | tf_op jit(solution)/shard_map/ppermute | solution.py:483
  11.9 8.7 %collective-permute-start.8 = (bf16[96,640]{1,0:T(8,128)(2,1)S(1)}, bf16[96,640]{1,0:T(8,128)(2,1)S(1)}, u32[]{:S(2)}, u32[]{:S(2)}) collective-permute-start(bf16[96,640]{1,0:T(8,128)(2,1)S(1)} %get-tuple-element.42), channel_id=1, source_target_pairs={{0,1},{1,0},{2,3},{3,2},{4,5},{5,4},{6,7},{7,6},{8,9},{9,8},{10,11... | collective-permute-start | bytes 368648 | tf_op jit(solution)/shard_map/ppermute | solution.py:483
  14.9 1.9 %copy-start = (bf16[640,1216]{0,1:T(8,128)(2,1)S(1)}, bf16[640,1216]{0,1:T(8,128)(2,1)}, u32[]{:S(2)}) copy-start(bf16[640,1216]{0,1:T(8,128)(2,1)} %param.17) | copy-start | bytes 4669444
  14.9 1.9 %collective-permute-start.4 = (bf16[288,640]{1,0:T(8,128)(2,1)S(1)}, bf16[288,640]{1,0:T(8,128)(2,1)S(1)}, u32[]{:S(2)}, u32[]{:S(2)}) collective-permute-start(bf16[288,640]{1,0:T(8,128)(2,1)S(1)} %norm.1.refs_4_.got_ref.refs_6_), channel_id=1, source_target_pairs={{0,2},{2,0},{1,3},{3,1},{4,6},{6,4},{5,7},{7,5},{8,10},{10,8},{9,1... | collective-permute-start | bytes 1105928 | tf_op jit(solution)/shard_map/ppermute | solution.py:492
  17.9 6.8 %collective-permute-start.7 = (bf16[48,1280]{1,0:T(8,128)(2,1)S(1)}, bf16[48,1280]{1,0:T(8,128)(2,1)S(1)}, u32[]{:S(2)}, u32[]{:S(2)}) collective-permute-start(bf16[48,1280]{1,0:T(8,128)(2,1)S(1)} %get-tuple-element.41), channel_id=1, source_target_pairs={{0,1},{1,0},{2,3},{3,2},{4,5},{5,4},{6,7},{7,6},{8,9},{9,8},{10,11... | collective-permute-start | bytes 368648 | tf_op jit(solution)/shard_map/ppermute | solution.py:510
  20.4 6.1 %collective-permute-start.10 = (bf16[48,1152]{1,0:T(8,128)(2,1)S(1)}, bf16[48,1152]{1,0:T(8,128)(2,1)S(1)}, u32[]{:S(2)}, u32[]{:S(2)}) collective-permute-start(bf16[48,1152]{1,0:T(8,128)(2,1)S(1)} %rest.1), channel_id=1, source_target_pairs={{0,1},{1,0},{2,3},{3,2},{4,5},{5,4},{6,7},{7,6},{8,9},{9,8},{10,11... | collective-permute-start | bytes 331784 | tf_op jit(solution)/shard_map/ppermute | solution.py:519
  22.7 13.1 %collective-permute-start.9 = (bf16[96,2432]{1,0:T(8,128)(2,1)S(1)}, bf16[96,2432]{1,0:T(8,128)(2,1)S(1)}, u32[]{:S(2)}, u32[]{:S(2)}) collective-permute-start(bf16[96,2432]{1,0:T(8,128)(2,1)S(1)} %second.1), channel_id=1, source_target_pairs={{0,1},{1,0},{2,3},{3,2},{4,5},{5,4},{6,7},{7,6},{8,9},{9,8},{10,11... | collective-permute-start | bytes 1400840 | tf_op jit(solution)/shard_map/ppermute | solution.py:530
  24.7 1.9 %copy-start.3 = (f32[24,384]{1,0:T(8,128)S(1)}, f32[24,384]{1,0:T(8,128)}, u32[]{:S(2)}) copy-start(f32[24,384]{1,0:T(8,128)} %latent_ref.3) | copy-start | bytes 110596

commit v13 on v12

--- a/solution.py
+++ b/solution.py
@@ -260,7 +260,7 @@
     def keep(at, to, product):
         out_ref[:, at:to] = product
 
-    project(attended[...], weight_refs, 0, out_ref.shape[1], keep)
+    project(attended[: out_ref.shape[0]], weight_refs, 0, out_ref.shape[1], keep)
 
 
 def rest_kernel(attended_ref, mine_ref, theirs_ref, out_ref):
@@ -270,7 +270,8 @@
     def keep(at, to, product):
         out_ref[:, at - start : to - start] = product
 
-    project(attended_ref[...], (mine_ref, theirs_ref), start, features, keep)
+    last = attended_ref[attended_ref.shape[0] - out_ref.shape[0] :]
+    project(last, (mine_ref, theirs_ref), start, features, keep)
 
 
 def in_order(x, is_first):
@@ -518,16 +519,23 @@
     )(heads, *weights)
     rest_got = lax.ppermute(rest, "col", SWAP)
     q_second, rest = lax.optimization_barrier((q_second, rest))
-    second = pl.pallas_call(
+    second, heads = pl.pallas_call(
         second_kernel,
-        out_shape=shape((tokens - cut, features)),
+        out_shape=(shape((cut, features)), shape((tokens - cut, width))),
         in_specs=[VMEM] * 10,
-        out_specs=VMEM,
-        scratch_shapes=[pltpu.VMEM((tokens - cut, width), jnp.bfloat16)],
+        out_specs=(VMEM, VMEM),
         compiler_params=params(),
         name="second",
     )(q_second, gains, *nearby, kv_got, kv_last, *weights)
-    second_got = lax.ppermute(second, "col", SWAP)
+    third = pl.pallas_call(
+        rest_kernel,
+        out_shape=shape((tokens - 2 * cut, features)),
+        in_specs=[VMEM] * 3,
+        out_specs=VMEM,
+        compiler_params=params(),
+        name="third",
+    )(heads, *weights)
+    second_got, third_got = (lax.ppermute(x, "col", SWAP) for x in (second, third))
     mixed = pl.pallas_call(
         own_kernel,
         out_shape=shape(mixed.shape, jnp.float32),
@@ -535,12 +543,12 @@
         out_specs=VMEM,
         scratch_shapes=[pltpu.VMEM((tokens, width), jnp.bfloat16)],
         compiler_params=params(),
-        cost_estimate=lasting(60),
+        cost_estimate=lasting(0),
         name="own",
     )(q_own, kv_got, kv_last, own_sum, own_total, *weights, mixed, mods, first_got)
     room = -(-tile_rows // 8) * 8 + 8
     results = ()
-    for (start, _), got in ((chunks[0], rest_got), (chunks[1], second_got)):
+    for start, got in zip(range(0, tokens, cut), (rest_got, second_got, third_got)):
         results = pl.pallas_call(
             functools.partial(final_kernel, start),
             out_shape=(shape(latent.shape, jnp.float32),) * 2,
@@ -551,6 +559,7 @@
                 pltpu.VMEM((latent.shape[1] // LANES, room * PATCH, LANES), jnp.float32),
             ],
             compiler_params=params(),
+            cost_estimate=lasting(30 if start == cut else 2 if start == 0 else 0),
             name="final",
         )(euler, mixed, got, mods, finals, latent, *results)
     return results

time: 37.2 us -> 37.1 us (level)
  waiting for transfers between devices: 11.6 us -> 9.95 us
  Pallas kernels: 13 us -> 14.4 us
    ppermute x1 -> x2, waiting for transfers between devices: 8.55 us -> 6.86 us  [on_device(): lax.ppermute(x, 'col', SWAP)]
    pallas_call x1 -> x2, Pallas kernels: 2.07 us -> 2.99 us  [the longest x1 2.01 us: on_device(): pl.pallas_call(second_kernel, out_shape=(shape((cut, features)), shape((t...]
    pallas_call x2 -> x3, Pallas kernels: 1.91 us -> 2.36 us  [on_device(): pl.pallas_call(functools.partial(final_kernel, start), out_shape=(shape(l...]
    ppermute x1 -> x2, starting transfers between devices: 2.03 us -> 2.16 us  [on_device(): lax.ppermute(x, 'col', SWAP)]
  transfers between devices with their start and end apart: 11 -> 12, of which waited for: 4 -> 5; matrix products, arithmetic and copies ran while one was open for 0% -> 0% of each run, Pallas kernels for 31% -> 36%
where the time goes in v13:
time: 37.1 us; the launch traced here: 36.9 us
  Pallas kernels  14.4 us (39%)
  starting transfers between devices  10.3 us (28%)
  waiting for transfers between devices  9.95 us (27%)
  between operations  2.23 us (6%)
    ppermute x2, waiting for transfers between devices, on_device(): lax.ppermute(x, 'col', SWAP)  6.86 us
    ppermute x1, starting transfers between devices, on_device(): lax.ppermute(kv_raw, 'col', SWAP)  2.63 us
    pallas_call x3, Pallas kernels, on_device(): pl.pallas_call(functools.partial(final_kernel, start), out_shape=(shape(l...  2.36 us
    ppermute x2, starting transfers between devices, on_device(): lax.ppermute(x, 'col', SWAP)  2.16 us
    ppermute x2, starting transfers between devices, on_device(): lax.ppermute(raw, 'col', SWAP)  2.09 us
    pallas_call x1, Pallas kernels, on_device(): pl.pallas_call(prep_own_kernel, out_shape=(shape((tokens + words, width))...  2.05 us
    pallas_call x1, Pallas kernels, on_device(): pl.pallas_call(second_kernel, out_shape=(shape((cut, features)), shape((t...  2.01 us
    ppermute x1, starting transfers between devices, on_device(): first_got = lax.ppermute(first, 'col', SWAP)  1.96 us
  transfers between devices with their start and end apart: 12, of which 5 were waited for; matrix products, arithmetic and copies ran while one was open for 0% of the time, Pallas kernels for 36%

profile of v13, /device:TPU:0, one launch (start us, length us, event | category | flops | bytes accessed | tf_op | source)
XLA Modules:
  0.0 36.9 jit_solution(10181232644152905406)
XLA Ops:
  0.6 0.0 copy-start.6
  0.6 0.0 copy-start.7
  0.7 0.0 copy-start.8
  0.7 0.0 copy-start.3
  0.7 0.5 %collective-permute-start.5 = (bf16[1216,640]{1,0:T(8,128)(2,1)}, bf16[1216,640]{1,0:T(8,128)(2,1)S(1)}, u32[]{:S(2)}, u32[]{:S(2)}) collective-permute-start(bf16[1216,640]{1,0:T(8,128)(2,1)} %bitcast.5), channel_id=1, source_target_pairs={{0,2},{2,0},{1,3},{3,1},{4,6},{6,4},{5,7},{7,5},{8,10},{10,8},{9,1... | collective-permute-start | bytes 4669448 | tf_op jit(solution)/shard_map/ppermute | solution.py:447
  1.2 1.3 %split.1 = (bf16[288,640]{1,0:T(8,128)(2,1)S(1)}, bf16[48,640]{1,0:T(8,128)(2,1)S(1)}, bf16[96,640]{1,0:T(8,128)(2,1)S(1)}) custom-call(bf16[144,3,1280]{2,1,0:T(4,128)(2,1)} %bitcast.11), custom_call_target="tpu_custom_call" | custom-call | tf_op jit(solution)/shard_map/split/pallas_call | solution.py:434
  2.5 2.6 %collective-permute-start = (bf16[288,640]{1,0:T(8,128)(2,1)S(1)}, bf16[288,640]{1,0:T(8,128)(2,1)S(1)}, u32[]{:S(2)}, u32[]{:S(2)}) collective-permute-start(bf16[288,640]{1,0:T(8,128)(2,1)S(1)} %get-tuple-element.31), channel_id=1, source_target_pairs={{0,1},{1,0},{2,3},{3,2},{4,5},{5,4},{6,7},{7,6},{8,9},{9,8},{10,11... | collective-permute-start | bytes 1105928 | tf_op jit(solution)/shard_map/ppermute | solution.py:492
  6.5 0.0 copy-done.6
  6.5 0.0 copy-done.7
  6.5 0.0 copy-done.8
  6.5 0.0 copy-done.3
  6.5 2.0 %prep_own.1 = (bf16[192,640]{1,0:T(8,128)(2,1)S(1)}, bf16[192,640]{1,0:T(8,128)(2,1)S(1)}, bf16[144,640]{1,0:T(8,128)(2,1)S(1)}, f32[3,64]{1,0:T(4,128)S(1)}, f32[1,384]{1,0:T(1,128)S(1)}) custom-call(s32[1]{0:T(128)S(6)} %copy.16.index_ref, s32[1]{0:T(128)S(6)} %copy.17.count_ref, bf16[144,3,1280]{2,1,0:T(4,128)(2,1)} %bitcast.12, ...), custom_call_target="tpu_custom_call" | custom-call | tf_op jit(solution)/shard_map/prep_own/pallas_call | solution.py:449
  8.6 0.2 collective-permute-start.1
  8.8 0.3 collective-permute-start.2
  9.2 0.2 collective-permute-start.3
  9.3 1.4 %collective-permute-done.3.refs_9_ = bf16[64,1216]{1,0:T(8,128)(2,1)S(1)} collective-permute-done((bf16[64,1216]{1,0:T(8,128)(2,1)S(1)}, bf16[64,1216]{1,0:T(8,128)(2,1)S(1)}, u32[]{:S(2)}, u32[]{:S(2)}) %collective-permute-start.3) | collective-permute-done | bytes 155680 | tf_op jit(solution)/shard_map/ppermute | solution.py:448
  10.7 0.1 collective-permute-start.6
  10.9 0.0 collective-permute-done.1.refs_3_.refs_2_.refs_4_
  10.9 0.0 collective-permute-done.2.refs_4_.refs_3_.refs_5_
  10.9 1.0 %early.1 = (f32[144,640]{1,0:T(8,128)S(1)}, f32[144,640]{1,0:T(8,128)S(1)}, f32[144,2432]{1,0:T(8,128)S(1)}, f32[3,64]{1,0:T(4,128)S(1)}, f32[3,2432]{1,0:T(4,12...) custom-call(bf16[144,640]{1,0:T(8,128)(2,1)S(1)} %get-tuple-element.30.refs_0_, ...), custom_call_target="tpu_custom_call", output_to_operand_aliasing={{6}: (10, {})} | custom-call | tf_op jit(solution)/shard_map/early/pallas_call | solution.py:467
  11.9 2.0 %collective-permute-start.8 = (bf16[96,640]{1,0:T(8,128)(2,1)S(1)}, bf16[96,640]{1,0:T(8,128)(2,1)S(1)}, u32[]{:S(2)}, u32[]{:S(2)}) collective-permute-start(bf16[96,640]{1,0:T(8,128)(2,1)S(1)} %get-tuple-element.46), channel_id=1, source_target_pairs={{0,1},{1,0},{2,3},{3,2},{4,5},{5,4},{6,7},{7,6},{8,9},{9,8},{10,11... | collective-permute-start | bytes 368648 | tf_op jit(solution)/shard_map/ppermute | solution.py:484
  13.9 0.7 %collective-permute-done.x_ref = bf16[288,640]{1,0:T(8,128)(2,1)S(1)} collective-permute-done((bf16[288,640]{1,0:T(8,128)(2,1)S(1)}, bf16[288,640]{1,0:T(8,128)(2,1)S(1)}, u32[]{:S(2)}, u32[]{:S(2)}) %collective-permute-start) | collective-permute-done | bytes 368672 | tf_op jit(solution)/shard_map/ppermute | solution.py:492
  14.6 0.3 norm.1.refs_4_.got_ref.refs_6_
  14.9 0.0 copy-start
  14.9 0.1 collective-permute-start.4
  15.0 0.9 %collective-permute-done.6.x_ref = bf16[48,640]{1,0:T(8,128)(2,1)S(1)} collective-permute-done((bf16[48,640]{1,0:T(8,128)(2,1)S(1)}, bf16[48,640]{1,0:T(8,128)(2,1)S(1)}, u32[]{:S(2)}, u32[]{:S(2)}) %collective-permute-start.6) | collective-permute-done | bytes 61472 | tf_op jit(solution)/shard_map/ppermute | solution.py:484
  15.9 0.9 %part.1 = (bf16[48,640]{1,0:T(8,128)(2,1)S(1)}, f32[48,640]{1,0:T(8,128)S(1)}, f32[48,640]{1,0:T(8,128)S(1)}) custom-call(bf16[48,640]{1,0:T(8,128)(2,1)S(1)} %collective-permute-done.6.x_ref, f32[3,64]{1,0:T(4,128)S(1)} %get-tuple-element.36.gains.refs_1_, bf16[192,640]{1,0:T(8,128)(2,1)S(1)} %get-tuple-element.32.refs_1_.refs_0_.refs_2_, ...), custom_call_target="tpu_custom_call" | custom-call | flops 4499999744 | bytes 13500000 | tf_op jit(solution)/shard_map/part/pallas_call | solution.py:494
  16.8 0.0 collective-permute-done.4.last_ref.refs_7_
  16.8 0.0 collective-permute-done.5.theirs_ref.refs_9_
  16.8 0.0 copy-done
  16.9 1.1 %first.1 = (bf16[48,1280]{1,0:T(8,128)(2,1)S(1)}, bf16[48,640]{1,0:T(8,128)(2,1)S(1)}) custom-call(bf16[48,640]{1,0:T(8,128)(2,1)S(1)} %get-tuple-element.42.q_ref, bf16[288,640]{1,0:T(8,128)(2,1)S(1)} %collective-permute-done.4.last_ref.refs_7_, f32[48,640]{1,0:T(8,128)S(1)} %get-tuple-element.43.sum_ref, f32[48,640]{1,0:T(8,128)S(1)} %get-tuple-element.44.total_ref, ...), custom_call_target="tpu_custom_call" | custom-call | tf_op jit(solution)/shard_map/first/pallas_call | solution.py:503
  17.9 2.0 %collective-permute-start.7 = (bf16[48,1280]{1,0:T(8,128)(2,1)S(1)}, bf16[48,1280]{1,0:T(8,128)(2,1)S(1)}, u32[]{:S(2)}, u32[]{:S(2)}) collective-permute-start(bf16[48,1280]{1,0:T(8,128)(2,1)S(1)} %get-tuple-element.45), channel_id=1, source_target_pairs={{0,1},{1,0},{2,3},{3,2},{4,5},{5,4},{6,7},{7,6},{8,9},{9,8},{10,11... | collective-permute-start | bytes 368648 | tf_op jit(solution)/shard_map/ppermute | solution.py:511
  19.9 0.5 %rest.1 = bf16[48,1152]{1,0:T(8,128)(2,1)S(1)} custom-call(bf16[48,640]{1,0:T(8,128)(2,1)S(1)} %get-tuple-element.47.attended_ref, bf16[1216,640]{1,0:T(8,128)(2,1)S(1)} %bitcast.7, bf16[1216,640]{1,0:T(8,128)(2,1)S(1)} %collective-permute-done.5.theirs_ref.refs_9_), custom_call_target="tpu_custom_call" | custom-call | tf_op jit(solution)/shard_map/rest/pallas_call | solution.py:512
  20.4 0.1 collective-permute-start.11
  20.6 0.0 collective-permute-done.8.refs_0_
  20.6 2.0 %second.1 = (bf16[48,2432]{1,0:T(8,128)(2,1)S(1)}, bf16[96,640]{1,0:T(8,128)(2,1)S(1)}) custom-call(bf16[96,640]{1,0:T(8,128)(2,1)S(1)} %collective-permute-done.8.refs_0_, f32[3,64]{1,0:T(4,128)S(1)} %get-tuple-element.36.gains.refs_1_, bf16[192,640]{1,0:T(8,128)(2,1)S(1)} %get-tuple-element.32.refs_1_.refs_0_.refs_2_, ...), custom_call_target="tpu_custom_call" | custom-call | tf_op jit(solution)/shard_map/second/pallas_call | solution.py:522
  22.6 2.0 %collective-permute-start.10 = (bf16[48,2432]{1,0:T(8,128)(2,1)S(1)}, bf16[48,2432]{1,0:T(8,128)(2,1)S(1)}, u32[]{:S(2)}, u32[]{:S(2)}) collective-permute-start(bf16[48,2432]{1,0:T(8,128)(2,1)S(1)} %get-tuple-element.51), channel_id=1, source_target_pairs={{0,1},{1,0},{2,3},{3,2},{4,5},{5,4},{6,7},{7,6},{8,9},{9,8},{10,11... | collective-permute-start | bytes 700424 | tf_op jit(solution)/shard_map/ppermute | solution.py:538
  24.6 1.0 %third.1 = bf16[48,2432]{1,0:T(8,128)(2,1)S(1)} custom-call(bf16[96,640]{1,0:T(8,128)(2,1)S(1)} %get-tuple-element.49.attended_ref, bf16[1216,640]{1,0:T(8,128)(2,1)S(1)} %bitcast.9, bf16[1216,640]{1,0:T(8,128)(2,1)S(1)} %collective-permute-done.5.theirs_ref.refs_9_), custom_call_target="tpu_custom_call" | custom-call | tf_op jit(solution)/shard_map/third/pallas_call | solution.py:530
  25.6 0.1 collective-permute-start.9
  25.8 0.0 collective-permute-done.7.first_ref
  25.8 1.9 %own.1.mixed_ref = f32[144,2432]{1,0:T(8,128)S(1)} custom-call(bf16[144,640]{1,0:T(8,128)(2,1)S(1)} %get-tuple-element.30.refs_0_.q_ref, bf16[288,640]{1,0:T(8,128)(2,1)S(1)} %norm.1.refs_4_.got_ref.refs_6_, bf16[288,640]{1,0:T(8,128)(2,1)S(1)} %collective-permute-done.4.last_ref.refs_7_, f32[144,640]{1,0:T(8,128)S(1)} %get-tuple-element.37.sum_ref, ...), custom_call_target="tpu_custom_call" | custom-call | tf_op jit(solution)/shard_map/own/pallas_call | solution.py:539
  27.7 0.0 collective-permute-done.11.rest_ref
  27.7 0.0 copy-done.5
  27.7 0.6 %final.3 = (f32[24,384]{1,0:T(8,128)S(1)}, f32[24,384]{1,0:T(8,128)S(1)}) custom-call(f32[1,384]{1,0:T(1,128)S(1)} %get-tuple-element.29.euler_ref, f32[144,2432]{1,0:T(8,128)S(1)} %own.1.mixed_ref, bf16[48,1152]{1,0:T(8,128)(2,1)S(1)} %collective-permute-done.11.rest_ref, f32[3,2432]{1,0:T(4,128)S(1)} %get-tuple-element.40.mod_ref, ...), custom_call_target="tpu_custom_call" | custom-call | flops 2000000000 | bytes 6000000 | tf_op jit(solution)/shard_map/final/pallas_call | solution.py:552
  28.3 3.2 %collective-permute-done.10.rest_ref = bf16[48,2432]{1,0:T(8,128)(2,1)S(1)} collective-permute-done((bf16[48,2432]{1,0:T(8,128)(2,1)S(1)}, bf16[48,2432]{1,0:T(8,128)(2,1)S(1)}, u32[]{:S(2)}, u32[]{:S(2)}) %collective-permute-start.10) | collective-permute-done | bytes 233504 | tf_op jit(solution)/shard_map/ppermute | solution.py:538
  31.5 0.6 %final.4 = (f32[24,384]{1,0:T(8,128)S(1)}, f32[24,384]{1,0:T(8,128)S(1)}) custom-call(f32[1,384]{1,0:T(1,128)S(1)} %get-tuple-element.29.euler_ref, f32[144,2432]{1,0:T(8,128)S(1)} %own.1.mixed_ref, bf16[48,2432]{1,0:T(8,128)(2,1)S(1)} %collective-permute-done.10.rest_ref, f32[3,2432]{1,0:T(4,128)S(1)} %get-tuple-element.40.mod_ref, ...), custom_call_target="tpu_custom_call" | custom-call | flops 30000001024 | bytes 90000000 | tf_op jit(solution)/shard_map/final/pallas_call | solution.py:552
  32.1 3.6 %collective-permute-done.9.rest_ref = bf16[48,2432]{1,0:T(8,128)(2,1)S(1)} collective-permute-done((bf16[48,2432]{1,0:T(8,128)(2,1)S(1)}, bf16[48,2432]{1,0:T(8,128)(2,1)S(1)}, u32[]{:S(2)}, u32[]{:S(2)}) %collective-permute-start.9) | collective-permute-done | bytes 233504 | tf_op jit(solution)/shard_map/ppermute | solution.py:538
  35.7 1.2 %final.5 = (f32[24,384]{1,0:T(8,128)}, f32[24,384]{1,0:T(8,128)}) custom-call(f32[1,384]{1,0:T(1,128)S(1)} %get-tuple-element.29.euler_ref, f32[144,2432]{1,0:T(8,128)S(1)} %own.1.mixed_ref, bf16[48,2432]{1,0:T(8,128)(2,1)S(1)} %collective-permute-done.9.rest_ref, f32[3,2432]{1,0:T(4,128)S(1)} %get-tuple-element.40.mod_ref, ...), custom_call_target="tpu_custom_call" | custom-call | tf_op jit(solution)/shard_map/final/pallas_call | solution.py:552
  (8 shorter events, 0.0 us)
Async XLA Ops:
  0.6 5.8 %copy-start.6 = (f32[64]{0:T(128)S(1)}, f32[64]{0:T(128)}, u32[]{:S(2)}) copy-start(f32[64]{0:T(128)} %param.16) | copy-start | bytes 772
  0.6 5.8 %copy-start.7 = (f32[64]{0:T(128)S(1)}, f32[64]{0:T(128)}, u32[]{:S(2)}) copy-start(f32[64]{0:T(128)} %param.15) | copy-start | bytes 772
  0.7 5.8 %copy-start.8 = (f32[64]{0:T(128)S(1)}, f32[64]{0:T(128)}, u32[]{:S(2)}) copy-start(f32[64]{0:T(128)} %param.14) | copy-start | bytes 772
  0.7 5.9 %copy-start.3 = (bf16[48,2,640]{2,1,0:T(2,128)(2,1)S(1)}, bf16[48,2,640]{2,1,0:T(2,128)(2,1)}, u32[]{:S(2)}) copy-start(bf16[48,2,640]{2,1,0:T(2,128)(2,1)} %text_ref.1) | copy-start | bytes 368644
  0.7 16.2 %collective-permute-start.5 = (bf16[1216,640]{1,0:T(8,128)(2,1)}, bf16[1216,640]{1,0:T(8,128)(2,1)S(1)}, u32[]{:S(2)}, u32[]{:S(2)}) collective-permute-start(bf16[1216,640]{1,0:T(8,128)(2,1)} %bitcast.5), channel_id=1, source_target_pairs={{0,2},{2,0},{1,3},{3,1},{4,6},{6,4},{5,7},{7,5},{8,10},{10,8},{9,1... | collective-permute-start | bytes 4669448 | tf_op jit(solution)/shard_map/ppermute | solution.py:447
  1.2 8.0 %copy-start.2 = (bf16[64,1216]{1,0:T(8,128)(2,1)S(1)}, bf16[64,1216]{1,0:T(8,128)(2,1)}, u32[]{:S(2)}) copy-start(bf16[64,1216]{1,0:T(8,128)(2,1)} %refs_8_.1) | copy-start | bytes 466948
  1.2 9.7 %copy-start.1 = (bf16[12,12,2432]{2,1,0:T(8,128)(2,1)S(1)}, bf16[12,12,2432]{2,1,0:T(8,128)(2,1)}, u32[]{:S(2)}) copy-start(bf16[12,12,2432]{2,1,0:T(8,128)(2,1)} %refs_6_.1) | copy-start | bytes 2101252
  1.2 9.7 %copy-start.4 = (f32[3,2432]{1,0:T(4,128)S(1)}, f32[3,2432]{1,0:T(4,128)}, u32[]{:S(2)}) copy-start(f32[3,2432]{1,0:T(4,128)} %refs_7_.1) | copy-start | bytes 87556
  2.5 12.1 %collective-permute-start = (bf16[288,640]{1,0:T(8,128)(2,1)S(1)}, bf16[288,640]{1,0:T(8,128)(2,1)S(1)}, u32[]{:S(2)}, u32[]{:S(2)}) collective-permute-start(bf16[288,640]{1,0:T(8,128)(2,1)S(1)} %get-tuple-element.31), channel_id=1, source_target_pairs={{0,1},{1,0},{2,3},{3,2},{4,5},{5,4},{6,7},{7,6},{8,9},{9,8},{10,11... | collective-permute-start | bytes 1105928 | tf_op jit(solution)/shard_map/ppermute | solution.py:492
  8.6 2.3 %collective-permute-start.1 = (bf16[192,640]{1,0:T(8,128)(2,1)S(1)}, bf16[192,640]{1,0:T(8,128)(2,1)S(1)}, u32[]{:S(2)}, u32[]{:S(2)}) collective-permute-start(bf16[192,640]{1,0:T(8,128)(2,1)S(1)} %get-tuple-element.32.refs_1_.refs_0_.refs_2_), channel_id=1, source_target_pairs={{0,2},{2,0},{1,3},{3,1},{4,6},{6,4},{5,7},{7,5},{8,10},{10,8},{9,1... | collective-permute-start | bytes 737288 | tf_op jit(solution)/shard_map/ppermute | solution.py:465
  8.8 2.0 %collective-permute-start.2 = (bf16[192,640]{1,0:T(8,128)(2,1)S(1)}, bf16[192,640]{1,0:T(8,128)(2,1)S(1)}, u32[]{:S(2)}, u32[]{:S(2)}) collective-permute-start(bf16[192,640]{1,0:T(8,128)(2,1)S(1)} %get-tuple-element.33.refs_2_.refs_1_.refs_3_), channel_id=1, source_target_pairs={{0,2},{2,0},{1,3},{3,1},{4,6},{6,4},{5,7},{7,5},{8,10},{10,8},{9,1... | collective-permute-start | bytes 737288 | tf_op jit(solution)/shard_map/ppermute | solution.py:465
  9.2 1.6 %collective-permute-start.3 = (bf16[64,1216]{1,0:T(8,128)(2,1)S(1)}, bf16[64,1216]{1,0:T(8,128)(2,1)S(1)}, u32[]{:S(2)}, u32[]{:S(2)}) collective-permute-start(bf16[64,1216]{1,0:T(8,128)(2,1)S(1)} %copy-done.2), channel_id=1, source_target_pairs={{0,2},{2,0},{1,3},{3,1},{4,6},{6,4},{5,7},{7,5},{8,10},{10,8},{9,1... | collective-permute-start | bytes 466952 | tf_op jit(solution)/shard_map/ppermute | solution.py:448
  10.7 5.2 %collective-permute-start.6 = (bf16[48,640]{1,0:T(8,128)(2,1)S(1)}, bf16[48,640]{1,0:T(8,128)(2,1)S(1)}, u32[]{:S(2)}, u32[]{:S(2)}) collective-permute-start(bf16[48,640]{1,0:T(8,128)(2,1)S(1)} %get-tuple-element.41), channel_id=1, source_target_pairs={{0,1},{1,0},{2,3},{3,2},{4,5},{5,4},{6,7},{7,6},{8,9},{9,8},{10,11... | collective-permute-start | bytes 184328 | tf_op jit(solution)/shard_map/ppermute | solution.py:484
  11.9 8.7 %collective-permute-start.8 = (bf16[96,640]{1,0:T(8,128)(2,1)S(1)}, bf16[96,640]{1,0:T(8,128)(2,1)S(1)}, u32[]{:S(2)}, u32[]{:S(2)}) collective-permute-start(bf16[96,640]{1,0:T(8,128)(2,1)S(1)} %get-tuple-element.46), channel_id=1, source_target_pairs={{0,1},{1,0},{2,3},{3,2},{4,5},{5,4},{6,7},{7,6},{8,9},{9,8},{10,11... | collective-permute-start | bytes 368648 | tf_op jit(solution)/shard_map/ppermute | solution.py:484
  14.9 1.9 %copy-start = (bf16[640,1216]{0,1:T(8,128)(2,1)S(1)}, bf16[640,1216]{0,1:T(8,128)(2,1)}, u32[]{:S(2)}) copy-start(bf16[640,1216]{0,1:T(8,128)(2,1)} %param.17) | copy-start | bytes 4669444
  14.9 1.9 %collective-permute-start.4 = (bf16[288,640]{1,0:T(8,128)(2,1)S(1)}, bf16[288,640]{1,0:T(8,128)(2,1)S(1)}, u32[]{:S(2)}, u32[]{:S(2)}) collective-permute-start(bf16[288,640]{1,0:T(8,128)(2,1)S(1)} %norm.1.refs_4_.got_ref.refs_6_), channel_id=1, source_target_pairs={{0,2},{2,0},{1,3},{3,1},{4,6},{6,4},{5,7},{7,5},{8,10},{10,8},{9,1... | collective-permute-start | bytes 1105928 | tf_op jit(solution)/shard_map/ppermute | solution.py:493
  17.9 7.9 %collective-permute-start.7 = (bf16[48,1280]{1,0:T(8,128)(2,1)S(1)}, bf16[48,1280]{1,0:T(8,128)(2,1)S(1)}, u32[]{:S(2)}, u32[]{:S(2)}) collective-permute-start(bf16[48,1280]{1,0:T(8,128)(2,1)S(1)} %get-tuple-element.45), channel_id=1, source_target_pairs={{0,1},{1,0},{2,3},{3,2},{4,5},{5,4},{6,7},{7,6},{8,9},{9,8},{10,11... | collective-permute-start | bytes 368648 | tf_op jit(solution)/shard_map/ppermute | solution.py:511
  20.4 7.2 %collective-permute-start.11 = (bf16[48,1152]{1,0:T(8,128)(2,1)S(1)}, bf16[48,1152]{1,0:T(8,128)(2,1)S(1)}, u32[]{:S(2)}, u32[]{:S(2)}) collective-permute-start(bf16[48,1152]{1,0:T(8,128)(2,1)S(1)} %rest.1), channel_id=1, source_target_pairs={{0,1},{1,0},{2,3},{3,2},{4,5},{5,4},{6,7},{7,6},{8,9},{9,8},{10,11... | collective-permute-start | bytes 331784 | tf_op jit(solution)/shard_map/ppermute | solution.py:520
  22.6 8.9 %collective-permute-start.10 = (bf16[48,2432]{1,0:T(8,128)(2,1)S(1)}, bf16[48,2432]{1,0:T(8,128)(2,1)S(1)}, u32[]{:S(2)}, u32[]{:S(2)}) collective-permute-start(bf16[48,2432]{1,0:T(8,128)(2,1)S(1)} %get-tuple-element.51), channel_id=1, source_target_pairs={{0,1},{1,0},{2,3},{3,2},{4,5},{5,4},{6,7},{7,6},{8,9},{9,8},{10,11... | collective-permute-start | bytes 700424 | tf_op jit(solution)/shard_map/ppermute | solution.py:538
  25.6 10.1 %collective-permute-start.9 = (bf16[48,2432]{1,0:T(8,128)(2,1)S(1)}, bf16[48,2432]{1,0:T(8,128)(2,1)S(1)}, u32[]{:S(2)}, u32[]{:S(2)}) collective-permute-start(bf16[48,2432]{1,0:T(8,128)(2,1)S(1)} %third.1), channel_id=1, source_target_pairs={{0,1},{1,0},{2,3},{3,2},{4,5},{5,4},{6,7},{7,6},{8,9},{9,8},{10,11... | collective-permute-start | bytes 700424 | tf_op jit(solution)/shard_map/ppermute | solution.py:538
  25.8 1.9 %copy-start.5 = (f32[24,384]{1,0:T(8,128)S(1)}, f32[24,384]{1,0:T(8,128)}, u32[]{:S(2)}) copy-start(f32[24,384]{1,0:T(8,128)} %latent_ref.5) | copy-start | bytes 110596

commit v14 on v13

--- a/solution.py
+++ b/solution.py
@@ -20,7 +20,7 @@
 VMEM_OWN = 52 * 1024 * 1024
 LOADS = 3
 FIRST = 1280
-STEP = 640
+STEP = 1280
 SWAP = [(0, 1), (1, 0)]
 
 

time: 37.1 us -> 37.1 us (level)
  no operation moved by 1% of the time
where the time goes in v14:
time: 37.1 us; the launch traced here: 36.9 us
  Pallas kernels  14.4 us (39%)
  starting transfers between devices  10.4 us (28%)
  waiting for transfers between devices  9.89 us (27%)
  between operations  2.19 us (6%)
    ppermute x2, waiting for transfers between devices, on_device(): lax.ppermute(x, 'col', SWAP)  6.8 us
    ppermute x1, starting transfers between devices, on_device(): lax.ppermute(kv_raw, 'col', SWAP)  2.63 us
    pallas_call x3, Pallas kernels, on_device(): pl.pallas_call(functools.partial(final_kernel, start), out_shape=(shape(l...  2.36 us
    ppermute x2, starting transfers between devices, on_device(): lax.ppermute(x, 'col', SWAP)  2.16 us
    ppermute x2, starting transfers between devices, on_device(): lax.ppermute(raw, 'col', SWAP)  2.09 us
    pallas_call x1, Pallas kernels, on_device(): pl.pallas_call(prep_own_kernel, out_shape=(shape((tokens + words, width))...  2.05 us
    pallas_call x1, Pallas kernels, on_device(): pl.pallas_call(second_kernel, out_shape=(shape((cut, features)), shape((t...  2.02 us
    ppermute x1, starting transfers between devices, on_device(): first_got = lax.ppermute(first, 'col', SWAP)  2.01 us
  transfers between devices with their start and end apart: 12, of which 5 were waited for; matrix products, arithmetic and copies ran while one was open for 0% of the time, Pallas kernels for 36%

profile of v14, /device:TPU:0, one launch (start us, length us, event | category | flops | bytes accessed | tf_op | source)
XLA Modules:
  0.0 36.9 jit_solution(11122108982750769721)
XLA Ops:
  0.6 0.0 copy-start.6
  0.6 0.0 copy-start.7
  0.7 0.0 copy-start.8
  0.7 0.0 copy-start.3
  0.7 0.5 %collective-permute-start.5 = (bf16[1216,640]{1,0:T(8,128)(2,1)}, bf16[1216,640]{1,0:T(8,128)(2,1)S(1)}, u32[]{:S(2)}, u32[]{:S(2)}) collective-permute-start(bf16[1216,640]{1,0:T(8,128)(2,1)} %bitcast.5), channel_id=1, source_target_pairs={{0,2},{2,0},{1,3},{3,1},{4,6},{6,4},{5,7},{7,5},{8,10},{10,8},{9,1... | collective-permute-start | bytes 4669448 | tf_op jit(solution)/shard_map/ppermute | solution.py:447
  1.2 1.3 %split.1 = (bf16[288,640]{1,0:T(8,128)(2,1)S(1)}, bf16[48,640]{1,0:T(8,128)(2,1)S(1)}, bf16[96,640]{1,0:T(8,128)(2,1)S(1)}) custom-call(bf16[144,3,1280]{2,1,0:T(4,128)(2,1)} %bitcast.11), custom_call_target="tpu_custom_call" | custom-call | tf_op jit(solution)/shard_map/split/pallas_call | solution.py:434
  2.5 2.6 %collective-permute-start = (bf16[288,640]{1,0:T(8,128)(2,1)S(1)}, bf16[288,640]{1,0:T(8,128)(2,1)S(1)}, u32[]{:S(2)}, u32[]{:S(2)}) collective-permute-start(bf16[288,640]{1,0:T(8,128)(2,1)S(1)} %get-tuple-element.31), channel_id=1, source_target_pairs={{0,1},{1,0},{2,3},{3,2},{4,5},{5,4},{6,7},{7,6},{8,9},{9,8},{10,11... | collective-permute-start | bytes 1105928 | tf_op jit(solution)/shard_map/ppermute | solution.py:492
  6.5 0.0 copy-done.6
  6.5 0.0 copy-done.7
  6.5 0.0 copy-done.8
  6.5 0.0 copy-done.3
  6.5 2.0 %prep_own.1 = (bf16[192,640]{1,0:T(8,128)(2,1)S(1)}, bf16[192,640]{1,0:T(8,128)(2,1)S(1)}, bf16[144,640]{1,0:T(8,128)(2,1)S(1)}, f32[3,64]{1,0:T(4,128)S(1)}, f32[1,384]{1,0:T(1,128)S(1)}) custom-call(s32[1]{0:T(128)S(6)} %copy.16.index_ref, s32[1]{0:T(128)S(6)} %copy.17.count_ref, bf16[144,3,1280]{2,1,0:T(4,128)(2,1)} %bitcast.12, ...), custom_call_target="tpu_custom_call" | custom-call | tf_op jit(solution)/shard_map/prep_own/pallas_call | solution.py:449
  8.6 0.2 collective-permute-start.1
  8.8 0.3 collective-permute-start.2
  9.2 0.2 collective-permute-start.3
  9.3 1.4 %collective-permute-done.3.refs_9_ = bf16[64,1216]{1,0:T(8,128)(2,1)S(1)} collective-permute-done((bf16[64,1216]{1,0:T(8,128)(2,1)S(1)}, bf16[64,1216]{1,0:T(8,128)(2,1)S(1)}, u32[]{:S(2)}, u32[]{:S(2)}) %collective-permute-start.3) | collective-permute-done | bytes 155680 | tf_op jit(solution)/shard_map/ppermute | solution.py:448
  10.7 0.1 collective-permute-start.6
  10.9 0.0 collective-permute-done.1.refs_3_.refs_2_.refs_4_
  10.9 0.0 collective-permute-done.2.refs_4_.refs_3_.refs_5_
  10.9 0.0 copy-done.1
  10.9 0.0 copy-done.4
  10.9 1.0 %early.1 = (f32[144,640]{1,0:T(8,128)S(1)}, f32[144,640]{1,0:T(8,128)S(1)}, f32[144,2432]{1,0:T(8,128)S(1)}, f32[3,64]{1,0:T(4,128)S(1)}, f32[3,2432]{1,0:T(4,12...) custom-call(bf16[144,640]{1,0:T(8,128)(2,1)S(1)} %get-tuple-element.30.refs_0_, ...), custom_call_target="tpu_custom_call", output_to_operand_aliasing={{6}: (10, {})} | custom-call | tf_op jit(solution)/shard_map/early/pallas_call | solution.py:467
  11.9 2.0 %collective-permute-start.8 = (bf16[96,640]{1,0:T(8,128)(2,1)S(1)}, bf16[96,640]{1,0:T(8,128)(2,1)S(1)}, u32[]{:S(2)}, u32[]{:S(2)}) collective-permute-start(bf16[96,640]{1,0:T(8,128)(2,1)S(1)} %get-tuple-element.46), channel_id=1, source_target_pairs={{0,1},{1,0},{2,3},{3,2},{4,5},{5,4},{6,7},{7,6},{8,9},{9,8},{10,11... | collective-permute-start | bytes 368648 | tf_op jit(solution)/shard_map/ppermute | solution.py:484
  13.9 0.7 %collective-permute-done.x_ref = bf16[288,640]{1,0:T(8,128)(2,1)S(1)} collective-permute-done((bf16[288,640]{1,0:T(8,128)(2,1)S(1)}, bf16[288,640]{1,0:T(8,128)(2,1)S(1)}, u32[]{:S(2)}, u32[]{:S(2)}) %collective-permute-start) | collective-permute-done | bytes 368672 | tf_op jit(solution)/shard_map/ppermute | solution.py:492
  14.6 0.3 norm.1.refs_4_.got_ref.refs_6_
  14.9 0.0 copy-start
  14.9 0.1 collective-permute-start.4
  15.0 0.9 %collective-permute-done.6.x_ref = bf16[48,640]{1,0:T(8,128)(2,1)S(1)} collective-permute-done((bf16[48,640]{1,0:T(8,128)(2,1)S(1)}, bf16[48,640]{1,0:T(8,128)(2,1)S(1)}, u32[]{:S(2)}, u32[]{:S(2)}) %collective-permute-start.6) | collective-permute-done | bytes 61472 | tf_op jit(solution)/shard_map/ppermute | solution.py:484
  15.9 0.9 %part.1 = (bf16[48,640]{1,0:T(8,128)(2,1)S(1)}, f32[48,640]{1,0:T(8,128)S(1)}, f32[48,640]{1,0:T(8,128)S(1)}) custom-call(bf16[48,640]{1,0:T(8,128)(2,1)S(1)} %collective-permute-done.6.x_ref, f32[3,64]{1,0:T(4,128)S(1)} %get-tuple-element.36.gains.refs_1_, bf16[192,640]{1,0:T(8,128)(2,1)S(1)} %get-tuple-element.32.refs_1_.refs_0_.refs_2_, ...), custom_call_target="tpu_custom_call" | custom-call | flops 4499999744 | bytes 13500000 | tf_op jit(solution)/shard_map/part/pallas_call | solution.py:494
  16.8 0.0 collective-permute-done.4.last_ref.refs_7_
  16.8 0.0 collective-permute-done.5.theirs_ref.refs_9_
  16.9 1.0 %first.1 = (bf16[48,1280]{1,0:T(8,128)(2,1)S(1)}, bf16[48,640]{1,0:T(8,128)(2,1)S(1)}) custom-call(bf16[48,640]{1,0:T(8,128)(2,1)S(1)} %get-tuple-element.42.q_ref, bf16[288,640]{1,0:T(8,128)(2,1)S(1)} %collective-permute-done.4.last_ref.refs_7_, f32[48,640]{1,0:T(8,128)S(1)} %get-tuple-element.43.sum_ref, f32[48,640]{1,0:T(8,128)S(1)} %get-tuple-element.44.total_ref, ...), custom_call_target="tpu_custom_call" | custom-call | tf_op jit(solution)/shard_map/first/pallas_call | solution.py:503
  17.9 2.0 %collective-permute-start.7 = (bf16[48,1280]{1,0:T(8,128)(2,1)S(1)}, bf16[48,1280]{1,0:T(8,128)(2,1)S(1)}, u32[]{:S(2)}, u32[]{:S(2)}) collective-permute-start(bf16[48,1280]{1,0:T(8,128)(2,1)S(1)} %get-tuple-element.45), channel_id=1, source_target_pairs={{0,1},{1,0},{2,3},{3,2},{4,5},{5,4},{6,7},{7,6},{8,9},{9,8},{10,11... | collective-permute-start | bytes 368648 | tf_op jit(solution)/shard_map/ppermute | solution.py:511
  19.9 0.5 %rest.1 = bf16[48,1152]{1,0:T(8,128)(2,1)S(1)} custom-call(bf16[48,640]{1,0:T(8,128)(2,1)S(1)} %get-tuple-element.47.attended_ref, bf16[1216,640]{1,0:T(8,128)(2,1)S(1)} %bitcast.7, bf16[1216,640]{1,0:T(8,128)(2,1)S(1)} %collective-permute-done.5.theirs_ref.refs_9_), custom_call_target="tpu_custom_call" | custom-call | tf_op jit(solution)/shard_map/rest/pallas_call | solution.py:512
  20.5 0.1 collective-permute-start.11
  20.6 0.0 collective-permute-done.8.refs_0_
  20.6 2.0 %second.1 = (bf16[48,2432]{1,0:T(8,128)(2,1)S(1)}, bf16[96,640]{1,0:T(8,128)(2,1)S(1)}) custom-call(bf16[96,640]{1,0:T(8,128)(2,1)S(1)} %collective-permute-done.8.refs_0_, f32[3,64]{1,0:T(4,128)S(1)} %get-tuple-element.36.gains.refs_1_, bf16[192,640]{1,0:T(8,128)(2,1)S(1)} %get-tuple-element.32.refs_1_.refs_0_.refs_2_, ...), custom_call_target="tpu_custom_call" | custom-call | tf_op jit(solution)/shard_map/second/pallas_call | solution.py:522
  22.7 2.0 %collective-permute-start.10 = (bf16[48,2432]{1,0:T(8,128)(2,1)S(1)}, bf16[48,2432]{1,0:T(8,128)(2,1)S(1)}, u32[]{:S(2)}, u32[]{:S(2)}) collective-permute-start(bf16[48,2432]{1,0:T(8,128)(2,1)S(1)} %get-tuple-element.51), channel_id=1, source_target_pairs={{0,1},{1,0},{2,3},{3,2},{4,5},{5,4},{6,7},{7,6},{8,9},{9,8},{10,11... | collective-permute-start | bytes 700424 | tf_op jit(solution)/shard_map/ppermute | solution.py:538
  24.7 1.0 %third.1 = bf16[48,2432]{1,0:T(8,128)(2,1)S(1)} custom-call(bf16[96,640]{1,0:T(8,128)(2,1)S(1)} %get-tuple-element.49.attended_ref, bf16[1216,640]{1,0:T(8,128)(2,1)S(1)} %bitcast.9, bf16[1216,640]{1,0:T(8,128)(2,1)S(1)} %collective-permute-done.5.theirs_ref.refs_9_), custom_call_target="tpu_custom_call" | custom-call | tf_op jit(solution)/shard_map/third/pallas_call | solution.py:530
  25.7 0.1 collective-permute-start.9
  25.8 0.0 collective-permute-done.7.first_ref
  25.9 1.9 %own.1.mixed_ref = f32[144,2432]{1,0:T(8,128)S(1)} custom-call(bf16[144,640]{1,0:T(8,128)(2,1)S(1)} %get-tuple-element.30.refs_0_.q_ref, bf16[288,640]{1,0:T(8,128)(2,1)S(1)} %norm.1.refs_4_.got_ref.refs_6_, bf16[288,640]{1,0:T(8,128)(2,1)S(1)} %collective-permute-done.4.last_ref.refs_7_, f32[144,640]{1,0:T(8,128)S(1)} %get-tuple-element.37.sum_ref, ...), custom_call_target="tpu_custom_call" | custom-call | tf_op jit(solution)/shard_map/own/pallas_call | solution.py:539
  27.8 0.0 collective-permute-done.11.rest_ref
  27.8 0.6 %final.3 = (f32[24,384]{1,0:T(8,128)S(1)}, f32[24,384]{1,0:T(8,128)S(1)}) custom-call(f32[1,384]{1,0:T(1,128)S(1)} %get-tuple-element.29.euler_ref, f32[144,2432]{1,0:T(8,128)S(1)} %own.1.mixed_ref, bf16[48,1152]{1,0:T(8,128)(2,1)S(1)} %collective-permute-done.11.rest_ref, f32[3,2432]{1,0:T(4,128)S(1)} %get-tuple-element.40.mod_ref, ...), custom_call_target="tpu_custom_call" | custom-call | flops 2000000000 | bytes 6000000 | tf_op jit(solution)/shard_map/final/pallas_call | solution.py:552
  28.4 3.1 %collective-permute-done.10.rest_ref = bf16[48,2432]{1,0:T(8,128)(2,1)S(1)} collective-permute-done((bf16[48,2432]{1,0:T(8,128)(2,1)S(1)}, bf16[48,2432]{1,0:T(8,128)(2,1)S(1)}, u32[]{:S(2)}, u32[]{:S(2)}) %collective-permute-start.10) | collective-permute-done | bytes 233504 | tf_op jit(solution)/shard_map/ppermute | solution.py:538
  31.5 0.6 %final.4 = (f32[24,384]{1,0:T(8,128)S(1)}, f32[24,384]{1,0:T(8,128)S(1)}) custom-call(f32[1,384]{1,0:T(1,128)S(1)} %get-tuple-element.29.euler_ref, f32[144,2432]{1,0:T(8,128)S(1)} %own.1.mixed_ref, bf16[48,2432]{1,0:T(8,128)(2,1)S(1)} %collective-permute-done.10.rest_ref, f32[3,2432]{1,0:T(4,128)S(1)} %get-tuple-element.40.mod_ref, ...), custom_call_target="tpu_custom_call" | custom-call | flops 30000001024 | bytes 90000000 | tf_op jit(solution)/shard_map/final/pallas_call | solution.py:552
  32.1 3.7 %collective-permute-done.9.rest_ref = bf16[48,2432]{1,0:T(8,128)(2,1)S(1)} collective-permute-done((bf16[48,2432]{1,0:T(8,128)(2,1)S(1)}, bf16[48,2432]{1,0:T(8,128)(2,1)S(1)}, u32[]{:S(2)}, u32[]{:S(2)}) %collective-permute-start.9) | collective-permute-done | bytes 233504 | tf_op jit(solution)/shard_map/ppermute | solution.py:538
  35.7 1.2 %final.5 = (f32[24,384]{1,0:T(8,128)}, f32[24,384]{1,0:T(8,128)}) custom-call(f32[1,384]{1,0:T(1,128)S(1)} %get-tuple-element.29.euler_ref, f32[144,2432]{1,0:T(8,128)S(1)} %own.1.mixed_ref, bf16[48,2432]{1,0:T(8,128)(2,1)S(1)} %collective-permute-done.9.rest_ref, f32[3,2432]{1,0:T(4,128)S(1)} %get-tuple-element.40.mod_ref, ...), custom_call_target="tpu_custom_call" | custom-call | tf_op jit(solution)/shard_map/final/pallas_call | solution.py:552
  (8 shorter events, 0.0 us)
Async XLA Ops:
  0.6 5.8 %copy-start.6 = (f32[64]{0:T(128)S(1)}, f32[64]{0:T(128)}, u32[]{:S(2)}) copy-start(f32[64]{0:T(128)} %param.16) | copy-start | bytes 772
  0.6 5.8 %copy-start.7 = (f32[64]{0:T(128)S(1)}, f32[64]{0:T(128)}, u32[]{:S(2)}) copy-start(f32[64]{0:T(128)} %param.15) | copy-start | bytes 772
  0.7 5.8 %copy-start.8 = (f32[64]{0:T(128)S(1)}, f32[64]{0:T(128)}, u32[]{:S(2)}) copy-start(f32[64]{0:T(128)} %param.14) | copy-start | bytes 772
  0.7 5.9 %copy-start.3 = (bf16[48,2,640]{2,1,0:T(2,128)(2,1)S(1)}, bf16[48,2,640]{2,1,0:T(2,128)(2,1)}, u32[]{:S(2)}) copy-start(bf16[48,2,640]{2,1,0:T(2,128)(2,1)} %text_ref.1) | copy-start | bytes 368644
  0.7 16.2 %collective-permute-start.5 = (bf16[1216,640]{1,0:T(8,128)(2,1)}, bf16[1216,640]{1,0:T(8,128)(2,1)S(1)}, u32[]{:S(2)}, u32[]{:S(2)}) collective-permute-start(bf16[1216,640]{1,0:T(8,128)(2,1)} %bitcast.5), channel_id=1, source_target_pairs={{0,2},{2,0},{1,3},{3,1},{4,6},{6,4},{5,7},{7,5},{8,10},{10,8},{9,1... | collective-permute-start | bytes 4669448 | tf_op jit(solution)/shard_map/ppermute | solution.py:447
  1.2 8.0 %copy-start.2 = (bf16[64,1216]{1,0:T(8,128)(2,1)S(1)}, bf16[64,1216]{1,0:T(8,128)(2,1)}, u32[]{:S(2)}) copy-start(bf16[64,1216]{1,0:T(8,128)(2,1)} %refs_8_.1) | copy-start | bytes 466948
  1.2 9.7 %copy-start.1 = (bf16[12,12,2432]{2,1,0:T(8,128)(2,1)S(1)}, bf16[12,12,2432]{2,1,0:T(8,128)(2,1)}, u32[]{:S(2)}) copy-start(bf16[12,12,2432]{2,1,0:T(8,128)(2,1)} %refs_6_.1) | copy-start | bytes 2101252
  1.2 9.7 %copy-start.4 = (f32[3,2432]{1,0:T(4,128)S(1)}, f32[3,2432]{1,0:T(4,128)}, u32[]{:S(2)}) copy-start(f32[3,2432]{1,0:T(4,128)} %refs_7_.1) | copy-start | bytes 87556
  2.5 12.1 %collective-permute-start = (bf16[288,640]{1,0:T(8,128)(2,1)S(1)}, bf16[288,640]{1,0:T(8,128)(2,1)S(1)}, u32[]{:S(2)}, u32[]{:S(2)}) collective-permute-start(bf16[288,640]{1,0:T(8,128)(2,1)S(1)} %get-tuple-element.31), channel_id=1, source_target_pairs={{0,1},{1,0},{2,3},{3,2},{4,5},{5,4},{6,7},{7,6},{8,9},{9,8},{10,11... | collective-permute-start | bytes 1105928 | tf_op jit(solution)/shard_map/ppermute | solution.py:492
  8.6 2.3 %collective-permute-start.1 = (bf16[192,640]{1,0:T(8,128)(2,1)S(1)}, bf16[192,640]{1,0:T(8,128)(2,1)S(1)}, u32[]{:S(2)}, u32[]{:S(2)}) collective-permute-start(bf16[192,640]{1,0:T(8,128)(2,1)S(1)} %get-tuple-element.32.refs_1_.refs_0_.refs_2_), channel_id=1, source_target_pairs={{0,2},{2,0},{1,3},{3,1},{4,6},{6,4},{5,7},{7,5},{8,10},{10,8},{9,1... | collective-permute-start | bytes 737288 | tf_op jit(solution)/shard_map/ppermute | solution.py:465
  8.8 2.0 %collective-permute-start.2 = (bf16[192,640]{1,0:T(8,128)(2,1)S(1)}, bf16[192,640]{1,0:T(8,128)(2,1)S(1)}, u32[]{:S(2)}, u32[]{:S(2)}) collective-permute-start(bf16[192,640]{1,0:T(8,128)(2,1)S(1)} %get-tuple-element.33.refs_2_.refs_1_.refs_3_), channel_id=1, source_target_pairs={{0,2},{2,0},{1,3},{3,1},{4,6},{6,4},{5,7},{7,5},{8,10},{10,8},{9,1... | collective-permute-start | bytes 737288 | tf_op jit(solution)/shard_map/ppermute | solution.py:465
  9.2 1.6 %collective-permute-start.3 = (bf16[64,1216]{1,0:T(8,128)(2,1)S(1)}, bf16[64,1216]{1,0:T(8,128)(2,1)S(1)}, u32[]{:S(2)}, u32[]{:S(2)}) collective-permute-start(bf16[64,1216]{1,0:T(8,128)(2,1)S(1)} %copy-done.2), channel_id=1, source_target_pairs={{0,2},{2,0},{1,3},{3,1},{4,6},{6,4},{5,7},{7,5},{8,10},{10,8},{9,1... | collective-permute-start | bytes 466952 | tf_op jit(solution)/shard_map/ppermute | solution.py:448
  10.7 5.2 %collective-permute-start.6 = (bf16[48,640]{1,0:T(8,128)(2,1)S(1)}, bf16[48,640]{1,0:T(8,128)(2,1)S(1)}, u32[]{:S(2)}, u32[]{:S(2)}) collective-permute-start(bf16[48,640]{1,0:T(8,128)(2,1)S(1)} %get-tuple-element.41), channel_id=1, source_target_pairs={{0,1},{1,0},{2,3},{3,2},{4,5},{5,4},{6,7},{7,6},{8,9},{9,8},{10,11... | collective-permute-start | bytes 184328 | tf_op jit(solution)/shard_map/ppermute | solution.py:484
  11.9 8.7 %collective-permute-start.8 = (bf16[96,640]{1,0:T(8,128)(2,1)S(1)}, bf16[96,640]{1,0:T(8,128)(2,1)S(1)}, u32[]{:S(2)}, u32[]{:S(2)}) collective-permute-start(bf16[96,640]{1,0:T(8,128)(2,1)S(1)} %get-tuple-element.46), channel_id=1, source_target_pairs={{0,1},{1,0},{2,3},{3,2},{4,5},{5,4},{6,7},{7,6},{8,9},{9,8},{10,11... | collective-permute-start | bytes 368648 | tf_op jit(solution)/shard_map/ppermute | solution.py:484
  14.9 1.9 %copy-start = (bf16[640,1216]{0,1:T(8,128)(2,1)S(1)}, bf16[640,1216]{0,1:T(8,128)(2,1)}, u32[]{:S(2)}) copy-start(bf16[640,1216]{0,1:T(8,128)(2,1)} %param.17) | copy-start | bytes 4669444
  14.9 1.9 %collective-permute-start.4 = (bf16[288,640]{1,0:T(8,128)(2,1)S(1)}, bf16[288,640]{1,0:T(8,128)(2,1)S(1)}, u32[]{:S(2)}, u32[]{:S(2)}) collective-permute-start(bf16[288,640]{1,0:T(8,128)(2,1)S(1)} %norm.1.refs_4_.got_ref.refs_6_), channel_id=1, source_target_pairs={{0,2},{2,0},{1,3},{3,1},{4,6},{6,4},{5,7},{7,5},{8,10},{10,8},{9,1... | collective-permute-start | bytes 1105928 | tf_op jit(solution)/shard_map/ppermute | solution.py:493
  17.9 7.9 %collective-permute-start.7 = (bf16[48,1280]{1,0:T(8,128)(2,1)S(1)}, bf16[48,1280]{1,0:T(8,128)(2,1)S(1)}, u32[]{:S(2)}, u32[]{:S(2)}) collective-permute-start(bf16[48,1280]{1,0:T(8,128)(2,1)S(1)} %get-tuple-element.45), channel_id=1, source_target_pairs={{0,1},{1,0},{2,3},{3,2},{4,5},{5,4},{6,7},{7,6},{8,9},{9,8},{10,11... | collective-permute-start | bytes 368648 | tf_op jit(solution)/shard_map/ppermute | solution.py:511
  20.5 7.3 %collective-permute-start.11 = (bf16[48,1152]{1,0:T(8,128)(2,1)S(1)}, bf16[48,1152]{1,0:T(8,128)(2,1)S(1)}, u32[]{:S(2)}, u32[]{:S(2)}) collective-permute-start(bf16[48,1152]{1,0:T(8,128)(2,1)S(1)} %rest.1), channel_id=1, source_target_pairs={{0,1},{1,0},{2,3},{3,2},{4,5},{5,4},{6,7},{7,6},{8,9},{9,8},{10,11... | collective-permute-start | bytes 331784 | tf_op jit(solution)/shard_map/ppermute | solution.py:520
  22.7 8.8 %collective-permute-start.10 = (bf16[48,2432]{1,0:T(8,128)(2,1)S(1)}, bf16[48,2432]{1,0:T(8,128)(2,1)S(1)}, u32[]{:S(2)}, u32[]{:S(2)}) collective-permute-start(bf16[48,2432]{1,0:T(8,128)(2,1)S(1)} %get-tuple-element.51), channel_id=1, source_target_pairs={{0,1},{1,0},{2,3},{3,2},{4,5},{5,4},{6,7},{7,6},{8,9},{9,8},{10,11... | collective-permute-start | bytes 700424 | tf_op jit(solution)/shard_map/ppermute | solution.py:538
  25.7 10.0 %collective-permute-start.9 = (bf16[48,2432]{1,0:T(8,128)(2,1)S(1)}, bf16[48,2432]{1,0:T(8,128)(2,1)S(1)}, u32[]{:S(2)}, u32[]{:S(2)}) collective-permute-start(bf16[48,2432]{1,0:T(8,128)(2,1)S(1)} %third.1), channel_id=1, source_target_pairs={{0,1},{1,0},{2,3},{3,2},{4,5},{5,4},{6,7},{7,6},{8,9},{9,8},{10,11... | collective-permute-start | bytes 700424 | tf_op jit(solution)/shard_map/ppermute | solution.py:538
  25.8 1.9 %copy-start.5 = (f32[24,384]{1,0:T(8,128)S(1)}, f32[24,384]{1,0:T(8,128)}, u32[]{:S(2)}) copy-start(f32[24,384]{1,0:T(8,128)} %latent_ref.5) | copy-start | bytes 110596
